TPU v7x, 32 devices: a whole 2x2x4 slice. The times are simulated.
32 devices in a mesh: tok: 4 (over z), hid: 8 (over y, x, core).
Axes of the slice: x: 2, y: 2, z: 4, core: 2. Of those that a mesh axis runs over, the one named last changes fastest.
Arguments:
- resid_in: bfloat16 [128, 8192], P('hid', 'tok'), may hold values from -64 to 64
- norm_gain: float32 [8192], P('tok'), may hold values from 0.1 to 1.9
- gate_weight: bfloat16 [8192, 28672], P('tok', 'hid'), may hold values from -0.0625 to 0.0625
- up_weight: bfloat16 [8192, 28672], P('tok', 'hid'), may hold values from -0.0625 to 0.0625
- down_weight: bfloat16 [28672, 8192], P('hid', 'tok'), may hold values from -0.046875 to 0.046875
- labels: int32 [128], replicated, may hold values from 0 to 63
Outputs:
- gram: float32 [8192, 8192], P(('tok', 'hid'))
- cross: float32 [8192, 64], P(('tok', 'hid'))
All inputs are finite; a program needn't handle non-finite values.
Results may differ from a plain program's by a relative error of at most 0.014.
Values may be sent and summed in bfloat16 or wider, within the bound.
No kernel may reach another device: no remote copies, remote signals or barrier semaphores. Data moves between devices by JAX's collectives and lax.ppermute only.
A program may use at most 128 MiB of HBM per device.

v0:
```python
import jax
import jax.numpy as jnp
from jax import lax
from jax.sharding import PartitionSpec as P

D = 8192
CLASSES = 64


def on_device(resid_in, norm_gain, gate_weight, up_weight, down_weight, labels):
    gathered = lax.all_gather(resid_in, "hid", axis=0, tiled=True)
    xf = gathered.astype(jnp.float32)
    local_sq = jnp.sum(xf * xf, axis=1)
    total_sq = lax.psum(local_sq, "tok")
    scale_rows = lax.rsqrt(total_sq / float(D) + 1e-05)
    normed = (xf * scale_rows[:, None] * norm_gain[None, :]).astype(jnp.bfloat16)
    both_weights = jnp.concatenate([gate_weight, up_weight], axis=1)
    shard_ff = gate_weight.shape[1]
    paired = lax.psum_scatter(
        jnp.dot(normed, both_weights, preferred_element_type=jnp.float32).astype(jnp.bfloat16),
        "tok",
        scatter_dimension=0,
        tiled=True,
    ).astype(jnp.float32)
    hidden = (jax.nn.silu(paired[:, :shard_ff]) * paired[:, shard_ff:]).astype(jnp.bfloat16)
    partial_out = jnp.dot(
        lax.all_gather(hidden, "tok", axis=0, tiled=True),
        down_weight,
        preferred_element_type=jnp.float32,
    )
    ntok = xf.shape[0]
    panel = xf.shape[1] // lax.axis_size("hid")
    offset = lax.axis_index("hid") * panel
    summed = lax.psum_scatter(
        partial_out.astype(jnp.bfloat16), "hid", scatter_dimension=1, tiled=True
    ).astype(jnp.float32)
    x_cols = lax.dynamic_slice_in_dim(xf, offset, panel, 1)
    resid_cols = (x_cols + summed).astype(jnp.bfloat16)
    prod = lax.dot_general(
        resid_cols,
        lax.all_gather(resid_cols, ("tok", "hid"), axis=1, tiled=True),
        (((0,), (0,)), ((), ())),
        preferred_element_type=jnp.float32,
    )
    gram = prod / float(ntok)
    onehot = (labels[:, None] == jnp.arange(CLASSES, dtype=jnp.int32)[None, :]).astype(jnp.bfloat16)
    counts = jnp.sum(onehot.astype(jnp.float32), axis=0)
    class_sums = lax.dot_general(
        resid_cols, onehot, (((0,), (0,)), ((), ())), preferred_element_type=jnp.float32
    )
    cross = class_sums / jnp.maximum(counts, 1.0)[None, :]
    return (gram, cross)


def solution(mesh):
    return jax.shard_map(
        on_device,
        mesh=mesh,
        in_specs=(
            P("hid", "tok"),
            P("tok"),
            P("tok", "hid"),
            P("tok", "hid"),
            P("hid", "tok"),
            P(),
        ),
        out_specs=(P(("tok", "hid"), None), P(("tok", "hid"), None)),
        check_vma=False,
    )
```

profile of v0, /device:TPU:0, one launch (start us, length us, event | category | flops | bytes accessed | tf_op | source)
XLA Modules:
  0.0 215.8 jit_solution(10918161253458267836)
XLA Ops:
  7.2 0.0 reduce-scatter.3.cloned.1.call-start
  7.2 11.6 %all_gather.9 = bf16[128,2048]{1,0:T(8,128)(2,1)S(1)} all-gather(bf16[16,2048]{1,0:T(8,128)(2,1)} %param.6), channel_id=1, replica_groups=mesh['tok'=4,'hid'=8] {'hid'}, dimensions={0}, use_global_device_ids=true | all-gather | bytes 589824 | tf_op jit(solution)/shard_map/all_gather | solution.py:11
  18.8 0.2 multiply_reduce_fusion
  19.0 12.0 %psum.7 = f32[128]{0:T(128)S(1)} all-reduce(f32[128]{0:T(128)S(1)} %multiply_reduce_fusion), channel_id=1, replica_groups=mesh['tok'=4,'hid'=8] {'tok'}, use_global_device_ids=true, to_apply=%region_1.0 | all-reduce | flops 128 | bytes 1024 | tf_op jit(solution)/shard_map/psum | solution.py:14
  31.0 12.5 %fusion.4 = bf16[128,7168]{1,0:T(8,128)(2,1)} fusion(bf16[2048,3584]{1,0:T(8,128)(2,1)} %param.9, bf16[2048,3584]{1,0:T(8,128)(2,1)} %param.8, f32[2048]{0:T(1024)} %param.7, f32[128]{0:T(128)S(1)} %add_rsqrt_fusion, bf16[128,2048]{1,0:T(8,128)(2,1)S(1)} %all_gather.9), kind=kOutput, calls=%fused_computation.5 | convolution fusion | flops 3818782720 | bytes 31728128 | tf_op jit(solution)/shard_map/dot_general | solution.py:20
  43.5 0.0 reduce-scatter.3.cloned.1.call-update
  43.5 0.0 copy-start
  43.5 0.0 reduce-scatter.5.cloned.1.call-start
  43.5 36.7 %reduce-scatter.3.cloned.1.call-done = bf16[32,7168]{1,0:T(8,128)(2,1)} async-done(((bf16[128,7168]{1,0:T(8,128)(2,1)}), bf16[32,7168]{1,0:T(8,128)(2,1)}) %reduce-scatter.3.cloned.1.call-update) | async-done | bytes 458768 | tf_op jit(solution)/shard_map/reduce_scatter | solution.py:19
  80.3 1.1 convert_element_type.33
  81.4 0.1 fusion.10
  81.5 19.4 %all_gather.10 = bf16[128,3584]{1,0:T(8,128)(2,1)S(1)} all-gather(bf16[32,3584]{1,0:T(8,128)(2,1)S(1)} %fusion.10), channel_id=1, replica_groups=mesh['tok'=4,'hid'=8] {'tok'}, dimensions={0}, use_global_device_ids=true | all-gather | bytes 1146880 | tf_op jit(solution)/shard_map/all_gather | solution.py:27
  100.9 8.3 %convolution_convert_fusion = bf16[128,2048]{1,0:T(8,128)(2,1)} fusion(bf16[128,3584]{1,0:T(8,128)(2,1)S(1)} %all_gather.10, bf16[3584,2048]{1,0:T(8,128)(2,1)} %param.10), kind=kOutput, calls=%fused_computation.6 | convolution fusion | flops 1879310336 | bytes 16121856 | tf_op jit(solution)/shard_map/dot_general | solution.py:26
  109.2 0.0 reduce-scatter.5.cloned.1.call-update
  109.2 0.0 all-gather.2.cloned.1.call-start
  109.3 0.1 convert_element_type.30
  109.4 33.6 %reduce-scatter.5.cloned.1.call-done = bf16[128,256]{1,0:T(8,128)(2,1)} async-done(((bf16[128,2048]{1,0:T(8,128)(2,1)}), bf16[128,256]{1,0:T(8,128)(2,1)}) %reduce-scatter.5.cloned.1.call-update) | async-done | bytes 65552 | tf_op jit(solution)/shard_map/reduce_scatter | solution.py:34
  143.0 1.5 add_convert_fusion
  144.4 0.0 all-gather.2.cloned.1.call-update
  144.5 0.0 copy-done
  144.5 0.1 convert_reduce_fusion
  144.6 1.6 convolution_divide_fusion
  146.2 56.8 %all-gather.2.cloned.1.call-done = bf16[128,8192]{1,0:T(8,128)(2,1)} async-done(((bf16[128,256]{1,0:T(8,128)(2,1)}), bf16[128,8192]{1,0:T(8,128)(2,1)}) %all-gather.2.cloned.1.call-update) | async-done | bytes 2097168 | tf_op jit(solution)/shard_map/all_gather | solution.py:41
  203.0 6.3 %convolution_multiply_fusion = f32[256,8192]{1,0:T(8,128)} fusion(bf16[128,256]{1,0:T(8,128)(2,1)} %add_convert_fusion, bf16[128,8192]{1,0:T(8,128)(2,1)} %all-gather.2.cloned.1.call-done), kind=kOutput, calls=%fused_computation.4 | convolution fusion | flops 538968064 | bytes 10551296 | tf_op jit(solution)/shard_map/dot_general | solution.py:39
  (2 shorter events, 0.0 us)
Async XLA Ops:
  7.2 73.1 %reduce-scatter.3.cloned.1.call-start = ((), (), s32[]{:S(2)}) async-start(), calls=%async_computation.2 | async-start | bytes 2293760 | tf_op jit(solution)/shard_map/reduce_scatter | solution.py:19
  43.5 101.0 %copy-start = (s32[128]{0:T(128)S(1)}, s32[128]{0:T(128)}, u32[]{:S(2)}) copy-start(s32[128]{0:T(128)} %param.11) | copy-start | bytes 1540
  43.5 99.5 %reduce-scatter.5.cloned.1.call-start = ((), (), s32[]{:S(2)}) async-start(), calls=%async_computation.3 | async-start | bytes 589824 | tf_op jit(solution)/shard_map/reduce_scatter | solution.py:34
  109.2 93.8 %all-gather.2.cloned.1.call-start = ((), (), s32[]{:S(2)}) async-start(), calls=%async_computation.4 | async-start | bytes 2162688 | tf_op jit(solution)/shard_map/all_gather | solution.py:41
Sparse Core Ops, SparseCore 0:
  43.6 36.6 reduce-scatter.2
  109.3 33.5 reduce-scatter.4
  146.3 56.6 all-gather.1
where the time goes:
time: 216 us
  waiting for transfers between devices  127 us (59%)
  blocking collectives  42.9 us (20%)
  matrix products  28.7 us (13%)
  between operations  13.8 us (6%)
  other arithmetic  3.08 us (1%)
    all_gather x1, waiting for transfers between devices, on_device(): lax.all_gather(resid_cols, ('tok', 'hid'), axis=1, tiled=True)  56.8 us
    reduce_scatter x1, waiting for transfers between devices, on_device(): lax.psum_scatter(jnp.dot(normed, both_weights, preferred_element_type=jnp...  36.7 us
    reduce_scatter x1, waiting for transfers between devices, on_device(): lax.psum_scatter(partial_out.astype(jnp.bfloat16), 'hid', scatter_dimensi...  33.6 us
    all_gather x1, blocking collectives, on_device(): lax.all_gather(hidden, 'tok', axis=0, tiled=True)  19.4 us
    dot_general x1, matrix products, on_device(): jnp.dot(normed, both_weights, preferred_element_type=jnp.float32)  12.5 us
    psum x1, blocking collectives, on_device(): total_sq = lax.psum(local_sq, 'tok')  12 us
    all_gather x1, blocking collectives, on_device(): gathered = lax.all_gather(resid_in, 'hid', axis=0, tiled=True)  11.6 us
    dot_general x1, matrix products, on_device(): jnp.dot(lax.all_gather(hidden, 'tok', axis=0, tiled=True), down_weight, p...  8.32 us
  transfers between devices with their start and end apart: 3, of which 3 were waited for; matrix products, arithmetic and copies ran while one was open for 1% of the time, Pallas kernels for 0%

commit v1 on v0

v1 whole, which is shorter than its diff:
```python
import functools
import jax
import jax.numpy as jnp
from jax import lax
from jax.experimental import pallas as pl
from jax.experimental.pallas import tpu as pltpu
from jax.sharding import PartitionSpec as P

D = 8192
CLASSES = 64
BF16 = jnp.bfloat16
F32 = jnp.float32


def swap(value, axis, size, mask):
    return lax.ppermute(value, axis, [(i, i ^ mask) for i in range(size)])


def pick(cases, key):
    out = cases[-1][1]
    for number, value in reversed(cases[:-1]):
        out = jnp.where(key == number, value, out)
    return out


def gather_tokens(own, h, n_hid):
    chips = n_hid // 2
    rows = own.shape[0]
    near = [own] + [swap(own, "hid", n_hid, 2 * e) for e in range(1, chips)]
    near = jnp.concatenate(near, axis=0)
    far = swap(near, "hid", n_hid, 1)
    both = jnp.concatenate([near, far], axis=0)
    ntok = both.shape[0]
    place = jnp.arange(ntok, dtype=jnp.int32)
    slot = place // rows
    owner = h ^ (2 * (slot % chips) + slot // chips)
    token = owner * rows + place % rows
    order = (jnp.arange(ntok, dtype=jnp.int32)[:, None] == token[None, :]).astype(BF16)
    return jnp.dot(order, both, preferred_element_type=F32)


def chain_sums(parts, rows, dist, n_tok, to_end):
    count = len(parts)
    sums = []
    got = None
    for t in range(count + n_tok - 1):
        cases = [(j, parts[t - j][rows]) for j in range(n_tok) if 0 <= t - j < count]
        value = pick(cases, dist).astype(F32)
        if got is not None:
            value = value + got.astype(F32)
        if t >= n_tok - 1:
            sums.append(value)
        if t <= count + n_tok - 3:
            pairs = [(to_end(j), to_end(j + 1)) for j in range(n_tok - 1) if 0 <= t - j < count]
            got = lax.ppermute(value.astype(BF16), "tok", pairs)
    return sums


def chain_copies(blocks, dist, n_tok, to_end):
    count = len(blocks)
    got = []
    for s in range(count + n_tok - 2):
        cases = []
        if s < count:
            cases.append((0, blocks[s]))
        if s > 0:
            cases.append((1, got[s - 1]))
        value = blocks[s] if s == 0 else (jnp.where(dist == 0, blocks[s], got[s - 1]) if s < count else got[s - 1])
        pairs = [(to_end(j), to_end(j + 1)) for j in range(n_tok - 1) if 0 <= s - j < count]
        got.append(lax.ppermute(value, "tok", pairs))
    return [
        pick([(0, blocks[k])] + [(j, got[k + j - 1]) for j in range(1, n_tok)], dist)
        for k in range(count)
    ]


def gram_kernel(n_hid, n_tok, ntok, own_ref, *refs):
    chips = n_hid // 2
    groups, (out_ref, tiles, sems) = refs[:-3], refs[-3:]
    z = lax.axis_index("tok")
    h = lax.axis_index("hid")
    width = own_ref.shape[1]
    left = own_ref[...].T
    copies = []
    for number, (zmask, hmask, ref, at) in enumerate(slots_of(groups, chips, n_tok)):
        tiles[number] = jnp.dot(left, ref[at], preferred_element_type=F32) * (1.0 / ntok)
        column = ((z ^ zmask) * n_hid + (h ^ hmask)) * width
        copy = pltpu.make_async_copy(
            tiles.at[number], out_ref.at[:, pl.ds(pl.multiple_of(column, width), width)], sems.at[number]
        )
        copy.start()
        copies.append(copy)
    for copy in copies:
        copy.wait()


def slots_of(groups, chips, n_tok):
    for core in range(2):
        for e in range(chips):
            yield 0, 2 * e + core, groups[core], e
    for core in range(2):
        for e in range(chips):
            for d in range(1, n_tok):
                yield d, 2 * e + core, groups[2 + core], e * (n_tok - 1) + d - 1


def gram_of(resid_cols, n_tok, n_hid):
    chips = n_hid // 2
    ntok, width = resid_cols.shape
    line = jnp.stack([swap(resid_cols, "tok", n_tok, d) for d in range(1, n_tok)])
    plane = jnp.stack([resid_cols] + [swap(resid_cols, "hid", n_hid, 2 * e) for e in range(1, chips)])
    plane_far = swap(plane, "hid", n_hid, 1)
    lines = jnp.concatenate([line] + [swap(line, "hid", n_hid, 2 * e) for e in range(1, chips)], axis=0)
    lines_far = swap(lines, "hid", n_hid, 1)
    vmem = pl.BlockSpec(memory_space=pltpu.VMEM)
    blocks = n_tok * n_hid
    return pl.pallas_call(
        functools.partial(gram_kernel, n_hid, n_tok, ntok),
        out_shape=jax.ShapeDtypeStruct((width, width * blocks), F32),
        in_specs=[vmem] * 5,
        out_specs=pl.BlockSpec(memory_space=pl.ANY),
        scratch_shapes=[pltpu.VMEM((blocks, width, width), F32), pltpu.SemaphoreType.DMA((blocks,))],
        compiler_params=pltpu.CompilerParams(vmem_limit_bytes=32 * 1024 * 1024),
        cost_estimate=pl.CostEstimate(
            flops=2 * ntok * width * width * blocks,
            bytes_accessed=4 * width * width * blocks,
            transcendentals=0,
        ),
        name="gram",
    )(resid_cols, plane, plane_far, lines, lines_far)


def on_device(n_tok, n_hid, resid_in, norm_gain, gate_weight, up_weight, down_weight, labels):
    z = lax.axis_index("tok")
    h = lax.axis_index("hid")
    core = h % 2
    chip = h // 2
    chips = n_hid // 2

    x = gather_tokens(resid_in, h, n_hid)
    ntok, block = x.shape
    half = ntok // 2
    total_sq = jnp.sum(x * x, axis=1, keepdims=True)
    d = 1
    while d < n_tok:
        total_sq = total_sq + swap(total_sq, "tok", n_tok, d)
        d *= 2
    scale_rows = lax.rsqrt(total_sq / float(D) + 1e-05)
    lhs = (x * norm_gain[None, :]).astype(BF16)

    shard_ff = gate_weight.shape[1]
    count = 4
    wide = shard_ff // count
    parts = []
    for k in range(count):
        cols = slice(k * wide, (k + 1) * wide)
        weights = jnp.concatenate([gate_weight[:, cols], up_weight[:, cols]], axis=1)
        parts.append(jnp.dot(lhs, weights, preferred_element_type=F32).astype(BF16))

    first, second = slice(0, half), slice(half, ntok)
    down_line, up_line = (lambda j: n_tok - 1 - j), (lambda j: j)
    sums_a = chain_sums(parts, first, n_tok - 1 - z, n_tok, down_line)
    sums_b = chain_sums(parts, second, z, n_tok, up_line)

    def hidden_of(sums, scale):
        both = sums * scale
        return (jax.nn.silu(both[:, :wide]) * both[:, wide:]).astype(BF16)

    hidden_a = chain_copies([hidden_of(s, scale_rows[first]) for s in sums_a], z, n_tok, up_line)
    hidden_b = chain_copies([hidden_of(s, scale_rows[second]) for s in sums_b], n_tok - 1 - z, n_tok, down_line)

    partial_out = None
    for k in range(count):
        rows = jnp.concatenate([hidden_a[k], hidden_b[k]], axis=0)
        term = jnp.dot(rows, down_weight[k * wide:(k + 1) * wide], preferred_element_type=F32)
        partial_out = term if partial_out is None else partial_out + term

    panel = block // n_hid
    by_panel = partial_out.reshape(ntok, chips, 2, panel)
    mine = jnp.where(core == 0, by_panel[:, :, 0], by_panel[:, :, 1]).reshape(ntok, chips * panel)
    other = jnp.where(core == 0, by_panel[:, :, 1], by_panel[:, :, 0]).reshape(ntok, chips * panel)
    chip_sum = mine + swap(other.astype(BF16), "hid", n_hid, 1).astype(F32)

    def panel_for(mask):
        return lax.dynamic_slice_in_dim(chip_sum, (chip ^ mask) * panel, panel, 1)

    summed = panel_for(0)
    for e in range(1, chips):
        summed = summed + swap(panel_for(e).astype(BF16), "hid", n_hid, 2 * e).astype(F32)
    x_cols = lax.dynamic_slice_in_dim(x, h * panel, panel, 1)
    resid_cols = (x_cols + summed).astype(BF16)

    if panel % 128 == 0:
        gram = gram_of(resid_cols, n_tok, n_hid)
    else:
        everyone = lax.all_gather(resid_cols, ("tok", "hid"), axis=1, tiled=True)
        gram = lax.dot_general(
            resid_cols, everyone, (((0,), (0,)), ((), ())), preferred_element_type=F32
        ) / float(ntok)

    onehot = (labels[:, None] == jnp.arange(CLASSES, dtype=jnp.int32)[None, :]).astype(BF16)
    counts = jnp.sum(onehot.astype(F32), axis=0)
    class_sums = lax.dot_general(
        resid_cols, onehot, (((0,), (0,)), ((), ())), preferred_element_type=F32
    )
    cross = class_sums / jnp.maximum(counts, 1.0)[None, :]
    return (gram, cross)


def solution(mesh):
    return jax.shard_map(
        functools.partial(on_device, mesh.shape["tok"], mesh.shape["hid"]),
        mesh=mesh,
        in_specs=(
            P("hid", "tok"),
            P("tok"),
            P("tok", "hid"),
            P("tok", "hid"),
            P("hid", "tok"),
            P(),
        ),
        out_specs=(P(("tok", "hid"), None), P(("tok", "hid"), None)),
        check_vma=False,
    )
```

time: 216 us -> 177 us (0.82)
  waiting for transfers between devices: 127 us -> 53.6 us
  starting transfers between devices: 0.12 us -> 71.3 us
  blocking collectives: 42.9 us -> 0 us
  local copies, waits for them, and re-layouts: 0.01 us -> 20.6 us
  between operations: 13.8 us -> 1.58 us
  matrix products: 28.7 us -> 19.7 us
  Pallas kernels: 0 us -> 3.79 us
  other arithmetic: 3.08 us -> 5.29 us
    ppermute x0 -> x45, starting transfers between devices: none -> 71.3 us  [the longest x21 25 us: swap(): return lax.ppermute(value, axis, [(i, i ^ mask) for i in range(size)])]
    reduce_scatter x2 -> x0, waiting for transfers between devices: 70.3 us -> none  [the longest x1 36.7 us: on_device(): lax.psum_scatter(jnp.dot(normed, both_weights, preferred_element_type=jnp...]
    all_gather x1 -> x0, waiting for transfers between devices: 56.8 us -> none  [on_device(): lax.all_gather(resid_cols, ('tok', 'hid'), axis=1, tiled=True)]
    ppermute x0 -> x45, waiting for transfers between devices: none -> 53.6 us  [the longest x12 20.1 us: chain_sums(): got = lax.ppermute(value.astype(BF16), 'tok', pairs)]
    all_gather x2 -> x0, blocking collectives: 31 us -> none  [the longest x1 19.4 us: on_device(): lax.all_gather(hidden, 'tok', axis=0, tiled=True)]
    slice x0 -> x3, local copies, waits for them, and re-layouts: none -> 18.4 us  [the longest x1 17.6 us: on_device(): gate_weight[:, cols]]
    psum x1 -> x0, blocking collectives: 12 us -> none  [on_device(): total_sq = lax.psum(local_sq, 'tok')]
    dot_general x3 -> x9, matrix products: 27.1 us -> 18.9 us  [the longest x4 11.1 us: on_device(): jnp.dot(rows, down_weight[k * wide:(k + 1) * wide], preferred_element_typ...]
  transfers between devices with their start and end apart: 3 -> 45, of which waited for: 3 -> 25; matrix products, arithmetic and copies ran while one was open for 1% -> 15% of each run, Pallas kernels for 0% -> 0%
where the time goes in v1:
time: 177 us; the launch traced here: 176 us
  starting transfers between devices  71.3 us (40%)
  waiting for transfers between devices  53.6 us (30%)
  local copies, waits for them, and re-layouts  20.6 us (12%)
  matrix products  19.7 us (11%)
  other arithmetic  5.29 us (3%)
  Pallas kernels  3.79 us (2%)
    ppermute x21, starting transfers between devices, swap(): return lax.ppermute(value, axis, [(i, i ^ mask) for i in range(size)])  25 us
    ppermute x12, starting transfers between devices, chain_sums(): got = lax.ppermute(value.astype(BF16), 'tok', pairs)  24.1 us
    ppermute x12, starting transfers between devices, chain_copies(): got.append(lax.ppermute(value, 'tok', pairs))  22.2 us
    ppermute x12, waiting for transfers between devices, chain_sums(): got = lax.ppermute(value.astype(BF16), 'tok', pairs)  20.1 us
    ppermute x21, waiting for transfers between devices, swap(): return lax.ppermute(value, axis, [(i, i ^ mask) for i in range(size)])  19.8 us
    slice x1, local copies, waits for them, and re-layouts, on_device(): gate_weight[:, cols]  17.6 us
    ppermute x12, waiting for transfers between devices, chain_copies(): got.append(lax.ppermute(value, 'tok', pairs))  13.7 us
    dot_general x4, matrix products, on_device(): jnp.dot(rows, down_weight[k * wide:(k + 1) * wide], preferred_element_typ...  11.1 us
  transfers between devices with their start and end apart: 45, of which 25 were waited for; matrix products, arithmetic and copies ran while one was open for 15% of the time, Pallas kernels for 0%

profile of v1, /device:TPU:0, one launch (start us, length us, event | category | flops | bytes accessed | tf_op | source)
XLA Modules:
  0.0 175.9 jit_solution(11447801829996319053)
XLA Ops:
  0.6 3.0 %collective-permute-start = (bf16[16,2048]{1,0:T(8,128)(2,1)}, bf16[16,2048]{1,0:T(8,128)(2,1)S(1)}, u32[]{:S(2)}, u32[]{:S(2)}) collective-permute-start(bf16[16,2048]{1,0:T(8,128)(2,1)} %param.6), channel_id=1, source_target_pairs={{0,2},{1,3},{2,0},{3,1},{4,6},{5,7},{6,4},{7,5},{8,10},{9,11},{10,... | collective-permute-start | bytes 196616 | tf_op jit(solution)/shard_map/ppermute | solution.py:16
  6.1 17.6 %fusion.98 = (bf16[2048,896]{1,0:T(8,128)(2,1)S(1)}, bf16[2048,896]{1,0:T(8,128)(2,1)S(1)}, bf16[2048,896]{1,0:T(8,128)(2,1)}, bf16[2048,896]{1,0:T(8,128)(2,1)}...) fusion(bf16[2048,3584]{1,0:T(8,128)(2,1)} %param.8, ...), kind=kLoop, calls=%fused_computation.160 | loop fusion | bytes 58720256 | tf_op jit(solution)/shard_map/slice | solution.py:157
  25.8 4.0 %fusion.33 = bf16[128,1792]{1,0:T(8,128)(2,1)S(1)} fusion(bf16[128,2048]{1,0:T(8,128)(2,1)S(1)} %get-tuple-element.43, bf16[2048,896]{1,0:T(8,128)(2,1)} %get-tuple-element.67, bf16[2048,896]{1,0:T(8,128)(2,1)} %get-tuple-element.24), kind=kOutput, calls=%fused_computation.27 | convolution fusion | flops 954433536 | bytes 8323072 | tf_op jit(solution)/shard_map/dot_general | solution.py:158
  29.8 4.2 %collective-permute-start.14 = (bf16[64,1792]{1,0:T(8,128)(2,1)S(1)}, bf16[64,1792]{1,0:T(8,128)(2,1)S(1)}, u32[]{:S(2)}, u32[]{:S(2)}) collective-permute-start(bf16[64,1792]{1,0:T(8,128)(2,1)S(1)} %get-tuple-element.54), channel_id=1, source_target_pairs={{0,8},{1,9},{2,10},{3,11},{4,12},{5,13},{6,14},{7,15}} | collective-permute-start | bytes 688136 | tf_op jit(solution)/shard_map/ppermute | solution.py:55
  39.4 4.4 %collective-permute-start.15 = (bf16[64,1792]{1,0:T(8,128)(2,1)S(1)}, bf16[64,1792]{1,0:T(8,128)(2,1)S(1)}, u32[]{:S(2)}, u32[]{:S(2)}) collective-permute-start(bf16[64,1792]{1,0:T(8,128)(2,1)S(1)} %get-tuple-element.47), channel_id=1, source_target_pairs={{0,8},{8,16},{1,9},{9,17},{2,10},{10,18},{3,11},{11,19},{4,12},{12... | collective-permute-start | bytes 688136 | tf_op jit(solution)/shard_map/ppermute | solution.py:55
  45.6 5.0 %collective-permute-start.8 = (f32[128,1]{0,1:T(1,128)S(1)}, f32[128,1]{0,1:T(1,128)S(1)}, u32[]{:S(2)}, u32[]{:S(2)}) collective-permute-start(f32[128,1]{0,1:T(1,128)S(1)} %bitcast_add_fusion), channel_id=1, source_target_pairs={{0,16},{8,24},{16,0},{24,8},{1,17},{9,25},{17,1},{25,9},{2,18},{10... | collective-permute-start | bytes 1544 | tf_op jit(solution)/shard_map/ppermute | solution.py:16
  50.9 5.7 %collective-permute-start.16 = (bf16[64,1792]{1,0:T(8,128)(2,1)S(1)}, bf16[64,1792]{1,0:T(8,128)(2,1)S(1)}, u32[]{:S(2)}, u32[]{:S(2)}) collective-permute-start(bf16[64,1792]{1,0:T(8,128)(2,1)S(1)} %get-tuple-element.35), channel_id=1, source_target_pairs={{0,8},{8,16},{16,24},{1,9},{9,17},{17,25},{2,10},{10,18},{18,26},{... | collective-permute-start | bytes 688136 | tf_op jit(solution)/shard_map/ppermute | solution.py:55
  60.1 4.4 %collective-permute-done.6 = bf16[64,1792]{1,0:T(8,128)(2,1)S(1)} collective-permute-done((bf16[64,1792]{1,0:T(8,128)(2,1)S(1)}, bf16[64,1792]{1,0:T(8,128)(2,1)S(1)}, u32[]{:S(2)}, u32[]{:S(2)}) %collective-permute-start.6) | collective-permute-done | bytes 229408 | tf_op jit(solution)/shard_map/ppermute | solution.py:55
  68.3 4.6 %collective-permute-start.9 = (bf16[64,896]{1,0:T(8,128)(2,1)S(1)}, bf16[64,896]{1,0:T(8,128)(2,1)S(1)}, u32[]{:S(2)}, u32[]{:S(2)}) collective-permute-start(bf16[64,896]{1,0:T(8,128)(2,1)S(1)} %fusion.64), channel_id=1, source_target_pairs={{0,8},{1,9},{2,10},{3,11},{4,12},{5,13},{6,14},{7,15}} | collective-permute-start | bytes 344072 | tf_op jit(solution)/shard_map/ppermute | solution.py:70
  75.3 4.3 %collective-permute-start.11 = (bf16[64,896]{1,0:T(8,128)(2,1)S(1)}, bf16[64,896]{1,0:T(8,128)(2,1)S(1)}, u32[]{:S(2)}, u32[]{:S(2)}) collective-permute-start(bf16[64,896]{1,0:T(8,128)(2,1)S(1)} %get-tuple-element.6), channel_id=1, source_target_pairs={{0,8},{8,16},{1,9},{9,17},{2,10},{10,18},{3,11},{11,19},{4,12},{12... | collective-permute-start | bytes 344072 | tf_op jit(solution)/shard_map/ppermute | solution.py:70
  82.6 5.8 %collective-permute-done.12 = bf16[64,1792]{1,0:T(8,128)(2,1)S(1)} collective-permute-done((bf16[64,1792]{1,0:T(8,128)(2,1)S(1)}, bf16[64,1792]{1,0:T(8,128)(2,1)S(1)}, u32[]{:S(2)}, u32[]{:S(2)}) %collective-permute-start.12) | collective-permute-done | bytes 229408 | tf_op jit(solution)/shard_map/ppermute | solution.py:55
  88.7 2.5 %collective-permute-start.13 = (bf16[64,896]{1,0:T(8,128)(2,1)S(1)}, bf16[64,896]{1,0:T(8,128)(2,1)S(1)}, u32[]{:S(2)}, u32[]{:S(2)}) collective-permute-start(bf16[64,896]{1,0:T(8,128)(2,1)S(1)} %get-tuple-element.4), channel_id=1, source_target_pairs={{0,8},{8,16},{16,24},{1,9},{9,17},{17,25},{2,10},{10,18},{18,26},{... | collective-permute-start | bytes 344072 | tf_op jit(solution)/shard_map/ppermute | solution.py:70
  94.6 4.5 %collective-permute-done.22 = bf16[64,1792]{1,0:T(8,128)(2,1)S(1)} collective-permute-done((bf16[64,1792]{1,0:T(8,128)(2,1)S(1)}, bf16[64,1792]{1,0:T(8,128)(2,1)S(1)}, u32[]{:S(2)}, u32[]{:S(2)}) %collective-permute-start.22) | collective-permute-done | bytes 229408 | tf_op jit(solution)/shard_map/ppermute | solution.py:55
  104.5 4.2 %collective-permute-done.25 = bf16[64,896]{1,0:T(8,128)(2,1)S(1)} collective-permute-done((bf16[64,896]{1,0:T(8,128)(2,1)S(1)}, bf16[64,896]{1,0:T(8,128)(2,1)S(1)}, u32[]{:S(2)}, u32[]{:S(2)}) %collective-permute-start.25) | collective-permute-done | bytes 114720 | tf_op jit(solution)/shard_map/ppermute | solution.py:70
  111.4 4.2 %collective-permute-done.27 = bf16[64,896]{1,0:T(8,128)(2,1)} collective-permute-done((bf16[64,896]{1,0:T(8,128)(2,1)S(1)}, bf16[64,896]{1,0:T(8,128)(2,1)}, u32[]{:S(2)}, u32[]{:S(2)}) %collective-permute-start.27) | collective-permute-done | bytes 114720 | tf_op jit(solution)/shard_map/ppermute | solution.py:70
  118.2 4.2 %collective-permute-done.29 = bf16[64,896]{1,0:T(8,128)(2,1)S(1)} collective-permute-done((bf16[64,896]{1,0:T(8,128)(2,1)}, bf16[64,896]{1,0:T(8,128)(2,1)S(1)}, u32[]{:S(2)}, u32[]{:S(2)}) %collective-permute-start.29) | collective-permute-done | bytes 114720 | tf_op jit(solution)/shard_map/ppermute | solution.py:70
  123.6 2.8 %fusion.20 = f32[128,2048]{1,0:T(8,128)S(1)} fusion(bf16[3584,2048]{1,0:T(8,128)(2,1)} %param.10, bf16[64,896]{1,0:T(8,128)(2,1)S(1)} %get-tuple-element.61, bf16[64,896]{1,0:T(8,128)(2,1)S(1)} %get-tuple-element.57), kind=kOutput, calls=%fused_computation.20 | convolution fusion | flops 470220800 | bytes 4947968 | tf_op jit(solution)/shard_map/dot_general | solution.py:175
  126.3 2.8 %fusion.18 = f32[128,2048]{1,0:T(8,128)S(1)} fusion(bf16[3584,2048]{1,0:T(8,128)(2,1)} %param.10, bf16[64,896]{1,0:T(8,128)(2,1)S(1)} %get-tuple-element.60, bf16[64,896]{1,0:T(8,128)(2,1)S(1)} %get-tuple-element.56), kind=kOutput, calls=%fused_computation.18 | convolution fusion | flops 470220800 | bytes 4947968 | tf_op jit(solution)/shard_map/dot_general | solution.py:175
  129.1 2.8 %fusion.30 = f32[128,2048]{1,0:T(8,128)S(1)} fusion(f32[128,2048]{1,0:T(8,128)S(1)} %fusion.18, f32[128,2048]{1,0:T(8,128)S(1)} %fusion.20, bf16[3584,2048]{1,0:T(8,128)(2,1)} %param.10, bf16[64,896]{1,0:T(8,128)(2,1)S(1)} %get-tuple-element.62, bf16[64,896]{1,0:T(8,128)(2,1)S(1)} %get-tuple-element.58), kind=kOutput, calls=%fused_computation.26 | convolution fusion | flops 470745088 | bytes 7045120 | tf_op jit(solution)/shard_map/dot_general | solution.py:175
  131.9 2.8 %fusion.27 = f32[128,2048]{1,0:T(8,128)S(1)} fusion(f32[128,2048]{1,0:T(8,128)S(1)} %fusion.30, bf16[3584,2048]{1,0:T(8,128)(2,1)} %param.10, bf16[64,896]{1,0:T(8,128)(2,1)S(1)} %get-tuple-element.59, bf16[64,896]{1,0:T(8,128)(2,1)S(1)} %get-tuple-element.55), kind=kOutput, calls=%fused_computation.25 | convolution fusion | flops 470482944 | bytes 5996544 | tf_op jit(solution)/shard_map/dot_general | solution.py:175
  146.9 4.3 %collective-permute-start.40 = (bf16[128,256]{1,0:T(8,128)(2,1)S(1)}, bf16[128,256]{1,0:T(8,128)(2,1)S(1)}, u32[]{:S(2)}, u32[]{:S(2)}) collective-permute-start(bf16[128,256]{1,0:T(8,128)(2,1)S(1)} %add_convert_fusion.4.own_ref), channel_id=1, source_target_pairs={{0,24},{8,16},{16,8},{24,0},{1,25},{9,17},{17,9},{25,1},{2,26},{10... | collective-permute-start | bytes 196616 | tf_op jit(solution)/shard_map/ppermute | solution.py:16
  155.3 2.5 %collective-permute-start.43 = (bf16[3,128,256]{2,1,0:T(8,128)(2,1)S(1)}, bf16[3,128,256]{2,1,0:T(8,128)(2,1)S(1)}, u32[]{:S(2)}, u32[]{:S(2)}) collective-permute-start(bf16[3,128,256]{2,1,0:T(8,128)(2,1)S(1)} %pad_maximum_fusion.2), channel_id=1, source_target_pairs={{0,6},{1,7},{2,4},{3,5},{4,2},{5,3},{6,0},{7,1},{8,14},{9,15},{10,... | collective-permute-start | bytes 589832 | tf_op jit(solution)/shard_map/ppermute | solution.py:16
  157.8 2.5 %collective-permute-done.41 = bf16[3,128,256]{2,1,0:T(8,128)(2,1)S(1)} collective-permute-done((bf16[3,128,256]{2,1,0:T(8,128)(2,1)S(1)}, bf16[3,128,256]{2,1,0:T(8,128)(2,1)S(1)}, u32[]{:S(2)}, u32[]{:S(2)}) %collective-permute-start.41) | collective-permute-done | bytes 196640 | tf_op jit(solution)/shard_map/ppermute | solution.py:16
  171.9 3.8 %gram.1 = f32[256,8192]{1,0:T(8,128)} custom-call(bf16[128,256]{1,0:T(8,128)(2,1)S(1)} %add_convert_fusion.4.own_ref, bf16[4,128,256]{2,1,0:T(8,128)(2,1)S(1)} %pad_maximum_fusion.1.refs_0_, bf16[4,128,256]{2,1,0:T(8,128)(2,1)S(1)} %collective-permute-done.37.refs_1_, bf16[12,128,256]{2,1,0:T(8,128)(2,1)S(1)} %constant_dynamic-update-slice_fusion.5.refs_2_, ...), custom_call_target="tpu_custom_call" | custom-call | flops 536870912 | bytes 8388608 | tf_op jit(solution)/shard_map/gram/pallas_call | solution.py:117
  (144 shorter events, 67.4 us)
Async XLA Ops:
  0.6 23.0 %collective-permute-start = (bf16[16,2048]{1,0:T(8,128)(2,1)}, bf16[16,2048]{1,0:T(8,128)(2,1)S(1)}, u32[]{:S(2)}, u32[]{:S(2)}) collective-permute-start(bf16[16,2048]{1,0:T(8,128)(2,1)} %param.6), channel_id=1, source_target_pairs={{0,2},{1,3},{2,0},{3,1},{4,6},{5,7},{6,4},{7,5},{8,10},{9,11},{10,... | collective-permute-start | bytes 196616 | tf_op jit(solution)/shard_map/ppermute | solution.py:16
  3.6 20.0 %collective-permute-start.1 = (bf16[16,2048]{1,0:T(8,128)(2,1)}, bf16[16,2048]{1,0:T(8,128)(2,1)S(1)}, u32[]{:S(2)}, u32[]{:S(2)}) collective-permute-start(bf16[16,2048]{1,0:T(8,128)(2,1)} %param.6), channel_id=1, source_target_pairs={{0,4},{1,5},{2,6},{3,7},{4,0},{5,1},{6,2},{7,3},{8,12},{9,13},{10,... | collective-permute-start | bytes 196616 | tf_op jit(solution)/shard_map/ppermute | solution.py:16
  5.2 18.5 %collective-permute-start.2 = (bf16[16,2048]{1,0:T(8,128)(2,1)}, bf16[16,2048]{1,0:T(8,128)(2,1)S(1)}, u32[]{:S(2)}, u32[]{:S(2)}) collective-permute-start(bf16[16,2048]{1,0:T(8,128)(2,1)} %param.6), channel_id=1, source_target_pairs={{0,6},{1,7},{2,4},{3,5},{4,2},{5,3},{6,0},{7,1},{8,14},{9,15},{10,... | collective-permute-start | bytes 196616 | tf_op jit(solution)/shard_map/ppermute | solution.py:16
  29.8 9.3 %collective-permute-start.14 = (bf16[64,1792]{1,0:T(8,128)(2,1)S(1)}, bf16[64,1792]{1,0:T(8,128)(2,1)S(1)}, u32[]{:S(2)}, u32[]{:S(2)}) collective-permute-start(bf16[64,1792]{1,0:T(8,128)(2,1)S(1)} %get-tuple-element.54), channel_id=1, source_target_pairs={{0,8},{1,9},{2,10},{3,11},{4,12},{5,13},{6,14},{7,15}} | collective-permute-start | bytes 688136 | tf_op jit(solution)/shard_map/ppermute | solution.py:55
  34.7 10.9 %collective-permute-start.7 = (f32[128,1]{0,1:T(1,128)S(1)}, f32[128,1]{0,1:T(1,128)S(1)}, u32[]{:S(2)}, u32[]{:S(2)}) collective-permute-start(f32[128,1]{0,1:T(1,128)S(1)} %bitcast.41), channel_id=1, source_target_pairs={{0,8},{8,0},{16,24},{24,16},{1,9},{9,1},{17,25},{25,17},{2,10},{10... | collective-permute-start | bytes 1544 | tf_op jit(solution)/shard_map/ppermute | solution.py:16
  39.4 11.3 %collective-permute-start.15 = (bf16[64,1792]{1,0:T(8,128)(2,1)S(1)}, bf16[64,1792]{1,0:T(8,128)(2,1)S(1)}, u32[]{:S(2)}, u32[]{:S(2)}) collective-permute-start(bf16[64,1792]{1,0:T(8,128)(2,1)S(1)} %get-tuple-element.47), channel_id=1, source_target_pairs={{0,8},{8,16},{1,9},{9,17},{2,10},{10,18},{3,11},{11,19},{4,12},{12... | collective-permute-start | bytes 688136 | tf_op jit(solution)/shard_map/ppermute | solution.py:55
  45.6 12.3 %collective-permute-start.8 = (f32[128,1]{0,1:T(1,128)S(1)}, f32[128,1]{0,1:T(1,128)S(1)}, u32[]{:S(2)}, u32[]{:S(2)}) collective-permute-start(f32[128,1]{0,1:T(1,128)S(1)} %bitcast_add_fusion), channel_id=1, source_target_pairs={{0,16},{8,24},{16,0},{24,8},{1,17},{9,25},{17,1},{25,9},{2,18},{10... | collective-permute-start | bytes 1544 | tf_op jit(solution)/shard_map/ppermute | solution.py:16
  50.9 9.3 %collective-permute-start.16 = (bf16[64,1792]{1,0:T(8,128)(2,1)S(1)}, bf16[64,1792]{1,0:T(8,128)(2,1)S(1)}, u32[]{:S(2)}, u32[]{:S(2)}) collective-permute-start(bf16[64,1792]{1,0:T(8,128)(2,1)S(1)} %get-tuple-element.35), channel_id=1, source_target_pairs={{0,8},{8,16},{16,24},{1,9},{9,17},{17,25},{2,10},{10,18},{18,26},{... | collective-permute-start | bytes 688136 | tf_op jit(solution)/shard_map/ppermute | solution.py:55
  56.6 7.9 %collective-permute-start.6 = (bf16[64,1792]{1,0:T(8,128)(2,1)S(1)}, bf16[64,1792]{1,0:T(8,128)(2,1)S(1)}, u32[]{:S(2)}, u32[]{:S(2)}) collective-permute-start(bf16[64,1792]{1,0:T(8,128)(2,1)S(1)} %get-tuple-element.34), channel_id=1, source_target_pairs={{24,16},{16,8},{8,0},{25,17},{17,9},{9,1},{26,18},{18,10},{10,2},{... | collective-permute-start | bytes 688136 | tf_op jit(solution)/shard_map/ppermute | solution.py:55
  64.9 8.7 %collective-permute-start.18 = (bf16[64,1792]{1,0:T(8,128)(2,1)S(1)}, bf16[64,1792]{1,0:T(8,128)(2,1)S(1)}, u32[]{:S(2)}, u32[]{:S(2)}) collective-permute-start(bf16[64,1792]{1,0:T(8,128)(2,1)S(1)} %fusion.51), channel_id=1, source_target_pairs={{0,8},{8,16},{16,24},{1,9},{9,17},{17,25},{2,10},{10,18},{18,26},{... | collective-permute-start | bytes 688136 | tf_op jit(solution)/shard_map/ppermute | solution.py:55
  66.9 7.9 %collective-permute-start.10 = (bf16[64,1792]{1,0:T(8,128)(2,1)S(1)}, bf16[64,1792]{1,0:T(8,128)(2,1)S(1)}, u32[]{:S(2)}, u32[]{:S(2)}) collective-permute-start(bf16[64,1792]{1,0:T(8,128)(2,1)S(1)} %fusion.45), channel_id=1, source_target_pairs={{24,16},{16,8},{8,0},{25,17},{17,9},{9,1},{26,18},{18,10},{10,2},{... | collective-permute-start | bytes 688136 | tf_op jit(solution)/shard_map/ppermute | solution.py:55
  72.9 8.8 %collective-permute-start.17 = (bf16[64,896]{1,0:T(8,128)(2,1)S(1)}, bf16[64,896]{1,0:T(8,128)(2,1)S(1)}, u32[]{:S(2)}, u32[]{:S(2)}) collective-permute-start(bf16[64,896]{1,0:T(8,128)(2,1)S(1)} %fusion.61), channel_id=1, source_target_pairs={{24,16},{25,17},{26,18},{27,19},{28,20},{29,21},{30,22},{31,23}} | collective-permute-start | bytes 344072 | tf_op jit(solution)/shard_map/ppermute | solution.py:70
  75.3 13.3 %collective-permute-start.11 = (bf16[64,896]{1,0:T(8,128)(2,1)S(1)}, bf16[64,896]{1,0:T(8,128)(2,1)S(1)}, u32[]{:S(2)}, u32[]{:S(2)}) collective-permute-start(bf16[64,896]{1,0:T(8,128)(2,1)S(1)} %get-tuple-element.6), channel_id=1, source_target_pairs={{0,8},{8,16},{1,9},{9,17},{2,10},{10,18},{3,11},{11,19},{4,12},{12... | collective-permute-start | bytes 344072 | tf_op jit(solution)/shard_map/ppermute | solution.py:70
  80.5 7.9 %collective-permute-start.12 = (bf16[64,1792]{1,0:T(8,128)(2,1)S(1)}, bf16[64,1792]{1,0:T(8,128)(2,1)S(1)}, u32[]{:S(2)}, u32[]{:S(2)}) collective-permute-start(bf16[64,1792]{1,0:T(8,128)(2,1)S(1)} %fusion.47), channel_id=1, source_target_pairs={{16,8},{8,0},{17,9},{9,1},{18,10},{10,2},{19,11},{11,3},{20,12},{1... | collective-permute-start | bytes 688136 | tf_op jit(solution)/shard_map/ppermute | solution.py:55
  81.9 11.4 %collective-permute-start.19 = (bf16[64,896]{1,0:T(8,128)(2,1)S(1)}, bf16[64,896]{1,0:T(8,128)(2,1)S(1)}, u32[]{:S(2)}, u32[]{:S(2)}) collective-permute-start(bf16[64,896]{1,0:T(8,128)(2,1)S(1)} %get-tuple-element.16), channel_id=1, source_target_pairs={{24,16},{16,8},{25,17},{17,9},{26,18},{18,10},{27,19},{19,11},{28,... | collective-permute-start | bytes 344072 | tf_op jit(solution)/shard_map/ppermute | solution.py:70
  88.7 10.6 %collective-permute-start.13 = (bf16[64,896]{1,0:T(8,128)(2,1)S(1)}, bf16[64,896]{1,0:T(8,128)(2,1)S(1)}, u32[]{:S(2)}, u32[]{:S(2)}) collective-permute-start(bf16[64,896]{1,0:T(8,128)(2,1)S(1)} %get-tuple-element.4), channel_id=1, source_target_pairs={{0,8},{8,16},{16,24},{1,9},{9,17},{17,25},{2,10},{10,18},{18,26},{... | collective-permute-start | bytes 344072 | tf_op jit(solution)/shard_map/ppermute | solution.py:70
  91.3 7.9 %collective-permute-start.22 = (bf16[64,1792]{1,0:T(8,128)(2,1)S(1)}, bf16[64,1792]{1,0:T(8,128)(2,1)S(1)}, u32[]{:S(2)}, u32[]{:S(2)}) collective-permute-start(bf16[64,1792]{1,0:T(8,128)(2,1)S(1)} %get-tuple-element.36), channel_id=1, source_target_pairs={{8,0},{9,1},{10,2},{11,3},{12,4},{13,5},{14,6},{15,7}} | collective-permute-start | bytes 688136 | tf_op jit(solution)/shard_map/ppermute | solution.py:55
  93.3 8.4 %collective-permute-start.21 = (bf16[64,896]{1,0:T(8,128)(2,1)S(1)}, bf16[64,896]{1,0:T(8,128)(2,1)S(1)}, u32[]{:S(2)}, u32[]{:S(2)}) collective-permute-start(bf16[64,896]{1,0:T(8,128)(2,1)S(1)} %get-tuple-element.14), channel_id=1, source_target_pairs={{24,16},{16,8},{8,0},{25,17},{17,9},{9,1},{26,18},{18,10},{10,2},{... | collective-permute-start | bytes 344072 | tf_op jit(solution)/shard_map/ppermute | solution.py:70
  101.8 7.0 %collective-permute-start.25 = (bf16[64,896]{1,0:T(8,128)(2,1)S(1)}, bf16[64,896]{1,0:T(8,128)(2,1)S(1)}, u32[]{:S(2)}, u32[]{:S(2)}) collective-permute-start(bf16[64,896]{1,0:T(8,128)(2,1)S(1)} %get-tuple-element.12), channel_id=1, source_target_pairs={{24,16},{16,8},{8,0},{25,17},{17,9},{9,1},{26,18},{18,10},{10,2},{... | collective-permute-start | bytes 344072 | tf_op jit(solution)/shard_map/ppermute | solution.py:70
  110.1 7.0 %collective-permute-start.28 = (bf16[64,896]{1,0:T(8,128)(2,1)}, bf16[64,896]{1,0:T(8,128)(2,1)}, u32[]{:S(2)}, u32[]{:S(2)}) collective-permute-start(bf16[64,896]{1,0:T(8,128)(2,1)} %collective-permute-done.26), channel_id=1, source_target_pairs={{16,24},{17,25},{18,26},{19,27},{20,28},{21,29},{22,30},{23,31}} | collective-permute-start | bytes 344072 | tf_op jit(solution)/shard_map/ppermute | solution.py:70
  146.9 7.3 %collective-permute-start.40 = (bf16[128,256]{1,0:T(8,128)(2,1)S(1)}, bf16[128,256]{1,0:T(8,128)(2,1)S(1)}, u32[]{:S(2)}, u32[]{:S(2)}) collective-permute-start(bf16[128,256]{1,0:T(8,128)(2,1)S(1)} %add_convert_fusion.4.own_ref), channel_id=1, source_target_pairs={{0,24},{8,16},{16,8},{24,0},{1,25},{9,17},{17,9},{25,1},{2,26},{10... | collective-permute-start | bytes 196616 | tf_op jit(solution)/shard_map/ppermute | solution.py:16
  154.8 7.9 %collective-permute-start.42 = (bf16[3,128,256]{2,1,0:T(8,128)(2,1)S(1)}, bf16[3,128,256]{2,1,0:T(8,128)(2,1)S(1)}, u32[]{:S(2)}, u32[]{:S(2)}) collective-permute-start(bf16[3,128,256]{2,1,0:T(8,128)(2,1)S(1)} %pad_maximum_fusion.2), channel_id=1, source_target_pairs={{0,4},{1,5},{2,6},{3,7},{4,0},{5,1},{6,2},{7,3},{8,12},{9,13},{10,... | collective-permute-start | bytes 589832 | tf_op jit(solution)/shard_map/ppermute | solution.py:16
  155.3 7.5 %collective-permute-start.43 = (bf16[3,128,256]{2,1,0:T(8,128)(2,1)S(1)}, bf16[3,128,256]{2,1,0:T(8,128)(2,1)S(1)}, u32[]{:S(2)}, u32[]{:S(2)}) collective-permute-start(bf16[3,128,256]{2,1,0:T(8,128)(2,1)S(1)} %pad_maximum_fusion.2), channel_id=1, source_target_pairs={{0,6},{1,7},{2,4},{3,5},{4,2},{5,3},{6,0},{7,1},{8,14},{9,15},{10,... | collective-permute-start | bytes 589832 | tf_op jit(solution)/shard_map/ppermute | solution.py:16
  162.8 9.1 %collective-permute-start.44 = (bf16[12,128,256]{2,1,0:T(8,128)(2,1)S(1)}, bf16[12,128,256]{2,1,0:T(8,128)(2,1)S(1)}, u32[]{:S(2)}, u32[]{:S(2)}) collective-permute-start(bf16[12,128,256]{2,1,0:T(8,128)(2,1)S(1)} %constant_dynamic-update-slice_fusion.5.refs_2_), channel_id=1, source_target_pairs={{0,1},{1,0},{2,3},{3,2},{4,5},{5,4},{6,7},{7,6},{8,9},{9,8},{10,11... | collective-permute-start | bytes 2359304 | tf_op jit(solution)/shard_map/ppermute | solution.py:16
  (29 other events, 210.2 us)

commit v2 on v0

v2 whole, which is shorter than its diff:
```python
import functools
import jax
import jax.numpy as jnp
from jax import lax
from jax.experimental import pallas as pl
from jax.experimental.pallas import tpu as pltpu
from jax.sharding import PartitionSpec as P

D = 8192
CLASSES = 64
BF16 = jnp.bfloat16
F32 = jnp.float32


def swap(value, axis, size, mask):
    return lax.ppermute(value, axis, [(i, i ^ mask) for i in range(size)])


def gather_tokens(own, h, n_hid):
    chips = n_hid // 2
    rows = own.shape[0]
    near = [own] + [swap(own, "hid", n_hid, 2 * e) for e in range(1, chips)]
    near = jnp.concatenate(near, axis=0)
    far = swap(near, "hid", n_hid, 1)
    both = jnp.concatenate([near, far], axis=0)
    ntok = both.shape[0]
    place = jnp.arange(ntok, dtype=jnp.int32)
    slot = place // rows
    owner = h ^ (2 * (slot % chips) + slot // chips)
    token = owner * rows + place % rows
    order = (jnp.arange(ntok, dtype=jnp.int32)[:, None] == token[None, :]).astype(BF16)
    return jnp.dot(order, both, preferred_element_type=F32)


def tile_of(width):
    for tile in (256, 128):
        if width % tile == 0:
            return tile
    return width


def gate_up_kernel(lhs_ref, gate_ref, up_ref, out_ref):
    tile = gate_ref.shape[1]
    lhs = lhs_ref[...]
    out_ref[:, :tile] = jnp.dot(lhs, gate_ref[...], preferred_element_type=F32).astype(BF16)
    out_ref[:, tile:] = jnp.dot(lhs, up_ref[...], preferred_element_type=F32).astype(BF16)


def gate_up(lhs, gate_weight, up_weight, start, width, tile):
    ntok, depth = lhs.shape
    at = start // tile
    weight = pl.BlockSpec((depth, tile), lambda i: (0, at + i))
    return pl.pallas_call(
        gate_up_kernel,
        grid=(width // tile,),
        out_shape=jax.ShapeDtypeStruct((ntok, 2 * width), BF16),
        in_specs=[pl.BlockSpec((ntok, depth), lambda i: (0, 0)), weight, weight],
        out_specs=pl.BlockSpec((ntok, 2 * tile), lambda i: (0, i)),
        compiler_params=pltpu.CompilerParams(vmem_limit_bytes=24 * 1024 * 1024),
        cost_estimate=pl.CostEstimate(
            flops=4 * ntok * depth * width, bytes_accessed=4 * depth * width, transcendentals=0
        ),
        name="gate_up",
    )(lhs, gate_weight, up_weight)


def down_kernel(order_ref, lhs_ref, weight_ref, out_ref):
    out_ref[...] = jnp.dot(lhs_ref[...], weight_ref[...], preferred_element_type=F32).astype(out_ref.dtype)


def down(hidden, weight, order, panel, kind):
    ntok, depth = hidden.shape
    count = order.shape[0]
    return pl.pallas_call(
        down_kernel,
        grid_spec=pltpu.PrefetchScalarGridSpec(
            num_scalar_prefetch=1,
            grid=(count,),
            in_specs=[
                pl.BlockSpec((ntok, depth), lambda i, order: (0, 0)),
                pl.BlockSpec((depth, panel), lambda i, order: (0, order[i])),
            ],
            out_specs=pl.BlockSpec((None, ntok, panel), lambda i, order: (i, 0, 0)),
        ),
        out_shape=jax.ShapeDtypeStruct((count, ntok, panel), kind),
        compiler_params=pltpu.CompilerParams(vmem_limit_bytes=24 * 1024 * 1024),
        cost_estimate=pl.CostEstimate(
            flops=2 * ntok * depth * panel * count, bytes_accessed=2 * depth * panel * count, transcendentals=0
        ),
        name="down",
    )(order, hidden, weight)


def gram_kernel(core, n_hid, n_tok, ntok, own_ref, *refs):
    chips = n_hid // 2
    stacks, (out_ref, tiles, sems) = refs[:chips], refs[-3:]
    z = lax.axis_index("tok")
    h = lax.axis_index("hid")
    width = own_ref.shape[1]
    left = own_ref[...].T
    copies = []
    for e in range(chips):
        for d in range(n_tok):
            number = e * n_tok + d
            tiles[number] = jnp.dot(left, stacks[e][d], preferred_element_type=F32) * (1.0 / ntok)
            column = ((z ^ d) * n_hid + (h ^ (2 * e + core))) * width
            copy = pltpu.make_async_copy(
                tiles.at[number], out_ref.at[:, pl.ds(pl.multiple_of(column, width), width)], sems.at[number]
            )
            copy.start()
            copies.append(copy)
    for copy in copies:
        copy.wait()


def gram_part(resid_cols, stacks, core, n_tok, n_hid, before):
    ntok, width = resid_cols.shape
    blocks = n_tok * n_hid
    vmem = pl.BlockSpec(memory_space=pltpu.VMEM)
    anywhere = pl.BlockSpec(memory_space=pl.ANY)
    operands = [resid_cols, *stacks] + ([] if before is None else [before])
    return pl.pallas_call(
        functools.partial(gram_kernel, core, n_hid, n_tok, ntok),
        out_shape=jax.ShapeDtypeStruct((width, width * blocks), F32),
        in_specs=[vmem] * (1 + len(stacks)) + ([] if before is None else [anywhere]),
        out_specs=anywhere,
        input_output_aliases={} if before is None else {1 + len(stacks): 0},
        scratch_shapes=[pltpu.VMEM((blocks // 2, width, width), F32), pltpu.SemaphoreType.DMA((blocks // 2,))],
        compiler_params=pltpu.CompilerParams(vmem_limit_bytes=24 * 1024 * 1024),
        cost_estimate=pl.CostEstimate(
            flops=ntok * width * width * blocks, bytes_accessed=2 * width * width * blocks, transcendentals=0
        ),
        name="gram",
    )(*operands)


def gram_of(resid_cols, n_tok, n_hid):
    chips = n_hid // 2
    line = jnp.stack([resid_cols] + [swap(resid_cols, "tok", n_tok, d) for d in range(1, n_tok)])
    stacks = [line] + [swap(line, "hid", n_hid, 2 * e) for e in range(1, chips)]
    first_far = swap(line, "hid", n_hid, 1)
    rest_far = swap(jnp.stack(stacks[1:]), "hid", n_hid, 1)
    near = gram_part(resid_cols, stacks, 0, n_tok, n_hid, None)
    far = [first_far] + [rest_far[e - 1] for e in range(1, chips)]
    return gram_part(resid_cols, far, 1, n_tok, n_hid, near)


def on_device(n_tok, n_hid, resid_in, norm_gain, gate_weight, up_weight, down_weight, labels):
    h = lax.axis_index("hid")
    chips = n_hid // 2

    x = gather_tokens(resid_in, h, n_hid)
    ntok, block = x.shape
    total_sq = jnp.sum(x * x, axis=1, keepdims=True)
    d = 1
    while d < n_tok:
        total_sq = total_sq + swap(total_sq, "tok", n_tok, d)
        d *= 2
    scale_rows = lax.rsqrt(total_sq / float(D) + 1e-05)
    rows = ntok // n_tok
    own_scale = lax.dynamic_slice_in_dim(scale_rows, lax.axis_index("tok") * rows, rows, 0)
    lhs = (x * norm_gain[None, :]).astype(BF16)

    shard_ff = gate_weight.shape[1]
    tile = tile_of(shard_ff)
    count = 2 if shard_ff % (2 * tile) == 0 else 1
    wide = shard_ff // count
    hidden = []
    for k in range(count):
        pair = gate_up(lhs, gate_weight, up_weight, k * wide, wide, tile)
        sums = lax.psum_scatter(pair, "tok", scatter_dimension=0, tiled=True).astype(F32) * own_scale
        pieces = [
            jax.nn.silu(sums[:, at:at + tile]) * sums[:, at + tile:at + 2 * tile]
            for at in range(0, 2 * wide, 2 * tile)
        ]
        mine = jnp.concatenate(pieces, axis=1).astype(BF16)
        hidden.append(lax.all_gather(mine, "tok", axis=0, tiled=True))
    hidden = jnp.concatenate(hidden, axis=1)

    panel = block // n_hid
    x_cols = lax.dynamic_slice_in_dim(x, h * panel, panel, 1)
    if panel % 128 == 0:
        near_order = jnp.stack([h ^ (2 * e) for e in range(chips)]).astype(jnp.int32)
        other = down(hidden, down_weight, near_order ^ 1, panel, BF16)
        swapped = swap(other, "hid", n_hid, 1)
        mine = down(hidden, down_weight, near_order, panel, F32)
        chip_sum = mine + swapped.astype(F32)
        summed = chip_sum[0]
        for e in range(1, chips):
            summed = summed + swap(chip_sum[e].astype(BF16), "hid", n_hid, 2 * e).astype(F32)
        resid_cols = (x_cols + summed).astype(BF16)
        gram = gram_of(resid_cols, n_tok, n_hid)
    else:
        partial_out = jnp.dot(hidden, down_weight, preferred_element_type=F32).astype(BF16)
        summed = lax.psum_scatter(partial_out, "hid", scatter_dimension=1, tiled=True).astype(F32)
        resid_cols = (x_cols + summed).astype(BF16)
        everyone = lax.all_gather(resid_cols, ("tok", "hid"), axis=1, tiled=True)
        gram = lax.dot_general(
            resid_cols, everyone, (((0,), (0,)), ((), ())), preferred_element_type=F32
        ) / float(ntok)

    onehot = (labels[:, None] == jnp.arange(CLASSES, dtype=jnp.int32)[None, :]).astype(BF16)
    counts = jnp.sum(onehot.astype(F32), axis=0)
    class_sums = lax.dot_general(
        resid_cols, onehot, (((0,), (0,)), ((), ())), preferred_element_type=F32
    )
    cross = class_sums / jnp.maximum(counts, 1.0)[None, :]
    return (gram, cross)


def solution(mesh):
    return jax.shard_map(
        functools.partial(on_device, mesh.shape["tok"], mesh.shape["hid"]),
        mesh=mesh,
        in_specs=(
            P("hid", "tok"),
            P("tok"),
            P("tok", "hid"),
            P("tok", "hid"),
            P("hid", "tok"),
            P(),
        ),
        out_specs=(P(("tok", "hid"), None), P(("tok", "hid"), None)),
        check_vma=False,
    )
```

time: 216 us -> 179 us (0.83)
  waiting for transfers between devices: 127 us -> 53.6 us
  local copies, waits for them, and re-layouts: 0.01 us -> 32.2 us
  matrix products: 28.7 us -> 1.85 us
  Pallas kernels: 0 us -> 21.4 us
  starting transfers between devices: 0.12 us -> 21.4 us
  blocking collectives: 42.9 us -> 30.6 us
    all_gather x1 -> x0, waiting for transfers between devices: 56.8 us -> none  [on_device(): lax.all_gather(resid_cols, ('tok', 'hid'), axis=1, tiled=True)]
    reduce_scatter x2, waiting for transfers between devices: 70.3 us -> 28.1 us  [on_device(): lax.psum_scatter(pair, 'tok', scatter_dimension=0, tiled=True).astype(F32)]
    unnamed x2 -> x19, local copies, waits for them, and re-layouts: 0.01 us -> 32 us
    dot_general x3 -> x1, matrix products: 27.1 us -> 1.07 us  [gather_tokens(): return jnp.dot(order, both, preferred_element_type=F32)]
    ppermute x0 -> x18, waiting for transfers between devices: none -> 25.5 us  [swap(): return lax.ppermute(value, axis, [(i, i ^ mask) for i in range(size)])]
    pallas_call x0 -> x6, Pallas kernels: none -> 21.4 us  [the longest x2 10 us: gate_up(): pl.pallas_call(gate_up_kernel, grid=(width // tile,), out_shape=jax.Shape...]
    ppermute x0 -> x18, starting transfers between devices: none -> 21.3 us  [swap(): return lax.ppermute(value, axis, [(i, i ^ mask) for i in range(size)])]
    psum x1 -> x0, blocking collectives: 12 us -> none  [on_device(): total_sq = lax.psum(local_sq, 'tok')]
  transfers between devices with their start and end apart: 3 -> 20, of which waited for: 3 -> 15; matrix products, arithmetic and copies ran while one was open for 1% -> 1% of each run, Pallas kernels for 0% -> 6%
where the time goes in v2:
time: 179 us; the launch traced here: 178 us
  waiting for transfers between devices  53.6 us (30%)
  local copies, waits for them, and re-layouts  32.2 us (18%)
  blocking collectives  30.6 us (17%)
  starting transfers between devices  21.4 us (12%)
  Pallas kernels  21.4 us (12%)
  between operations  14.4 us (8%)
  other arithmetic  2.77 us (2%)
  matrix products  1.85 us (1%)
    unnamed x19, local copies, waits for them, and re-layouts  32 us
    all_gather x2, blocking collectives, on_device(): hidden.append(lax.all_gather(mine, 'tok', axis=0, tiled=True))  30.6 us
    reduce_scatter x2, waiting for transfers between devices, on_device(): lax.psum_scatter(pair, 'tok', scatter_dimension=0, tiled=True).astype(F32)  28.1 us
    ppermute x18, waiting for transfers between devices, swap(): return lax.ppermute(value, axis, [(i, i ^ mask) for i in range(size)])  25.5 us
    ppermute x18, starting transfers between devices, swap(): return lax.ppermute(value, axis, [(i, i ^ mask) for i in range(size)])  21.3 us
    pallas_call x2, Pallas kernels, gate_up(): pl.pallas_call(gate_up_kernel, grid=(width // tile,), out_shape=jax.Shape...  10 us
    pallas_call x2, Pallas kernels, down(): pl.pallas_call(down_kernel, grid_spec=pltpu.PrefetchScalarGridSpec(num_sc...  6.64 us
    pallas_call x2, Pallas kernels, gram_part(): pl.pallas_call(functools.partial(gram_kernel, core, n_hid, n_tok, ntok),...  4.78 us
  transfers between devices with their start and end apart: 20, of which 15 were waited for; matrix products, arithmetic and copies ran while one was open for 1% of the time, Pallas kernels for 6%

profile of v2, /device:TPU:0, one launch (start us, length us, event | category | flops | bytes accessed | tf_op | source)
XLA Modules:
  0.0 178.2 jit_solution(7619473117867472085)
XLA Ops:
  7.2 3.0 %collective-permute-start = (bf16[16,2048]{1,0:T(8,128)(2,1)}, bf16[16,2048]{1,0:T(8,128)(2,1)S(1)}, u32[]{:S(2)}, u32[]{:S(2)}) collective-permute-start(bf16[16,2048]{1,0:T(8,128)(2,1)} %param.6), channel_id=1, source_target_pairs={{0,2},{1,3},{2,0},{3,1},{4,6},{5,7},{6,4},{7,5},{8,10},{9,11},{10,... | collective-permute-start | bytes 196616 | tf_op jit(solution)/shard_map/ppermute | solution.py:16
  14.7 2.4 %collective-permute-done.2 = bf16[16,2048]{1,0:T(8,128)(2,1)S(1)} collective-permute-done((bf16[16,2048]{1,0:T(8,128)(2,1)}, bf16[16,2048]{1,0:T(8,128)(2,1)S(1)}, u32[]{:S(2)}, u32[]{:S(2)}) %collective-permute-start.2) | collective-permute-done | bytes 65568 | tf_op jit(solution)/shard_map/ppermute | solution.py:16
  20.7 5.2 %copy-done.2 = bf16[2048,3584]{1,0:T(8,128)(2,1)S(1)} copy-done((bf16[2048,3584]{1,0:T(8,128)(2,1)S(1)}, bf16[2048,3584]{1,0:T(8,128)(2,1)}, u32[]{:S(2)}) %copy-start.2) | copy-done | bytes 14680088
  25.8 5.2 %copy-done.4 = bf16[2048,3584]{1,0:T(8,128)(2,1)S(1)} copy-done((bf16[2048,3584]{1,0:T(8,128)(2,1)S(1)}, bf16[2048,3584]{1,0:T(8,128)(2,1)}, u32[]{:S(2)}) %copy-start.4) | copy-done | bytes 14680088
  31.0 5.0 %gate_up.2 = bf16[128,3584]{1,0:T(8,128)(2,1)} custom-call(bf16[128,2048]{1,0:T(8,128)(2,1)S(1)} %get-tuple-element.7.lhs_ref, bf16[2048,3584]{1,0:T(8,128)(2,1)S(1)} %copy-done.2, bf16[2048,3584]{1,0:T(8,128)(2,1)S(1)} %copy-done.4), custom_call_target="tpu_custom_call" | custom-call | flops 1879048192 | bytes 14680064 | tf_op jit(solution)/shard_map/gate_up/pallas_call | solution.py:53
  36.1 5.2 %copy-done.3 = bf16[2048,3584]{1,0:T(8,128)(2,1)S(1)} copy-done((bf16[2048,3584]{1,0:T(8,128)(2,1)S(1)}, bf16[2048,3584]{1,0:T(8,128)(2,1)}, u32[]{:S(2)}) %copy-start.3) | copy-done | bytes 14680088
  41.3 5.2 %copy-done.5 = bf16[2048,3584]{1,0:T(8,128)(2,1)S(1)} copy-done((bf16[2048,3584]{1,0:T(8,128)(2,1)S(1)}, bf16[2048,3584]{1,0:T(8,128)(2,1)}, u32[]{:S(2)}) %copy-start.5) | copy-done | bytes 14680088
  46.5 5.0 %gate_up.3 = bf16[128,3584]{1,0:T(8,128)(2,1)} custom-call(bf16[128,2048]{1,0:T(8,128)(2,1)S(1)} %get-tuple-element.7.lhs_ref, bf16[2048,3584]{1,0:T(8,128)(2,1)S(1)} %copy-done.3, bf16[2048,3584]{1,0:T(8,128)(2,1)S(1)} %copy-done.5), custom_call_target="tpu_custom_call" | custom-call | flops 1879048192 | bytes 14680064 | tf_op jit(solution)/shard_map/gate_up/pallas_call | solution.py:53
  55.1 2.8 %collective-permute-start.5 = (f32[128,1]{0,1:T(1,128)S(1)}, f32[128,1]{0,1:T(1,128)S(1)}, u32[]{:S(2)}, u32[]{:S(2)}) collective-permute-start(f32[128,1]{0,1:T(1,128)S(1)} %bitcast_add_fusion), channel_id=1, source_target_pairs={{0,16},{8,24},{16,0},{24,8},{1,17},{9,25},{17,1},{25,9},{2,18},{10... | collective-permute-start | bytes 1544 | tf_op jit(solution)/shard_map/ppermute | solution.py:16
  60.7 27.0 %reduce-scatter.5.cloned.1.call-done = bf16[32,3584]{1,0:T(8,128)(2,1)} async-done(((bf16[128,3584]{1,0:T(8,128)(2,1)}), bf16[32,3584]{1,0:T(8,128)(2,1)}) %reduce-scatter.5.cloned.1.call-update) | async-done | bytes 229392 | tf_op jit(solution)/shard_map/reduce_scatter | solution.py:171
  89.1 15.6 %all_gather.7 = bf16[128,1792]{1,0:T(8,128)(2,1)S(1)} all-gather(bf16[32,1792]{1,0:T(8,128)(2,1)S(1)} %constant_dynamic-update-slice_fusion.12), channel_id=1, replica_groups=mesh['tok'=4,'hid'=8] {'tok'}, dimensions={0}, use_global_device_ids=true | all-gather | bytes 573440 | tf_op jit(solution)/shard_map/all_gather | solution.py:177
  104.9 15.0 %all_gather.6 = bf16[128,1792]{1,0:T(8,128)(2,1)S(1)} all-gather(bf16[32,1792]{1,0:T(8,128)(2,1)S(1)} %constant_dynamic-update-slice_fusion.5), channel_id=1, replica_groups=mesh['tok'=4,'hid'=8] {'tok'}, dimensions={0}, use_global_device_ids=true | all-gather | bytes 573440 | tf_op jit(solution)/shard_map/all_gather | solution.py:177
  120.0 5.2 %copy-done = bf16[3584,2048]{1,0:T(8,128)(2,1)S(1)} copy-done((bf16[3584,2048]{1,0:T(8,128)(2,1)S(1)}, bf16[3584,2048]{1,0:T(8,128)(2,1)}, u32[]{:S(2)}) %copy-start) | copy-done | bytes 14680088
  125.1 3.3 %down.3 = bf16[4,128,256]{2,1,0:T(8,128)(2,1)S(1)} custom-call(s32[4]{0:T(128)S(1)} %get-tuple-element.4.order_ref, bf16[128,3584]{1,0:T(8,128)(2,1)S(1)} %constant_dynamic-update-slice_fusion.19.lhs_ref, bf16[3584,2048]{1,0:T(8,128)(2,1)S(1)} %copy-done), custom_call_target="tpu_custom_call" | custom-call | flops 939524096 | bytes 7340032 | tf_op jit(solution)/shard_map/down/pallas_call | solution.py:74
  128.5 5.2 %copy-done.1 = bf16[3584,2048]{1,0:T(8,128)(2,1)S(1)} copy-done((bf16[3584,2048]{1,0:T(8,128)(2,1)S(1)}, bf16[3584,2048]{1,0:T(8,128)(2,1)}, u32[]{:S(2)}) %copy-start.1) | copy-done | bytes 14680088
  133.7 3.3 %down.2 = f32[4,128,256]{2,1,0:T(8,128)S(1)} custom-call(s32[4]{0:T(128)S(1)} %get-tuple-element.5.order_ref, bf16[128,3584]{1,0:T(8,128)(2,1)S(1)} %constant_dynamic-update-slice_fusion.19.lhs_ref, bf16[3584,2048]{1,0:T(8,128)(2,1)S(1)} %copy-done.1), custom_call_target="tpu_custom_call" | custom-call | flops 939524096 | bytes 7340032 | tf_op jit(solution)/shard_map/down/pallas_call | solution.py:74
  142.9 2.1 %collective-permute-done.9 = bf16[128,256]{1,0:T(8,128)(2,1)S(1)} collective-permute-done((bf16[128,256]{1,0:T(8,128)(2,1)S(1)}, bf16[128,256]{1,0:T(8,128)(2,1)S(1)}, u32[]{:S(2)}, u32[]{:S(2)}) %collective-permute-start.9) | collective-permute-done | bytes 65568 | tf_op jit(solution)/shard_map/ppermute | solution.py:16
  146.5 3.0 %collective-permute-start.12 = (bf16[128,256]{1,0:T(8,128)(2,1)S(1)}, bf16[128,256]{1,0:T(8,128)(2,1)S(1)}, u32[]{:S(2)}, u32[]{:S(2)}) collective-permute-start(bf16[128,256]{1,0:T(8,128)(2,1)S(1)} %fusion.4.own_ref), channel_id=1, source_target_pairs={{0,24},{8,16},{16,8},{24,0},{1,25},{9,17},{17,9},{25,1},{2,26},{10... | collective-permute-start | bytes 196616 | tf_op jit(solution)/shard_map/ppermute | solution.py:16
  149.5 2.3 %collective-permute-done.11 = bf16[128,256]{1,0:T(8,128)(2,1)S(1)} collective-permute-done((bf16[128,256]{1,0:T(8,128)(2,1)S(1)}, bf16[128,256]{1,0:T(8,128)(2,1)S(1)}, u32[]{:S(2)}, u32[]{:S(2)}) %collective-permute-start.11) | collective-permute-done | bytes 65568 | tf_op jit(solution)/shard_map/ppermute | solution.py:16
  154.0 2.2 %collective-permute-start.16 = (bf16[4,128,256]{2,1,0:T(8,128)(2,1)S(1)}, bf16[4,128,256]{2,1,0:T(8,128)(2,1)S(1)}, u32[]{:S(2)}, u32[]{:S(2)}) collective-permute-start(bf16[4,128,256]{2,1,0:T(8,128)(2,1)S(1)} %pad_maximum_fusion.2.refs_0_), channel_id=1, source_target_pairs={{0,6},{1,7},{2,4},{3,5},{4,2},{5,3},{6,0},{7,1},{8,14},{9,15},{10,... | collective-permute-start | bytes 786440 | tf_op jit(solution)/shard_map/ppermute | solution.py:16
  156.2 5.5 %collective-permute-done.14.refs_1_ = bf16[4,128,256]{2,1,0:T(8,128)(2,1)S(1)} collective-permute-done((bf16[4,128,256]{2,1,0:T(8,128)(2,1)S(1)}, bf16[4,128,256]{2,1,0:T(8,128)(2,1)S(1)}, u32[]{:S(2)}, u32[]{:S(2)}) %collective-permute-start.14) | collective-permute-done | bytes 262176 | tf_op jit(solution)/shard_map/ppermute | solution.py:16
  161.7 3.2 %collective-permute-done.15.refs_2_ = bf16[4,128,256]{2,1,0:T(8,128)(2,1)S(1)} collective-permute-done((bf16[4,128,256]{2,1,0:T(8,128)(2,1)S(1)}, bf16[4,128,256]{2,1,0:T(8,128)(2,1)S(1)}, u32[]{:S(2)}, u32[]{:S(2)}) %collective-permute-start.15) | collective-permute-done | bytes 262176 | tf_op jit(solution)/shard_map/ppermute | solution.py:16
  166.4 2.4 %gram.2.refs_4_ = f32[256,8192]{1,0:T(8,128)} custom-call(bf16[128,256]{1,0:T(8,128)(2,1)S(1)} %fusion.4.own_ref, bf16[4,128,256]{2,1,0:T(8,128)(2,1)S(1)} %pad_maximum_fusion.2.refs_0_, bf16[4,128,256]{2,1,0:T(8,128)(2,1)S(1)} %collective-permute-done.14.refs_1_, bf16[4,128,256]{2,1,0:T(8,128)(2,1)S(1)} %collective-permute-done.15.refs_2_, ...), custom_call_target="tpu_custom_call" | custom-call | flops 268435456 | bytes 4194304 | tf_op jit(solution)/shard_map/gram/pallas_call | solution.py:122
  168.9 2.4 %gram.3 = f32[256,8192]{1,0:T(8,128)} custom-call(bf16[128,256]{1,0:T(8,128)(2,1)S(1)} %fusion.4.own_ref, bf16[4,128,256]{2,1,0:T(8,128)(2,1)S(1)} %collective-permute-done.13.refs_0_, bf16[4,128,256]{2,1,0:T(8,128)(2,1)S(1)} %get-tuple-element.10.refs_1_, bf16[4,128,256]{2,1,0:T(8,128)(2,1)S(1)} %get-tuple-element.9.refs_2_, ...), custom_call_target="tpu_custom_call", output_to_operand_aliasing={{}: (5, {})} | custom-call | flops 268435456 | bytes 4194304 | tf_op jit(solution)/shard_map/gram/pallas_call | solution.py:122
  (78 shorter events, 27.2 us)
Async XLA Ops:
  7.2 53.6 %reduce-scatter.3.cloned.1.call-start = ((), (), s32[]{:S(2)}) async-start(), calls=%async_computation.2 | async-start | bytes 1146880 | tf_op jit(solution)/shard_map/reduce_scatter | solution.py:171
  7.2 5.7 %collective-permute-start = (bf16[16,2048]{1,0:T(8,128)(2,1)}, bf16[16,2048]{1,0:T(8,128)(2,1)S(1)}, u32[]{:S(2)}, u32[]{:S(2)}) collective-permute-start(bf16[16,2048]{1,0:T(8,128)(2,1)} %param.6), channel_id=1, source_target_pairs={{0,2},{1,3},{2,0},{3,1},{4,6},{5,7},{6,4},{7,5},{8,10},{9,11},{10,... | collective-permute-start | bytes 196616 | tf_op jit(solution)/shard_map/ppermute | solution.py:16
  10.2 4.5 %collective-permute-start.1 = (bf16[16,2048]{1,0:T(8,128)(2,1)}, bf16[16,2048]{1,0:T(8,128)(2,1)S(1)}, u32[]{:S(2)}, u32[]{:S(2)}) collective-permute-start(bf16[16,2048]{1,0:T(8,128)(2,1)} %param.6), channel_id=1, source_target_pairs={{0,4},{1,5},{2,6},{3,7},{4,0},{5,1},{6,2},{7,3},{8,12},{9,13},{10,... | collective-permute-start | bytes 196616 | tf_op jit(solution)/shard_map/ppermute | solution.py:16
  11.7 5.4 %collective-permute-start.2 = (bf16[16,2048]{1,0:T(8,128)(2,1)}, bf16[16,2048]{1,0:T(8,128)(2,1)S(1)}, u32[]{:S(2)}, u32[]{:S(2)}) collective-permute-start(bf16[16,2048]{1,0:T(8,128)(2,1)} %param.6), channel_id=1, source_target_pairs={{0,6},{1,7},{2,4},{3,5},{4,2},{5,3},{6,0},{7,1},{8,14},{9,15},{10,... | collective-permute-start | bytes 196616 | tf_op jit(solution)/shard_map/ppermute | solution.py:16
  18.0 1.6 collective-permute-start.3
  20.7 5.2 %copy-start.2 = (bf16[2048,3584]{1,0:T(8,128)(2,1)S(1)}, bf16[2048,3584]{1,0:T(8,128)(2,1)}, u32[]{:S(2)}) copy-start(bf16[2048,3584]{1,0:T(8,128)(2,1)} %gate_ref.3) | copy-start | bytes 44040196
  36.1 51.7 %reduce-scatter.5.cloned.1.call-start = ((), (), s32[]{:S(2)}) async-start(), calls=%async_computation.3 | async-start | bytes 1146880 | tf_op jit(solution)/shard_map/reduce_scatter | solution.py:171
  41.3 5.2 %copy-start.5 = (bf16[2048,3584]{1,0:T(8,128)(2,1)S(1)}, bf16[2048,3584]{1,0:T(8,128)(2,1)}, u32[]{:S(2)}) copy-start(bf16[2048,3584]{1,0:T(8,128)(2,1)} %up_ref.3) | copy-start | bytes 44040196
  51.5 3.6 %collective-permute-start.4 = (f32[128,1]{0,1:T(1,128)S(1)}, f32[128,1]{0,1:T(1,128)S(1)}, u32[]{:S(2)}, u32[]{:S(2)}) collective-permute-start(f32[128,1]{0,1:T(1,128)S(1)} %bitcast.48), channel_id=1, source_target_pairs={{0,8},{8,0},{16,24},{24,16},{1,9},{9,1},{17,25},{25,17},{2,10},{10... | collective-permute-start | bytes 1544 | tf_op jit(solution)/shard_map/ppermute | solution.py:16
  55.1 4.4 %collective-permute-start.5 = (f32[128,1]{0,1:T(1,128)S(1)}, f32[128,1]{0,1:T(1,128)S(1)}, u32[]{:S(2)}, u32[]{:S(2)}) collective-permute-start(f32[128,1]{0,1:T(1,128)S(1)} %bitcast_add_fusion), channel_id=1, source_target_pairs={{0,16},{8,24},{16,0},{24,8},{1,17},{9,25},{17,1},{25,9},{2,18},{10... | collective-permute-start | bytes 1544 | tf_op jit(solution)/shard_map/ppermute | solution.py:16
  120.0 5.2 %copy-start = (bf16[3584,2048]{1,0:T(8,128)(2,1)S(1)}, bf16[3584,2048]{1,0:T(8,128)(2,1)}, u32[]{:S(2)}) copy-start(bf16[3584,2048]{1,0:T(8,128)(2,1)} %weight_ref.3) | copy-start | bytes 44040196
  125.1 39.9 %copy-start.6 = (s32[128]{0:T(128)S(1)}, s32[128]{0:T(128)}, u32[]{:S(2)}) copy-start(s32[128]{0:T(128)} %param.11) | copy-start | bytes 1540
  128.5 8.6 %collective-permute-start.6 = (bf16[4,128,256]{2,1,0:T(8,128)(2,1)S(1)}, bf16[4,128,256]{2,1,0:T(8,128)(2,1)S(1)}, u32[]{:S(2)}, u32[]{:S(2)}) collective-permute-start(bf16[4,128,256]{2,1,0:T(8,128)(2,1)S(1)} %down.3), channel_id=1, source_target_pairs={{0,1},{1,0},{2,3},{3,2},{4,5},{5,4},{6,7},{7,6},{8,9},{9,8},{10,11... | collective-permute-start | bytes 786440 | tf_op jit(solution)/shard_map/ppermute | solution.py:16
  137.2 4.6 %collective-permute-start.7 = (bf16[128,256]{1,0:T(8,128)(2,1)S(1)}, bf16[128,256]{1,0:T(8,128)(2,1)S(1)}, u32[]{:S(2)}, u32[]{:S(2)}) collective-permute-start(bf16[128,256]{1,0:T(8,128)(2,1)S(1)} %get-tuple-element.11), channel_id=1, source_target_pairs={{0,2},{1,3},{2,0},{3,1},{4,6},{5,7},{6,4},{7,5},{8,10},{9,11},{10,... | collective-permute-start | bytes 196616 | tf_op jit(solution)/shard_map/ppermute | solution.py:16
  138.7 4.3 %collective-permute-start.8 = (bf16[128,256]{1,0:T(8,128)(2,1)S(1)}, bf16[128,256]{1,0:T(8,128)(2,1)S(1)}, u32[]{:S(2)}, u32[]{:S(2)}) collective-permute-start(bf16[128,256]{1,0:T(8,128)(2,1)S(1)} %get-tuple-element.13), channel_id=1, source_target_pairs={{0,4},{1,5},{2,6},{3,7},{4,0},{5,1},{6,2},{7,3},{8,12},{9,13},{10,... | collective-permute-start | bytes 196616 | tf_op jit(solution)/shard_map/ppermute | solution.py:16
  139.9 5.2 %collective-permute-start.9 = (bf16[128,256]{1,0:T(8,128)(2,1)S(1)}, bf16[128,256]{1,0:T(8,128)(2,1)S(1)}, u32[]{:S(2)}, u32[]{:S(2)}) collective-permute-start(bf16[128,256]{1,0:T(8,128)(2,1)S(1)} %get-tuple-element.12), channel_id=1, source_target_pairs={{0,6},{1,7},{2,4},{3,5},{4,2},{5,3},{6,0},{7,1},{8,14},{9,15},{10,... | collective-permute-start | bytes 196616 | tf_op jit(solution)/shard_map/ppermute | solution.py:16
  145.1 4.5 %collective-permute-start.10 = (bf16[128,256]{1,0:T(8,128)(2,1)S(1)}, bf16[128,256]{1,0:T(8,128)(2,1)S(1)}, u32[]{:S(2)}, u32[]{:S(2)}) collective-permute-start(bf16[128,256]{1,0:T(8,128)(2,1)S(1)} %fusion.4.own_ref), channel_id=1, source_target_pairs={{0,8},{8,0},{16,24},{24,16},{1,9},{9,1},{17,25},{25,17},{2,10},{10... | collective-permute-start | bytes 196616 | tf_op jit(solution)/shard_map/ppermute | solution.py:16
  145.2 6.7 %collective-permute-start.11 = (bf16[128,256]{1,0:T(8,128)(2,1)S(1)}, bf16[128,256]{1,0:T(8,128)(2,1)S(1)}, u32[]{:S(2)}, u32[]{:S(2)}) collective-permute-start(bf16[128,256]{1,0:T(8,128)(2,1)S(1)} %fusion.4.own_ref), channel_id=1, source_target_pairs={{0,16},{8,24},{16,0},{24,8},{1,17},{9,25},{17,1},{25,9},{2,18},{10... | collective-permute-start | bytes 196616 | tf_op jit(solution)/shard_map/ppermute | solution.py:16
  146.5 6.1 %collective-permute-start.12 = (bf16[128,256]{1,0:T(8,128)(2,1)S(1)}, bf16[128,256]{1,0:T(8,128)(2,1)S(1)}, u32[]{:S(2)}, u32[]{:S(2)}) collective-permute-start(bf16[128,256]{1,0:T(8,128)(2,1)S(1)} %fusion.4.own_ref), channel_id=1, source_target_pairs={{0,24},{8,16},{16,8},{24,0},{1,25},{9,17},{17,9},{25,1},{2,26},{10... | collective-permute-start | bytes 196616 | tf_op jit(solution)/shard_map/ppermute | solution.py:16
  152.6 9.0 %collective-permute-start.14 = (bf16[4,128,256]{2,1,0:T(8,128)(2,1)S(1)}, bf16[4,128,256]{2,1,0:T(8,128)(2,1)S(1)}, u32[]{:S(2)}, u32[]{:S(2)}) collective-permute-start(bf16[4,128,256]{2,1,0:T(8,128)(2,1)S(1)} %pad_maximum_fusion.2.refs_0_), channel_id=1, source_target_pairs={{0,2},{1,3},{2,0},{3,1},{4,6},{5,7},{6,4},{7,5},{8,10},{9,11},{10,... | collective-permute-start | bytes 786440 | tf_op jit(solution)/shard_map/ppermute | solution.py:16
  153.3 11.6 %collective-permute-start.15 = (bf16[4,128,256]{2,1,0:T(8,128)(2,1)S(1)}, bf16[4,128,256]{2,1,0:T(8,128)(2,1)S(1)}, u32[]{:S(2)}, u32[]{:S(2)}) collective-permute-start(bf16[4,128,256]{2,1,0:T(8,128)(2,1)S(1)} %pad_maximum_fusion.2.refs_0_), channel_id=1, source_target_pairs={{0,4},{1,5},{2,6},{3,7},{4,0},{5,1},{6,2},{7,3},{8,12},{9,13},{10,... | collective-permute-start | bytes 786440 | tf_op jit(solution)/shard_map/ppermute | solution.py:16
  154.0 10.8 %collective-permute-start.16 = (bf16[4,128,256]{2,1,0:T(8,128)(2,1)S(1)}, bf16[4,128,256]{2,1,0:T(8,128)(2,1)S(1)}, u32[]{:S(2)}, u32[]{:S(2)}) collective-permute-start(bf16[4,128,256]{2,1,0:T(8,128)(2,1)S(1)} %pad_maximum_fusion.2.refs_0_), channel_id=1, source_target_pairs={{0,6},{1,7},{2,4},{3,5},{4,2},{5,3},{6,0},{7,1},{8,14},{9,15},{10,... | collective-permute-start | bytes 786440 | tf_op jit(solution)/shard_map/ppermute | solution.py:16
  165.0 3.9 %collective-permute-start.17 = (bf16[3,4,128,256]{3,2,1,0:T(8,128)(2,1)S(1)}, bf16[3,4,128,256]{3,2,1,0:T(8,128)(2,1)S(1)}, u32[]{:S(2)}, u32[]{:S(2)}) collective-permute-start(bf16[3,4,128,256]{3,2,1,0:T(8,128)(2,1)S(1)} %pad_maximum_fusion), channel_id=1, source_target_pairs={{0,1},{1,0},{2,3},{3,2},{4,5},{5,4},{6,7},{7,6},{8,9},{9,8},{10,11... | collective-permute-start | bytes 2359304 | tf_op jit(solution)/shard_map/ppermute | solution.py:16
  166.0 3.0 %collective-permute-start.13 = (bf16[4,128,256]{2,1,0:T(8,128)(2,1)S(1)}, bf16[4,128,256]{2,1,0:T(8,128)(2,1)S(1)}, u32[]{:S(2)}, u32[]{:S(2)}) collective-permute-start(bf16[4,128,256]{2,1,0:T(8,128)(2,1)S(1)} %pad_maximum_fusion.2.refs_0_), channel_id=1, source_target_pairs={{0,1},{1,0},{2,3},{3,2},{4,5},{5,4},{6,7},{7,6},{8,9},{9,8},{10,11... | collective-permute-start | bytes 786440 | tf_op jit(solution)/shard_map/ppermute | solution.py:16
  (3 other events, 15.5 us)
Sparse Core Ops, SparseCore 0:
  36.2 24.4 reduce-scatter.2
  63.6 24.0 reduce-scatter.4

commit v3 on v2

v3 whole, which is shorter than its diff:
```python
import functools
import jax
import jax.numpy as jnp
from jax import lax
from jax.experimental import pallas as pl
from jax.experimental.pallas import tpu as pltpu
from jax.sharding import PartitionSpec as P

D = 8192
CLASSES = 64
BF16 = jnp.bfloat16
F32 = jnp.float32
STREAM = 52 * 1024 * 1024
SMALL = 16 * 1024 * 1024
WHOLE = pl.BlockSpec(memory_space=pltpu.VMEM)
ANYWHERE = pl.BlockSpec(memory_space=pl.ANY)


def swap(value, axis, size, mask):
    return lax.ppermute(value, axis, [(i, i ^ mask) for i in range(size)])


def params(limit):
    return pltpu.CompilerParams(vmem_limit_bytes=limit)


def cost(flops, bytes_accessed):
    return pl.CostEstimate(flops=flops, bytes_accessed=bytes_accessed, transcendentals=0)


def tile_of(width):
    for tile in (256, 128):
        if width % tile == 0:
            return tile
    return width


def tokens_kernel(chips, panel, *refs):
    near, (far, gain, lhs, cols, squares, x) = refs[:chips], refs[chips:]
    h = lax.axis_index("hid")
    rows = near[0].shape[0]
    for e in range(chips):
        for core, block in ((0, near[e][...]), (1, far[e * rows:(e + 1) * rows, :])):
            at = pl.multiple_of((h ^ (2 * e + core)) * rows, rows)
            x[pl.ds(at, rows), :] = block
    values = x[...].astype(F32)
    lhs[...] = (values * gain[...]).astype(BF16)
    squares[...] = jnp.sum(values * values, axis=1, keepdims=True)
    cols[...] = x[:, pl.ds(pl.multiple_of(h * panel, panel), panel)].astype(F32)


def gather_tokens(own, gain, n_hid):
    chips = n_hid // 2
    rows, block = own.shape
    ntok, panel = rows * n_hid, block // n_hid
    near = [own] + [swap(own, "hid", n_hid, 2 * e) for e in range(1, chips)]
    far = swap(jnp.concatenate(near, axis=0), "hid", n_hid, 1)
    if panel % 128 == 0:
        return pl.pallas_call(
            functools.partial(tokens_kernel, chips, panel),
            out_shape=(
                jax.ShapeDtypeStruct((ntok, block), BF16),
                jax.ShapeDtypeStruct((ntok, panel), F32),
                jax.ShapeDtypeStruct((ntok, 1), F32),
            ),
            in_specs=[WHOLE] * (chips + 2),
            out_specs=(WHOLE, WHOLE, WHOLE),
            scratch_shapes=[pltpu.VMEM((ntok, block), BF16)],
            compiler_params=params(SMALL),
            cost_estimate=cost(4 * ntok * block, 4 * ntok * block),
            name="tokens",
        )(*near, far, gain[None, :])
    h = lax.axis_index("hid")
    both = jnp.concatenate(near + [far], axis=0)
    place = jnp.arange(ntok, dtype=jnp.int32)
    slot = place // rows
    token = (h ^ (2 * (slot % chips) + slot // chips)) * rows + place % rows
    order = (place[:, None] == token[None, :]).astype(BF16)
    x = jnp.dot(order, both, preferred_element_type=F32)
    cols = lax.dynamic_slice_in_dim(x, h * panel, panel, 1)
    return (x * gain[None, :]).astype(BF16), cols, jnp.sum(x * x, axis=1, keepdims=True)


def gate_up_kernel(lhs_ref, gate_ref, up_ref, *refs):
    outs, both = refs[:-1], refs[-1]
    tile = gate_ref.shape[1]
    lhs = lhs_ref[...]
    both[:, :tile] = jnp.dot(lhs, gate_ref[...], preferred_element_type=F32)
    both[:, tile:] = jnp.dot(lhs, up_ref[...], preferred_element_type=F32)
    rows = outs[0].shape[0]
    for d, out in enumerate(outs):
        at = pl.multiple_of((lax.axis_index("tok") ^ d) * rows, rows) if len(outs) > 1 else 0
        out[...] = both[pl.ds(at, rows), :].astype(BF16)


def gate_up(lhs, gate_weight, up_weight, start, width, tile, blocks):
    ntok, depth = lhs.shape
    at = start // tile
    weight = pl.BlockSpec((depth, tile), lambda i: (0, at + i))
    return pl.pallas_call(
        gate_up_kernel,
        grid=(width // tile,),
        out_shape=[jax.ShapeDtypeStruct((ntok // blocks, 2 * width), BF16)] * blocks,
        in_specs=[pl.BlockSpec((ntok, depth), lambda i: (0, 0)), weight, weight],
        out_specs=[pl.BlockSpec((ntok // blocks, 2 * tile), lambda i: (0, i))] * blocks,
        scratch_shapes=[pltpu.VMEM((ntok, 2 * tile), F32)],
        compiler_params=params(STREAM),
        cost_estimate=cost(4 * ntok * depth * width, 4 * depth * width),
        name="gate_up",
    )(lhs, gate_weight, up_weight)


def copy_kernel(value_ref, after_ref, out_ref):
    out_ref[...] = value_ref[...]


def copy_after(value, after):
    return pl.pallas_call(
        copy_kernel,
        out_shape=jax.ShapeDtypeStruct(value.shape, value.dtype),
        in_specs=[WHOLE, ANYWHERE],
        out_specs=WHOLE,
        compiler_params=params(SMALL),
        cost_estimate=cost(0, 4 * value.size),
        name="copy",
    )(value, after)


def line_terms(mine, n_tok, after):
    def plus(one, two):
        return (one.astype(F32) + two.astype(F32)).astype(BF16)

    inward, middle = [(0, 1), (3, 2)], [(1, 2), (2, 1)]
    first = mine[3] if after is None else copy_after(mine[3], after)
    far_in = lax.ppermute(first, "tok", inward)
    far_over = lax.ppermute(plus(mine[2], far_in), "tok", middle)
    near_in = lax.ppermute(mine[2], "tok", inward)
    near_over = lax.ppermute(plus(mine[3], near_in), "tok", middle)
    last = swap(plus(mine[1], far_over), "tok", n_tok, 1)
    return last, near_over, far_in


def hidden_kernel(tile, own_ref, one_ref, two_ref, scale_ref, out_ref):
    scale = scale_ref[...]

    def total(at):
        cols = slice(at, at + tile)
        return (
            own_ref[:, cols].astype(F32) + one_ref[:, cols].astype(F32) + two_ref[:, cols].astype(F32)
        ) * scale

    for at in range(0, out_ref.shape[1], tile):
        gate, up = total(2 * at), total(2 * at + tile)
        out_ref[:, at:at + tile] = (jax.nn.silu(gate) * up).astype(BF16)


def hidden_rows(own, one, two, scale, tile):
    rows, width = one.shape
    return pl.pallas_call(
        functools.partial(hidden_kernel, tile),
        out_shape=jax.ShapeDtypeStruct((rows, width // 2), BF16),
        in_specs=[WHOLE] * 4,
        out_specs=WHOLE,
        compiler_params=params(SMALL),
        cost_estimate=cost(10 * rows * width, 8 * rows * width),
        name="hidden",
    )(own, one, two, scale)


def line_gather(own, z, n_tok):
    beside = swap(own, "tok", n_tok, 1)
    over = lax.ppermute(jnp.stack([own, beside]), "tok", [(1, 2), (2, 1)])
    out = lax.ppermute(over, "tok", [(1, 0), (2, 3)])
    inner = (z == 1) | (z == 2)
    return [own, beside, jnp.where(inner, over[1], out[0]), jnp.where(inner, over[0], out[1])]


def token_blocks(own, n_tok):
    if n_tok == 4:
        return jnp.concatenate(line_gather(own, lax.axis_index("tok"), n_tok), axis=0)
    return lax.all_gather(own, "tok", axis=0, tiled=True)


def down_kernel(order_ref, lhs_ref, weight_ref, *refs):
    total = jnp.dot(lhs_ref[...], weight_ref[...], preferred_element_type=F32)
    if len(refs) == 2:
        total = total + refs[0][...]
    refs[-1][...] = total.astype(refs[-1].dtype)


def down(hidden, weight, order, panel, kind, chunk, before, skip=0):
    ntok, depth = hidden.shape
    count = order.shape[0]
    each = pl.BlockSpec((None, ntok, panel), lambda i, order: (i, 0, 0))
    added = [] if before is None else [before]
    return pl.pallas_call(
        down_kernel,
        grid_spec=pltpu.PrefetchScalarGridSpec(
            num_scalar_prefetch=1,
            grid=(count,),
            in_specs=[
                pl.BlockSpec((ntok, depth), lambda i, order: (0, 0)),
                pl.BlockSpec((depth, panel), lambda i, order: (chunk, order[i])),
            ] + [pl.BlockSpec((None, ntok, panel), lambda i, order: (i + skip, 0, 0))] * len(added),
            out_specs=each,
        ),
        out_shape=jax.ShapeDtypeStruct((count, ntok, panel), kind),
        compiler_params=params(STREAM),
        cost_estimate=cost(2 * ntok * depth * panel * count, 2 * depth * panel * count),
        name="down",
    )(order, hidden, weight, *added)


def gram_kernel(masks, n_hid, ntok, own_ref, *refs):
    stacks, (out_ref, tiles, sems) = refs[:len(masks)], refs[-3:]
    z = lax.axis_index("tok")
    h = lax.axis_index("hid")
    width = own_ref.shape[1]
    left = own_ref[...].T
    copies = []
    for stack, here in zip(stacks, masks):
        for at, mask in enumerate(here):
            for d in range(stack.shape[1]):
                number = len(copies)
                tiles[number] = jnp.dot(left, stack[at, d], preferred_element_type=F32) * (1.0 / ntok)
                column = ((z ^ d) * n_hid + (h ^ mask)) * width
                copy = pltpu.make_async_copy(
                    tiles.at[number], out_ref.at[:, pl.ds(pl.multiple_of(column, width), width)], sems.at[number]
                )
                copy.start()
                copies.append(copy)
    for copy in copies:
        copy.wait()


def gram_part(resid_cols, stacks, masks, n_tok, n_hid, before):
    ntok, width = resid_cols.shape
    here = n_tok * sum(len(m) for m in masks)
    operands = [resid_cols, *stacks] + ([] if before is None else [before])
    return pl.pallas_call(
        functools.partial(gram_kernel, masks, n_hid, ntok),
        out_shape=jax.ShapeDtypeStruct((width, width * n_tok * n_hid), F32),
        in_specs=[WHOLE] * (1 + len(stacks)) + ([] if before is None else [ANYWHERE]),
        out_specs=ANYWHERE,
        input_output_aliases={} if before is None else {1 + len(stacks): 0},
        scratch_shapes=[pltpu.VMEM((here, width, width), F32), pltpu.SemaphoreType.DMA((here,))],
        compiler_params=params(SMALL),
        cost_estimate=cost(2 * ntok * width * width * here, 4 * width * width * here),
        name="gram",
    )(*operands)


def gram_of(resid_cols, n_tok, n_hid):
    masks = range(2, n_hid, 2)
    line = jnp.stack([resid_cols] + [swap(resid_cols, "tok", n_tok, d) for d in range(1, n_tok)])
    others = [swap(line, "hid", n_hid, mask) for mask in masks]
    line_far = swap(line, "hid", n_hid, 1)
    others_far = swap(jnp.stack(others), "hid", n_hid, 1)
    gram = gram_part(resid_cols, [line[None], line_far[None]], [[0], [1]], n_tok, n_hid, None)
    gram = gram_part(resid_cols, [o[None] for o in others], [[m] for m in masks], n_tok, n_hid, gram)
    return gram_part(resid_cols, [others_far], [[m + 1 for m in masks]], n_tok, n_hid, gram)


def on_device(n_tok, n_hid, resid_in, norm_gain, gate_weight, up_weight, down_weight, labels):
    z = lax.axis_index("tok")
    h = lax.axis_index("hid")
    chips = n_hid // 2

    lhs, x_cols, total_sq = gather_tokens(resid_in, norm_gain, n_hid)
    ntok, block = lhs.shape
    d = 1
    while d < n_tok:
        total_sq = total_sq + swap(total_sq, "tok", n_tok, d)
        d *= 2
    rows = ntok // n_tok
    own_scale = lax.rsqrt(lax.dynamic_slice_in_dim(total_sq, z * rows, rows, 0) / float(D) + 1e-05)

    shard_ff = gate_weight.shape[1]
    tile = tile_of(shard_ff)
    count = 2 if shard_ff % (2 * tile) == 0 else 1
    wide = shard_ff // count
    hidden, after = [], None
    for k in range(count):
        pair = gate_up(lhs, gate_weight, up_weight, k * wide, wide, tile, 4 if n_tok == 4 else 1)
        if n_tok == 4:
            one, two, after = line_terms(pair, n_tok, after)
            own = hidden_rows(pair[0], one, two, own_scale, tile)
        else:
            sums = lax.psum_scatter(pair[0], "tok", scatter_dimension=0, tiled=True).astype(F32) * own_scale
            pieces = [
                jax.nn.silu(sums[:, at:at + tile]) * sums[:, at + tile:at + 2 * tile]
                for at in range(0, 2 * wide, 2 * tile)
            ]
            own = jnp.concatenate(pieces, axis=1).astype(BF16)
        hidden.append(token_blocks(own, n_tok))

    panel = block // n_hid
    if n_tok == 4 and panel % 128 == 0:
        order = jnp.stack([h ^ m for m in [2 * e + 1 for e in range(chips)] + [2 * e for e in range(chips)]])
        order = order.astype(jnp.int32)
        before = None
        for k in range(count - 1):
            before = down(hidden[k], down_weight, order, panel, F32, k, before)
        other = down(hidden[-1], down_weight, order[:chips], panel, BF16, count - 1, before)
        mine = down(hidden[-1], down_weight, order[chips:], panel, F32, count - 1, before, chips)
        chip_sum = mine + swap(other, "hid", n_hid, 1).astype(F32)
        summed = chip_sum[0]
        for e in range(1, chips):
            summed = summed + swap(chip_sum[e].astype(BF16), "hid", n_hid, 2 * e).astype(F32)
        summed = jnp.concatenate(
            [lax.dynamic_slice_in_dim(summed, (z ^ d) * rows, rows, 0) for d in range(n_tok)], axis=0
        )
        resid_cols = (x_cols + summed).astype(BF16)
        gram = gram_of(resid_cols, n_tok, n_hid)
    else:
        partial_out = jnp.dot(jnp.concatenate(hidden, axis=1), down_weight, preferred_element_type=F32)
        summed = lax.psum_scatter(
            partial_out.astype(BF16), "hid", scatter_dimension=1, tiled=True
        ).astype(F32)
        if n_tok == 4:
            summed = jnp.concatenate(
                [lax.dynamic_slice_in_dim(summed, (z ^ d) * rows, rows, 0) for d in range(n_tok)], axis=0
            )
        resid_cols = (x_cols + summed).astype(BF16)
        everyone = lax.all_gather(resid_cols, ("tok", "hid"), axis=1, tiled=True)
        gram = lax.dot_general(
            resid_cols, everyone, (((0,), (0,)), ((), ())), preferred_element_type=F32
        ) / float(ntok)

    onehot = (labels[:, None] == jnp.arange(CLASSES, dtype=jnp.int32)[None, :]).astype(BF16)
    counts = jnp.sum(onehot.astype(F32), axis=0)
    class_sums = lax.dot_general(
        resid_cols, onehot, (((0,), (0,)), ((), ())), preferred_element_type=F32
    )
    cross = class_sums / jnp.maximum(counts, 1.0)[None, :]
    return (gram, cross)


def solution(mesh):
    return jax.shard_map(
        functools.partial(on_device, mesh.shape["tok"], mesh.shape["hid"]),
        mesh=mesh,
        in_specs=(
            P("hid", "tok"),
            P("tok"),
            P("tok", "hid"),
            P("tok", "hid"),
            P("hid", "tok"),
            P(),
        ),
        out_specs=(P(("tok", "hid"), None), P(("tok", "hid"), None)),
        check_vma=False,
    )
```

time: 179 us -> 155 us (0.87)
  blocking collectives: 30.6 us -> 0 us
  local copies, waits for them, and re-layouts: 32.2 us -> 1.68 us
  starting transfers between devices: 21.4 us -> 51.6 us
  Pallas kernels: 21.4 us -> 38 us
  between operations: 14.4 us -> 1.06 us
  waiting for transfers between devices: 53.6 us -> 59.5 us
    all_gather x2 -> x0, blocking collectives: 30.6 us -> none  [on_device(): hidden.append(lax.all_gather(mine, 'tok', axis=0, tiled=True))]
    unnamed x19 -> x8, local copies, waits for them, and re-layouts: 32 us -> 1.55 us
    reduce_scatter x2 -> x0, waiting for transfers between devices: 28.1 us -> none  [on_device(): lax.psum_scatter(pair, 'tok', scatter_dimension=0, tiled=True).astype(F32)]
    ppermute x0 -> x12, waiting for transfers between devices: none -> 22 us  [the longest x2 11.9 us: line_gather(): out = lax.ppermute(over, 'tok', [(1, 0), (2, 3)])]
    ppermute x18 -> x22, starting transfers between devices: 21.3 us -> 37.5 us  [swap(): return lax.ppermute(value, axis, [(i, i ^ mask) for i in range(size)])]
    ppermute x0 -> x12, starting transfers between devices: none -> 14 us  [the longest x2 4.8 us: line_terms(): far_in = lax.ppermute(first, 'tok', inward)]
    ppermute x18 -> x22, waiting for transfers between devices: 25.5 us -> 37.5 us  [swap(): return lax.ppermute(value, axis, [(i, i ^ mask) for i in range(size)])]
    pallas_call x2 -> x3, Pallas kernels: 6.64 us -> 14.9 us  [down(): pl.pallas_call(down_kernel, grid_spec=pltpu.PrefetchScalarGridSpec(num_sc...]
  transfers between devices with their start and end apart: 20 -> 34, of which waited for: 15 -> 21; matrix products, arithmetic and copies ran while one was open for 1% -> 1% of each run, Pallas kernels for 6% -> 11%
where the time goes in v3:
time: 155 us; the launch traced here: 154 us
  waiting for transfers between devices  59.5 us (38%)
  starting transfers between devices  51.6 us (33%)
  Pallas kernels  38 us (25%)
  other arithmetic  1.9 us (1%)
  local copies, waits for them, and re-layouts  1.68 us (1%)
    ppermute x22, starting transfers between devices, swap(): return lax.ppermute(value, axis, [(i, i ^ mask) for i in range(size)])  37.5 us
    ppermute x22, waiting for transfers between devices, swap(): return lax.ppermute(value, axis, [(i, i ^ mask) for i in range(size)])  37.5 us
    pallas_call x2, Pallas kernels, gate_up(): pl.pallas_call(gate_up_kernel, grid=(width // tile,), out_shape=[jax.Shap...  16.9 us
    pallas_call x3, Pallas kernels, down(): pl.pallas_call(down_kernel, grid_spec=pltpu.PrefetchScalarGridSpec(num_sc...  14.9 us
    ppermute x2, waiting for transfers between devices, line_gather(): out = lax.ppermute(over, 'tok', [(1, 0), (2, 3)])  11.9 us
    ppermute x2, waiting for transfers between devices, line_terms(): near_in = lax.ppermute(mine[2], 'tok', inward)  6.71 us
    pallas_call x3, Pallas kernels, gram_part(): pl.pallas_call(functools.partial(gram_kernel, masks, n_hid, ntok), out_sh...  5.65 us
    ppermute x2, starting transfers between devices, line_terms(): far_in = lax.ppermute(first, 'tok', inward)  4.8 us
  transfers between devices with their start and end apart: 34, of which 21 were waited for; matrix products, arithmetic and copies ran while one was open for 1% of the time, Pallas kernels for 11%

profile of v3, /device:TPU:0, one launch (start us, length us, event | category | flops | bytes accessed | tf_op | source)
XLA Modules:
  0.0 154.5 jit_solution(1063745786879413517)
XLA Ops:
  0.6 3.0 %collective-permute-start = (bf16[16,2048]{1,0:T(8,128)(2,1)}, bf16[16,2048]{1,0:T(8,128)(2,1)S(1)}, u32[]{:S(2)}, u32[]{:S(2)}) collective-permute-start(bf16[16,2048]{1,0:T(8,128)(2,1)} %refs_0_.1), channel_id=1, source_target_pairs={{0,2},{1,3},{2,0},{3,1},{4,6},{5,7},{6,4},{7,5},{8,10},{9,11},{10,... | collective-permute-start | bytes 196616 | tf_op jit(solution)/shard_map/ppermute | solution.py:20
  8.1 2.4 %collective-permute-done.2.refs_3_ = bf16[16,2048]{1,0:T(8,128)(2,1)S(1)} collective-permute-done((bf16[16,2048]{1,0:T(8,128)(2,1)}, bf16[16,2048]{1,0:T(8,128)(2,1)S(1)}, u32[]{:S(2)}, u32[]{:S(2)}) %collective-permute-start.2) | collective-permute-done | bytes 65568 | tf_op jit(solution)/shard_map/ppermute | solution.py:20
  14.8 8.4 %gate_up.3 = (bf16[32,3584]{1,0:T(8,128)(2,1)S(1)}, bf16[32,3584]{1,0:T(8,128)(2,1)S(1)}, bf16[32,3584]{1,0:T(8,128)(2,1)S(1)}, bf16[32,3584]{1,0:T(8,128)(2,1)S(1)}) custom-call(bf16[128,2048]{1,0:T(8,128)(2,1)S(1)} %get-tuple-element.14.lhs_ref, bf16[2048,3584]{1,0:T(8,128)(2,1)} %gate_ref.3, bf16[2048,3584]{1,0:T(8,128)(2,1)} %up_ref.3), custom_call_target="tpu_custom_call" | custom-call | flops 1879048192 | bytes 14680064 | tf_op jit(solution)/shard_map/gate_up/pallas_call | solution.py:100
  23.3 3.5 %collective-permute-start.4 = (bf16[32,3584]{1,0:T(8,128)(2,1)S(1)}, bf16[32,3584]{1,0:T(8,128)(2,1)S(1)}, u32[]{:S(2)}, u32[]{:S(2)}) collective-permute-start(bf16[32,3584]{1,0:T(8,128)(2,1)S(1)} %get-tuple-element.19), channel_id=1, source_target_pairs={{0,8},{24,16},{1,9},{25,17},{2,10},{26,18},{3,11},{27,19},{4,12},{... | collective-permute-start | bytes 688136 | tf_op jit(solution)/shard_map/ppermute | solution.py:135
  26.8 8.4 %gate_up.2 = (bf16[32,3584]{1,0:T(8,128)(2,1)S(1)}, bf16[32,3584]{1,0:T(8,128)(2,1)S(1)}, bf16[32,3584]{1,0:T(8,128)(2,1)S(1)}, bf16[32,3584]{1,0:T(8,128)(2,1)S(1)}) custom-call(bf16[128,2048]{1,0:T(8,128)(2,1)S(1)} %get-tuple-element.14.lhs_ref, bf16[2048,3584]{1,0:T(8,128)(2,1)} %gate_ref.3, bf16[2048,3584]{1,0:T(8,128)(2,1)} %up_ref.3), custom_call_target="tpu_custom_call" | custom-call | flops 1879048192 | bytes 14680064 | tf_op jit(solution)/shard_map/gate_up/pallas_call | solution.py:100
  39.2 3.3 %collective-permute-done.8 = bf16[32,3584]{1,0:T(8,128)(2,1)S(1)} collective-permute-done((bf16[32,3584]{1,0:T(8,128)(2,1)S(1)}, bf16[32,3584]{1,0:T(8,128)(2,1)S(1)}, u32[]{:S(2)}, u32[]{:S(2)}) %collective-permute-start.8) | collective-permute-done | bytes 229408 | tf_op jit(solution)/shard_map/ppermute | solution.py:137
  43.9 3.4 %collective-permute-done.17 = bf16[32,3584]{1,0:T(8,128)(2,1)S(1)} collective-permute-done((bf16[32,3584]{1,0:T(8,128)(2,1)S(1)}, bf16[32,3584]{1,0:T(8,128)(2,1)S(1)}, u32[]{:S(2)}, u32[]{:S(2)}) %collective-permute-start.17) | collective-permute-done | bytes 229408 | tf_op jit(solution)/shard_map/ppermute | solution.py:137
  48.1 3.4 %collective-permute-done.5 = bf16[32,3584]{1,0:T(8,128)(2,1)S(1)} collective-permute-done((bf16[32,3584]{1,0:T(8,128)(2,1)S(1)}, bf16[32,3584]{1,0:T(8,128)(2,1)S(1)}, u32[]{:S(2)}, u32[]{:S(2)}) %collective-permute-start.5) | collective-permute-done | bytes 229408 | tf_op jit(solution)/shard_map/ppermute | solution.py:135
  52.3 7.3 %collective-permute-start.16 = (bf16[32,3584]{1,0:T(8,128)(2,1)S(1)}, bf16[32,3584]{1,0:T(8,128)(2,1)S(1)}, u32[]{:S(2)}, u32[]{:S(2)}) collective-permute-start(bf16[32,3584]{1,0:T(8,128)(2,1)S(1)} %add_convert_fusion.1), channel_id=1, source_target_pairs={{0,8},{8,0},{16,24},{24,16},{1,9},{9,1},{17,25},{25,17},{2,10},{10... | collective-permute-start | bytes 688136 | tf_op jit(solution)/shard_map/ppermute | solution.py:20
  59.7 8.1 %collective-permute-start.7 = (bf16[32,3584]{1,0:T(8,128)(2,1)S(1)}, bf16[32,3584]{1,0:T(8,128)(2,1)S(1)}, u32[]{:S(2)}, u32[]{:S(2)}) collective-permute-start(bf16[32,3584]{1,0:T(8,128)(2,1)S(1)} %add_convert_fusion.4), channel_id=1, source_target_pairs={{0,8},{8,0},{16,24},{24,16},{1,9},{9,1},{17,25},{25,17},{2,10},{10... | collective-permute-start | bytes 688136 | tf_op jit(solution)/shard_map/ppermute | solution.py:20
  67.9 5.5 %collective-permute-done.10 = f32[128,1]{1,0:T(8,128)S(1)} collective-permute-done((f32[128,1]{1,0:T(8,128)S(1)}, f32[128,1]{1,0:T(8,128)S(1)}, u32[]{:S(2)}, u32[]{:S(2)}) %collective-permute-start.10) | collective-permute-done | bytes 544 | tf_op jit(solution)/shard_map/ppermute | solution.py:20
  75.6 3.1 %collective-permute-done.11 = f32[128,1]{1,0:T(8,128)S(1)} collective-permute-done((f32[128,1]{1,0:T(8,128)S(1)}, f32[128,1]{1,0:T(8,128)S(1)}, u32[]{:S(2)}, u32[]{:S(2)}) %collective-permute-start.11) | collective-permute-done | bytes 544 | tf_op jit(solution)/shard_map/ppermute | solution.py:20
  78.9 2.9 %collective-permute-start.19 = (bf16[32,1792]{1,0:T(8,128)(2,1)S(1)}, bf16[32,1792]{1,0:T(8,128)(2,1)S(1)}, u32[]{:S(2)}, u32[]{:S(2)}) collective-permute-start(bf16[32,1792]{1,0:T(8,128)(2,1)S(1)} %hidden.3), channel_id=1, source_target_pairs={{0,8},{8,0},{16,24},{24,16},{1,9},{9,1},{17,25},{25,17},{2,10},{10... | collective-permute-start | bytes 344072 | tf_op jit(solution)/shard_map/ppermute | solution.py:20
  82.0 2.5 %collective-permute-done.19 = bf16[32,1792]{1,0:T(8,128)(2,1)S(1)} collective-permute-done((bf16[32,1792]{1,0:T(8,128)(2,1)S(1)}, bf16[32,1792]{1,0:T(8,128)(2,1)S(1)}, u32[]{:S(2)}, u32[]{:S(2)}) %collective-permute-start.19) | collective-permute-done | bytes 114720 | tf_op jit(solution)/shard_map/ppermute | solution.py:20
  90.2 9.5 %collective-permute-done.21 = bf16[2,32,1792]{2,1,0:T(8,128)(2,1)S(1)} collective-permute-done((bf16[2,32,1792]{2,1,0:T(8,128)(2,1)S(1)}, bf16[2,32,1792]{2,1,0:T(8,128)(2,1)S(1)}, u32[]{:S(2)}, u32[]{:S(2)}) %collective-permute-start.21) | collective-permute-done | bytes 229408 | tf_op jit(solution)/shard_map/ppermute | solution.py:173
  99.7 2.5 %collective-permute-done.14 = bf16[2,32,1792]{2,1,0:T(8,128)(2,1)S(1)} collective-permute-done((bf16[2,32,1792]{2,1,0:T(8,128)(2,1)S(1)}, bf16[2,32,1792]{2,1,0:T(8,128)(2,1)S(1)}, u32[]{:S(2)}, u32[]{:S(2)}) %collective-permute-start.14) | collective-permute-done | bytes 229408 | tf_op jit(solution)/shard_map/ppermute | solution.py:173
  102.3 7.0 %down.3.refs_0_ = f32[8,128,256]{2,1,0:T(8,128)S(1)} custom-call(s32[8]{0:T(128)S(1)} %stack.88.order_ref, bf16[128,1792]{1,0:T(8,128)(2,1)S(1)} %pad_maximum_fusion.2.lhs_ref, bf16[3584,2048]{1,0:T(8,128)(2,1)} %weight_ref.5), custom_call_target="tpu_custom_call" | custom-call | flops 939524096 | bytes 7340032 | tf_op jit(solution)/shard_map/down/pallas_call | solution.py:196
  109.4 3.9 %down.5 = bf16[4,128,256]{2,1,0:T(8,128)(2,1)S(1)} custom-call(s32[4]{0:T(128)S(1)} %pad_add_fusion.1.order_ref, bf16[128,1792]{1,0:T(8,128)(2,1)S(1)} %pad_maximum_fusion.1.lhs_ref, bf16[3584,2048]{1,0:T(8,128)(2,1)} %weight_ref.5, f32[8,128,256]{2,1,0:T(8,128)S(1)} %down.3.refs_0_), custom_call_target="tpu_custom_call" | custom-call | flops 469762048 | bytes 3670016 | tf_op jit(solution)/shard_map/down/pallas_call | solution.py:196
  113.5 4.0 %down.4 = f32[4,128,256]{2,1,0:T(8,128)S(1)} custom-call(s32[4]{0:T(128)S(1)} %pad_add_fusion.order_ref, bf16[128,1792]{1,0:T(8,128)(2,1)S(1)} %pad_maximum_fusion.1.lhs_ref, bf16[3584,2048]{1,0:T(8,128)(2,1)} %weight_ref.5, f32[8,128,256]{2,1,0:T(8,128)} %copy-done), custom_call_target="tpu_custom_call" | custom-call | flops 469762048 | bytes 3670016 | tf_op jit(solution)/shard_map/down/pallas_call | solution.py:196
  118.7 2.4 %collective-permute-start.25 = (bf16[128,256]{1,0:T(8,128)(2,1)S(1)}, bf16[128,256]{1,0:T(8,128)(2,1)S(1)}, u32[]{:S(2)}, u32[]{:S(2)}) collective-permute-start(bf16[128,256]{1,0:T(8,128)(2,1)S(1)} %get-tuple-element.33), channel_id=1, source_target_pairs={{0,6},{1,7},{2,4},{3,5},{4,2},{5,3},{6,0},{7,1},{8,14},{9,15},{10,... | collective-permute-start | bytes 196616 | tf_op jit(solution)/shard_map/ppermute | solution.py:20
  124.0 3.0 %collective-permute-start.27 = (bf16[128,256]{1,0:T(8,128)(2,1)S(1)}, bf16[128,256]{1,0:T(8,128)(2,1)S(1)}, u32[]{:S(2)}, u32[]{:S(2)}) collective-permute-start(bf16[128,256]{1,0:T(8,128)(2,1)S(1)} %fusion.3.own_ref), channel_id=1, source_target_pairs={{0,16},{8,24},{16,0},{24,8},{1,17},{9,25},{17,1},{25,9},{2,18},{10... | collective-permute-start | bytes 196616 | tf_op jit(solution)/shard_map/ppermute | solution.py:20
  129.7 3.4 %collective-permute-done.28 = bf16[128,256]{1,0:T(8,128)(2,1)S(1)} collective-permute-done((bf16[128,256]{1,0:T(8,128)(2,1)S(1)}, bf16[128,256]{1,0:T(8,128)(2,1)S(1)}, u32[]{:S(2)}, u32[]{:S(2)}) %collective-permute-start.28) | collective-permute-done | bytes 65568 | tf_op jit(solution)/shard_map/ppermute | solution.py:20
  136.7 5.3 %collective-permute-done.29 = bf16[4,128,256]{2,1,0:T(8,128)(2,1)S(1)} collective-permute-done((bf16[4,128,256]{2,1,0:T(8,128)(2,1)S(1)}, bf16[4,128,256]{2,1,0:T(8,128)(2,1)S(1)}, u32[]{:S(2)}, u32[]{:S(2)}) %collective-permute-start.29) | collective-permute-done | bytes 262176 | tf_op jit(solution)/shard_map/ppermute | solution.py:20
  142.0 4.0 %collective-permute-done.30 = bf16[4,128,256]{2,1,0:T(8,128)(2,1)S(1)} collective-permute-done((bf16[4,128,256]{2,1,0:T(8,128)(2,1)S(1)}, bf16[4,128,256]{2,1,0:T(8,128)(2,1)S(1)}, u32[]{:S(2)}, u32[]{:S(2)}) %collective-permute-start.30) | collective-permute-done | bytes 262176 | tf_op jit(solution)/shard_map/ppermute | solution.py:20
  (91 shorter events, 43.1 us)
Async XLA Ops:
  0.6 5.7 %collective-permute-start = (bf16[16,2048]{1,0:T(8,128)(2,1)}, bf16[16,2048]{1,0:T(8,128)(2,1)S(1)}, u32[]{:S(2)}, u32[]{:S(2)}) collective-permute-start(bf16[16,2048]{1,0:T(8,128)(2,1)} %refs_0_.1), channel_id=1, source_target_pairs={{0,2},{1,3},{2,0},{3,1},{4,6},{5,7},{6,4},{7,5},{8,10},{9,11},{10,... | collective-permute-start | bytes 196616 | tf_op jit(solution)/shard_map/ppermute | solution.py:20
  5.2 5.4 %collective-permute-start.2 = (bf16[16,2048]{1,0:T(8,128)(2,1)}, bf16[16,2048]{1,0:T(8,128)(2,1)S(1)}, u32[]{:S(2)}, u32[]{:S(2)}) collective-permute-start(bf16[16,2048]{1,0:T(8,128)(2,1)} %refs_0_.1), channel_id=1, source_target_pairs={{0,6},{1,7},{2,4},{3,5},{4,2},{5,3},{6,0},{7,1},{8,14},{9,15},{10,... | collective-permute-start | bytes 196616 | tf_op jit(solution)/shard_map/ppermute | solution.py:20
  23.3 14.6 %collective-permute-start.4 = (bf16[32,3584]{1,0:T(8,128)(2,1)S(1)}, bf16[32,3584]{1,0:T(8,128)(2,1)S(1)}, u32[]{:S(2)}, u32[]{:S(2)}) collective-permute-start(bf16[32,3584]{1,0:T(8,128)(2,1)S(1)} %get-tuple-element.19), channel_id=1, source_target_pairs={{0,8},{24,16},{1,9},{25,17},{2,10},{26,18},{3,11},{27,19},{4,12},{... | collective-permute-start | bytes 688136 | tf_op jit(solution)/shard_map/ppermute | solution.py:135
  35.2 7.3 %collective-permute-start.8 = (bf16[32,3584]{1,0:T(8,128)(2,1)S(1)}, bf16[32,3584]{1,0:T(8,128)(2,1)S(1)}, u32[]{:S(2)}, u32[]{:S(2)}) collective-permute-start(bf16[32,3584]{1,0:T(8,128)(2,1)S(1)} %get-tuple-element.17), channel_id=1, source_target_pairs={{0,8},{24,16},{1,9},{25,17},{2,10},{26,18},{3,11},{27,19},{4,12},{... | collective-permute-start | bytes 688136 | tf_op jit(solution)/shard_map/ppermute | solution.py:137
  36.5 10.9 %collective-permute-start.17 = (bf16[32,3584]{1,0:T(8,128)(2,1)S(1)}, bf16[32,3584]{1,0:T(8,128)(2,1)S(1)}, u32[]{:S(2)}, u32[]{:S(2)}) collective-permute-start(bf16[32,3584]{1,0:T(8,128)(2,1)S(1)} %get-tuple-element.23), channel_id=1, source_target_pairs={{0,8},{24,16},{1,9},{25,17},{2,10},{26,18},{3,11},{27,19},{4,12},{... | collective-permute-start | bytes 688136 | tf_op jit(solution)/shard_map/ppermute | solution.py:137
  37.9 13.6 %collective-permute-start.5 = (bf16[32,3584]{1,0:T(8,128)(2,1)S(1)}, bf16[32,3584]{1,0:T(8,128)(2,1)S(1)}, u32[]{:S(2)}, u32[]{:S(2)}) collective-permute-start(bf16[32,3584]{1,0:T(8,128)(2,1)S(1)} %copy.13), channel_id=1, source_target_pairs={{0,8},{24,16},{1,9},{25,17},{2,10},{26,18},{3,11},{27,19},{4,12},{... | collective-permute-start | bytes 688136 | tf_op jit(solution)/shard_map/ppermute | solution.py:135
  42.5 39.2 %collective-permute-start.9 = (bf16[32,3584]{1,0:T(8,128)(2,1)S(1)}, bf16[32,3584]{1,0:T(8,128)(2,1)S(1)}, u32[]{:S(2)}, u32[]{:S(2)}) collective-permute-start(bf16[32,3584]{1,0:T(8,128)(2,1)S(1)} %add_convert_fusion.3), channel_id=1, source_target_pairs={{8,16},{16,8},{9,17},{17,9},{10,18},{18,10},{11,19},{19,11},{12,20... | collective-permute-start | bytes 688136 | tf_op jit(solution)/shard_map/ppermute | solution.py:138
  43.3 9.0 %collective-permute-start.15 = (bf16[32,3584]{1,0:T(8,128)(2,1)S(1)}, bf16[32,3584]{1,0:T(8,128)(2,1)S(1)}, u32[]{:S(2)}, u32[]{:S(2)}) collective-permute-start(bf16[32,3584]{1,0:T(8,128)(2,1)S(1)} %add_convert_fusion.2), channel_id=1, source_target_pairs={{8,16},{16,8},{9,17},{17,9},{10,18},{18,10},{11,19},{19,11},{12,20... | collective-permute-start | bytes 688136 | tf_op jit(solution)/shard_map/ppermute | solution.py:136
  47.4 31.3 %collective-permute-start.18 = (bf16[32,3584]{1,0:T(8,128)(2,1)S(1)}, bf16[32,3584]{1,0:T(8,128)(2,1)S(1)}, u32[]{:S(2)}, u32[]{:S(2)}) collective-permute-start(bf16[32,3584]{1,0:T(8,128)(2,1)S(1)} %add_convert_fusion), channel_id=1, source_target_pairs={{8,16},{16,8},{9,17},{17,9},{10,18},{18,10},{11,19},{19,11},{12,20... | collective-permute-start | bytes 688136 | tf_op jit(solution)/shard_map/ppermute | solution.py:138
  51.5 8.1 %collective-permute-start.6 = (bf16[32,3584]{1,0:T(8,128)(2,1)S(1)}, bf16[32,3584]{1,0:T(8,128)(2,1)S(1)}, u32[]{:S(2)}, u32[]{:S(2)}) collective-permute-start(bf16[32,3584]{1,0:T(8,128)(2,1)S(1)} %add_convert_fusion.5), channel_id=1, source_target_pairs={{8,16},{16,8},{9,17},{17,9},{10,18},{18,10},{11,19},{19,11},{12,20... | collective-permute-start | bytes 688136 | tf_op jit(solution)/shard_map/ppermute | solution.py:136
  52.3 26.4 %collective-permute-start.16 = (bf16[32,3584]{1,0:T(8,128)(2,1)S(1)}, bf16[32,3584]{1,0:T(8,128)(2,1)S(1)}, u32[]{:S(2)}, u32[]{:S(2)}) collective-permute-start(bf16[32,3584]{1,0:T(8,128)(2,1)S(1)} %add_convert_fusion.1), channel_id=1, source_target_pairs={{0,8},{8,0},{16,24},{24,16},{1,9},{9,1},{17,25},{25,17},{2,10},{10... | collective-permute-start | bytes 688136 | tf_op jit(solution)/shard_map/ppermute | solution.py:20
  59.7 22.1 %collective-permute-start.7 = (bf16[32,3584]{1,0:T(8,128)(2,1)S(1)}, bf16[32,3584]{1,0:T(8,128)(2,1)S(1)}, u32[]{:S(2)}, u32[]{:S(2)}) collective-permute-start(bf16[32,3584]{1,0:T(8,128)(2,1)S(1)} %add_convert_fusion.4), channel_id=1, source_target_pairs={{0,8},{8,0},{16,24},{24,16},{1,9},{9,1},{17,25},{25,17},{2,10},{10... | collective-permute-start | bytes 688136 | tf_op jit(solution)/shard_map/ppermute | solution.py:20
  67.8 5.6 %collective-permute-start.10 = (f32[128,1]{1,0:T(8,128)S(1)}, f32[128,1]{1,0:T(8,128)S(1)}, u32[]{:S(2)}, u32[]{:S(2)}) collective-permute-start(f32[128,1]{1,0:T(8,128)S(1)} %get-tuple-element.20), channel_id=1, source_target_pairs={{0,8},{8,0},{16,24},{24,16},{1,9},{9,1},{17,25},{25,17},{2,10},{10... | collective-permute-start | bytes 1544 | tf_op jit(solution)/shard_map/ppermute | solution.py:20
  73.4 5.3 %collective-permute-start.11 = (f32[128,1]{1,0:T(8,128)S(1)}, f32[128,1]{1,0:T(8,128)S(1)}, u32[]{:S(2)}, u32[]{:S(2)}) collective-permute-start(f32[128,1]{1,0:T(8,128)S(1)} %add.61), channel_id=1, source_target_pairs={{0,16},{8,24},{16,0},{24,8},{1,17},{9,25},{17,1},{25,9},{2,18},{10... | collective-permute-start | bytes 1544 | tf_op jit(solution)/shard_map/ppermute | solution.py:20
  78.9 5.6 %collective-permute-start.19 = (bf16[32,1792]{1,0:T(8,128)(2,1)S(1)}, bf16[32,1792]{1,0:T(8,128)(2,1)S(1)}, u32[]{:S(2)}, u32[]{:S(2)}) collective-permute-start(bf16[32,1792]{1,0:T(8,128)(2,1)S(1)} %hidden.3), channel_id=1, source_target_pairs={{0,8},{8,0},{16,24},{24,16},{1,9},{9,1},{17,25},{25,17},{2,10},{10... | collective-permute-start | bytes 344072 | tf_op jit(solution)/shard_map/ppermute | solution.py:20
  87.4 12.3 %collective-permute-start.21 = (bf16[2,32,1792]{2,1,0:T(8,128)(2,1)S(1)}, bf16[2,32,1792]{2,1,0:T(8,128)(2,1)S(1)}, u32[]{:S(2)}, u32[]{:S(2)}) collective-permute-start(bf16[2,32,1792]{2,1,0:T(8,128)(2,1)S(1)} %collective-permute-done.20), channel_id=1, source_target_pairs={{8,0},{16,24},{9,1},{17,25},{10,2},{18,26},{11,3},{19,27},{12,4},{... | collective-permute-start | bytes 688136 | tf_op jit(solution)/shard_map/ppermute | solution.py:173
  88.8 13.4 %collective-permute-start.14 = (bf16[2,32,1792]{2,1,0:T(8,128)(2,1)S(1)}, bf16[2,32,1792]{2,1,0:T(8,128)(2,1)S(1)}, u32[]{:S(2)}, u32[]{:S(2)}) collective-permute-start(bf16[2,32,1792]{2,1,0:T(8,128)(2,1)S(1)} %collective-permute-done.13), channel_id=1, source_target_pairs={{8,0},{16,24},{9,1},{17,25},{10,2},{18,26},{11,3},{19,27},{12,4},{... | collective-permute-start | bytes 688136 | tf_op jit(solution)/shard_map/ppermute | solution.py:173
  118.7 5.2 %collective-permute-start.25 = (bf16[128,256]{1,0:T(8,128)(2,1)S(1)}, bf16[128,256]{1,0:T(8,128)(2,1)S(1)}, u32[]{:S(2)}, u32[]{:S(2)}) collective-permute-start(bf16[128,256]{1,0:T(8,128)(2,1)S(1)} %get-tuple-element.33), channel_id=1, source_target_pairs={{0,6},{1,7},{2,4},{3,5},{4,2},{5,3},{6,0},{7,1},{8,14},{9,15},{10,... | collective-permute-start | bytes 196616 | tf_op jit(solution)/shard_map/ppermute | solution.py:20
  124.0 5.7 %collective-permute-start.27 = (bf16[128,256]{1,0:T(8,128)(2,1)S(1)}, bf16[128,256]{1,0:T(8,128)(2,1)S(1)}, u32[]{:S(2)}, u32[]{:S(2)}) collective-permute-start(bf16[128,256]{1,0:T(8,128)(2,1)S(1)} %fusion.3.own_ref), channel_id=1, source_target_pairs={{0,16},{8,24},{16,0},{24,8},{1,17},{9,25},{17,1},{25,9},{2,18},{10... | collective-permute-start | bytes 196616 | tf_op jit(solution)/shard_map/ppermute | solution.py:20
  127.0 6.1 %collective-permute-start.28 = (bf16[128,256]{1,0:T(8,128)(2,1)S(1)}, bf16[128,256]{1,0:T(8,128)(2,1)S(1)}, u32[]{:S(2)}, u32[]{:S(2)}) collective-permute-start(bf16[128,256]{1,0:T(8,128)(2,1)S(1)} %fusion.3.own_ref), channel_id=1, source_target_pairs={{0,24},{8,16},{16,8},{24,0},{1,25},{9,17},{17,9},{25,1},{2,26},{10... | collective-permute-start | bytes 196616 | tf_op jit(solution)/shard_map/ppermute | solution.py:20
  133.1 8.8 %collective-permute-start.29 = (bf16[4,128,256]{2,1,0:T(8,128)(2,1)S(1)}, bf16[4,128,256]{2,1,0:T(8,128)(2,1)S(1)}, u32[]{:S(2)}, u32[]{:S(2)}) collective-permute-start(bf16[4,128,256]{2,1,0:T(8,128)(2,1)S(1)} %get-tuple-element.31), channel_id=1, source_target_pairs={{0,2},{1,3},{2,0},{3,1},{4,6},{5,7},{6,4},{7,5},{8,10},{9,11},{10,... | collective-permute-start | bytes 786440 | tf_op jit(solution)/shard_map/ppermute | solution.py:20
  134.7 11.3 %collective-permute-start.30 = (bf16[4,128,256]{2,1,0:T(8,128)(2,1)S(1)}, bf16[4,128,256]{2,1,0:T(8,128)(2,1)S(1)}, u32[]{:S(2)}, u32[]{:S(2)}) collective-permute-start(bf16[4,128,256]{2,1,0:T(8,128)(2,1)S(1)} %get-tuple-element.31), channel_id=1, source_target_pairs={{0,4},{1,5},{2,6},{3,7},{4,0},{5,1},{6,2},{7,3},{8,12},{9,13},{10,... | collective-permute-start | bytes 786440 | tf_op jit(solution)/shard_map/ppermute | solution.py:20
  136.2 9.8 %collective-permute-start.31 = (bf16[4,128,256]{2,1,0:T(8,128)(2,1)S(1)}, bf16[4,128,256]{2,1,0:T(8,128)(2,1)S(1)}, u32[]{:S(2)}, u32[]{:S(2)}) collective-permute-start(bf16[4,128,256]{2,1,0:T(8,128)(2,1)S(1)} %get-tuple-element.31), channel_id=1, source_target_pairs={{0,6},{1,7},{2,4},{3,5},{4,2},{5,3},{6,0},{7,1},{8,14},{9,15},{10,... | collective-permute-start | bytes 786440 | tf_op jit(solution)/shard_map/ppermute | solution.py:20
  146.1 6.4 %collective-permute-start.32 = (bf16[3,4,128,256]{3,2,1,0:T(8,128)(2,1)S(1)}, bf16[3,4,128,256]{3,2,1,0:T(8,128)(2,1)S(1)}, u32[]{:S(2)}, u32[]{:S(2)}) collective-permute-start(bf16[3,4,128,256]{3,2,1,0:T(8,128)(2,1)S(1)} %pad_maximum_fusion), channel_id=1, source_target_pairs={{0,1},{1,0},{2,3},{3,2},{4,5},{5,4},{6,7},{7,6},{8,9},{9,8},{10,11... | collective-permute-start | bytes 2359304 | tf_op jit(solution)/shard_map/ppermute | solution.py:20
  (14 other events, 75.1 us)

commit v4 on v0

v4 whole, which is shorter than its diff:
```python
import functools
import jax
import jax.numpy as jnp
from jax import lax
from jax.experimental import pallas as pl
from jax.experimental.pallas import tpu as pltpu
from jax.sharding import PartitionSpec as P

D = 8192
CLASSES = 64
TILE = 256
CHUNKS = 2
BF16 = jnp.bfloat16
F32 = jnp.float32
WHOLE = pl.BlockSpec(memory_space=pltpu.VMEM)
ANYWHERE = pl.BlockSpec(memory_space=pl.ANY)
INWARD, MIDDLE, OUTWARD = [(0, 1), (3, 2)], [(1, 2), (2, 1)], [(1, 0), (2, 3)]


def swap(value, axis, size, mask):
    return lax.ppermute(value, axis, [(i, i ^ mask) for i in range(size)])


def run(body, name, out_shape, operands, flops, bytes_accessed, in_specs=None, out_specs=WHOLE, **more):
    return pl.pallas_call(
        body,
        out_shape=out_shape,
        in_specs=[WHOLE] * len(operands) if in_specs is None else in_specs,
        out_specs=out_specs,
        compiler_params=pltpu.CompilerParams(vmem_limit_bytes=16 * 1024 * 1024),
        cost_estimate=pl.CostEstimate(flops=flops, bytes_accessed=bytes_accessed, transcendentals=0),
        name=name,
        **more,
    )(*operands)


def fetch(pieces, after, name):
    count = len(pieces)
    copies = []
    for number, (array, row, rows, column, columns) in enumerate(pieces):
        step = min(rows, 256)
        copies += [(number, at, step, row + at, column, columns) for at in range(0, rows, step)]

    def body(*refs):
        sources, targets, sems = refs[:count], refs[-1 - count:-1], refs[-1]
        started = []
        for sem, (number, at, step, row, column, columns) in enumerate(copies):
            copy = pltpu.make_async_copy(
                sources[number].at[pl.ds(row, step), pl.ds(column, columns)],
                targets[number].at[pl.ds(at, step), :],
                sems.at[sem],
            )
            copy.start()
            started.append(copy)
        for copy in started:
            copy.wait()

    size = sum(rows * columns * array.dtype.itemsize for array, _, rows, _, columns in pieces)
    return run(
        body, name,
        [pltpu.VMEM((rows, columns), array.dtype) for array, _, rows, _, columns in pieces],
        [pltpu.with_memory_space_constraint(piece[0], pltpu.HBM) for piece in pieces] + list(after),
        0, 2 * size,
        in_specs=[ANYWHERE] * (count + len(after)),
        out_specs=[WHOLE] * count,
        scratch_shapes=[pltpu.SemaphoreType.DMA((len(copies),))],
    )


def tokens_kernel(masks, panel, *refs):
    blocks, (gain, lhs, cols, squares, x) = refs[:len(masks)], refs[len(masks):]
    h = lax.axis_index("hid")
    rows = blocks[0].shape[0]
    for mask, block in zip(masks, blocks):
        x[pl.ds(pl.multiple_of((h ^ mask) * rows, rows), rows), :] = block[...]
    values = x[...].astype(F32)
    lhs[...] = (values * gain[...]).astype(BF16)
    squares[...] = jnp.sum(values * values, axis=1, keepdims=True)
    cols[...] = x[:, pl.ds(pl.multiple_of(h * panel, panel), panel)].astype(F32)


def gate_up_kernel(lhs_ref, gate_ref, up_ref, *refs):
    outs, both = refs[:-1], refs[-1]
    rows = outs[0].shape[0]
    z = lax.axis_index("tok")
    lhs = lhs_ref[...]
    for tile in range(gate_ref.shape[1] // TILE):
        cols = slice(tile * TILE, (tile + 1) * TILE)
        both[:, :TILE] = jnp.dot(lhs, gate_ref[:, cols], preferred_element_type=F32)
        both[:, TILE:] = jnp.dot(lhs, up_ref[:, cols], preferred_element_type=F32)
        for d, out in enumerate(outs):
            at = pl.multiple_of((z ^ d) * rows, rows)
            out[:, 2 * tile * TILE:2 * (tile + 1) * TILE] = both[pl.ds(at, rows), :].astype(BF16)


def gate_up(lhs, gate, up, n_tok):
    ntok, depth = lhs.shape
    width = gate.shape[1]
    return run(
        gate_up_kernel, "gate_up",
        [jax.ShapeDtypeStruct((ntok // n_tok, 2 * width), BF16)] * n_tok,
        [lhs, gate, up],
        4 * ntok * depth * width, 4 * depth * width,
        out_specs=[WHOLE] * n_tok,
        scratch_shapes=[pltpu.VMEM((ntok, 2 * TILE), F32)],
    )


def total_after(terms, after):
    count = len(terms)

    def body(*refs):
        total = refs[0][...]
        if count > 1:
            total = total.astype(F32)
            for ref in refs[1:count]:
                total = total + ref[...].astype(F32)
        refs[-1][...] = total.astype(BF16)

    size = terms[0].size
    return run(
        body, "total", jax.ShapeDtypeStruct(terms[0].shape, BF16), [*terms, *after],
        count * size, 2 * size * (count + 1),
        in_specs=[WHOLE] * count + [ANYWHERE] * len(after),
    )


def hidden_kernel(own_ref, one_ref, two_ref, square_ref, out_ref):
    rows = out_ref.shape[0]
    at = pl.multiple_of(lax.axis_index("tok") * rows, rows)
    scale = lax.rsqrt(square_ref[pl.ds(at, rows), :] / float(D) + 1e-05)

    def total(at):
        cols = slice(at, at + TILE)
        return (
            own_ref[:, cols].astype(F32) + one_ref[:, cols].astype(F32) + two_ref[:, cols].astype(F32)
        ) * scale

    for at in range(0, out_ref.shape[1], TILE):
        gate, up = total(2 * at), total(2 * at + TILE)
        out_ref[:, at:at + TILE] = (jax.nn.silu(gate) * up).astype(BF16)


def hidden_rows(own, one, two, squares):
    rows, width = one.shape
    return run(
        hidden_kernel, "hidden", jax.ShapeDtypeStruct((rows, width // 2), BF16),
        [own, one, two, squares], 10 * rows * width, 8 * rows * width,
    )


def down_kernel(masks, skip, panel, counts, *refs):
    blocks, refs = refs[:sum(counts)], refs[sum(counts):]
    weight, lhs, out = refs[0], refs[-1], refs[-2]
    before = refs[1] if len(refs) == 4 else None
    z = lax.axis_index("tok")
    h = lax.axis_index("hid")
    rows = blocks[0].shape[0]
    at = 0
    for d, count in enumerate(counts):
        block = blocks[at][...]
        for extra in blocks[at + 1:at + count]:
            block = block + extra[...]
        at += count
        lhs[pl.ds(pl.multiple_of((z ^ d) * rows, rows), rows), :] = block
    values = lhs[...]
    for slot, mask in enumerate(masks):
        column = pl.multiple_of((h ^ mask) * panel, panel)
        total = jnp.dot(values, weight[:, pl.ds(column, panel)], preferred_element_type=F32)
        if before is not None:
            total = total + before[skip + slot]
        out[slot] = total.astype(out.dtype)


def down(hidden, weight, masks, panel, kind, before=None, skip=0):
    blocks = [block for terms in hidden for block in terms]
    rows, depth = blocks[0].shape
    ntok = rows * len(hidden)
    counts = [len(terms) for terms in hidden]
    return run(
        functools.partial(down_kernel, masks, skip, panel, counts), "down",
        jax.ShapeDtypeStruct((len(masks), ntok, panel), kind),
        blocks + [weight] + ([] if before is None else [before]),
        2 * ntok * depth * panel * len(masks), 2 * depth * panel * len(masks),
        scratch_shapes=[pltpu.VMEM((ntok, depth), BF16)],
    )


def chip_sum_kernel(mine_ref, other_ref, own_ref, *outs):
    own_ref[...] = mine_ref[0] + other_ref[0].astype(F32)
    for e, out in enumerate(outs):
        out[...] = (mine_ref[e + 1] + other_ref[e + 1].astype(F32)).astype(BF16)


def gram_kernel(masks, n_hid, ntok, own_ref, *refs):
    stacks, (out_ref, tiles, sems) = refs[:len(masks)], refs[-3:]
    z = lax.axis_index("tok")
    h = lax.axis_index("hid")
    width = own_ref.shape[1]
    left = own_ref[...].T
    copies = []
    for mask, stack in zip(masks, stacks):
        for d in range(stack.shape[0]):
            number = len(copies)
            tiles[number] = jnp.dot(left, stack[d], preferred_element_type=F32) * (1.0 / ntok)
            column = ((z ^ d) * n_hid + (h ^ mask)) * width
            copy = pltpu.make_async_copy(
                tiles.at[number], out_ref.at[:, pl.ds(pl.multiple_of(column, width), width)], sems.at[number]
            )
            copy.start()
            copies.append(copy)
    for copy in copies:
        copy.wait()


def gram_part(resid_cols, stacks, masks, n_tok, n_hid, before):
    ntok, width = resid_cols.shape
    here = n_tok * len(stacks)
    return run(
        functools.partial(gram_kernel, masks, n_hid, ntok), "gram",
        pltpu.HBM((width, width * n_tok * n_hid), F32),
        [resid_cols, *stacks] + ([] if before is None else [before]),
        2 * ntok * width * width * here, 4 * width * width * here,
        in_specs=[WHOLE] * (1 + len(stacks)) + ([] if before is None else [ANYWHERE]),
        out_specs=ANYWHERE,
        input_output_aliases={} if before is None else {1 + len(stacks): 0},
        scratch_shapes=[pltpu.VMEM((here, width, width), F32), pltpu.SemaphoreType.DMA((here,))],
    )


def class_means(resid_cols, labels):
    onehot = (labels[:, None] == jnp.arange(CLASSES, dtype=jnp.int32)[None, :]).astype(BF16)
    counts = jnp.sum(onehot.astype(F32), axis=0)
    class_sums = lax.dot_general(
        resid_cols, onehot, (((0,), (0,)), ((), ())), preferred_element_type=F32
    )
    return class_sums / jnp.maximum(counts, 1.0)[None, :]


def on_line(n_tok, n_hid, resid_in, norm_gain, gate_weight, up_weight, down_weight, labels):
    rows, block = resid_in.shape
    ntok, panel = rows * n_hid, block // n_hid
    depth, shard_ff = gate_weight.shape
    wide = shard_ff // CHUNKS
    chip_masks = list(range(2, n_hid, 2))

    def weights(k, after):
        part = (0, depth, k * wide, wide)
        return fetch([(gate_weight, *part), (up_weight, *part)], after, "fetch_gate_up")

    near = [resid_in] + [swap(resid_in, "hid", n_hid, mask) for mask in chip_masks]
    gate, up, own_x, gain = fetch(
        [
            (gate_weight, 0, depth, 0, wide),
            (up_weight, 0, depth, 0, wide),
            (resid_in, 0, rows, 0, block),
            (norm_gain[None, :], 0, 1, 0, block),
        ],
        (), "fetch_first",
    )
    far = [near[0], total_after([near[1]], (gain,)), *near[2:]]
    far = [swap(piece, "hid", n_hid, 1) for piece in far]
    masks = [0] + chip_masks + [1] + [mask + 1 for mask in chip_masks]
    lhs, x_cols, squares = run(
        functools.partial(tokens_kernel, masks, panel), "tokens",
        (
            jax.ShapeDtypeStruct((ntok, block), BF16),
            jax.ShapeDtypeStruct((ntok, panel), F32),
            jax.ShapeDtypeStruct((ntok, 1), F32),
        ),
        [own_x, *near[1:], *far, gain],
        4 * ntok * block, 4 * ntok * block,
        out_specs=(WHOLE, WHOLE, WHOLE),
        scratch_shapes=[pltpu.VMEM((ntok, block), BF16)],
    )
    squares = sum([swap(squares, "tok", n_tok, d) for d in range(1, n_tok)], squares)

    a = gate_up(lhs, gate, up, n_tok)
    a_far = lax.ppermute(a[3], "tok", INWARD)
    a_near = lax.ppermute(a[2], "tok", INWARD)
    b = gate_up(lhs, *weights(1, (a[3],)), n_tok)
    send = total_after([a[2], a_far], ())
    a_far = lax.ppermute(send, "tok", MIDDLE)
    send = total_after([b[3]], (send,))
    b_far = lax.ppermute(send, "tok", INWARD)
    send = total_after([a[3], a_near], (send,))
    a_near = lax.ppermute(send, "tok", MIDDLE)
    send = total_after([b[2]], (send,))
    b_near = lax.ppermute(send, "tok", INWARD)
    down_a, = fetch([(down_weight, 0, wide, 0, block)], (send,), "fetch_down")
    send = total_after([a[1], a_far], (send,))
    a_last = swap(send, "tok", n_tok, 1)
    send = total_after([b[2], b_far], (send,))
    b_far = lax.ppermute(send, "tok", MIDDLE)
    down_b, = fetch([(down_weight, wide, wide, 0, block)], (send,), "fetch_down")
    send = total_after([b[3], b_near], (send,))
    b_near = lax.ppermute(send, "tok", MIDDLE)
    send = total_after([b[1], b_far], (send,))
    b_last = swap(send, "tok", n_tok, 1)

    own = hidden_rows(a[0], a_last, a_near, squares)
    beside = swap(own, "tok", n_tok, 1)
    over_own = lax.ppermute(own, "tok", MIDDLE)
    over_beside = lax.ppermute(beside, "tok", MIDDLE)
    out_own = lax.ppermute(over_own, "tok", OUTWARD)
    out_beside = lax.ppermute(over_beside, "tok", OUTWARD)
    hidden_a = [[own], [beside], [over_beside, out_own], [over_own, out_beside]]
    own = hidden_rows(b[0], b_last, b_near, squares)
    hidden_b = [[own]] + [[swap(own, "tok", n_tok, d)] for d in range(1, n_tok)]

    here = [0] + chip_masks
    there = [mask + 1 for mask in here]
    first = down(hidden_a, down_a, there + here, panel, F32)
    other = down(hidden_b, down_b, there, panel, BF16, first, 0)
    other = swap(other, "hid", n_hid, 1)
    mine = down(hidden_b, down_b, here, panel, F32, first, len(there))
    summed, *sends = run(
        chip_sum_kernel, "chip_sum",
        [jax.ShapeDtypeStruct((ntok, panel), F32)] + [jax.ShapeDtypeStruct((ntok, panel), BF16)] * len(chip_masks),
        [mine, other], mine.size, 8 * mine.size,
        out_specs=[WHOLE] * len(here),
    )
    for mask, value in zip(chip_masks, sends):
        summed = summed + swap(value, "hid", n_hid, mask).astype(F32)
    resid_cols = (x_cols + summed).astype(BF16)
    cross = class_means(resid_cols, labels)

    line = jnp.stack([resid_cols] + [swap(resid_cols, "tok", n_tok, d) for d in range(1, n_tok)])
    others = [swap(line, "hid", n_hid, mask) for mask in chip_masks]
    line_far = swap(line, "hid", n_hid, 1)
    gram = gram_part(resid_cols, [line, line_far], [0, 1], n_tok, n_hid, None)
    others_far = [swap(total_after([others[0]], (pltpu.with_memory_space_constraint(gram, pltpu.HBM),)), "hid", n_hid, 1)]
    others_far += [swap(piece, "hid", n_hid, 1) for piece in others[1:]]
    gram = gram_part(resid_cols, others, chip_masks, n_tok, n_hid, gram)
    gram = gram_part(resid_cols, others_far, [mask + 1 for mask in chip_masks], n_tok, n_hid, gram)
    return (gram, cross)


def plain(n_tok, n_hid, resid_in, norm_gain, gate_weight, up_weight, down_weight, labels):
    x = lax.all_gather(resid_in, "hid", axis=0, tiled=True).astype(F32)
    ntok, block = x.shape
    total_sq = lax.psum(jnp.sum(x * x, axis=1), "tok")
    normed = (x * lax.rsqrt(total_sq / float(D) + 1e-05)[:, None] * norm_gain[None, :]).astype(BF16)

    def summed_over_tok(weight):
        product = jnp.dot(normed, weight, preferred_element_type=F32).astype(BF16)
        return lax.psum_scatter(product, "tok", scatter_dimension=0, tiled=True).astype(F32)

    hidden = (jax.nn.silu(summed_over_tok(gate_weight)) * summed_over_tok(up_weight)).astype(BF16)
    hidden = lax.all_gather(hidden, "tok", axis=0, tiled=True)
    partial_out = jnp.dot(hidden, down_weight, preferred_element_type=F32).astype(BF16)
    summed = lax.psum_scatter(partial_out, "hid", scatter_dimension=1, tiled=True).astype(F32)
    panel = block // n_hid
    x_cols = lax.dynamic_slice_in_dim(x, lax.axis_index("hid") * panel, panel, 1)
    resid_cols = (x_cols + summed).astype(BF16)
    everyone = lax.all_gather(resid_cols, ("tok", "hid"), axis=1, tiled=True)
    gram = lax.dot_general(
        resid_cols, everyone, (((0,), (0,)), ((), ())), preferred_element_type=F32
    ) / float(ntok)
    return (gram, class_means(resid_cols, labels))


def on_device(n_tok, n_hid, resid_in, norm_gain, gate_weight, *rest):
    panel = resid_in.shape[1] // n_hid
    fits = n_tok == 4 and n_hid == 8 and panel % 128 == 0 and gate_weight.shape[1] % (CHUNKS * TILE) == 0
    body = on_line if fits else plain
    return body(n_tok, n_hid, resid_in, norm_gain, gate_weight, *rest)


def solution(mesh):
    return jax.shard_map(
        functools.partial(on_device, mesh.shape["tok"], mesh.shape["hid"]),
        mesh=mesh,
        in_specs=(
            P("hid", "tok"),
            P("tok"),
            P("tok", "hid"),
            P("tok", "hid"),
            P("hid", "tok"),
            P(),
        ),
        out_specs=(P(("tok", "hid"), None), P(("tok", "hid"), None)),
        check_vma=False,
    )
```

time: 216 us -> 120 us (0.56)
  waiting for transfers between devices: 127 us -> 27.9 us
  starting transfers between devices: 0.12 us -> 58.5 us
  blocking collectives: 42.9 us -> 0 us
  Pallas kernels: 0 us -> 31.2 us
  matrix products: 28.7 us -> 0.77 us
  between operations: 13.8 us -> 1.3 us
  other arithmetic: 3.08 us -> 0.2 us
    reduce_scatter x2 -> x0, waiting for transfers between devices: 70.3 us -> none  [the longest x1 36.7 us: on_device(): lax.psum_scatter(jnp.dot(normed, both_weights, preferred_element_type=jnp...]
    ppermute x0 -> x42, starting transfers between devices: none -> 58.5 us  [the longest x30 36.3 us: swap(): return lax.ppermute(value, axis, [(i, i ^ mask) for i in range(size)])]
    all_gather x1 -> x0, waiting for transfers between devices: 56.8 us -> none  [on_device(): lax.all_gather(resid_cols, ('tok', 'hid'), axis=1, tiled=True)]
    pallas_call x0 -> x26, Pallas kernels: none -> 31.2 us  [run(): pl.pallas_call(body, out_shape=out_shape, in_specs=[WHOLE] * len(operands...]
    all_gather x2 -> x0, blocking collectives: 31 us -> none  [the longest x1 19.4 us: on_device(): lax.all_gather(hidden, 'tok', axis=0, tiled=True)]
    dot_general x4 -> x1, matrix products: 28.7 us -> 0.77 us  [class_means(): lax.dot_general(resid_cols, onehot, (((0,), (0,)), ((), ())), preferred_e...]
    ppermute x0 -> x42, waiting for transfers between devices: none -> 27.9 us  [the longest x30 27.2 us: swap(): return lax.ppermute(value, axis, [(i, i ^ mask) for i in range(size)])]
    psum x1 -> x0, blocking collectives: 12 us -> none  [on_device(): total_sq = lax.psum(local_sq, 'tok')]
  transfers between devices with their start and end apart: 3 -> 42, of which waited for: 3 -> 15; matrix products, arithmetic and copies ran while one was open for 1% -> 1% of each run, Pallas kernels for 0% -> 22%
where the time goes in v4:
time: 120 us
  starting transfers between devices  58.5 us (49%)
  Pallas kernels  31.2 us (26%)
  waiting for transfers between devices  27.9 us (23%)
  between operations  1.3 us (1%)
    ppermute x30, starting transfers between devices, swap(): return lax.ppermute(value, axis, [(i, i ^ mask) for i in range(size)])  36.3 us
    pallas_call x26, Pallas kernels, run(): pl.pallas_call(body, out_shape=out_shape, in_specs=[WHOLE] * len(operands...  31.2 us
    ppermute x30, waiting for transfers between devices, swap(): return lax.ppermute(value, axis, [(i, i ^ mask) for i in range(size)])  27.2 us
    ppermute x1, starting transfers between devices, on_line(): b_far = lax.ppermute(send, 'tok', INWARD)  5.8 us
    ppermute x1, starting transfers between devices, on_line(): b_near = lax.ppermute(send, 'tok', INWARD)  4.39 us
    ppermute x1, starting transfers between devices, on_line(): a_far = lax.ppermute(a[3], 'tok', INWARD)  3.96 us
  transfers between devices with their start and end apart: 42, of which 15 were waited for; matrix products, arithmetic and copies ran while one was open for 1% of the time, Pallas kernels for 22%

profile of v4, /device:TPU:0, one launch (start us, length us, event | category | flops | bytes accessed | tf_op | source)
XLA Modules:
  0.0 119.9 jit_solution(8387862493199748787)
XLA Ops:
  0.6 3.0 %collective-permute-start = (bf16[16,2048]{1,0:T(8,128)(2,1)}, bf16[16,2048]{1,0:T(8,128)(2,1)S(1)}, u32[]{:S(2)}, u32[]{:S(2)}) collective-permute-start(bf16[16,2048]{1,0:T(8,128)(2,1)} %refs_2_.1), channel_id=1, source_target_pairs={{0,2},{1,3},{2,0},{3,1},{4,6},{5,7},{6,4},{7,5},{8,10},{9,11},{10,... | collective-permute-start | bytes 196616 | tf_op jit(solution)/shard_map/ppermute | solution.py:21
  5.2 5.5 %fetch_first.1 = (bf16[2048,1792]{1,0:T(8,128)(2,1)S(1)}, bf16[2048,1792]{1,0:T(8,128)(2,1)S(1)}, bf16[16,2048]{1,0:T(8,128)(2,1)S(1)}, f32[1,2048]{1,0:T(1,128)S(1)}) custom-call(bf16[2048,3584]{1,0:T(8,128)(2,1)} %refs_0_.5, bf16[2048,3584]{1,0:T(8,128)(2,1)} %refs_1_.3, bf16[16,2048]{1,0:T(8,128)(2,1)} %refs_2_.1, f32[1,2048]{1,0:T(1,128)} %bitcast.10), custom_call_target="tpu_custom_call" | custom-call | bytes 29507584 | tf_op jit(solution)/shard_map/fetch_first/pallas_call | solution.py:25
  13.0 2.3 %gate_up.2 = (bf16[32,3584]{1,0:T(8,128)(2,1)S(1)}, bf16[32,3584]{1,0:T(8,128)(2,1)S(1)}, bf16[32,3584]{1,0:T(8,128)(2,1)S(1)}, bf16[32,3584]{1,0:T(8,128)(2,1)S(1)}) custom-call(bf16[128,2048]{1,0:T(8,128)(2,1)S(1)} %get-tuple-element.26.lhs_ref, bf16[2048,1792]{1,0:T(8,128)(2,1)S(1)} %get-tuple-element.27.gate_ref, ...), custom_call_target="tpu_custom_call" | custom-call | flops 1879048192 | bytes 14680064 | tf_op jit(solution)/shard_map/gate_up/pallas_call | solution.py:25
  15.3 4.0 %collective-permute-start.7 = (bf16[32,3584]{1,0:T(8,128)(2,1)S(1)}, bf16[32,3584]{1,0:T(8,128)(2,1)S(1)}, u32[]{:S(2)}, u32[]{:S(2)}) collective-permute-start(bf16[32,3584]{1,0:T(8,128)(2,1)S(1)} %get-tuple-element.29.refs_2_.refs_0_), channel_id=1, source_target_pairs={{0,8},{24,16},{1,9},{25,17},{2,10},{26,18},{3,11},{27,19},{4,12},{... | collective-permute-start | bytes 688136 | tf_op jit(solution)/shard_map/ppermute | solution.py:279
  19.3 5.4 %fetch_gate_up.1 = (bf16[2048,1792]{1,0:T(8,128)(2,1)S(1)}, bf16[2048,1792]{1,0:T(8,128)(2,1)S(1)}) custom-call(bf16[2048,3584]{1,0:T(8,128)(2,1)} %refs_0_.5, bf16[2048,3584]{1,0:T(8,128)(2,1)} %refs_1_.3, bf16[32,3584]{1,0:T(8,128)(2,1)S(1)} %get-tuple-element.29.refs_2_.refs_0_), custom_call_target="tpu_custom_call" | custom-call | bytes 29360128 | tf_op jit(solution)/shard_map/fetch_gate_up/pallas_call | solution.py:25
  26.7 2.2 %gate_up.3 = (bf16[32,3584]{1,0:T(8,128)(2,1)S(1)}, bf16[32,3584]{1,0:T(8,128)(2,1)S(1)}, bf16[32,3584]{1,0:T(8,128)(2,1)S(1)}, bf16[32,3584]{1,0:T(8,128)(2,1)S(1)}) custom-call(bf16[128,2048]{1,0:T(8,128)(2,1)S(1)} %get-tuple-element.26.lhs_ref, bf16[2048,1792]{1,0:T(8,128)(2,1)S(1)} %get-tuple-element.30.gate_ref, ...), custom_call_target="tpu_custom_call" | custom-call | flops 1879048192 | bytes 14680064 | tf_op jit(solution)/shard_map/gate_up/pallas_call | solution.py:25
  29.0 5.8 %collective-permute-start.8 = (bf16[32,3584]{1,0:T(8,128)(2,1)S(1)}, bf16[32,3584]{1,0:T(8,128)(2,1)S(1)}, u32[]{:S(2)}, u32[]{:S(2)}) collective-permute-start(bf16[32,3584]{1,0:T(8,128)(2,1)S(1)} %total.12.refs_2_), channel_id=1, source_target_pairs={{0,8},{24,16},{1,9},{25,17},{2,10},{26,18},{3,11},{27,19},{4,12},{... | collective-permute-start | bytes 688136 | tf_op jit(solution)/shard_map/ppermute | solution.py:285
  34.9 1.9 %collective-permute-start.16 = (f32[128,1]{1,0:T(8,128)S(1)}, f32[128,1]{1,0:T(8,128)S(1)}, u32[]{:S(2)}, u32[]{:S(2)}) collective-permute-start(f32[128,1]{1,0:T(8,128)S(1)} %get-tuple-element.38), channel_id=1, source_target_pairs={{0,16},{8,24},{16,0},{24,8},{1,17},{9,25},{17,1},{25,9},{2,18},{10... | collective-permute-start | bytes 1544 | tf_op jit(solution)/shard_map/ppermute | solution.py:21
  36.8 2.5 %collective-permute-start.17 = (f32[128,1]{1,0:T(8,128)S(1)}, f32[128,1]{1,0:T(8,128)S(1)}, u32[]{:S(2)}, u32[]{:S(2)}) collective-permute-start(f32[128,1]{1,0:T(8,128)S(1)} %get-tuple-element.38), channel_id=1, source_target_pairs={{0,24},{8,16},{16,8},{24,0},{1,25},{9,17},{17,9},{25,1},{2,26},{10... | collective-permute-start | bytes 1544 | tf_op jit(solution)/shard_map/ppermute | solution.py:21
  40.8 4.4 %collective-permute-start.12 = (bf16[32,3584]{1,0:T(8,128)(2,1)S(1)}, bf16[32,3584]{1,0:T(8,128)(2,1)S(1)}, u32[]{:S(2)}, u32[]{:S(2)}) collective-permute-start(bf16[32,3584]{1,0:T(8,128)(2,1)S(1)} %total.14.refs_2_.refs_1_), channel_id=1, source_target_pairs={{0,8},{24,16},{1,9},{25,17},{2,10},{26,18},{3,11},{27,19},{4,12},{... | collective-permute-start | bytes 688136 | tf_op jit(solution)/shard_map/ppermute | solution.py:289
  46.1 7.0 %collective-permute-done.21.one_ref = bf16[32,3584]{1,0:T(8,128)(2,1)S(1)} collective-permute-done((bf16[32,3584]{1,0:T(8,128)(2,1)S(1)}, bf16[32,3584]{1,0:T(8,128)(2,1)S(1)}, u32[]{:S(2)}, u32[]{:S(2)}) %collective-permute-start.21) | collective-permute-done | bytes 229408 | tf_op jit(solution)/shard_map/ppermute | solution.py:21
  53.3 2.6 %collective-permute-start.23 = (bf16[32,1792]{1,0:T(8,128)(2,1)S(1)}, bf16[32,1792]{1,0:T(8,128)(2,1)S(1)}, u32[]{:S(2)}, u32[]{:S(2)}) collective-permute-start(bf16[32,1792]{1,0:T(8,128)(2,1)S(1)} %hidden.3.refs_0_), channel_id=1, source_target_pairs={{0,8},{8,0},{16,24},{24,16},{1,9},{9,1},{17,25},{25,17},{2,10},{10... | collective-permute-start | bytes 344072 | tf_op jit(solution)/shard_map/ppermute | solution.py:21
  63.4 7.0 %collective-permute-start.18 = (bf16[32,1792]{1,0:T(8,128)(2,1)S(1)}, bf16[32,1792]{1,0:T(8,128)(2,1)S(1)}, u32[]{:S(2)}, u32[]{:S(2)}) collective-permute-start(bf16[32,1792]{1,0:T(8,128)(2,1)S(1)} %hidden.2.refs_0_), channel_id=1, source_target_pairs={{0,8},{8,0},{16,24},{24,16},{1,9},{9,1},{17,25},{25,17},{2,10},{10... | collective-permute-start | bytes 344072 | tf_op jit(solution)/shard_map/ppermute | solution.py:21
  70.7 2.2 %collective-permute-start.20 = (bf16[32,1792]{1,0:T(8,128)(2,1)S(1)}, bf16[32,1792]{1,0:T(8,128)(2,1)S(1)}, u32[]{:S(2)}, u32[]{:S(2)}) collective-permute-start(bf16[32,1792]{1,0:T(8,128)(2,1)S(1)} %hidden.2.refs_0_), channel_id=1, source_target_pairs={{0,24},{8,16},{16,8},{24,0},{1,25},{9,17},{17,9},{25,1},{2,26},{10... | collective-permute-start | bytes 344072 | tf_op jit(solution)/shard_map/ppermute | solution.py:21
  72.8 3.2 %fetch_down.3.refs_6_ = bf16[1792,2048]{1,0:T(8,128)(2,1)S(1)} custom-call(bf16[3584,2048]{1,0:T(8,128)(2,1)} %refs_0_.7, bf16[32,3584]{1,0:T(8,128)(2,1)S(1)} %total.14.refs_2_.refs_1_), custom_call_target="tpu_custom_call" | custom-call | bytes 14680064 | tf_op jit(solution)/shard_map/fetch_down/pallas_call | solution.py:25
  76.0 3.2 %fetch_down.2.refs_4_ = bf16[1792,2048]{1,0:T(8,128)(2,1)S(1)} custom-call(bf16[3584,2048]{1,0:T(8,128)(2,1)} %refs_0_.7, bf16[32,3584]{1,0:T(8,128)(2,1)S(1)} %total.16.refs_2_.refs_1_), custom_call_target="tpu_custom_call" | custom-call | bytes 14680064 | tf_op jit(solution)/shard_map/fetch_down/pallas_call | solution.py:25
  88.7 2.4 %collective-permute-done.31 = bf16[128,256]{1,0:T(8,128)(2,1)S(1)} collective-permute-done((bf16[128,256]{1,0:T(8,128)(2,1)S(1)}, bf16[128,256]{1,0:T(8,128)(2,1)S(1)}, u32[]{:S(2)}, u32[]{:S(2)}) %collective-permute-start.31) | collective-permute-done | bytes 65568 | tf_op jit(solution)/shard_map/ppermute | solution.py:21
  93.5 2.2 %collective-permute-start.34 = (bf16[128,256]{1,0:T(8,128)(2,1)S(1)}, bf16[128,256]{1,0:T(8,128)(2,1)S(1)}, u32[]{:S(2)}, u32[]{:S(2)}) collective-permute-start(bf16[128,256]{1,0:T(8,128)(2,1)S(1)} %add_convert_fusion.own_ref), channel_id=1, source_target_pairs={{0,24},{8,16},{16,8},{24,0},{1,25},{9,17},{17,9},{25,1},{2,26},{10... | collective-permute-start | bytes 196616 | tf_op jit(solution)/shard_map/ppermute | solution.py:21
  95.7 2.6 %collective-permute-done.33 = bf16[128,256]{1,0:T(8,128)(2,1)S(1)} collective-permute-done((bf16[128,256]{1,0:T(8,128)(2,1)S(1)}, bf16[128,256]{1,0:T(8,128)(2,1)S(1)}, u32[]{:S(2)}, u32[]{:S(2)}) %collective-permute-start.33) | collective-permute-done | bytes 65568 | tf_op jit(solution)/shard_map/ppermute | solution.py:21
  100.9 2.4 %collective-permute-start.40 = (bf16[4,128,256]{2,1,0:T(8,128)(2,1)S(1)}, bf16[4,128,256]{2,1,0:T(8,128)(2,1)S(1)}, u32[]{:S(2)}, u32[]{:S(2)}) collective-permute-start(bf16[4,128,256]{2,1,0:T(8,128)(2,1)S(1)} %pad_maximum_fusion.refs_0_), channel_id=1, source_target_pairs={{0,6},{1,7},{2,4},{3,5},{4,2},{5,3},{6,0},{7,1},{8,14},{9,15},{10,... | collective-permute-start | bytes 786440 | tf_op jit(solution)/shard_map/ppermute | solution.py:21
  105.1 3.9 %collective-permute-done.35.refs_0_ = bf16[4,128,256]{2,1,0:T(8,128)(2,1)S(1)} collective-permute-done((bf16[4,128,256]{2,1,0:T(8,128)(2,1)S(1)}, bf16[4,128,256]{2,1,0:T(8,128)(2,1)S(1)}, u32[]{:S(2)}, u32[]{:S(2)}) %collective-permute-start.35) | collective-permute-done | bytes 262176 | tf_op jit(solution)/shard_map/ppermute | solution.py:21
  109.0 5.3 %collective-permute-done.38.refs_1_ = bf16[4,128,256]{2,1,0:T(8,128)(2,1)S(1)} collective-permute-done((bf16[4,128,256]{2,1,0:T(8,128)(2,1)S(1)}, bf16[4,128,256]{2,1,0:T(8,128)(2,1)S(1)}, u32[]{:S(2)}, u32[]{:S(2)}) %collective-permute-start.38) | collective-permute-done | bytes 262176 | tf_op jit(solution)/shard_map/ppermute | solution.py:21
  115.7 2.0 %gram.4.refs_3_ = f32[256,8192]{1,0:T(8,128)} custom-call(bf16[128,256]{1,0:T(8,128)(2,1)S(1)} %add_convert_fusion.own_ref, bf16[4,128,256]{2,1,0:T(8,128)(2,1)S(1)} %collective-permute-done.35.refs_0_, bf16[4,128,256]{2,1,0:T(8,128)(2,1)S(1)} %collective-permute-done.38.refs_1_, ...), custom_call_target="tpu_custom_call", output_to_operand_aliasing={{}: (4, {})} | custom-call | flops 201326592 | bytes 3145728 | tf_op jit(solution)/shard_map/gram/pallas_call | solution.py:25
  117.7 2.0 %gram.5 = f32[256,8192]{1,0:T(8,128)} custom-call(bf16[128,256]{1,0:T(8,128)(2,1)S(1)} %add_convert_fusion.own_ref, bf16[4,128,256]{2,1,0:T(8,128)(2,1)S(1)} %collective-permute-done.37.refs_0_, bf16[4,128,256]{2,1,0:T(8,128)(2,1)S(1)} %collective-permute-done.39.refs_1_, ...), custom_call_target="tpu_custom_call", output_to_operand_aliasing={{}: (4, {})} | custom-call | flops 201326592 | bytes 3145728 | tf_op jit(solution)/shard_map/gram/pallas_call | solution.py:25
  (94 shorter events, 33.7 us)
Async XLA Ops:
  0.6 10.1 %collective-permute-start = (bf16[16,2048]{1,0:T(8,128)(2,1)}, bf16[16,2048]{1,0:T(8,128)(2,1)S(1)}, u32[]{:S(2)}, u32[]{:S(2)}) collective-permute-start(bf16[16,2048]{1,0:T(8,128)(2,1)} %refs_2_.1), channel_id=1, source_target_pairs={{0,2},{1,3},{2,0},{3,1},{4,6},{5,7},{6,4},{7,5},{8,10},{9,11},{10,... | collective-permute-start | bytes 196616 | tf_op jit(solution)/shard_map/ppermute | solution.py:21
  3.6 7.7 %collective-permute-start.1 = (bf16[16,2048]{1,0:T(8,128)(2,1)}, bf16[16,2048]{1,0:T(8,128)(2,1)S(1)}, u32[]{:S(2)}, u32[]{:S(2)}) collective-permute-start(bf16[16,2048]{1,0:T(8,128)(2,1)} %refs_2_.1), channel_id=1, source_target_pairs={{0,4},{1,5},{2,6},{3,7},{4,0},{5,1},{6,2},{7,3},{8,12},{9,13},{10,... | collective-permute-start | bytes 196616 | tf_op jit(solution)/shard_map/ppermute | solution.py:21
  5.2 6.6 %collective-permute-start.3 = (bf16[16,2048]{1,0:T(8,128)(2,1)}, bf16[16,2048]{1,0:T(8,128)(2,1)S(1)}, u32[]{:S(2)}, u32[]{:S(2)}) collective-permute-start(bf16[16,2048]{1,0:T(8,128)(2,1)} %refs_2_.1), channel_id=1, source_target_pairs={{0,1},{1,0},{2,3},{3,2},{4,5},{5,4},{6,7},{7,6},{8,9},{9,8},{10,11... | collective-permute-start | bytes 196616 | tf_op jit(solution)/shard_map/ppermute | solution.py:21
  15.3 10.7 %collective-permute-start.7 = (bf16[32,3584]{1,0:T(8,128)(2,1)S(1)}, bf16[32,3584]{1,0:T(8,128)(2,1)S(1)}, u32[]{:S(2)}, u32[]{:S(2)}) collective-permute-start(bf16[32,3584]{1,0:T(8,128)(2,1)S(1)} %get-tuple-element.29.refs_2_.refs_0_), channel_id=1, source_target_pairs={{0,8},{24,16},{1,9},{25,17},{2,10},{26,18},{3,11},{27,19},{4,12},{... | collective-permute-start | bytes 688136 | tf_op jit(solution)/shard_map/ppermute | solution.py:279
  24.7 12.1 %collective-permute-start.10 = (bf16[32,3584]{1,0:T(8,128)(2,1)S(1)}, bf16[32,3584]{1,0:T(8,128)(2,1)S(1)}, u32[]{:S(2)}, u32[]{:S(2)}) collective-permute-start(bf16[32,3584]{1,0:T(8,128)(2,1)S(1)} %get-tuple-element.36.refs_0_), channel_id=1, source_target_pairs={{0,8},{24,16},{1,9},{25,17},{2,10},{26,18},{3,11},{27,19},{4,12},{... | collective-permute-start | bytes 688136 | tf_op jit(solution)/shard_map/ppermute | solution.py:280
  26.1 13.3 %collective-permute-start.9 = (bf16[32,3584]{1,0:T(8,128)(2,1)S(1)}, bf16[32,3584]{1,0:T(8,128)(2,1)S(1)}, u32[]{:S(2)}, u32[]{:S(2)}) collective-permute-start(bf16[32,3584]{1,0:T(8,128)(2,1)S(1)} %total.11.refs_1_), channel_id=1, source_target_pairs={{8,16},{16,8},{9,17},{17,9},{10,18},{18,10},{11,19},{19,11},{12,20... | collective-permute-start | bytes 688136 | tf_op jit(solution)/shard_map/ppermute | solution.py:283
  29.0 11.8 %collective-permute-start.8 = (bf16[32,3584]{1,0:T(8,128)(2,1)S(1)}, bf16[32,3584]{1,0:T(8,128)(2,1)S(1)}, u32[]{:S(2)}, u32[]{:S(2)}) collective-permute-start(bf16[32,3584]{1,0:T(8,128)(2,1)S(1)} %total.12.refs_2_), channel_id=1, source_target_pairs={{0,8},{24,16},{1,9},{25,17},{2,10},{26,18},{3,11},{27,19},{4,12},{... | collective-permute-start | bytes 688136 | tf_op jit(solution)/shard_map/ppermute | solution.py:285
  34.8 10.5 %collective-permute-start.15 = (f32[128,1]{1,0:T(8,128)S(1)}, f32[128,1]{1,0:T(8,128)S(1)}, u32[]{:S(2)}, u32[]{:S(2)}) collective-permute-start(f32[128,1]{1,0:T(8,128)S(1)} %get-tuple-element.38), channel_id=1, source_target_pairs={{0,8},{8,0},{16,24},{24,16},{1,9},{9,1},{17,25},{25,17},{2,10},{10... | collective-permute-start | bytes 1544 | tf_op jit(solution)/shard_map/ppermute | solution.py:21
  34.9 10.5 %collective-permute-start.16 = (f32[128,1]{1,0:T(8,128)S(1)}, f32[128,1]{1,0:T(8,128)S(1)}, u32[]{:S(2)}, u32[]{:S(2)}) collective-permute-start(f32[128,1]{1,0:T(8,128)S(1)} %get-tuple-element.38), channel_id=1, source_target_pairs={{0,16},{8,24},{16,0},{24,8},{1,17},{9,25},{17,1},{25,9},{2,18},{10... | collective-permute-start | bytes 1544 | tf_op jit(solution)/shard_map/ppermute | solution.py:21
  36.8 9.3 %collective-permute-start.17 = (f32[128,1]{1,0:T(8,128)S(1)}, f32[128,1]{1,0:T(8,128)S(1)}, u32[]{:S(2)}, u32[]{:S(2)}) collective-permute-start(f32[128,1]{1,0:T(8,128)S(1)} %get-tuple-element.38), channel_id=1, source_target_pairs={{0,24},{8,16},{16,8},{24,0},{1,25},{9,17},{17,9},{25,1},{2,26},{10... | collective-permute-start | bytes 1544 | tf_op jit(solution)/shard_map/ppermute | solution.py:21
  39.4 6.8 %collective-permute-start.22 = (bf16[32,3584]{1,0:T(8,128)(2,1)S(1)}, bf16[32,3584]{1,0:T(8,128)(2,1)S(1)}, u32[]{:S(2)}, u32[]{:S(2)}) collective-permute-start(bf16[32,3584]{1,0:T(8,128)(2,1)S(1)} %total.13.refs_1_), channel_id=1, source_target_pairs={{8,16},{16,8},{9,17},{17,9},{10,18},{18,10},{11,19},{19,11},{12,20... | collective-permute-start | bytes 688136 | tf_op jit(solution)/shard_map/ppermute | solution.py:287
  40.8 15.1 %collective-permute-start.12 = (bf16[32,3584]{1,0:T(8,128)(2,1)S(1)}, bf16[32,3584]{1,0:T(8,128)(2,1)S(1)}, u32[]{:S(2)}, u32[]{:S(2)}) collective-permute-start(bf16[32,3584]{1,0:T(8,128)(2,1)S(1)} %total.14.refs_2_.refs_1_), channel_id=1, source_target_pairs={{0,8},{24,16},{1,9},{25,17},{2,10},{26,18},{3,11},{27,19},{4,12},{... | collective-permute-start | bytes 688136 | tf_op jit(solution)/shard_map/ppermute | solution.py:289
  45.3 7.8 %collective-permute-start.21 = (bf16[32,3584]{1,0:T(8,128)(2,1)S(1)}, bf16[32,3584]{1,0:T(8,128)(2,1)S(1)}, u32[]{:S(2)}, u32[]{:S(2)}) collective-permute-start(bf16[32,3584]{1,0:T(8,128)(2,1)S(1)} %total.15.refs_2_), channel_id=1, source_target_pairs={{0,8},{8,0},{16,24},{24,16},{1,9},{9,1},{17,25},{25,17},{2,10},{10... | collective-permute-start | bytes 688136 | tf_op jit(solution)/shard_map/ppermute | solution.py:21
  45.4 11.2 %collective-permute-start.11 = (bf16[32,3584]{1,0:T(8,128)(2,1)S(1)}, bf16[32,3584]{1,0:T(8,128)(2,1)S(1)}, u32[]{:S(2)}, u32[]{:S(2)}) collective-permute-start(bf16[32,3584]{1,0:T(8,128)(2,1)S(1)} %total.16.refs_2_.refs_1_), channel_id=1, source_target_pairs={{8,16},{16,8},{9,17},{17,9},{10,18},{18,10},{11,19},{19,11},{12,20... | collective-permute-start | bytes 688136 | tf_op jit(solution)/shard_map/ppermute | solution.py:294
  56.0 7.3 %collective-permute-start.14 = (bf16[32,3584]{1,0:T(8,128)(2,1)S(1)}, bf16[32,3584]{1,0:T(8,128)(2,1)S(1)}, u32[]{:S(2)}, u32[]{:S(2)}) collective-permute-start(bf16[32,3584]{1,0:T(8,128)(2,1)S(1)} %total.17.refs_2_), channel_id=1, source_target_pairs={{8,16},{16,8},{9,17},{17,9},{10,18},{18,10},{11,19},{19,11},{12,20... | collective-permute-start | bytes 688136 | tf_op jit(solution)/shard_map/ppermute | solution.py:297
  60.4 18.8 %collective-permute-start.26 = (bf16[32,1792]{1,0:T(8,128)(2,1)S(1)}, bf16[32,1792]{1,0:T(8,128)(2,1)S(1)}, u32[]{:S(2)}, u32[]{:S(2)}) collective-permute-start(bf16[32,1792]{1,0:T(8,128)(2,1)S(1)} %collective-permute-done.25.refs_4_), channel_id=1, source_target_pairs={{8,0},{16,24},{9,1},{17,25},{10,2},{18,26},{11,3},{19,27},{12,4},{... | collective-permute-start | bytes 344072 | tf_op jit(solution)/shard_map/ppermute | solution.py:305
  61.7 17.5 %collective-permute-start.27 = (bf16[32,1792]{1,0:T(8,128)(2,1)S(1)}, bf16[32,1792]{1,0:T(8,128)(2,1)S(1)}, u32[]{:S(2)}, u32[]{:S(2)}) collective-permute-start(bf16[32,1792]{1,0:T(8,128)(2,1)S(1)} %collective-permute-done.24.refs_2_), channel_id=1, source_target_pairs={{8,0},{16,24},{9,1},{17,25},{10,2},{18,26},{11,3},{19,27},{12,4},{... | collective-permute-start | bytes 344072 | tf_op jit(solution)/shard_map/ppermute | solution.py:306
  63.4 17.1 %collective-permute-start.18 = (bf16[32,1792]{1,0:T(8,128)(2,1)S(1)}, bf16[32,1792]{1,0:T(8,128)(2,1)S(1)}, u32[]{:S(2)}, u32[]{:S(2)}) collective-permute-start(bf16[32,1792]{1,0:T(8,128)(2,1)S(1)} %hidden.2.refs_0_), channel_id=1, source_target_pairs={{0,8},{8,0},{16,24},{24,16},{1,9},{9,1},{17,25},{25,17},{2,10},{10... | collective-permute-start | bytes 344072 | tf_op jit(solution)/shard_map/ppermute | solution.py:21
  70.4 10.1 %collective-permute-start.19 = (bf16[32,1792]{1,0:T(8,128)(2,1)S(1)}, bf16[32,1792]{1,0:T(8,128)(2,1)S(1)}, u32[]{:S(2)}, u32[]{:S(2)}) collective-permute-start(bf16[32,1792]{1,0:T(8,128)(2,1)S(1)} %hidden.2.refs_0_), channel_id=1, source_target_pairs={{0,16},{8,24},{16,0},{24,8},{1,17},{9,25},{17,1},{25,9},{2,18},{10... | collective-permute-start | bytes 344072 | tf_op jit(solution)/shard_map/ppermute | solution.py:21
  70.7 9.9 %collective-permute-start.20 = (bf16[32,1792]{1,0:T(8,128)(2,1)S(1)}, bf16[32,1792]{1,0:T(8,128)(2,1)S(1)}, u32[]{:S(2)}, u32[]{:S(2)}) collective-permute-start(bf16[32,1792]{1,0:T(8,128)(2,1)S(1)} %hidden.2.refs_0_), channel_id=1, source_target_pairs={{0,24},{8,16},{16,8},{24,0},{1,25},{9,17},{17,9},{25,1},{2,26},{10... | collective-permute-start | bytes 344072 | tf_op jit(solution)/shard_map/ppermute | solution.py:21
  99.8 9.2 %collective-permute-start.35 = (bf16[4,128,256]{2,1,0:T(8,128)(2,1)S(1)}, bf16[4,128,256]{2,1,0:T(8,128)(2,1)S(1)}, u32[]{:S(2)}, u32[]{:S(2)}) collective-permute-start(bf16[4,128,256]{2,1,0:T(8,128)(2,1)S(1)} %pad_maximum_fusion.refs_0_), channel_id=1, source_target_pairs={{0,2},{1,3},{2,0},{3,1},{4,6},{5,7},{6,4},{7,5},{8,10},{9,11},{10,... | collective-permute-start | bytes 786440 | tf_op jit(solution)/shard_map/ppermute | solution.py:21
  100.4 14.0 %collective-permute-start.38 = (bf16[4,128,256]{2,1,0:T(8,128)(2,1)S(1)}, bf16[4,128,256]{2,1,0:T(8,128)(2,1)S(1)}, u32[]{:S(2)}, u32[]{:S(2)}) collective-permute-start(bf16[4,128,256]{2,1,0:T(8,128)(2,1)S(1)} %pad_maximum_fusion.refs_0_), channel_id=1, source_target_pairs={{0,4},{1,5},{2,6},{3,7},{4,0},{5,1},{6,2},{7,3},{8,12},{9,13},{10,... | collective-permute-start | bytes 786440 | tf_op jit(solution)/shard_map/ppermute | solution.py:21
  100.9 13.5 %collective-permute-start.40 = (bf16[4,128,256]{2,1,0:T(8,128)(2,1)S(1)}, bf16[4,128,256]{2,1,0:T(8,128)(2,1)S(1)}, u32[]{:S(2)}, u32[]{:S(2)}) collective-permute-start(bf16[4,128,256]{2,1,0:T(8,128)(2,1)S(1)} %pad_maximum_fusion.refs_0_), channel_id=1, source_target_pairs={{0,6},{1,7},{2,4},{3,5},{4,2},{5,3},{6,0},{7,1},{8,14},{9,15},{10,... | collective-permute-start | bytes 786440 | tf_op jit(solution)/shard_map/ppermute | solution.py:21
  109.0 8.7 %collective-permute-start.37 = (bf16[4,128,256]{2,1,0:T(8,128)(2,1)S(1)}, bf16[4,128,256]{2,1,0:T(8,128)(2,1)S(1)}, u32[]{:S(2)}, u32[]{:S(2)}) collective-permute-start(bf16[4,128,256]{2,1,0:T(8,128)(2,1)S(1)} %total.19), channel_id=1, source_target_pairs={{0,1},{1,0},{2,3},{3,2},{4,5},{5,4},{6,7},{7,6},{8,9},{9,8},{10,11... | collective-permute-start | bytes 786440 | tf_op jit(solution)/shard_map/ppermute | solution.py:21
  (19 other events, 92.4 us)

commit v5 on v4

v5 whole, which is shorter than its diff:
```python
import functools
import jax
import jax.numpy as jnp
from jax import lax
from jax.experimental import pallas as pl
from jax.experimental.pallas import tpu as pltpu
from jax.sharding import PartitionSpec as P

D = 8192
CLASSES = 64
TILE = 256
BF16 = jnp.bfloat16
F32 = jnp.float32
WHOLE = pl.BlockSpec(memory_space=pltpu.VMEM)
ANYWHERE = pl.BlockSpec(memory_space=pl.ANY)
SIDE = 128


def swap(value, axis, size, mask):
    return lax.ppermute(value, axis, [(i, i ^ mask) for i in range(size)])


def run(body, name, out_shape, operands, flops, bytes_accessed, in_specs=None, out_specs=WHOLE, **more):
    return pl.pallas_call(
        body,
        out_shape=out_shape,
        in_specs=[WHOLE] * len(operands) if in_specs is None else in_specs,
        out_specs=out_specs,
        compiler_params=pltpu.CompilerParams(vmem_limit_bytes=16 * 1024 * 1024),
        cost_estimate=pl.CostEstimate(flops=flops, bytes_accessed=bytes_accessed, transcendentals=0),
        name=name,
        **more,
    )(*operands)


def fetch(pieces, after, name):
    count = len(pieces)
    copies = []
    for number, (array, row, rows, column, columns) in enumerate(pieces):
        step = min(rows, 256)
        copies += [(number, at, step, row + at, column, columns) for at in range(0, rows, step)]

    def body(*refs):
        sources, targets, sems = refs[:count], refs[-1 - count:-1], refs[-1]
        started = []
        for sem, (number, at, step, row, column, columns) in enumerate(copies):
            copy = pltpu.make_async_copy(
                sources[number].at[pl.ds(row, step), pl.ds(column, columns)],
                targets[number].at[pl.ds(at, step), :],
                sems.at[sem],
            )
            copy.start()
            started.append(copy)
        for copy in started:
            copy.wait()

    size = sum(rows * columns * array.dtype.itemsize for array, _, rows, _, columns in pieces)
    return run(
        body, name,
        [pltpu.VMEM((rows, columns), array.dtype) for array, _, rows, _, columns in pieces],
        [pltpu.with_memory_space_constraint(piece[0], pltpu.HBM) for piece in pieces] + list(after),
        0, 0,
        in_specs=[ANYWHERE] * (count + len(after)),
        out_specs=[WHOLE] * count,
        scratch_shapes=[pltpu.SemaphoreType.DMA((len(copies),))],
    )


def tokens_kernel(masks, panel, *refs):
    blocks, gain, (lhs, cols, squares, x) = refs[:len(masks)], refs[len(masks)], refs[-4:]
    h = lax.axis_index("hid")
    rows = blocks[0].shape[0]
    for mask, block in zip(masks, blocks):
        x[pl.ds(pl.multiple_of((h ^ mask) * rows, rows), rows), :] = block[...]
    values = x[...].astype(F32)
    lhs[...] = (values * gain[...]).astype(BF16)
    squares[...] = jnp.sum(values * values, axis=1, keepdims=True)
    cols[...] = x[:, pl.ds(pl.multiple_of(h * panel, panel), panel)].astype(F32)


def split(value):
    lane = lax.broadcasted_iota(jnp.int32, (value.shape[0], SIDE), 1)
    out = jnp.zeros((value.shape[0], SIDE), F32)
    for part in range(3):
        rounded = value.astype(BF16).astype(F32)
        out = jnp.where(lane == part, rounded, out)
        value = value - rounded
    return out


def joined(parts):
    return jnp.sum(parts.astype(F32), axis=1, keepdims=True)


def gate_up_kernel(lhs_ref, gate_ref, up_ref, *refs):
    send_ref, keep_ref, both, side = refs[-4:]
    places = ((keep_ref, 0), (send_ref, 0), (keep_ref, 1), (send_ref, 1))
    rows = send_ref.shape[1]
    z = lax.axis_index("tok")
    lhs = lhs_ref[...]

    def hand_out(source, start, width):
        for d, (out, slot) in enumerate(places):
            at = pl.multiple_of((z ^ d) * rows, rows)
            out[slot, :, start:start + width] = source[pl.ds(at, rows), :].astype(BF16)

    for tile in range(gate_ref.shape[1] // TILE):
        cols = slice(tile * TILE, (tile + 1) * TILE)
        both[:, :TILE] = jnp.dot(lhs, gate_ref[:, cols], preferred_element_type=F32)
        both[:, TILE:] = jnp.dot(lhs, up_ref[:, cols], preferred_element_type=F32)
        hand_out(both, 2 * tile * TILE, 2 * TILE)
    if send_ref.shape[2] > 2 * gate_ref.shape[1]:
        side[...] = split(refs[0][...])
        hand_out(side, 2 * gate_ref.shape[1], SIDE)


def gate_up(lhs, gate, up, squares, n_tok, after=()):
    ntok, depth = lhs.shape
    width = gate.shape[1]
    rows = ntok // n_tok
    extra = [] if squares is None else [squares]
    shape = jax.ShapeDtypeStruct((2, rows, 2 * width + SIDE * len(extra)), BF16)
    return run(
        gate_up_kernel, "gate_up", [shape, shape], [lhs, gate, up, *extra, *after],
        0, 0,
        in_specs=[WHOLE] * (3 + len(extra)) + [ANYWHERE] * len(after),
        out_specs=[WHOLE] * 2,
        scratch_shapes=[pltpu.VMEM((ntok, 2 * TILE), F32), pltpu.VMEM((ntok, SIDE), F32)],
    )


def pair_total(keep, got, main, after):
    def body(keep_ref, got_ref, *refs):
        out = refs[-1]
        out[:, :main] = (keep_ref[1, :, :main].astype(F32) + got_ref[1, :, :main].astype(F32)).astype(BF16)
        if out.shape[1] > main:
            out[:, main:] = split(joined(keep_ref[1, :, main:]) + joined(got_ref[1, :, main:])).astype(BF16)

    size = keep.size // 2
    return run(
        body, "pair_total", jax.ShapeDtypeStruct(keep.shape[1:], BF16), [keep, got, *after],
        size, 6 * size, in_specs=[WHOLE] * 2 + [ANYWHERE] * len(after),
    )


def copy_after(value, after):
    def body(value_ref, *refs):
        refs[-1][...] = value_ref[...]

    return run(
        body, "copy", jax.ShapeDtypeStruct(value.shape, value.dtype), [value, *after],
        0, 4 * value.size, in_specs=[WHOLE] + [ANYWHERE] * len(after),
    )


def stack_after(blocks, after):
    stacks = [block if block.ndim == 3 else block[None] for block in blocks]
    total = sum(stack.shape[0] for stack in stacks)

    def body(*refs):
        at = 0
        for ref in refs[:len(stacks)]:
            refs[-1][at:at + ref.shape[0]] = ref[...]
            at += ref.shape[0]

    shape = jax.ShapeDtypeStruct((total, *stacks[0].shape[1:]), blocks[0].dtype)
    return run(
        body, "stack", shape, [*stacks, *after], 0, 4 * sum(stack.size for stack in stacks),
        in_specs=[WHOLE] * len(stacks) + [ANYWHERE] * len(after),
    )


def hidden_rows(chunks, widths, scale, after):
    rows = chunks[0][0].shape[1]
    given = [] if scale is None else [scale]

    def body(*refs):
        out_ref, scale_ref = refs[-2:]
        keep_ref, got_ref, over_ref = refs[:3]
        if scale is None:
            tail = slice(2 * widths[0], 2 * widths[0] + SIDE)
            squares = joined(keep_ref[0, :, tail]) + joined(got_ref[0, :, tail]) + joined(over_ref[:, tail])
            factor = lax.rsqrt(squares / float(D) + 1e-05)
        else:
            factor = refs[3 * len(chunks)][...]
        scale_ref[...] = factor
        start = 0
        for k, width in enumerate(widths):
            keep_ref, got_ref, over_ref = refs[3 * k:3 * k + 3]

            def total(at):
                cols = slice(at, at + TILE)
                return (
                    keep_ref[0, :, cols].astype(F32) + got_ref[0, :, cols].astype(F32) + over_ref[:, cols].astype(F32)
                ) * factor

            for at in range(0, width, TILE):
                gate, up = total(2 * at), total(2 * at + TILE)
                out_ref[:, start + at:start + at + TILE] = (jax.nn.silu(gate) * up).astype(BF16)
            start += width

    size = rows * sum(widths)
    return run(
        body, "hidden",
        [jax.ShapeDtypeStruct((rows, sum(widths)), BF16), jax.ShapeDtypeStruct((rows, 1), F32)],
        [part for chunk in chunks for part in chunk] + given + list(after), 20 * size, 14 * size,
        in_specs=[WHOLE] * (3 * len(chunks) + len(given)) + [ANYWHERE] * len(after),
        out_specs=[WHOLE] * 2,
    )


def down_kernel(masks, skip, panel, n_blocks, *refs):
    blocks, weight, lhs, out = refs[:n_blocks], refs[n_blocks], refs[-1], refs[-2]
    before = refs[n_blocks + 1] if len(refs) == n_blocks + 4 else None
    z = lax.axis_index("tok")
    h = lax.axis_index("hid")
    rows = blocks[0].shape[0]
    for d, block in enumerate(blocks):
        lhs[pl.ds(pl.multiple_of((z ^ d) * rows, rows), rows), :] = block[...]
    values = lhs[...]
    for slot, mask in enumerate(masks):
        column = pl.multiple_of((h ^ mask) * panel, panel)
        total = jnp.dot(values, weight[:, pl.ds(column, panel)], preferred_element_type=F32)
        if before is not None:
            total = total + before[skip + slot]
        out[slot] = total.astype(out.dtype)


def down(blocks, weight, masks, panel, kind, before=None, skip=0):
    rows, depth = blocks[0].shape
    ntok = rows * len(blocks)
    return run(
        functools.partial(down_kernel, masks, skip, panel, len(blocks)), "down",
        jax.ShapeDtypeStruct((len(masks), ntok, panel), kind),
        [*blocks, weight] + ([] if before is None else [before]),
        2 * ntok * depth * panel * len(masks), 2 * depth * panel * len(masks),
        scratch_shapes=[pltpu.VMEM((ntok, depth), BF16)],
    )


def chip_sum_kernel(mine_ref, other_ref, own_ref, *outs):
    own_ref[...] = mine_ref[0] + other_ref[0].astype(F32)
    for e, out in enumerate(outs):
        out[...] = (mine_ref[e + 1] + other_ref[e + 1].astype(F32)).astype(BF16)


def gram_kernel(slots, n_hid, ntok, classes, own_ref, *refs):
    stacks = refs[:len(slots)]
    outs, (tiles, sems) = refs[:-2], refs[-2:]
    out_ref = outs[-2] if classes else outs[-1]
    z = lax.axis_index("tok")
    h = lax.axis_index("hid")
    width = own_ref.shape[1]
    left = own_ref[...].T
    copies = []
    for stack, places in zip(stacks, slots):
        for at, (d, mask) in enumerate(places):
            number = len(copies)
            tiles[number] = jnp.dot(left, stack[at], preferred_element_type=F32) * (1.0 / ntok)
            column = ((z ^ d) * n_hid + (h ^ mask)) * width
            copy = pltpu.make_async_copy(
                tiles.at[number], out_ref.at[:, pl.ds(pl.multiple_of(column, width), width)], sems.at[number]
            )
            copy.start()
            copies.append(copy)
    if classes:
        labels, cross_ref = refs[len(slots)], outs[-1]
        onehot = (labels[...] == lax.broadcasted_iota(jnp.int32, (classes, ntok), 0)).astype(F32)
        counts = jnp.sum(onehot, axis=1, keepdims=True)
        sums = jnp.dot(onehot.astype(BF16), own_ref[...], preferred_element_type=F32)
        cross_ref[...] = sums / jnp.maximum(counts, 1.0)
    for copy in copies:
        copy.wait()


def gram_part(resid_cols, stacks, slots, n_tok, n_hid, before, labels=None):
    ntok, width = resid_cols.shape
    here = sum(len(places) for places in slots)
    gram_shape = pltpu.HBM((width, width * n_tok * n_hid), F32)
    extra, extra_specs = ([], []) if labels is None else ([labels[None, :]], [WHOLE])
    if before is not None:
        extra, extra_specs = extra + [before], extra_specs + [ANYWHERE]
    return run(
        functools.partial(gram_kernel, slots, n_hid, ntok, 0 if labels is None else CLASSES), "gram",
        [gram_shape] + ([] if labels is None else [jax.ShapeDtypeStruct((CLASSES, width), F32)]),
        [resid_cols, *stacks, *extra],
        2 * ntok * width * width * here, 4 * width * width * here,
        in_specs=[WHOLE] * (1 + len(stacks)) + extra_specs,
        out_specs=[ANYWHERE] + ([] if labels is None else [WHOLE]),
        input_output_aliases={} if before is None else {len(stacks) + len(extra): 0},
        scratch_shapes=[pltpu.VMEM((here, width, width), F32), pltpu.SemaphoreType.DMA((here,))],
    )


def class_means(resid_cols, labels):
    onehot = (labels[:, None] == jnp.arange(CLASSES, dtype=jnp.int32)[None, :]).astype(BF16)
    counts = jnp.sum(onehot.astype(F32), axis=0)
    class_sums = lax.dot_general(
        resid_cols, onehot, (((0,), (0,)), ((), ())), preferred_element_type=F32
    )
    return class_sums / jnp.maximum(counts, 1.0)[None, :]


def on_line(n_tok, n_hid, resid_in, norm_gain, gate_weight, up_weight, down_weight, labels):
    rows, block = resid_in.shape
    ntok, panel = rows * n_hid, block // n_hid
    depth, shard_ff = gate_weight.shape
    tiles = shard_ff // TILE
    ends = [TILE * (tiles * k // 3) for k in range(4)]
    chip_masks = list(range(2, n_hid, 2))

    def part(weight, k):
        return weight, 0, depth, ends[k], ends[k + 1] - ends[k]

    near = [resid_in] + [swap(resid_in, "hid", n_hid, mask) for mask in chip_masks]
    gate_0, up_0, own_x, gain = fetch(
        [
            part(gate_weight, 0),
            part(up_weight, 0),
            (resid_in, 0, rows, 0, block),
            (norm_gain[None, :], 0, 1, 0, block),
        ],
        (), "fetch_first",
    )
    relayed = copy_after(near[1], (gain,))
    gate_1, up_1 = fetch([part(gate_weight, 1), part(up_weight, 1)], (relayed,), "fetch_gate_up")
    far = [swap(piece, "hid", n_hid, 1) for piece in [near[0], relayed, *near[2:]]]
    masks = [0] + chip_masks + [1] + [mask + 1 for mask in chip_masks]
    lhs, x_cols, squares = run(
        functools.partial(tokens_kernel, masks, panel), "tokens",
        (
            jax.ShapeDtypeStruct((ntok, block), BF16),
            jax.ShapeDtypeStruct((ntok, panel), F32),
            jax.ShapeDtypeStruct((ntok, 1), F32),
        ),
        [own_x, *near[1:], *far, gain, gate_1],
        4 * ntok * block, 4 * ntok * block,
        in_specs=[WHOLE] * (n_hid + 1) + [ANYWHERE],
        out_specs=(WHOLE, WHOLE, WHOLE),
        scratch_shapes=[pltpu.VMEM((ntok, block), BF16)],
    )

    widths = [ends[k + 1] - ends[k] for k in range(3)]
    send_0, keep_0 = gate_up(lhs, gate_0, up_0, squares, n_tok)
    got_0 = swap(send_0, "tok", n_tok, 1)
    send_1, keep_1 = gate_up(lhs, gate_1, up_1, None, n_tok, (send_0,))
    got_1 = swap(send_1, "tok", n_tok, 1)
    sum_0 = pair_total(keep_0, got_0, 2 * widths[0], (send_1,))
    over_0 = swap(sum_0, "tok", n_tok, 2)
    gate_2, up_2 = fetch([part(gate_weight, 2), part(up_weight, 2)], (sum_0,), "fetch_gate_up")
    send_2, keep_2 = gate_up(lhs, gate_2, up_2, None, n_tok)
    got_2 = swap(send_2, "tok", n_tok, 1)
    sum_1 = pair_total(keep_1, got_1, 2 * widths[1], (send_2,))
    over_1 = swap(sum_1, "tok", n_tok, 2)
    sum_2 = pair_total(keep_2, got_2, 2 * widths[2], (sum_1,))
    over_2 = swap(sum_2, "tok", n_tok, 2)
    down_a, = fetch([(down_weight, 0, ends[2], 0, block)], (sum_2,), "fetch_down")

    a_own, scale = hidden_rows([(keep_0, got_0, over_0), (keep_1, got_1, over_1)], widths[:2], None, (down_a,))
    a_two = swap(a_own, "tok", n_tok, 2)
    a_one = swap(a_own, "tok", n_tok, 1)
    down_b, = fetch([(down_weight, ends[2], widths[2], 0, block)], (a_own,), "fetch_down")
    b_own, _ = hidden_rows([(keep_2, got_2, over_2)], widths[2:], scale, (down_b, a_one))
    b_two = swap(b_own, "tok", n_tok, 2)
    b_one = swap(b_own, "tok", n_tok, 1)
    a_three = swap(copy_after(a_two, (b_own,)), "tok", n_tok, 1)
    b_three = swap(b_two, "tok", n_tok, 1)
    hidden_a = [a_own, a_one, a_two, a_three]
    hidden_b = [b_own, b_one, b_two, b_three]

    here = [0] + chip_masks
    there = [mask + 1 for mask in here]
    first = down(hidden_a, down_a, there + here, panel, F32)
    other = down(hidden_b, down_b, there, panel, BF16, first, 0)
    other = swap(other, "hid", n_hid, 1)
    mine = down(hidden_b, down_b, here, panel, F32, first, len(there))
    summed, *sends = run(
        chip_sum_kernel, "chip_sum",
        [jax.ShapeDtypeStruct((ntok, panel), F32)] + [jax.ShapeDtypeStruct((ntok, panel), BF16)] * len(chip_masks),
        [mine, other], mine.size, 8 * mine.size,
        out_specs=[WHOLE] * len(here),
    )
    for mask, value in zip(chip_masks, sends):
        summed = summed + swap(value, "hid", n_hid, mask).astype(F32)
    resid_cols = (x_cols + summed).astype(BF16)

    column = [swap(resid_cols, "tok", n_tok, d) for d in range(1, n_tok)]
    across = swap(resid_cols, "hid", n_hid, 6)
    line = stack_after([resid_cols, *column], (across,))
    beside = [swap(line, "hid", n_hid, mask) for mask in (2, 4)]
    across_line = [swap(across, "tok", n_tok, d) for d in range(1, n_tok)]
    line_far = swap(line, "hid", n_hid, 1)
    across_far = swap(across, "hid", n_hid, 1)
    line_slots = [[(d, mask) for d in range(n_tok)] for mask in range(n_hid)]
    gram, cross = gram_part(
        resid_cols, [line, line_far, across[None], across_far[None]],
        [line_slots[0], line_slots[1], [(0, 6)], [(0, 7)]], n_tok, n_hid, None, labels,
    )
    done = pltpu.with_memory_space_constraint(gram, pltpu.HBM)
    near = stack_after([*beside, *across_line], (done,))
    far = swap(near, "hid", n_hid, 1)
    for stack, core in ((near, 0), (far, 1)):
        slots = line_slots[2 + core] + line_slots[4 + core] + line_slots[6 + core][1:]
        gram, = gram_part(resid_cols, [stack], [slots], n_tok, n_hid, gram)
    return (gram, cross.T)


def plain(n_tok, n_hid, resid_in, norm_gain, gate_weight, up_weight, down_weight, labels):
    x = lax.all_gather(resid_in, "hid", axis=0, tiled=True).astype(F32)
    ntok, block = x.shape
    total_sq = lax.psum(jnp.sum(x * x, axis=1), "tok")
    normed = (x * lax.rsqrt(total_sq / float(D) + 1e-05)[:, None] * norm_gain[None, :]).astype(BF16)

    def summed_over_tok(weight):
        product = jnp.dot(normed, weight, preferred_element_type=F32).astype(BF16)
        return lax.psum_scatter(product, "tok", scatter_dimension=0, tiled=True).astype(F32)

    hidden = (jax.nn.silu(summed_over_tok(gate_weight)) * summed_over_tok(up_weight)).astype(BF16)
    hidden = lax.all_gather(hidden, "tok", axis=0, tiled=True)
    partial_out = jnp.dot(hidden, down_weight, preferred_element_type=F32).astype(BF16)
    summed = lax.psum_scatter(partial_out, "hid", scatter_dimension=1, tiled=True).astype(F32)
    panel = block // n_hid
    x_cols = lax.dynamic_slice_in_dim(x, lax.axis_index("hid") * panel, panel, 1)
    resid_cols = (x_cols + summed).astype(BF16)
    everyone = lax.all_gather(resid_cols, ("tok", "hid"), axis=1, tiled=True)
    gram = lax.dot_general(
        resid_cols, everyone, (((0,), (0,)), ((), ())), preferred_element_type=F32
    ) / float(ntok)
    return (gram, class_means(resid_cols, labels))


def on_device(n_tok, n_hid, resid_in, norm_gain, gate_weight, *rest):
    panel = resid_in.shape[1] // n_hid
    fits = n_tok == 4 and n_hid == 8 and panel % 128 == 0 and gate_weight.shape[1] % TILE == 0 and gate_weight.shape[1] >= 3 * TILE
    body = on_line if fits else plain
    return body(n_tok, n_hid, resid_in, norm_gain, gate_weight, *rest)


def solution(mesh):
    return jax.shard_map(
        functools.partial(on_device, mesh.shape["tok"], mesh.shape["hid"]),
        mesh=mesh,
        in_specs=(
            P("hid", "tok"),
            P("tok"),
            P("tok", "hid"),
            P("tok", "hid"),
            P("hid", "tok"),
            P(),
        ),
        out_specs=(P(("tok", "hid"), None), P(("tok", "hid"), None)),
        check_vma=False,
    )
```

time: 120 us -> 109 us (0.908)
  starting transfers between devices: 58.5 us -> 39.8 us
  waiting for transfers between devices: 27.9 us -> 34.8 us
  Pallas kernels: 31.2 us -> 33.6 us
    ppermute x12 -> x0, starting transfers between devices: 22.2 us -> none  [the longest x1 5.8 us: on_line(): b_far = lax.ppermute(send, 'tok', INWARD)]
    ppermute x30 -> x35, waiting for transfers between devices: 27.2 us -> 34.8 us  [swap(): return lax.ppermute(value, axis, [(i, i ^ mask) for i in range(size)])]
    ppermute x30 -> x35, starting transfers between devices: 36.3 us -> 39.8 us  [swap(): return lax.ppermute(value, axis, [(i, i ^ mask) for i in range(size)])]
    pallas_call x26 -> x25, Pallas kernels: 31.2 us -> 33.6 us  [run(): pl.pallas_call(body, out_shape=out_shape, in_specs=[WHOLE] * len(operands...]
  transfers between devices with their start and end apart: 42 -> 35, of which waited for: 15 -> 16; matrix products, arithmetic and copies ran while one was open for 1% -> 0% of each run, Pallas kernels for 22% -> 27%
where the time goes in v5:
time: 109 us
  starting transfers between devices  39.8 us (37%)
  waiting for transfers between devices  34.8 us (32%)
  Pallas kernels  33.6 us (31%)
    ppermute x35, starting transfers between devices, swap(): return lax.ppermute(value, axis, [(i, i ^ mask) for i in range(size)])  39.8 us
    ppermute x35, waiting for transfers between devices, swap(): return lax.ppermute(value, axis, [(i, i ^ mask) for i in range(size)])  34.8 us
    pallas_call x25, Pallas kernels, run(): pl.pallas_call(body, out_shape=out_shape, in_specs=[WHOLE] * len(operands...  33.6 us
  transfers between devices with their start and end apart: 35, of which 16 were waited for; matrix products, arithmetic and copies ran while one was open for 0% of the time, Pallas kernels for 27%

profile of v5, /device:TPU:0, one launch (start us, length us, event | category | flops | bytes accessed | tf_op | source)
XLA Modules:
  0.0 109.1 jit_solution(6515868817305048347)
XLA Ops:
  0.6 3.0 %collective-permute-start.1 = (bf16[16,2048]{1,0:T(8,128)(2,1)}, bf16[16,2048]{1,0:T(8,128)(2,1)S(1)}, u32[]{:S(2)}, u32[]{:S(2)}) collective-permute-start(bf16[16,2048]{1,0:T(8,128)(2,1)} %refs_2_.1), channel_id=1, source_target_pairs={{0,4},{1,5},{2,6},{3,7},{4,0},{5,1},{6,2},{7,3},{8,12},{9,13},{10,... | collective-permute-start | bytes 196616 | tf_op jit(solution)/shard_map/ppermute | solution.py:20
  5.2 3.7 %fetch_first.1 = (bf16[2048,1024]{1,0:T(8,128)(2,1)S(1)}, bf16[2048,1024]{1,0:T(8,128)(2,1)S(1)}, bf16[16,2048]{1,0:T(8,128)(2,1)S(1)}, f32[1,2048]{1,0:T(1,128)S(1)}) custom-call(bf16[2048,3584]{1,0:T(8,128)(2,1)} %refs_0_.7, bf16[2048,3584]{1,0:T(8,128)(2,1)} %refs_1_.5, bf16[16,2048]{1,0:T(8,128)(2,1)} %refs_2_.1, f32[1,2048]{1,0:T(1,128)} %bitcast.22), custom_call_target="tpu_custom_call" | custom-call | tf_op jit(solution)/shard_map/fetch_first/pallas_call | solution.py:24
  10.1 4.3 %fetch_gate_up.2 = (bf16[2048,1280]{1,0:T(8,128)(2,1)S(1)}, bf16[2048,1280]{1,0:T(8,128)(2,1)S(1)}) custom-call(bf16[2048,3584]{1,0:T(8,128)(2,1)} %refs_0_.7, bf16[2048,3584]{1,0:T(8,128)(2,1)} %refs_1_.5, bf16[16,2048]{1,0:T(8,128)(2,1)S(1)} %copy.14.refs_2_), custom_call_target="tpu_custom_call" | custom-call | tf_op jit(solution)/shard_map/fetch_gate_up/pallas_call | solution.py:24
  16.2 2.1 %collective-permute-start.7 = (bf16[2,32,2176]{2,1,0:T(8,128)(2,1)S(1)}, bf16[2,32,2176]{2,1,0:T(8,128)(2,1)S(1)}, u32[]{:S(2)}, u32[]{:S(2)}) collective-permute-start(bf16[2,32,2176]{2,1,0:T(8,128)(2,1)S(1)} %get-tuple-element.37.refs_0_), channel_id=1, source_target_pairs={{0,8},{8,0},{16,24},{24,16},{1,9},{9,1},{17,25},{25,17},{2,10},{10... | collective-permute-start | bytes 835592 | tf_op jit(solution)/shard_map/ppermute | solution.py:20
  19.9 5.8 %collective-permute-done.7.got_ref.refs_1_ = bf16[2,32,2176]{2,1,0:T(8,128)(2,1)S(1)} collective-permute-done((bf16[2,32,2176]{2,1,0:T(8,128)(2,1)S(1)}, bf16[2,32,2176]{2,1,0:T(8,128)(2,1)S(1)}, u32[]{:S(2)}, u32[]{:S(2)}) %collective-permute-start.7) | collective-permute-done | bytes 278560 | tf_op jit(solution)/shard_map/ppermute | solution.py:20
  25.8 4.3 %fetch_gate_up.3 = (bf16[2048,1280]{1,0:T(8,128)(2,1)S(1)}, bf16[2048,1280]{1,0:T(8,128)(2,1)S(1)}) custom-call(bf16[2048,3584]{1,0:T(8,128)(2,1)} %refs_0_.7, bf16[2048,3584]{1,0:T(8,128)(2,1)} %refs_1_.5, bf16[32,2176]{1,0:T(8,128)(2,1)S(1)} %pair_total.3.refs_2_), custom_call_target="tpu_custom_call" | custom-call | tf_op jit(solution)/shard_map/fetch_gate_up/pallas_call | solution.py:24
  31.7 2.1 %collective-permute-start.8 = (bf16[2,32,2560]{2,1,0:T(8,128)(2,1)S(1)}, bf16[2,32,2560]{2,1,0:T(8,128)(2,1)S(1)}, u32[]{:S(2)}, u32[]{:S(2)}) collective-permute-start(bf16[2,32,2560]{2,1,0:T(8,128)(2,1)S(1)} %get-tuple-element.43.refs_0_), channel_id=1, source_target_pairs={{0,8},{8,0},{16,24},{24,16},{1,9},{9,1},{17,25},{25,17},{2,10},{10... | collective-permute-start | bytes 983048 | tf_op jit(solution)/shard_map/ppermute | solution.py:20
  33.9 2.7 %collective-permute-start.12 = (bf16[32,2560]{1,0:T(8,128)(2,1)S(1)}, bf16[32,2560]{1,0:T(8,128)(2,1)S(1)}, u32[]{:S(2)}, u32[]{:S(2)}) collective-permute-start(bf16[32,2560]{1,0:T(8,128)(2,1)S(1)} %pair_total.4.refs_0_), channel_id=1, source_target_pairs={{0,16},{8,24},{16,0},{24,8},{1,17},{9,25},{17,1},{25,9},{2,18},{10... | collective-permute-start | bytes 491528 | tf_op jit(solution)/shard_map/ppermute | solution.py:20
  36.9 9.7 %collective-permute-done.8.got_ref.refs_1_ = bf16[2,32,2560]{2,1,0:T(8,128)(2,1)S(1)} collective-permute-done((bf16[2,32,2560]{2,1,0:T(8,128)(2,1)S(1)}, bf16[2,32,2560]{2,1,0:T(8,128)(2,1)S(1)}, u32[]{:S(2)}, u32[]{:S(2)}) %collective-permute-start.8) | collective-permute-done | bytes 327712 | tf_op jit(solution)/shard_map/ppermute | solution.py:20
  47.0 3.8 %fetch_down.2.refs_6_.refs_4_ = bf16[2304,2048]{1,0:T(8,128)(2,1)S(1)} custom-call(bf16[3584,2048]{1,0:T(8,128)(2,1)} %refs_0_.9, bf16[32,2560]{1,0:T(8,128)(2,1)S(1)} %pair_total.5.refs_1_), custom_call_target="tpu_custom_call" | custom-call | tf_op jit(solution)/shard_map/fetch_down/pallas_call | solution.py:24
  50.8 2.2 %collective-permute-done.11.refs_2_ = bf16[32,2176]{1,0:T(8,128)(2,1)S(1)} collective-permute-done((bf16[32,2176]{1,0:T(8,128)(2,1)S(1)}, bf16[32,2176]{1,0:T(8,128)(2,1)S(1)}, u32[]{:S(2)}, u32[]{:S(2)}) %collective-permute-start.11) | collective-permute-done | bytes 139296 | tf_op jit(solution)/shard_map/ppermute | solution.py:20
  54.3 3.4 %collective-permute-start.17 = (bf16[32,2304]{1,0:T(8,128)(2,1)S(1)}, bf16[32,2304]{1,0:T(8,128)(2,1)S(1)}, u32[]{:S(2)}, u32[]{:S(2)}) collective-permute-start(bf16[32,2304]{1,0:T(8,128)(2,1)S(1)} %get-tuple-element.46.refs_1_.refs_0_), channel_id=1, source_target_pairs={{0,16},{8,24},{16,0},{24,8},{1,17},{9,25},{17,1},{25,9},{2,18},{10... | collective-permute-start | bytes 442376 | tf_op jit(solution)/shard_map/ppermute | solution.py:20
  57.8 2.5 %fetch_down.3.refs_4_ = bf16[1280,2048]{1,0:T(8,128)(2,1)S(1)} custom-call(bf16[3584,2048]{1,0:T(8,128)(2,1)} %refs_0_.9, bf16[32,2304]{1,0:T(8,128)(2,1)S(1)} %get-tuple-element.46.refs_1_.refs_0_), custom_call_target="tpu_custom_call" | custom-call | tf_op jit(solution)/shard_map/fetch_down/pallas_call | solution.py:24
  62.7 3.5 %collective-permute-start.15 = (bf16[32,1280]{1,0:T(8,128)(2,1)S(1)}, bf16[32,1280]{1,0:T(8,128)(2,1)S(1)}, u32[]{:S(2)}, u32[]{:S(2)}) collective-permute-start(bf16[32,1280]{1,0:T(8,128)(2,1)S(1)} %get-tuple-element.47.refs_0_), channel_id=1, source_target_pairs={{0,16},{8,24},{16,0},{24,8},{1,17},{9,25},{17,1},{25,9},{2,18},{10... | collective-permute-start | bytes 245768 | tf_op jit(solution)/shard_map/ppermute | solution.py:20
  66.3 2.4 %collective-permute-done.15.refs_2_ = bf16[32,1280]{1,0:T(8,128)(2,1)S(1)} collective-permute-done((bf16[32,1280]{1,0:T(8,128)(2,1)S(1)}, bf16[32,1280]{1,0:T(8,128)(2,1)S(1)}, u32[]{:S(2)}, u32[]{:S(2)}) %collective-permute-start.15) | collective-permute-done | bytes 81952 | tf_op jit(solution)/shard_map/ppermute | solution.py:20
  68.7 2.3 %collective-permute-start.16 = (bf16[32,1280]{1,0:T(8,128)(2,1)S(1)}, bf16[32,1280]{1,0:T(8,128)(2,1)S(1)}, u32[]{:S(2)}, u32[]{:S(2)}) collective-permute-start(bf16[32,1280]{1,0:T(8,128)(2,1)S(1)} %collective-permute-done.15.refs_2_), channel_id=1, source_target_pairs={{0,8},{8,0},{16,24},{24,16},{1,9},{9,1},{17,25},{25,17},{2,10},{10... | collective-permute-start | bytes 245768 | tf_op jit(solution)/shard_map/ppermute | solution.py:20
  81.6 2.5 %collective-permute-done.22 = bf16[128,256]{1,0:T(8,128)(2,1)S(1)} collective-permute-done((bf16[128,256]{1,0:T(8,128)(2,1)S(1)}, bf16[128,256]{1,0:T(8,128)(2,1)S(1)}, u32[]{:S(2)}, u32[]{:S(2)}) %collective-permute-start.22) | collective-permute-done | bytes 65568 | tf_op jit(solution)/shard_map/ppermute | solution.py:20
  84.5 2.2 %collective-permute-start.25 = (bf16[128,256]{1,0:T(8,128)(2,1)S(1)}, bf16[128,256]{1,0:T(8,128)(2,1)S(1)}, u32[]{:S(2)}, u32[]{:S(2)}) collective-permute-start(bf16[128,256]{1,0:T(8,128)(2,1)S(1)} %add_convert_fusion.own_ref), channel_id=1, source_target_pairs={{0,24},{8,16},{16,8},{24,0},{1,25},{9,17},{17,9},{25,1},{2,26},{10... | collective-permute-start | bytes 196616 | tf_op jit(solution)/shard_map/ppermute | solution.py:20
  95.8 1.8 %collective-permute-start.31 = (bf16[128,256]{1,0:T(8,128)(2,1)S(1)}, bf16[128,256]{1,0:T(8,128)(2,1)S(1)}, u32[]{:S(2)}, u32[]{:S(2)}) collective-permute-start(bf16[128,256]{1,0:T(8,128)(2,1)S(1)} %collective-permute-done.26.refs_4_), channel_id=1, source_target_pairs={{0,24},{8,16},{16,8},{24,0},{1,25},{9,17},{17,9},{25,1},{2,26},{10... | collective-permute-start | bytes 196616 | tf_op jit(solution)/shard_map/ppermute | solution.py:20
  98.4 1.8 %collective-permute-start.29 = (bf16[128,256]{1,0:T(8,128)(2,1)S(1)}, bf16[128,256]{1,0:T(8,128)(2,1)S(1)}, u32[]{:S(2)}, u32[]{:S(2)}) collective-permute-start(bf16[128,256]{1,0:T(8,128)(2,1)S(1)} %collective-permute-done.26.refs_4_), channel_id=1, source_target_pairs={{0,8},{8,0},{16,24},{24,16},{1,9},{9,1},{17,25},{25,17},{2,10},{10... | collective-permute-start | bytes 196616 | tf_op jit(solution)/shard_map/ppermute | solution.py:20
  100.2 2.4 %gram.3 = (f32[256,8192]{1,0:T(8,128)}, f32[64,256]{1,0:T(8,128)}) custom-call(bf16[128,256]{1,0:T(8,128)(2,1)S(1)} %add_convert_fusion.own_ref, bf16[4,128,256]{2,1,0:T(8,128)(2,1)S(1)} %stack.2.refs_0_, bf16[4,128,256]{2,1,0:T(8,128)(2,1)S(1)} %collective-permute-done.32.refs_1_, bf16[1,128,256]{2,1,0:T(8,128)(2,1)S(1)} %bitcast.13, ...), custom_call_target="tpu_custom_call" | custom-call | flops 167772160 | bytes 2621440 | tf_op jit(solution)/shard_map/gram/pallas_call | solution.py:24
  102.7 2.2 %collective-permute-done.30 = bf16[128,256]{1,0:T(8,128)(2,1)S(1)} collective-permute-done((bf16[128,256]{1,0:T(8,128)(2,1)S(1)}, bf16[128,256]{1,0:T(8,128)(2,1)S(1)}, u32[]{:S(2)}, u32[]{:S(2)}) %collective-permute-start.30) | collective-permute-done | bytes 65568 | tf_op jit(solution)/shard_map/ppermute | solution.py:20
  105.1 1.9 %gram.4.refs_1_ = f32[256,8192]{1,0:T(8,128)} custom-call(bf16[128,256]{1,0:T(8,128)(2,1)S(1)} %add_convert_fusion.own_ref, bf16[11,128,256]{2,1,0:T(8,128)(2,1)S(1)} %stack.3.refs_0_, f32[256,8192]{1,0:T(8,128)} %get-tuple-element.52.refs_5_.refs_1_), custom_call_target="tpu_custom_call", output_to_operand_aliasing={{}: (2, {})} | custom-call | flops 184549376 | bytes 2883584 | tf_op jit(solution)/shard_map/gram/pallas_call | solution.py:24
  107.3 1.9 %gram.5 = f32[256,8192]{1,0:T(8,128)} custom-call(bf16[128,256]{1,0:T(8,128)(2,1)S(1)} %add_convert_fusion.own_ref, bf16[11,128,256]{2,1,0:T(8,128)(2,1)S(1)} %collective-permute-done.34.refs_0_, f32[256,8192]{1,0:T(8,128)} %gram.4.refs_1_), custom_call_target="tpu_custom_call", output_to_operand_aliasing={{}: (2, {})} | custom-call | flops 184549376 | bytes 2883584 | tf_op jit(solution)/shard_map/gram/pallas_call | solution.py:24
  (74 shorter events, 33.7 us)
Async XLA Ops:
  0.6 8.3 %collective-permute-start.1 = (bf16[16,2048]{1,0:T(8,128)(2,1)}, bf16[16,2048]{1,0:T(8,128)(2,1)S(1)}, u32[]{:S(2)}, u32[]{:S(2)}) collective-permute-start(bf16[16,2048]{1,0:T(8,128)(2,1)} %refs_2_.1), channel_id=1, source_target_pairs={{0,4},{1,5},{2,6},{3,7},{4,0},{5,1},{6,2},{7,3},{8,12},{9,13},{10,... | collective-permute-start | bytes 196616 | tf_op jit(solution)/shard_map/ppermute | solution.py:20
  3.7 5.9 %collective-permute-start.2 = (bf16[16,2048]{1,0:T(8,128)(2,1)}, bf16[16,2048]{1,0:T(8,128)(2,1)S(1)}, u32[]{:S(2)}, u32[]{:S(2)}) collective-permute-start(bf16[16,2048]{1,0:T(8,128)(2,1)} %refs_2_.1), channel_id=1, source_target_pairs={{0,6},{1,7},{2,4},{3,5},{4,2},{5,3},{6,0},{7,1},{8,14},{9,15},{10,... | collective-permute-start | bytes 196616 | tf_op jit(solution)/shard_map/ppermute | solution.py:20
  5.2 9.2 %collective-permute-start.3 = (bf16[16,2048]{1,0:T(8,128)(2,1)}, bf16[16,2048]{1,0:T(8,128)(2,1)S(1)}, u32[]{:S(2)}, u32[]{:S(2)}) collective-permute-start(bf16[16,2048]{1,0:T(8,128)(2,1)} %refs_2_.1), channel_id=1, source_target_pairs={{0,1},{1,0},{2,3},{3,2},{4,5},{5,4},{6,7},{7,6},{8,9},{9,8},{10,11... | collective-permute-start | bytes 196616 | tf_op jit(solution)/shard_map/ppermute | solution.py:20
  9.0 5.4 %collective-permute-start.5 = (bf16[16,2048]{1,0:T(8,128)(2,1)S(1)}, bf16[16,2048]{1,0:T(8,128)(2,1)S(1)}, u32[]{:S(2)}, u32[]{:S(2)}) collective-permute-start(bf16[16,2048]{1,0:T(8,128)(2,1)S(1)} %collective-permute-done.1.refs_2_), channel_id=1, source_target_pairs={{0,1},{1,0},{2,3},{3,2},{4,5},{5,4},{6,7},{7,6},{8,9},{9,8},{10,11... | collective-permute-start | bytes 196616 | tf_op jit(solution)/shard_map/ppermute | solution.py:20
  16.2 9.5 %collective-permute-start.7 = (bf16[2,32,2176]{2,1,0:T(8,128)(2,1)S(1)}, bf16[2,32,2176]{2,1,0:T(8,128)(2,1)S(1)}, u32[]{:S(2)}, u32[]{:S(2)}) collective-permute-start(bf16[2,32,2176]{2,1,0:T(8,128)(2,1)S(1)} %get-tuple-element.37.refs_0_), channel_id=1, source_target_pairs={{0,8},{8,0},{16,24},{24,16},{1,9},{9,1},{17,25},{25,17},{2,10},{10... | collective-permute-start | bytes 835592 | tf_op jit(solution)/shard_map/ppermute | solution.py:20
  19.8 14.0 %collective-permute-start.9 = (bf16[2,32,2560]{2,1,0:T(8,128)(2,1)S(1)}, bf16[2,32,2560]{2,1,0:T(8,128)(2,1)S(1)}, u32[]{:S(2)}, u32[]{:S(2)}) collective-permute-start(bf16[2,32,2560]{2,1,0:T(8,128)(2,1)S(1)} %get-tuple-element.39.refs_0_), channel_id=1, source_target_pairs={{0,8},{8,0},{16,24},{24,16},{1,9},{9,1},{17,25},{25,17},{2,10},{10... | collective-permute-start | bytes 983048 | tf_op jit(solution)/shard_map/ppermute | solution.py:20
  31.7 14.9 %collective-permute-start.8 = (bf16[2,32,2560]{2,1,0:T(8,128)(2,1)S(1)}, bf16[2,32,2560]{2,1,0:T(8,128)(2,1)S(1)}, u32[]{:S(2)}, u32[]{:S(2)}) collective-permute-start(bf16[2,32,2560]{2,1,0:T(8,128)(2,1)S(1)} %get-tuple-element.43.refs_0_), channel_id=1, source_target_pairs={{0,8},{8,0},{16,24},{24,16},{1,9},{9,1},{17,25},{25,17},{2,10},{10... | collective-permute-start | bytes 983048 | tf_op jit(solution)/shard_map/ppermute | solution.py:20
  33.9 19.1 %collective-permute-start.12 = (bf16[32,2560]{1,0:T(8,128)(2,1)S(1)}, bf16[32,2560]{1,0:T(8,128)(2,1)S(1)}, u32[]{:S(2)}, u32[]{:S(2)}) collective-permute-start(bf16[32,2560]{1,0:T(8,128)(2,1)S(1)} %pair_total.4.refs_0_), channel_id=1, source_target_pairs={{0,16},{8,24},{16,0},{24,8},{1,17},{9,25},{17,1},{25,9},{2,18},{10... | collective-permute-start | bytes 491528 | tf_op jit(solution)/shard_map/ppermute | solution.py:20
  36.6 16.5 %collective-permute-start.11 = (bf16[32,2176]{1,0:T(8,128)(2,1)S(1)}, bf16[32,2176]{1,0:T(8,128)(2,1)S(1)}, u32[]{:S(2)}, u32[]{:S(2)}) collective-permute-start(bf16[32,2176]{1,0:T(8,128)(2,1)S(1)} %pair_total.3.refs_2_), channel_id=1, source_target_pairs={{0,16},{8,24},{16,0},{24,8},{1,17},{9,25},{17,1},{25,9},{2,18},{10... | collective-permute-start | bytes 417800 | tf_op jit(solution)/shard_map/ppermute | solution.py:20
  46.7 15.3 %collective-permute-start.10 = (bf16[32,2560]{1,0:T(8,128)(2,1)S(1)}, bf16[32,2560]{1,0:T(8,128)(2,1)S(1)}, u32[]{:S(2)}, u32[]{:S(2)}) collective-permute-start(bf16[32,2560]{1,0:T(8,128)(2,1)S(1)} %pair_total.5.refs_1_), channel_id=1, source_target_pairs={{0,16},{8,24},{16,0},{24,8},{1,17},{9,25},{17,1},{25,9},{2,18},{10... | collective-permute-start | bytes 491528 | tf_op jit(solution)/shard_map/ppermute | solution.py:20
  53.2 8.7 %collective-permute-start.13 = (bf16[32,2304]{1,0:T(8,128)(2,1)S(1)}, bf16[32,2304]{1,0:T(8,128)(2,1)S(1)}, u32[]{:S(2)}, u32[]{:S(2)}) collective-permute-start(bf16[32,2304]{1,0:T(8,128)(2,1)S(1)} %get-tuple-element.46.refs_1_.refs_0_), channel_id=1, source_target_pairs={{0,8},{8,0},{16,24},{24,16},{1,9},{9,1},{17,25},{25,17},{2,10},{10... | collective-permute-start | bytes 442376 | tf_op jit(solution)/shard_map/ppermute | solution.py:20
  54.3 8.3 %collective-permute-start.17 = (bf16[32,2304]{1,0:T(8,128)(2,1)S(1)}, bf16[32,2304]{1,0:T(8,128)(2,1)S(1)}, u32[]{:S(2)}, u32[]{:S(2)}) collective-permute-start(bf16[32,2304]{1,0:T(8,128)(2,1)S(1)} %get-tuple-element.46.refs_1_.refs_0_), channel_id=1, source_target_pairs={{0,16},{8,24},{16,0},{24,8},{1,17},{9,25},{17,1},{25,9},{2,18},{10... | collective-permute-start | bytes 442376 | tf_op jit(solution)/shard_map/ppermute | solution.py:20
  62.7 8.3 %collective-permute-start.18 = (bf16[32,2304]{1,0:T(8,128)(2,1)S(1)}, bf16[32,2304]{1,0:T(8,128)(2,1)S(1)}, u32[]{:S(2)}, u32[]{:S(2)}) collective-permute-start(bf16[32,2304]{1,0:T(8,128)(2,1)S(1)} %copy.15), channel_id=1, source_target_pairs={{0,8},{8,0},{16,24},{24,16},{1,9},{9,1},{17,25},{25,17},{2,10},{10... | collective-permute-start | bytes 442376 | tf_op jit(solution)/shard_map/ppermute | solution.py:20
  62.7 6.0 %collective-permute-start.15 = (bf16[32,1280]{1,0:T(8,128)(2,1)S(1)}, bf16[32,1280]{1,0:T(8,128)(2,1)S(1)}, u32[]{:S(2)}, u32[]{:S(2)}) collective-permute-start(bf16[32,1280]{1,0:T(8,128)(2,1)S(1)} %get-tuple-element.47.refs_0_), channel_id=1, source_target_pairs={{0,16},{8,24},{16,0},{24,8},{1,17},{9,25},{17,1},{25,9},{2,18},{10... | collective-permute-start | bytes 245768 | tf_op jit(solution)/shard_map/ppermute | solution.py:20
  66.2 6.4 %collective-permute-start.14 = (bf16[32,1280]{1,0:T(8,128)(2,1)S(1)}, bf16[32,1280]{1,0:T(8,128)(2,1)S(1)}, u32[]{:S(2)}, u32[]{:S(2)}) collective-permute-start(bf16[32,1280]{1,0:T(8,128)(2,1)S(1)} %get-tuple-element.47.refs_0_), channel_id=1, source_target_pairs={{0,8},{8,0},{16,24},{24,16},{1,9},{9,1},{17,25},{25,17},{2,10},{10... | collective-permute-start | bytes 245768 | tf_op jit(solution)/shard_map/ppermute | solution.py:20
  84.1 5.2 %collective-permute-start.26 = (bf16[128,256]{1,0:T(8,128)(2,1)S(1)}, bf16[128,256]{1,0:T(8,128)(2,1)S(1)}, u32[]{:S(2)}, u32[]{:S(2)}) collective-permute-start(bf16[128,256]{1,0:T(8,128)(2,1)S(1)} %add_convert_fusion.own_ref), channel_id=1, source_target_pairs={{0,6},{1,7},{2,4},{3,5},{4,2},{5,3},{6,0},{7,1},{8,14},{9,15},{10,... | collective-permute-start | bytes 196616 | tf_op jit(solution)/shard_map/ppermute | solution.py:20
  84.5 6.3 %collective-permute-start.25 = (bf16[128,256]{1,0:T(8,128)(2,1)S(1)}, bf16[128,256]{1,0:T(8,128)(2,1)S(1)}, u32[]{:S(2)}, u32[]{:S(2)}) collective-permute-start(bf16[128,256]{1,0:T(8,128)(2,1)S(1)} %add_convert_fusion.own_ref), channel_id=1, source_target_pairs={{0,24},{8,16},{16,8},{24,0},{1,25},{9,17},{17,9},{25,1},{2,26},{10... | collective-permute-start | bytes 196616 | tf_op jit(solution)/shard_map/ppermute | solution.py:20
  86.7 5.9 %collective-permute-start.24 = (bf16[128,256]{1,0:T(8,128)(2,1)S(1)}, bf16[128,256]{1,0:T(8,128)(2,1)S(1)}, u32[]{:S(2)}, u32[]{:S(2)}) collective-permute-start(bf16[128,256]{1,0:T(8,128)(2,1)S(1)} %add_convert_fusion.own_ref), channel_id=1, source_target_pairs={{0,16},{8,24},{16,0},{24,8},{1,17},{9,25},{17,1},{25,9},{2,18},{10... | collective-permute-start | bytes 196616 | tf_op jit(solution)/shard_map/ppermute | solution.py:20
  92.7 5.7 %collective-permute-start.32 = (bf16[4,128,256]{2,1,0:T(8,128)(2,1)S(1)}, bf16[4,128,256]{2,1,0:T(8,128)(2,1)S(1)}, u32[]{:S(2)}, u32[]{:S(2)}) collective-permute-start(bf16[4,128,256]{2,1,0:T(8,128)(2,1)S(1)} %stack.2.refs_0_), channel_id=1, source_target_pairs={{0,1},{1,0},{2,3},{3,2},{4,5},{5,4},{6,7},{7,6},{8,9},{9,8},{10,11... | collective-permute-start | bytes 786440 | tf_op jit(solution)/shard_map/ppermute | solution.py:20
  92.7 12.2 %collective-permute-start.28 = (bf16[4,128,256]{2,1,0:T(8,128)(2,1)S(1)}, bf16[4,128,256]{2,1,0:T(8,128)(2,1)S(1)}, u32[]{:S(2)}, u32[]{:S(2)}) collective-permute-start(bf16[4,128,256]{2,1,0:T(8,128)(2,1)S(1)} %stack.2.refs_0_), channel_id=1, source_target_pairs={{0,4},{1,5},{2,6},{3,7},{4,0},{5,1},{6,2},{7,3},{8,12},{9,13},{10,... | collective-permute-start | bytes 786440 | tf_op jit(solution)/shard_map/ppermute | solution.py:20
  94.3 10.6 %collective-permute-start.27 = (bf16[4,128,256]{2,1,0:T(8,128)(2,1)S(1)}, bf16[4,128,256]{2,1,0:T(8,128)(2,1)S(1)}, u32[]{:S(2)}, u32[]{:S(2)}) collective-permute-start(bf16[4,128,256]{2,1,0:T(8,128)(2,1)S(1)} %stack.2.refs_0_), channel_id=1, source_target_pairs={{0,2},{1,3},{2,0},{3,1},{4,6},{5,7},{6,4},{7,5},{8,10},{9,11},{10,... | collective-permute-start | bytes 786440 | tf_op jit(solution)/shard_map/ppermute | solution.py:20
  95.8 6.9 %collective-permute-start.31 = (bf16[128,256]{1,0:T(8,128)(2,1)S(1)}, bf16[128,256]{1,0:T(8,128)(2,1)S(1)}, u32[]{:S(2)}, u32[]{:S(2)}) collective-permute-start(bf16[128,256]{1,0:T(8,128)(2,1)S(1)} %collective-permute-done.26.refs_4_), channel_id=1, source_target_pairs={{0,24},{8,16},{16,8},{24,0},{1,25},{9,17},{17,9},{25,1},{2,26},{10... | collective-permute-start | bytes 196616 | tf_op jit(solution)/shard_map/ppermute | solution.py:20
  97.6 7.3 %collective-permute-start.30 = (bf16[128,256]{1,0:T(8,128)(2,1)S(1)}, bf16[128,256]{1,0:T(8,128)(2,1)S(1)}, u32[]{:S(2)}, u32[]{:S(2)}) collective-permute-start(bf16[128,256]{1,0:T(8,128)(2,1)S(1)} %collective-permute-done.26.refs_4_), channel_id=1, source_target_pairs={{0,16},{8,24},{16,0},{24,8},{1,17},{9,25},{17,1},{25,9},{2,18},{10... | collective-permute-start | bytes 196616 | tf_op jit(solution)/shard_map/ppermute | solution.py:20
  98.4 6.6 %collective-permute-start.29 = (bf16[128,256]{1,0:T(8,128)(2,1)S(1)}, bf16[128,256]{1,0:T(8,128)(2,1)S(1)}, u32[]{:S(2)}, u32[]{:S(2)}) collective-permute-start(bf16[128,256]{1,0:T(8,128)(2,1)S(1)} %collective-permute-done.26.refs_4_), channel_id=1, source_target_pairs={{0,8},{8,0},{16,24},{24,16},{1,9},{9,1},{17,25},{25,17},{2,10},{10... | collective-permute-start | bytes 196616 | tf_op jit(solution)/shard_map/ppermute | solution.py:20
  (12 other events, 70.6 us)

commit v6 on v5

--- a/solution.py
+++ b/solution.py
@@ -323,7 +323,6 @@
         (), "fetch_first",
     )
     relayed = copy_after(near[1], (gain,))
-    gate_1, up_1 = fetch([part(gate_weight, 1), part(up_weight, 1)], (relayed,), "fetch_gate_up")
     far = [swap(piece, "hid", n_hid, 1) for piece in [near[0], relayed, *near[2:]]]
     masks = [0] + chip_masks + [1] + [mask + 1 for mask in chip_masks]
     lhs, x_cols, squares = run(
@@ -333,9 +332,8 @@
             jax.ShapeDtypeStruct((ntok, panel), F32),
             jax.ShapeDtypeStruct((ntok, 1), F32),
         ),
-        [own_x, *near[1:], *far, gain, gate_1],
+        [own_x, *near[1:], *far, gain],
         4 * ntok * block, 4 * ntok * block,
-        in_specs=[WHOLE] * (n_hid + 1) + [ANYWHERE],
         out_specs=(WHOLE, WHOLE, WHOLE),
         scratch_shapes=[pltpu.VMEM((ntok, block), BF16)],
     )
@@ -343,7 +341,8 @@
     widths = [ends[k + 1] - ends[k] for k in range(3)]
     send_0, keep_0 = gate_up(lhs, gate_0, up_0, squares, n_tok)
     got_0 = swap(send_0, "tok", n_tok, 1)
-    send_1, keep_1 = gate_up(lhs, gate_1, up_1, None, n_tok, (send_0,))
+    gate_1, up_1 = fetch([part(gate_weight, 1), part(up_weight, 1)], (send_0,), "fetch_gate_up")
+    send_1, keep_1 = gate_up(lhs, gate_1, up_1, None, n_tok)
     got_1 = swap(send_1, "tok", n_tok, 1)
     sum_0 = pair_total(keep_0, got_0, 2 * widths[0], (send_1,))
     over_0 = swap(sum_0, "tok", n_tok, 2)
@@ -352,15 +351,15 @@
     got_2 = swap(send_2, "tok", n_tok, 1)
     sum_1 = pair_total(keep_1, got_1, 2 * widths[1], (send_2,))
     over_1 = swap(sum_1, "tok", n_tok, 2)
-    sum_2 = pair_total(keep_2, got_2, 2 * widths[2], (sum_1,))
+    down_b, = fetch([(down_weight, ends[2], widths[2], 0, block)], (sum_1,), "fetch_down")
+    sum_2 = pair_total(keep_2, got_2, 2 * widths[2], (down_b,))
     over_2 = swap(sum_2, "tok", n_tok, 2)
     down_a, = fetch([(down_weight, 0, ends[2], 0, block)], (sum_2,), "fetch_down")
 
     a_own, scale = hidden_rows([(keep_0, got_0, over_0), (keep_1, got_1, over_1)], widths[:2], None, (down_a,))
     a_two = swap(a_own, "tok", n_tok, 2)
     a_one = swap(a_own, "tok", n_tok, 1)
-    down_b, = fetch([(down_weight, ends[2], widths[2], 0, block)], (a_own,), "fetch_down")
-    b_own, _ = hidden_rows([(keep_2, got_2, over_2)], widths[2:], scale, (down_b, a_one))
+    b_own, _ = hidden_rows([(keep_2, got_2, over_2)], widths[2:], scale, ())
     b_two = swap(b_own, "tok", n_tok, 2)
     b_one = swap(b_own, "tok", n_tok, 1)
     a_three = swap(copy_after(a_two, (b_own,)), "tok", n_tok, 1)
@@ -380,7 +379,7 @@
         [mine, other], mine.size, 8 * mine.size,
         out_specs=[WHOLE] * len(here),
     )
-    for mask, value in zip(chip_masks, sends):
+    for mask, value in reversed(list(zip(chip_masks, sends))):
         summed = summed + swap(value, "hid", n_hid, mask).astype(F32)
     resid_cols = (x_cols + summed).astype(BF16)
 

time: 109 us -> 106 us (0.972)
  waiting for transfers between devices: 34.8 us -> 32.3 us
    ppermute x35, waiting for transfers between devices: 34.8 us -> 32.3 us  [swap(): return lax.ppermute(value, axis, [(i, i ^ mask) for i in range(size)])]
  transfers between devices with their start and end apart: 35 -> 35, of which waited for: 16 -> 19; matrix products, arithmetic and copies ran while one was open for 0% -> 0% of each run, Pallas kernels for 27% -> 28%
where the time goes in v6:
time: 106 us
  starting transfers between devices  39.1 us (37%)
  Pallas kernels  33.6 us (32%)
  waiting for transfers between devices  32.3 us (30%)
    ppermute x35, starting transfers between devices, swap(): return lax.ppermute(value, axis, [(i, i ^ mask) for i in range(size)])  39.1 us
    pallas_call x25, Pallas kernels, run(): pl.pallas_call(body, out_shape=out_shape, in_specs=[WHOLE] * len(operands...  33.6 us
    ppermute x35, waiting for transfers between devices, swap(): return lax.ppermute(value, axis, [(i, i ^ mask) for i in range(size)])  32.3 us
  transfers between devices with their start and end apart: 35, of which 19 were waited for; matrix products, arithmetic and copies ran while one was open for 0% of the time, Pallas kernels for 28%

profile of v6, /device:TPU:0, one launch (start us, length us, event | category | flops | bytes accessed | tf_op | source)
XLA Modules:
  0.0 105.8 jit_solution(6897772718262713314)
XLA Ops:
  0.6 3.0 %collective-permute-start.1 = (bf16[16,2048]{1,0:T(8,128)(2,1)}, bf16[16,2048]{1,0:T(8,128)(2,1)S(1)}, u32[]{:S(2)}, u32[]{:S(2)}) collective-permute-start(bf16[16,2048]{1,0:T(8,128)(2,1)} %refs_2_.1), channel_id=1, source_target_pairs={{0,4},{1,5},{2,6},{3,7},{4,0},{5,1},{6,2},{7,3},{8,12},{9,13},{10,... | collective-permute-start | bytes 196616 | tf_op jit(solution)/shard_map/ppermute | solution.py:20
  5.2 3.7 %fetch_first.1 = (bf16[2048,1024]{1,0:T(8,128)(2,1)S(1)}, bf16[2048,1024]{1,0:T(8,128)(2,1)S(1)}, bf16[16,2048]{1,0:T(8,128)(2,1)S(1)}, f32[1,2048]{1,0:T(1,128)S(1)}) custom-call(bf16[2048,3584]{1,0:T(8,128)(2,1)} %refs_0_.7, bf16[2048,3584]{1,0:T(8,128)(2,1)} %refs_1_.5, bf16[16,2048]{1,0:T(8,128)(2,1)} %refs_2_.1, f32[1,2048]{1,0:T(1,128)} %bitcast.22), custom_call_target="tpu_custom_call" | custom-call | tf_op jit(solution)/shard_map/fetch_first/pallas_call | solution.py:24
  12.7 2.1 %collective-permute-start.7 = (bf16[2,32,2176]{2,1,0:T(8,128)(2,1)S(1)}, bf16[2,32,2176]{2,1,0:T(8,128)(2,1)S(1)}, u32[]{:S(2)}, u32[]{:S(2)}) collective-permute-start(bf16[2,32,2176]{2,1,0:T(8,128)(2,1)S(1)} %get-tuple-element.36.refs_2_), channel_id=1, source_target_pairs={{0,8},{8,0},{16,24},{24,16},{1,9},{9,1},{17,25},{25,17},{2,10},{10... | collective-permute-start | bytes 835592 | tf_op jit(solution)/shard_map/ppermute | solution.py:20
  14.8 4.3 %fetch_gate_up.2 = (bf16[2048,1280]{1,0:T(8,128)(2,1)S(1)}, bf16[2048,1280]{1,0:T(8,128)(2,1)S(1)}) custom-call(bf16[2048,3584]{1,0:T(8,128)(2,1)} %refs_0_.7, bf16[2048,3584]{1,0:T(8,128)(2,1)} %refs_1_.5, bf16[2,32,2176]{2,1,0:T(8,128)(2,1)S(1)} %get-tuple-element.36.refs_2_), custom_call_target="tpu_custom_call" | custom-call | tf_op jit(solution)/shard_map/fetch_gate_up/pallas_call | solution.py:24
  22.1 4.3 %fetch_gate_up.3 = (bf16[2048,1280]{1,0:T(8,128)(2,1)S(1)}, bf16[2048,1280]{1,0:T(8,128)(2,1)S(1)}) custom-call(bf16[2048,3584]{1,0:T(8,128)(2,1)} %refs_0_.7, bf16[2048,3584]{1,0:T(8,128)(2,1)} %refs_1_.5, bf16[32,2176]{1,0:T(8,128)(2,1)S(1)} %pair_total.3.refs_2_), custom_call_target="tpu_custom_call" | custom-call | tf_op jit(solution)/shard_map/fetch_gate_up/pallas_call | solution.py:24
  30.5 2.7 %collective-permute-start.12 = (bf16[32,2560]{1,0:T(8,128)(2,1)S(1)}, bf16[32,2560]{1,0:T(8,128)(2,1)S(1)}, u32[]{:S(2)}, u32[]{:S(2)}) collective-permute-start(bf16[32,2560]{1,0:T(8,128)(2,1)S(1)} %pair_total.4.refs_1_), channel_id=1, source_target_pairs={{0,16},{8,24},{16,0},{24,8},{1,17},{9,25},{17,1},{25,9},{2,18},{10... | collective-permute-start | bytes 491528 | tf_op jit(solution)/shard_map/ppermute | solution.py:20
  33.5 2.5 %fetch_down.2.refs_0_.refs_4_ = bf16[1280,2048]{1,0:T(8,128)(2,1)S(1)} custom-call(bf16[3584,2048]{1,0:T(8,128)(2,1)} %refs_0_.9, bf16[32,2560]{1,0:T(8,128)(2,1)S(1)} %pair_total.4.refs_1_), custom_call_target="tpu_custom_call" | custom-call | tf_op jit(solution)/shard_map/fetch_down/pallas_call | solution.py:24
  36.0 7.8 %collective-permute-done.8.got_ref.refs_1_ = bf16[2,32,2560]{2,1,0:T(8,128)(2,1)S(1)} collective-permute-done((bf16[2,32,2560]{2,1,0:T(8,128)(2,1)S(1)}, bf16[2,32,2560]{2,1,0:T(8,128)(2,1)S(1)}, u32[]{:S(2)}, u32[]{:S(2)}) %collective-permute-start.8) | collective-permute-done | bytes 327712 | tf_op jit(solution)/shard_map/ppermute | solution.py:20
  44.3 3.8 %fetch_down.3.refs_6_.refs_4_ = bf16[2304,2048]{1,0:T(8,128)(2,1)S(1)} custom-call(bf16[3584,2048]{1,0:T(8,128)(2,1)} %refs_0_.9, bf16[32,2560]{1,0:T(8,128)(2,1)S(1)} %pair_total.5.refs_1_), custom_call_target="tpu_custom_call" | custom-call | tf_op jit(solution)/shard_map/fetch_down/pallas_call | solution.py:24
  48.1 1.9 %collective-permute-done.11.refs_2_ = bf16[32,2176]{1,0:T(8,128)(2,1)S(1)} collective-permute-done((bf16[32,2176]{1,0:T(8,128)(2,1)S(1)}, bf16[32,2176]{1,0:T(8,128)(2,1)S(1)}, u32[]{:S(2)}, u32[]{:S(2)}) %collective-permute-start.11) | collective-permute-done | bytes 139296 | tf_op jit(solution)/shard_map/ppermute | solution.py:20
  50.9 3.3 %collective-permute-start.16 = (bf16[32,2304]{1,0:T(8,128)(2,1)S(1)}, bf16[32,2304]{1,0:T(8,128)(2,1)S(1)}, u32[]{:S(2)}, u32[]{:S(2)}) collective-permute-start(bf16[32,2304]{1,0:T(8,128)(2,1)S(1)} %get-tuple-element.47.refs_0_), channel_id=1, source_target_pairs={{0,8},{8,0},{16,24},{24,16},{1,9},{9,1},{17,25},{25,17},{2,10},{10... | collective-permute-start | bytes 442376 | tf_op jit(solution)/shard_map/ppermute | solution.py:20
  55.7 4.1 %collective-permute-done.17.value_ref.refs_2_ = bf16[32,2304]{1,0:T(8,128)(2,1)S(1)} collective-permute-done((bf16[32,2304]{1,0:T(8,128)(2,1)S(1)}, bf16[32,2304]{1,0:T(8,128)(2,1)S(1)}, u32[]{:S(2)}, u32[]{:S(2)}) %collective-permute-start.17) | collective-permute-done | bytes 147488 | tf_op jit(solution)/shard_map/ppermute | solution.py:20
  59.9 3.0 %collective-permute-start.14 = (bf16[32,1280]{1,0:T(8,128)(2,1)S(1)}, bf16[32,1280]{1,0:T(8,128)(2,1)S(1)}, u32[]{:S(2)}, u32[]{:S(2)}) collective-permute-start(bf16[32,1280]{1,0:T(8,128)(2,1)S(1)} %get-tuple-element.46.refs_0_), channel_id=1, source_target_pairs={{0,16},{8,24},{16,0},{24,8},{1,17},{9,25},{17,1},{25,9},{2,18},{10... | collective-permute-start | bytes 245768 | tf_op jit(solution)/shard_map/ppermute | solution.py:20
  63.0 3.2 %collective-permute-done.14.refs_2_ = bf16[32,1280]{1,0:T(8,128)(2,1)S(1)} collective-permute-done((bf16[32,1280]{1,0:T(8,128)(2,1)S(1)}, bf16[32,1280]{1,0:T(8,128)(2,1)S(1)}, u32[]{:S(2)}, u32[]{:S(2)}) %collective-permute-start.14) | collective-permute-done | bytes 81952 | tf_op jit(solution)/shard_map/ppermute | solution.py:20
  66.2 2.5 %collective-permute-start.15 = (bf16[32,1280]{1,0:T(8,128)(2,1)S(1)}, bf16[32,1280]{1,0:T(8,128)(2,1)S(1)}, u32[]{:S(2)}, u32[]{:S(2)}) collective-permute-start(bf16[32,1280]{1,0:T(8,128)(2,1)S(1)} %collective-permute-done.14.refs_2_), channel_id=1, source_target_pairs={{0,8},{8,0},{16,24},{24,16},{1,9},{9,1},{17,25},{25,17},{2,10},{10... | collective-permute-start | bytes 245768 | tf_op jit(solution)/shard_map/ppermute | solution.py:20
  73.3 2.5 %collective-permute-start.20 = (bf16[128,256]{1,0:T(8,128)(2,1)S(1)}, bf16[128,256]{1,0:T(8,128)(2,1)S(1)}, u32[]{:S(2)}, u32[]{:S(2)}) collective-permute-start(bf16[128,256]{1,0:T(8,128)(2,1)S(1)} %get-tuple-element.49), channel_id=1, source_target_pairs={{0,6},{1,7},{2,4},{3,5},{4,2},{5,3},{6,0},{7,1},{8,14},{9,15},{10,... | collective-permute-start | bytes 196616 | tf_op jit(solution)/shard_map/ppermute | solution.py:20
  82.2 2.2 %collective-permute-start.25 = (bf16[128,256]{1,0:T(8,128)(2,1)S(1)}, bf16[128,256]{1,0:T(8,128)(2,1)S(1)}, u32[]{:S(2)}, u32[]{:S(2)}) collective-permute-start(bf16[128,256]{1,0:T(8,128)(2,1)S(1)} %add_convert_fusion.own_ref), channel_id=1, source_target_pairs={{0,24},{8,16},{16,8},{24,0},{1,25},{9,17},{17,9},{25,1},{2,26},{10... | collective-permute-start | bytes 196616 | tf_op jit(solution)/shard_map/ppermute | solution.py:20
  86.6 2.1 %collective-permute-done.25 = bf16[128,256]{1,0:T(8,128)(2,1)S(1)} collective-permute-done((bf16[128,256]{1,0:T(8,128)(2,1)S(1)}, bf16[128,256]{1,0:T(8,128)(2,1)S(1)}, u32[]{:S(2)}, u32[]{:S(2)}) %collective-permute-start.25) | collective-permute-done | bytes 65568 | tf_op jit(solution)/shard_map/ppermute | solution.py:20
  90.5 1.9 %collective-permute-start.28 = (bf16[4,128,256]{2,1,0:T(8,128)(2,1)S(1)}, bf16[4,128,256]{2,1,0:T(8,128)(2,1)S(1)}, u32[]{:S(2)}, u32[]{:S(2)}) collective-permute-start(bf16[4,128,256]{2,1,0:T(8,128)(2,1)S(1)} %stack.2.refs_0_), channel_id=1, source_target_pairs={{0,4},{1,5},{2,6},{3,7},{4,0},{5,1},{6,2},{7,3},{8,12},{9,13},{10,... | collective-permute-start | bytes 786440 | tf_op jit(solution)/shard_map/ppermute | solution.py:20
  92.6 2.0 %collective-permute-start.31 = (bf16[128,256]{1,0:T(8,128)(2,1)S(1)}, bf16[128,256]{1,0:T(8,128)(2,1)S(1)}, u32[]{:S(2)}, u32[]{:S(2)}) collective-permute-start(bf16[128,256]{1,0:T(8,128)(2,1)S(1)} %collective-permute-done.26.refs_4_), channel_id=1, source_target_pairs={{0,24},{8,16},{16,8},{24,0},{1,25},{9,17},{17,9},{25,1},{2,26},{10... | collective-permute-start | bytes 196616 | tf_op jit(solution)/shard_map/ppermute | solution.py:20
  95.1 1.9 %collective-permute-start.29 = (bf16[128,256]{1,0:T(8,128)(2,1)S(1)}, bf16[128,256]{1,0:T(8,128)(2,1)S(1)}, u32[]{:S(2)}, u32[]{:S(2)}) collective-permute-start(bf16[128,256]{1,0:T(8,128)(2,1)S(1)} %collective-permute-done.26.refs_4_), channel_id=1, source_target_pairs={{0,8},{8,0},{16,24},{24,16},{1,9},{9,1},{17,25},{25,17},{2,10},{10... | collective-permute-start | bytes 196616 | tf_op jit(solution)/shard_map/ppermute | solution.py:20
  97.0 2.4 %gram.3 = (f32[256,8192]{1,0:T(8,128)}, f32[64,256]{1,0:T(8,128)}) custom-call(bf16[128,256]{1,0:T(8,128)(2,1)S(1)} %add_convert_fusion.own_ref, bf16[4,128,256]{2,1,0:T(8,128)(2,1)S(1)} %stack.2.refs_0_, bf16[4,128,256]{2,1,0:T(8,128)(2,1)S(1)} %collective-permute-done.32.refs_1_, bf16[1,128,256]{2,1,0:T(8,128)(2,1)S(1)} %bitcast.13, ...), custom_call_target="tpu_custom_call" | custom-call | flops 167772160 | bytes 2621440 | tf_op jit(solution)/shard_map/gram/pallas_call | solution.py:24
  99.5 2.2 %collective-permute-done.30 = bf16[128,256]{1,0:T(8,128)(2,1)S(1)} collective-permute-done((bf16[128,256]{1,0:T(8,128)(2,1)S(1)}, bf16[128,256]{1,0:T(8,128)(2,1)S(1)}, u32[]{:S(2)}, u32[]{:S(2)}) %collective-permute-start.30) | collective-permute-done | bytes 65568 | tf_op jit(solution)/shard_map/ppermute | solution.py:20
  101.8 1.9 %gram.4.refs_1_ = f32[256,8192]{1,0:T(8,128)} custom-call(bf16[128,256]{1,0:T(8,128)(2,1)S(1)} %add_convert_fusion.own_ref, bf16[11,128,256]{2,1,0:T(8,128)(2,1)S(1)} %stack.3.refs_0_, f32[256,8192]{1,0:T(8,128)} %get-tuple-element.52.refs_5_.refs_1_), custom_call_target="tpu_custom_call", output_to_operand_aliasing={{}: (2, {})} | custom-call | flops 184549376 | bytes 2883584 | tf_op jit(solution)/shard_map/gram/pallas_call | solution.py:24
  (74 shorter events, 33.6 us)
Async XLA Ops:
  0.6 8.3 %collective-permute-start.1 = (bf16[16,2048]{1,0:T(8,128)(2,1)}, bf16[16,2048]{1,0:T(8,128)(2,1)S(1)}, u32[]{:S(2)}, u32[]{:S(2)}) collective-permute-start(bf16[16,2048]{1,0:T(8,128)(2,1)} %refs_2_.1), channel_id=1, source_target_pairs={{0,4},{1,5},{2,6},{3,7},{4,0},{5,1},{6,2},{7,3},{8,12},{9,13},{10,... | collective-permute-start | bytes 196616 | tf_op jit(solution)/shard_map/ppermute | solution.py:20
  3.7 5.9 %collective-permute-start.2 = (bf16[16,2048]{1,0:T(8,128)(2,1)}, bf16[16,2048]{1,0:T(8,128)(2,1)S(1)}, u32[]{:S(2)}, u32[]{:S(2)}) collective-permute-start(bf16[16,2048]{1,0:T(8,128)(2,1)} %refs_2_.1), channel_id=1, source_target_pairs={{0,6},{1,7},{2,4},{3,5},{4,2},{5,3},{6,0},{7,1},{8,14},{9,15},{10,... | collective-permute-start | bytes 196616 | tf_op jit(solution)/shard_map/ppermute | solution.py:20
  5.2 4.9 %collective-permute-start.3 = (bf16[16,2048]{1,0:T(8,128)(2,1)}, bf16[16,2048]{1,0:T(8,128)(2,1)S(1)}, u32[]{:S(2)}, u32[]{:S(2)}) collective-permute-start(bf16[16,2048]{1,0:T(8,128)(2,1)} %refs_2_.1), channel_id=1, source_target_pairs={{0,1},{1,0},{2,3},{3,2},{4,5},{5,4},{6,7},{7,6},{8,9},{9,8},{10,11... | collective-permute-start | bytes 196616 | tf_op jit(solution)/shard_map/ppermute | solution.py:20
  12.7 9.3 %collective-permute-start.7 = (bf16[2,32,2176]{2,1,0:T(8,128)(2,1)S(1)}, bf16[2,32,2176]{2,1,0:T(8,128)(2,1)S(1)}, u32[]{:S(2)}, u32[]{:S(2)}) collective-permute-start(bf16[2,32,2176]{2,1,0:T(8,128)(2,1)S(1)} %get-tuple-element.36.refs_2_), channel_id=1, source_target_pairs={{0,8},{8,0},{16,24},{24,16},{1,9},{9,1},{17,25},{25,17},{2,10},{10... | collective-permute-start | bytes 835592 | tf_op jit(solution)/shard_map/ppermute | solution.py:20
  20.7 9.8 %collective-permute-start.9 = (bf16[2,32,2560]{2,1,0:T(8,128)(2,1)S(1)}, bf16[2,32,2560]{2,1,0:T(8,128)(2,1)S(1)}, u32[]{:S(2)}, u32[]{:S(2)}) collective-permute-start(bf16[2,32,2560]{2,1,0:T(8,128)(2,1)S(1)} %get-tuple-element.39.refs_0_), channel_id=1, source_target_pairs={{0,8},{8,0},{16,24},{24,16},{1,9},{9,1},{17,25},{25,17},{2,10},{10... | collective-permute-start | bytes 983048 | tf_op jit(solution)/shard_map/ppermute | solution.py:20
  28.0 15.8 %collective-permute-start.8 = (bf16[2,32,2560]{2,1,0:T(8,128)(2,1)S(1)}, bf16[2,32,2560]{2,1,0:T(8,128)(2,1)S(1)}, u32[]{:S(2)}, u32[]{:S(2)}) collective-permute-start(bf16[2,32,2560]{2,1,0:T(8,128)(2,1)S(1)} %get-tuple-element.43.refs_0_), channel_id=1, source_target_pairs={{0,8},{8,0},{16,24},{24,16},{1,9},{9,1},{17,25},{25,17},{2,10},{10... | collective-permute-start | bytes 983048 | tf_op jit(solution)/shard_map/ppermute | solution.py:20
  30.5 19.5 %collective-permute-start.12 = (bf16[32,2560]{1,0:T(8,128)(2,1)S(1)}, bf16[32,2560]{1,0:T(8,128)(2,1)S(1)}, u32[]{:S(2)}, u32[]{:S(2)}) collective-permute-start(bf16[32,2560]{1,0:T(8,128)(2,1)S(1)} %pair_total.4.refs_1_), channel_id=1, source_target_pairs={{0,16},{8,24},{16,0},{24,8},{1,17},{9,25},{17,1},{25,9},{2,18},{10... | collective-permute-start | bytes 491528 | tf_op jit(solution)/shard_map/ppermute | solution.py:20
  33.2 16.8 %collective-permute-start.11 = (bf16[32,2176]{1,0:T(8,128)(2,1)S(1)}, bf16[32,2176]{1,0:T(8,128)(2,1)S(1)}, u32[]{:S(2)}, u32[]{:S(2)}) collective-permute-start(bf16[32,2176]{1,0:T(8,128)(2,1)S(1)} %pair_total.3.refs_2_), channel_id=1, source_target_pairs={{0,16},{8,24},{16,0},{24,8},{1,17},{9,25},{17,1},{25,9},{2,18},{10... | collective-permute-start | bytes 417800 | tf_op jit(solution)/shard_map/ppermute | solution.py:20
  43.9 11.2 %collective-permute-start.10 = (bf16[32,2560]{1,0:T(8,128)(2,1)S(1)}, bf16[32,2560]{1,0:T(8,128)(2,1)S(1)}, u32[]{:S(2)}, u32[]{:S(2)}) collective-permute-start(bf16[32,2560]{1,0:T(8,128)(2,1)S(1)} %pair_total.5.refs_1_), channel_id=1, source_target_pairs={{0,16},{8,24},{16,0},{24,8},{1,17},{9,25},{17,1},{25,9},{2,18},{10... | collective-permute-start | bytes 491528 | tf_op jit(solution)/shard_map/ppermute | solution.py:20
  50.2 9.6 %collective-permute-start.17 = (bf16[32,2304]{1,0:T(8,128)(2,1)S(1)}, bf16[32,2304]{1,0:T(8,128)(2,1)S(1)}, u32[]{:S(2)}, u32[]{:S(2)}) collective-permute-start(bf16[32,2304]{1,0:T(8,128)(2,1)S(1)} %get-tuple-element.47.refs_0_), channel_id=1, source_target_pairs={{0,16},{8,24},{16,0},{24,8},{1,17},{9,25},{17,1},{25,9},{2,18},{10... | collective-permute-start | bytes 442376 | tf_op jit(solution)/shard_map/ppermute | solution.py:20
  50.9 17.7 %collective-permute-start.16 = (bf16[32,2304]{1,0:T(8,128)(2,1)S(1)}, bf16[32,2304]{1,0:T(8,128)(2,1)S(1)}, u32[]{:S(2)}, u32[]{:S(2)}) collective-permute-start(bf16[32,2304]{1,0:T(8,128)(2,1)S(1)} %get-tuple-element.47.refs_0_), channel_id=1, source_target_pairs={{0,8},{8,0},{16,24},{24,16},{1,9},{9,1},{17,25},{25,17},{2,10},{10... | collective-permute-start | bytes 442376 | tf_op jit(solution)/shard_map/ppermute | solution.py:20
  59.8 8.8 %collective-permute-start.18 = (bf16[32,2304]{1,0:T(8,128)(2,1)S(1)}, bf16[32,2304]{1,0:T(8,128)(2,1)S(1)}, u32[]{:S(2)}, u32[]{:S(2)}) collective-permute-start(bf16[32,2304]{1,0:T(8,128)(2,1)S(1)} %copy.15), channel_id=1, source_target_pairs={{0,8},{8,0},{16,24},{24,16},{1,9},{9,1},{17,25},{25,17},{2,10},{10... | collective-permute-start | bytes 442376 | tf_op jit(solution)/shard_map/ppermute | solution.py:20
  59.9 6.3 %collective-permute-start.14 = (bf16[32,1280]{1,0:T(8,128)(2,1)S(1)}, bf16[32,1280]{1,0:T(8,128)(2,1)S(1)}, u32[]{:S(2)}, u32[]{:S(2)}) collective-permute-start(bf16[32,1280]{1,0:T(8,128)(2,1)S(1)} %get-tuple-element.46.refs_0_), channel_id=1, source_target_pairs={{0,16},{8,24},{16,0},{24,8},{1,17},{9,25},{17,1},{25,9},{2,18},{10... | collective-permute-start | bytes 245768 | tf_op jit(solution)/shard_map/ppermute | solution.py:20
  62.9 7.3 %collective-permute-start.13 = (bf16[32,1280]{1,0:T(8,128)(2,1)S(1)}, bf16[32,1280]{1,0:T(8,128)(2,1)S(1)}, u32[]{:S(2)}, u32[]{:S(2)}) collective-permute-start(bf16[32,1280]{1,0:T(8,128)(2,1)S(1)} %get-tuple-element.46.refs_0_), channel_id=1, source_target_pairs={{0,8},{8,0},{16,24},{24,16},{1,9},{9,1},{17,25},{25,17},{2,10},{10... | collective-permute-start | bytes 245768 | tf_op jit(solution)/shard_map/ppermute | solution.py:20
  66.2 4.9 %collective-permute-start.15 = (bf16[32,1280]{1,0:T(8,128)(2,1)S(1)}, bf16[32,1280]{1,0:T(8,128)(2,1)S(1)}, u32[]{:S(2)}, u32[]{:S(2)}) collective-permute-start(bf16[32,1280]{1,0:T(8,128)(2,1)S(1)} %collective-permute-done.14.refs_2_), channel_id=1, source_target_pairs={{0,8},{8,0},{16,24},{24,16},{1,9},{9,1},{17,25},{25,17},{2,10},{10... | collective-permute-start | bytes 245768 | tf_op jit(solution)/shard_map/ppermute | solution.py:20
  73.3 5.3 %collective-permute-start.20 = (bf16[128,256]{1,0:T(8,128)(2,1)S(1)}, bf16[128,256]{1,0:T(8,128)(2,1)S(1)}, u32[]{:S(2)}, u32[]{:S(2)}) collective-permute-start(bf16[128,256]{1,0:T(8,128)(2,1)S(1)} %get-tuple-element.49), channel_id=1, source_target_pairs={{0,6},{1,7},{2,4},{3,5},{4,2},{5,3},{6,0},{7,1},{8,14},{9,15},{10,... | collective-permute-start | bytes 196616 | tf_op jit(solution)/shard_map/ppermute | solution.py:20
  80.6 6.0 %collective-permute-start.26 = (bf16[128,256]{1,0:T(8,128)(2,1)S(1)}, bf16[128,256]{1,0:T(8,128)(2,1)S(1)}, u32[]{:S(2)}, u32[]{:S(2)}) collective-permute-start(bf16[128,256]{1,0:T(8,128)(2,1)S(1)} %add_convert_fusion.own_ref), channel_id=1, source_target_pairs={{0,6},{1,7},{2,4},{3,5},{4,2},{5,3},{6,0},{7,1},{8,14},{9,15},{10,... | collective-permute-start | bytes 196616 | tf_op jit(solution)/shard_map/ppermute | solution.py:20
  82.2 6.5 %collective-permute-start.25 = (bf16[128,256]{1,0:T(8,128)(2,1)S(1)}, bf16[128,256]{1,0:T(8,128)(2,1)S(1)}, u32[]{:S(2)}, u32[]{:S(2)}) collective-permute-start(bf16[128,256]{1,0:T(8,128)(2,1)S(1)} %add_convert_fusion.own_ref), channel_id=1, source_target_pairs={{0,24},{8,16},{16,8},{24,0},{1,25},{9,17},{17,9},{25,1},{2,26},{10... | collective-permute-start | bytes 196616 | tf_op jit(solution)/shard_map/ppermute | solution.py:20
  84.5 5.9 %collective-permute-start.24 = (bf16[128,256]{1,0:T(8,128)(2,1)S(1)}, bf16[128,256]{1,0:T(8,128)(2,1)S(1)}, u32[]{:S(2)}, u32[]{:S(2)}) collective-permute-start(bf16[128,256]{1,0:T(8,128)(2,1)S(1)} %add_convert_fusion.own_ref), channel_id=1, source_target_pairs={{0,16},{8,24},{16,0},{24,8},{1,17},{9,25},{17,1},{25,9},{2,18},{10... | collective-permute-start | bytes 196616 | tf_op jit(solution)/shard_map/ppermute | solution.py:20
  90.5 11.2 %collective-permute-start.28 = (bf16[4,128,256]{2,1,0:T(8,128)(2,1)S(1)}, bf16[4,128,256]{2,1,0:T(8,128)(2,1)S(1)}, u32[]{:S(2)}, u32[]{:S(2)}) collective-permute-start(bf16[4,128,256]{2,1,0:T(8,128)(2,1)S(1)} %stack.2.refs_0_), channel_id=1, source_target_pairs={{0,4},{1,5},{2,6},{3,7},{4,0},{5,1},{6,2},{7,3},{8,12},{9,13},{10,... | collective-permute-start | bytes 786440 | tf_op jit(solution)/shard_map/ppermute | solution.py:20
  92.4 9.3 %collective-permute-start.27 = (bf16[4,128,256]{2,1,0:T(8,128)(2,1)S(1)}, bf16[4,128,256]{2,1,0:T(8,128)(2,1)S(1)}, u32[]{:S(2)}, u32[]{:S(2)}) collective-permute-start(bf16[4,128,256]{2,1,0:T(8,128)(2,1)S(1)} %stack.2.refs_0_), channel_id=1, source_target_pairs={{0,2},{1,3},{2,0},{3,1},{4,6},{5,7},{6,4},{7,5},{8,10},{9,11},{10,... | collective-permute-start | bytes 786440 | tf_op jit(solution)/shard_map/ppermute | solution.py:20
  92.6 6.9 %collective-permute-start.31 = (bf16[128,256]{1,0:T(8,128)(2,1)S(1)}, bf16[128,256]{1,0:T(8,128)(2,1)S(1)}, u32[]{:S(2)}, u32[]{:S(2)}) collective-permute-start(bf16[128,256]{1,0:T(8,128)(2,1)S(1)} %collective-permute-done.26.refs_4_), channel_id=1, source_target_pairs={{0,24},{8,16},{16,8},{24,0},{1,25},{9,17},{17,9},{25,1},{2,26},{10... | collective-permute-start | bytes 196616 | tf_op jit(solution)/shard_map/ppermute | solution.py:20
  94.6 7.1 %collective-permute-start.30 = (bf16[128,256]{1,0:T(8,128)(2,1)S(1)}, bf16[128,256]{1,0:T(8,128)(2,1)S(1)}, u32[]{:S(2)}, u32[]{:S(2)}) collective-permute-start(bf16[128,256]{1,0:T(8,128)(2,1)S(1)} %collective-permute-done.26.refs_4_), channel_id=1, source_target_pairs={{0,16},{8,24},{16,0},{24,8},{1,17},{9,25},{17,1},{25,9},{2,18},{10... | collective-permute-start | bytes 196616 | tf_op jit(solution)/shard_map/ppermute | solution.py:20
  95.1 6.6 %collective-permute-start.29 = (bf16[128,256]{1,0:T(8,128)(2,1)S(1)}, bf16[128,256]{1,0:T(8,128)(2,1)S(1)}, u32[]{:S(2)}, u32[]{:S(2)}) collective-permute-start(bf16[128,256]{1,0:T(8,128)(2,1)S(1)} %collective-permute-done.26.refs_4_), channel_id=1, source_target_pairs={{0,8},{8,0},{16,24},{24,16},{1,9},{9,1},{17,25},{25,17},{2,10},{10... | collective-permute-start | bytes 196616 | tf_op jit(solution)/shard_map/ppermute | solution.py:20
  (12 other events, 59.2 us)

commit v7 on v6

--- a/solution.py
+++ b/solution.py
@@ -359,10 +359,10 @@
     a_own, scale = hidden_rows([(keep_0, got_0, over_0), (keep_1, got_1, over_1)], widths[:2], None, (down_a,))
     a_two = swap(a_own, "tok", n_tok, 2)
     a_one = swap(a_own, "tok", n_tok, 1)
-    b_own, _ = hidden_rows([(keep_2, got_2, over_2)], widths[2:], scale, ())
+    b_own, _ = hidden_rows([(keep_2, got_2, over_2)], widths[2:], scale, (a_one,))
     b_two = swap(b_own, "tok", n_tok, 2)
     b_one = swap(b_own, "tok", n_tok, 1)
-    a_three = swap(copy_after(a_two, (b_own,)), "tok", n_tok, 1)
+    a_three = swap(copy_after(a_two, (b_two, b_one)), "tok", n_tok, 1)
     b_three = swap(b_two, "tok", n_tok, 1)
     hidden_a = [a_own, a_one, a_two, a_three]
     hidden_b = [b_own, b_one, b_two, b_three]
@@ -385,9 +385,9 @@
 
     column = [swap(resid_cols, "tok", n_tok, d) for d in range(1, n_tok)]
     across = swap(resid_cols, "hid", n_hid, 6)
-    line = stack_after([resid_cols, *column], (across,))
+    across_line = [swap(across, "tok", n_tok, d) for d in range(1, n_tok)]
+    line = stack_after([resid_cols, *column], (across_line[0],))
     beside = [swap(line, "hid", n_hid, mask) for mask in (2, 4)]
-    across_line = [swap(across, "tok", n_tok, d) for d in range(1, n_tok)]
     line_far = swap(line, "hid", n_hid, 1)
     across_far = swap(across, "hid", n_hid, 1)
     line_slots = [[(d, mask) for d in range(n_tok)] for mask in range(n_hid)]

time: 106 us -> 109 us (1.028)
  waiting for transfers between devices: 32.3 us -> 35.7 us
    ppermute x35, waiting for transfers between devices: 32.3 us -> 35.7 us  [swap(): return lax.ppermute(value, axis, [(i, i ^ mask) for i in range(size)])]
  transfers between devices with their start and end apart: 35 -> 35, of which waited for: 19 -> 23; matrix products, arithmetic and copies ran while one was open for 0% -> 0% of each run, Pallas kernels for 28% -> 27%
where the time goes in v7:
time: 109 us
  starting transfers between devices  38.4 us (35%)
  waiting for transfers between devices  35.7 us (33%)
  Pallas kernels  33.6 us (31%)
    ppermute x35, starting transfers between devices, swap(): return lax.ppermute(value, axis, [(i, i ^ mask) for i in range(size)])  38.4 us
    ppermute x35, waiting for transfers between devices, swap(): return lax.ppermute(value, axis, [(i, i ^ mask) for i in range(size)])  35.7 us
    pallas_call x25, Pallas kernels, run(): pl.pallas_call(body, out_shape=out_shape, in_specs=[WHOLE] * len(operands...  33.6 us
  transfers between devices with their start and end apart: 35, of which 23 were waited for; matrix products, arithmetic and copies ran while one was open for 0% of the time, Pallas kernels for 27%

profile of v7, /device:TPU:0, one launch (start us, length us, event | category | flops | bytes accessed | tf_op | source)
XLA Modules:
  0.0 108.5 jit_solution(16322462408934754985)
XLA Ops:
  0.6 3.0 %collective-permute-start.1 = (bf16[16,2048]{1,0:T(8,128)(2,1)}, bf16[16,2048]{1,0:T(8,128)(2,1)S(1)}, u32[]{:S(2)}, u32[]{:S(2)}) collective-permute-start(bf16[16,2048]{1,0:T(8,128)(2,1)} %refs_2_.1), channel_id=1, source_target_pairs={{0,4},{1,5},{2,6},{3,7},{4,0},{5,1},{6,2},{7,3},{8,12},{9,13},{10,... | collective-permute-start | bytes 196616 | tf_op jit(solution)/shard_map/ppermute | solution.py:20
  5.2 3.7 %fetch_first.1 = (bf16[2048,1024]{1,0:T(8,128)(2,1)S(1)}, bf16[2048,1024]{1,0:T(8,128)(2,1)S(1)}, bf16[16,2048]{1,0:T(8,128)(2,1)S(1)}, f32[1,2048]{1,0:T(1,128)S(1)}) custom-call(bf16[2048,3584]{1,0:T(8,128)(2,1)} %refs_0_.7, bf16[2048,3584]{1,0:T(8,128)(2,1)} %refs_1_.5, bf16[16,2048]{1,0:T(8,128)(2,1)} %refs_2_.1, f32[1,2048]{1,0:T(1,128)} %bitcast.22), custom_call_target="tpu_custom_call" | custom-call | tf_op jit(solution)/shard_map/fetch_first/pallas_call | solution.py:24
  12.7 2.1 %collective-permute-start.7 = (bf16[2,32,2176]{2,1,0:T(8,128)(2,1)S(1)}, bf16[2,32,2176]{2,1,0:T(8,128)(2,1)S(1)}, u32[]{:S(2)}, u32[]{:S(2)}) collective-permute-start(bf16[2,32,2176]{2,1,0:T(8,128)(2,1)S(1)} %get-tuple-element.36.refs_2_), channel_id=1, source_target_pairs={{0,8},{8,0},{16,24},{24,16},{1,9},{9,1},{17,25},{25,17},{2,10},{10... | collective-permute-start | bytes 835592 | tf_op jit(solution)/shard_map/ppermute | solution.py:20
  14.8 4.3 %fetch_gate_up.2 = (bf16[2048,1280]{1,0:T(8,128)(2,1)S(1)}, bf16[2048,1280]{1,0:T(8,128)(2,1)S(1)}) custom-call(bf16[2048,3584]{1,0:T(8,128)(2,1)} %refs_0_.7, bf16[2048,3584]{1,0:T(8,128)(2,1)} %refs_1_.5, bf16[2,32,2176]{2,1,0:T(8,128)(2,1)S(1)} %get-tuple-element.36.refs_2_), custom_call_target="tpu_custom_call" | custom-call | tf_op jit(solution)/shard_map/fetch_gate_up/pallas_call | solution.py:24
  22.1 4.3 %fetch_gate_up.3 = (bf16[2048,1280]{1,0:T(8,128)(2,1)S(1)}, bf16[2048,1280]{1,0:T(8,128)(2,1)S(1)}) custom-call(bf16[2048,3584]{1,0:T(8,128)(2,1)} %refs_0_.7, bf16[2048,3584]{1,0:T(8,128)(2,1)} %refs_1_.5, bf16[32,2176]{1,0:T(8,128)(2,1)S(1)} %pair_total.3.refs_2_), custom_call_target="tpu_custom_call" | custom-call | tf_op jit(solution)/shard_map/fetch_gate_up/pallas_call | solution.py:24
  30.5 2.7 %collective-permute-start.12 = (bf16[32,2560]{1,0:T(8,128)(2,1)S(1)}, bf16[32,2560]{1,0:T(8,128)(2,1)S(1)}, u32[]{:S(2)}, u32[]{:S(2)}) collective-permute-start(bf16[32,2560]{1,0:T(8,128)(2,1)S(1)} %pair_total.4.refs_1_), channel_id=1, source_target_pairs={{0,16},{8,24},{16,0},{24,8},{1,17},{9,25},{17,1},{25,9},{2,18},{10... | collective-permute-start | bytes 491528 | tf_op jit(solution)/shard_map/ppermute | solution.py:20
  33.5 2.5 %fetch_down.2.refs_0_.refs_4_ = bf16[1280,2048]{1,0:T(8,128)(2,1)S(1)} custom-call(bf16[3584,2048]{1,0:T(8,128)(2,1)} %refs_0_.9, bf16[32,2560]{1,0:T(8,128)(2,1)S(1)} %pair_total.4.refs_1_), custom_call_target="tpu_custom_call" | custom-call | tf_op jit(solution)/shard_map/fetch_down/pallas_call | solution.py:24
  36.0 7.8 %collective-permute-done.8.got_ref.refs_1_ = bf16[2,32,2560]{2,1,0:T(8,128)(2,1)S(1)} collective-permute-done((bf16[2,32,2560]{2,1,0:T(8,128)(2,1)S(1)}, bf16[2,32,2560]{2,1,0:T(8,128)(2,1)S(1)}, u32[]{:S(2)}, u32[]{:S(2)}) %collective-permute-start.8) | collective-permute-done | bytes 327712 | tf_op jit(solution)/shard_map/ppermute | solution.py:20
  44.3 3.8 %fetch_down.3.refs_6_.refs_4_ = bf16[2304,2048]{1,0:T(8,128)(2,1)S(1)} custom-call(bf16[3584,2048]{1,0:T(8,128)(2,1)} %refs_0_.9, bf16[32,2560]{1,0:T(8,128)(2,1)S(1)} %pair_total.5.refs_1_), custom_call_target="tpu_custom_call" | custom-call | tf_op jit(solution)/shard_map/fetch_down/pallas_call | solution.py:24
  48.1 1.9 %collective-permute-done.11.refs_2_ = bf16[32,2176]{1,0:T(8,128)(2,1)S(1)} collective-permute-done((bf16[32,2176]{1,0:T(8,128)(2,1)S(1)}, bf16[32,2176]{1,0:T(8,128)(2,1)S(1)}, u32[]{:S(2)}, u32[]{:S(2)}) %collective-permute-start.11) | collective-permute-done | bytes 139296 | tf_op jit(solution)/shard_map/ppermute | solution.py:20
  50.9 3.5 %collective-permute-start.17 = (bf16[32,2304]{1,0:T(8,128)(2,1)S(1)}, bf16[32,2304]{1,0:T(8,128)(2,1)S(1)}, u32[]{:S(2)}, u32[]{:S(2)}) collective-permute-start(bf16[32,2304]{1,0:T(8,128)(2,1)S(1)} %get-tuple-element.46.refs_0_), channel_id=1, source_target_pairs={{0,16},{8,24},{16,0},{24,8},{1,17},{9,25},{17,1},{25,9},{2,18},{10... | collective-permute-start | bytes 442376 | tf_op jit(solution)/shard_map/ppermute | solution.py:20
  54.4 4.2 %collective-permute-done.13.refs_4_.refs_1_ = bf16[32,2304]{1,0:T(8,128)(2,1)S(1)} collective-permute-done((bf16[32,2304]{1,0:T(8,128)(2,1)S(1)}, bf16[32,2304]{1,0:T(8,128)(2,1)S(1)}, u32[]{:S(2)}, u32[]{:S(2)}) %collective-permute-start.13) | collective-permute-done | bytes 147488 | tf_op jit(solution)/shard_map/ppermute | solution.py:20
  60.0 2.5 %collective-permute-start.14 = (bf16[32,1280]{1,0:T(8,128)(2,1)S(1)}, bf16[32,1280]{1,0:T(8,128)(2,1)S(1)}, u32[]{:S(2)}, u32[]{:S(2)}) collective-permute-start(bf16[32,1280]{1,0:T(8,128)(2,1)S(1)} %get-tuple-element.47.refs_0_), channel_id=1, source_target_pairs={{0,8},{8,0},{16,24},{24,16},{1,9},{9,1},{17,25},{25,17},{2,10},{10... | collective-permute-start | bytes 245768 | tf_op jit(solution)/shard_map/ppermute | solution.py:20
  62.5 2.8 %collective-permute-done.15.refs_0_.refs_2_ = bf16[32,1280]{1,0:T(8,128)(2,1)S(1)} collective-permute-done((bf16[32,1280]{1,0:T(8,128)(2,1)S(1)}, bf16[32,1280]{1,0:T(8,128)(2,1)S(1)}, u32[]{:S(2)}, u32[]{:S(2)}) %collective-permute-start.15) | collective-permute-done | bytes 81952 | tf_op jit(solution)/shard_map/ppermute | solution.py:20
  65.6 2.3 %collective-permute-start.18 = (bf16[32,2304]{1,0:T(8,128)(2,1)S(1)}, bf16[32,2304]{1,0:T(8,128)(2,1)S(1)}, u32[]{:S(2)}, u32[]{:S(2)}) collective-permute-start(bf16[32,2304]{1,0:T(8,128)(2,1)S(1)} %copy.15), channel_id=1, source_target_pairs={{0,8},{8,0},{16,24},{24,16},{1,9},{9,1},{17,25},{25,17},{2,10},{10... | collective-permute-start | bytes 442376 | tf_op jit(solution)/shard_map/ppermute | solution.py:20
  68.0 3.0 %collective-permute-done.18.refs_3_ = bf16[32,2304]{1,0:T(8,128)(2,1)S(1)} collective-permute-done((bf16[32,2304]{1,0:T(8,128)(2,1)S(1)}, bf16[32,2304]{1,0:T(8,128)(2,1)S(1)}, u32[]{:S(2)}, u32[]{:S(2)}) %collective-permute-start.18) | collective-permute-done | bytes 147488 | tf_op jit(solution)/shard_map/ppermute | solution.py:20
  74.9 2.8 %collective-permute-start.20 = (bf16[128,256]{1,0:T(8,128)(2,1)S(1)}, bf16[128,256]{1,0:T(8,128)(2,1)S(1)}, u32[]{:S(2)}, u32[]{:S(2)}) collective-permute-start(bf16[128,256]{1,0:T(8,128)(2,1)S(1)} %get-tuple-element.49), channel_id=1, source_target_pairs={{0,6},{1,7},{2,4},{3,5},{4,2},{5,3},{6,0},{7,1},{8,14},{9,15},{10,... | collective-permute-start | bytes 196616 | tf_op jit(solution)/shard_map/ppermute | solution.py:20
  80.1 1.8 %collective-permute-done.21 = bf16[128,256]{1,0:T(8,128)(2,1)S(1)} collective-permute-done((bf16[128,256]{1,0:T(8,128)(2,1)S(1)}, bf16[128,256]{1,0:T(8,128)(2,1)S(1)}, u32[]{:S(2)}, u32[]{:S(2)}) %collective-permute-start.21) | collective-permute-done | bytes 65568 | tf_op jit(solution)/shard_map/ppermute | solution.py:20
  85.5 1.9 %collective-permute-start.24 = (bf16[128,256]{1,0:T(8,128)(2,1)S(1)}, bf16[128,256]{1,0:T(8,128)(2,1)S(1)}, u32[]{:S(2)}, u32[]{:S(2)}) collective-permute-start(bf16[128,256]{1,0:T(8,128)(2,1)S(1)} %add_convert_fusion.own_ref), channel_id=1, source_target_pairs={{0,16},{8,24},{16,0},{24,8},{1,17},{9,25},{17,1},{25,9},{2,18},{10... | collective-permute-start | bytes 196616 | tf_op jit(solution)/shard_map/ppermute | solution.py:20
  97.7 2.5 %gram.3 = (f32[256,8192]{1,0:T(8,128)}, f32[64,256]{1,0:T(8,128)}) custom-call(bf16[128,256]{1,0:T(8,128)(2,1)S(1)} %add_convert_fusion.own_ref, bf16[4,128,256]{2,1,0:T(8,128)(2,1)S(1)} %stack.2.refs_0_, bf16[4,128,256]{2,1,0:T(8,128)(2,1)S(1)} %collective-permute-done.32.refs_1_, bf16[1,128,256]{2,1,0:T(8,128)(2,1)S(1)} %bitcast.16, ...), custom_call_target="tpu_custom_call" | custom-call | flops 167772160 | bytes 2621440 | tf_op jit(solution)/shard_map/gram/pallas_call | solution.py:24
  100.1 1.9 %collective-permute-done.31 = bf16[128,256]{1,0:T(8,128)(2,1)S(1)} collective-permute-done((bf16[128,256]{1,0:T(8,128)(2,1)S(1)}, bf16[128,256]{1,0:T(8,128)(2,1)S(1)}, u32[]{:S(2)}, u32[]{:S(2)}) %collective-permute-start.31) | collective-permute-done | bytes 65568 | tf_op jit(solution)/shard_map/ppermute | solution.py:20
  102.0 2.3 %collective-permute-done.30 = bf16[128,256]{1,0:T(8,128)(2,1)S(1)} collective-permute-done((bf16[128,256]{1,0:T(8,128)(2,1)S(1)}, bf16[128,256]{1,0:T(8,128)(2,1)S(1)}, u32[]{:S(2)}, u32[]{:S(2)}) %collective-permute-start.30) | collective-permute-done | bytes 65568 | tf_op jit(solution)/shard_map/ppermute | solution.py:20
  104.5 1.9 %gram.4.refs_1_ = f32[256,8192]{1,0:T(8,128)} custom-call(bf16[128,256]{1,0:T(8,128)(2,1)S(1)} %add_convert_fusion.own_ref, bf16[11,128,256]{2,1,0:T(8,128)(2,1)S(1)} %stack.3.refs_0_, f32[256,8192]{1,0:T(8,128)} %get-tuple-element.52.refs_5_.refs_1_), custom_call_target="tpu_custom_call", output_to_operand_aliasing={{}: (2, {})} | custom-call | flops 184549376 | bytes 2883584 | tf_op jit(solution)/shard_map/gram/pallas_call | solution.py:24
  106.7 1.9 %gram.5 = f32[256,8192]{1,0:T(8,128)} custom-call(bf16[128,256]{1,0:T(8,128)(2,1)S(1)} %add_convert_fusion.own_ref, bf16[11,128,256]{2,1,0:T(8,128)(2,1)S(1)} %collective-permute-done.34.refs_0_, f32[256,8192]{1,0:T(8,128)} %gram.4.refs_1_), custom_call_target="tpu_custom_call", output_to_operand_aliasing={{}: (2, {})} | custom-call | flops 184549376 | bytes 2883584 | tf_op jit(solution)/shard_map/gram/pallas_call | solution.py:24
  (74 shorter events, 36.4 us)
Async XLA Ops:
  0.6 8.3 %collective-permute-start.1 = (bf16[16,2048]{1,0:T(8,128)(2,1)}, bf16[16,2048]{1,0:T(8,128)(2,1)S(1)}, u32[]{:S(2)}, u32[]{:S(2)}) collective-permute-start(bf16[16,2048]{1,0:T(8,128)(2,1)} %refs_2_.1), channel_id=1, source_target_pairs={{0,4},{1,5},{2,6},{3,7},{4,0},{5,1},{6,2},{7,3},{8,12},{9,13},{10,... | collective-permute-start | bytes 196616 | tf_op jit(solution)/shard_map/ppermute | solution.py:20
  3.7 5.9 %collective-permute-start.2 = (bf16[16,2048]{1,0:T(8,128)(2,1)}, bf16[16,2048]{1,0:T(8,128)(2,1)S(1)}, u32[]{:S(2)}, u32[]{:S(2)}) collective-permute-start(bf16[16,2048]{1,0:T(8,128)(2,1)} %refs_2_.1), channel_id=1, source_target_pairs={{0,6},{1,7},{2,4},{3,5},{4,2},{5,3},{6,0},{7,1},{8,14},{9,15},{10,... | collective-permute-start | bytes 196616 | tf_op jit(solution)/shard_map/ppermute | solution.py:20
  5.2 4.9 %collective-permute-start.3 = (bf16[16,2048]{1,0:T(8,128)(2,1)}, bf16[16,2048]{1,0:T(8,128)(2,1)S(1)}, u32[]{:S(2)}, u32[]{:S(2)}) collective-permute-start(bf16[16,2048]{1,0:T(8,128)(2,1)} %refs_2_.1), channel_id=1, source_target_pairs={{0,1},{1,0},{2,3},{3,2},{4,5},{5,4},{6,7},{7,6},{8,9},{9,8},{10,11... | collective-permute-start | bytes 196616 | tf_op jit(solution)/shard_map/ppermute | solution.py:20
  12.7 9.3 %collective-permute-start.7 = (bf16[2,32,2176]{2,1,0:T(8,128)(2,1)S(1)}, bf16[2,32,2176]{2,1,0:T(8,128)(2,1)S(1)}, u32[]{:S(2)}, u32[]{:S(2)}) collective-permute-start(bf16[2,32,2176]{2,1,0:T(8,128)(2,1)S(1)} %get-tuple-element.36.refs_2_), channel_id=1, source_target_pairs={{0,8},{8,0},{16,24},{24,16},{1,9},{9,1},{17,25},{25,17},{2,10},{10... | collective-permute-start | bytes 835592 | tf_op jit(solution)/shard_map/ppermute | solution.py:20
  20.7 9.8 %collective-permute-start.9 = (bf16[2,32,2560]{2,1,0:T(8,128)(2,1)S(1)}, bf16[2,32,2560]{2,1,0:T(8,128)(2,1)S(1)}, u32[]{:S(2)}, u32[]{:S(2)}) collective-permute-start(bf16[2,32,2560]{2,1,0:T(8,128)(2,1)S(1)} %get-tuple-element.39.refs_0_), channel_id=1, source_target_pairs={{0,8},{8,0},{16,24},{24,16},{1,9},{9,1},{17,25},{25,17},{2,10},{10... | collective-permute-start | bytes 983048 | tf_op jit(solution)/shard_map/ppermute | solution.py:20
  28.0 15.8 %collective-permute-start.8 = (bf16[2,32,2560]{2,1,0:T(8,128)(2,1)S(1)}, bf16[2,32,2560]{2,1,0:T(8,128)(2,1)S(1)}, u32[]{:S(2)}, u32[]{:S(2)}) collective-permute-start(bf16[2,32,2560]{2,1,0:T(8,128)(2,1)S(1)} %get-tuple-element.43.refs_0_), channel_id=1, source_target_pairs={{0,8},{8,0},{16,24},{24,16},{1,9},{9,1},{17,25},{25,17},{2,10},{10... | collective-permute-start | bytes 983048 | tf_op jit(solution)/shard_map/ppermute | solution.py:20
  30.5 19.5 %collective-permute-start.12 = (bf16[32,2560]{1,0:T(8,128)(2,1)S(1)}, bf16[32,2560]{1,0:T(8,128)(2,1)S(1)}, u32[]{:S(2)}, u32[]{:S(2)}) collective-permute-start(bf16[32,2560]{1,0:T(8,128)(2,1)S(1)} %pair_total.4.refs_1_), channel_id=1, source_target_pairs={{0,16},{8,24},{16,0},{24,8},{1,17},{9,25},{17,1},{25,9},{2,18},{10... | collective-permute-start | bytes 491528 | tf_op jit(solution)/shard_map/ppermute | solution.py:20
  33.2 16.8 %collective-permute-start.11 = (bf16[32,2176]{1,0:T(8,128)(2,1)S(1)}, bf16[32,2176]{1,0:T(8,128)(2,1)S(1)}, u32[]{:S(2)}, u32[]{:S(2)}) collective-permute-start(bf16[32,2176]{1,0:T(8,128)(2,1)S(1)} %pair_total.3.refs_2_), channel_id=1, source_target_pairs={{0,16},{8,24},{16,0},{24,8},{1,17},{9,25},{17,1},{25,9},{2,18},{10... | collective-permute-start | bytes 417800 | tf_op jit(solution)/shard_map/ppermute | solution.py:20
  43.9 14.6 %collective-permute-start.10 = (bf16[32,2560]{1,0:T(8,128)(2,1)S(1)}, bf16[32,2560]{1,0:T(8,128)(2,1)S(1)}, u32[]{:S(2)}, u32[]{:S(2)}) collective-permute-start(bf16[32,2560]{1,0:T(8,128)(2,1)S(1)} %pair_total.5.refs_1_), channel_id=1, source_target_pairs={{0,16},{8,24},{16,0},{24,8},{1,17},{9,25},{17,1},{25,9},{2,18},{10... | collective-permute-start | bytes 491528 | tf_op jit(solution)/shard_map/ppermute | solution.py:20
  50.2 8.3 %collective-permute-start.13 = (bf16[32,2304]{1,0:T(8,128)(2,1)S(1)}, bf16[32,2304]{1,0:T(8,128)(2,1)S(1)}, u32[]{:S(2)}, u32[]{:S(2)}) collective-permute-start(bf16[32,2304]{1,0:T(8,128)(2,1)S(1)} %get-tuple-element.46.refs_0_), channel_id=1, source_target_pairs={{0,8},{8,0},{16,24},{24,16},{1,9},{9,1},{17,25},{25,17},{2,10},{10... | collective-permute-start | bytes 442376 | tf_op jit(solution)/shard_map/ppermute | solution.py:20
  50.9 11.6 %collective-permute-start.17 = (bf16[32,2304]{1,0:T(8,128)(2,1)S(1)}, bf16[32,2304]{1,0:T(8,128)(2,1)S(1)}, u32[]{:S(2)}, u32[]{:S(2)}) collective-permute-start(bf16[32,2304]{1,0:T(8,128)(2,1)S(1)} %get-tuple-element.46.refs_0_), channel_id=1, source_target_pairs={{0,16},{8,24},{16,0},{24,8},{1,17},{9,25},{17,1},{25,9},{2,18},{10... | collective-permute-start | bytes 442376 | tf_op jit(solution)/shard_map/ppermute | solution.py:20
  59.1 6.2 %collective-permute-start.15 = (bf16[32,1280]{1,0:T(8,128)(2,1)S(1)}, bf16[32,1280]{1,0:T(8,128)(2,1)S(1)}, u32[]{:S(2)}, u32[]{:S(2)}) collective-permute-start(bf16[32,1280]{1,0:T(8,128)(2,1)S(1)} %get-tuple-element.47.refs_0_), channel_id=1, source_target_pairs={{0,16},{8,24},{16,0},{24,8},{1,17},{9,25},{17,1},{25,9},{2,18},{10... | collective-permute-start | bytes 245768 | tf_op jit(solution)/shard_map/ppermute | solution.py:20
  60.0 5.5 %collective-permute-start.14 = (bf16[32,1280]{1,0:T(8,128)(2,1)S(1)}, bf16[32,1280]{1,0:T(8,128)(2,1)S(1)}, u32[]{:S(2)}, u32[]{:S(2)}) collective-permute-start(bf16[32,1280]{1,0:T(8,128)(2,1)S(1)} %get-tuple-element.47.refs_0_), channel_id=1, source_target_pairs={{0,8},{8,0},{16,24},{24,16},{1,9},{9,1},{17,25},{25,17},{2,10},{10... | collective-permute-start | bytes 245768 | tf_op jit(solution)/shard_map/ppermute | solution.py:20
  65.6 5.4 %collective-permute-start.18 = (bf16[32,2304]{1,0:T(8,128)(2,1)S(1)}, bf16[32,2304]{1,0:T(8,128)(2,1)S(1)}, u32[]{:S(2)}, u32[]{:S(2)}) collective-permute-start(bf16[32,2304]{1,0:T(8,128)(2,1)S(1)} %copy.15), channel_id=1, source_target_pairs={{0,8},{8,0},{16,24},{24,16},{1,9},{9,1},{17,25},{25,17},{2,10},{10... | collective-permute-start | bytes 442376 | tf_op jit(solution)/shard_map/ppermute | solution.py:20
  67.9 4.7 %collective-permute-start.16 = (bf16[32,1280]{1,0:T(8,128)(2,1)S(1)}, bf16[32,1280]{1,0:T(8,128)(2,1)S(1)}, u32[]{:S(2)}, u32[]{:S(2)}) collective-permute-start(bf16[32,1280]{1,0:T(8,128)(2,1)S(1)} %collective-permute-done.15.refs_0_.refs_2_), channel_id=1, source_target_pairs={{0,8},{8,0},{16,24},{24,16},{1,9},{9,1},{17,25},{25,17},{2,10},{10... | collective-permute-start | bytes 245768 | tf_op jit(solution)/shard_map/ppermute | solution.py:20
  74.9 5.2 %collective-permute-start.20 = (bf16[128,256]{1,0:T(8,128)(2,1)S(1)}, bf16[128,256]{1,0:T(8,128)(2,1)S(1)}, u32[]{:S(2)}, u32[]{:S(2)}) collective-permute-start(bf16[128,256]{1,0:T(8,128)(2,1)S(1)} %get-tuple-element.49), channel_id=1, source_target_pairs={{0,6},{1,7},{2,4},{3,5},{4,2},{5,3},{6,0},{7,1},{8,14},{9,15},{10,... | collective-permute-start | bytes 196616 | tf_op jit(solution)/shard_map/ppermute | solution.py:20
  82.4 6.0 %collective-permute-start.26 = (bf16[128,256]{1,0:T(8,128)(2,1)S(1)}, bf16[128,256]{1,0:T(8,128)(2,1)S(1)}, u32[]{:S(2)}, u32[]{:S(2)}) collective-permute-start(bf16[128,256]{1,0:T(8,128)(2,1)S(1)} %add_convert_fusion.own_ref), channel_id=1, source_target_pairs={{0,6},{1,7},{2,4},{3,5},{4,2},{5,3},{6,0},{7,1},{8,14},{9,15},{10,... | collective-permute-start | bytes 196616 | tf_op jit(solution)/shard_map/ppermute | solution.py:20
  84.1 6.5 %collective-permute-start.25 = (bf16[128,256]{1,0:T(8,128)(2,1)S(1)}, bf16[128,256]{1,0:T(8,128)(2,1)S(1)}, u32[]{:S(2)}, u32[]{:S(2)}) collective-permute-start(bf16[128,256]{1,0:T(8,128)(2,1)S(1)} %add_convert_fusion.own_ref), channel_id=1, source_target_pairs={{0,24},{8,16},{16,8},{24,0},{1,25},{9,17},{17,9},{25,1},{2,26},{10... | collective-permute-start | bytes 196616 | tf_op jit(solution)/shard_map/ppermute | solution.py:20
  85.5 6.7 %collective-permute-start.24 = (bf16[128,256]{1,0:T(8,128)(2,1)S(1)}, bf16[128,256]{1,0:T(8,128)(2,1)S(1)}, u32[]{:S(2)}, u32[]{:S(2)}) collective-permute-start(bf16[128,256]{1,0:T(8,128)(2,1)S(1)} %add_convert_fusion.own_ref), channel_id=1, source_target_pairs={{0,16},{8,24},{16,0},{24,8},{1,17},{9,25},{17,1},{25,9},{2,18},{10... | collective-permute-start | bytes 196616 | tf_op jit(solution)/shard_map/ppermute | solution.py:20
  87.5 5.0 %collective-permute-start.23 = (bf16[128,256]{1,0:T(8,128)(2,1)S(1)}, bf16[128,256]{1,0:T(8,128)(2,1)S(1)}, u32[]{:S(2)}, u32[]{:S(2)}) collective-permute-start(bf16[128,256]{1,0:T(8,128)(2,1)S(1)} %add_convert_fusion.own_ref), channel_id=1, source_target_pairs={{0,8},{8,0},{16,24},{24,16},{1,9},{9,1},{17,25},{25,17},{2,10},{10... | collective-permute-start | bytes 196616 | tf_op jit(solution)/shard_map/ppermute | solution.py:20
  93.2 11.1 %collective-permute-start.29 = (bf16[4,128,256]{2,1,0:T(8,128)(2,1)S(1)}, bf16[4,128,256]{2,1,0:T(8,128)(2,1)S(1)}, u32[]{:S(2)}, u32[]{:S(2)}) collective-permute-start(bf16[4,128,256]{2,1,0:T(8,128)(2,1)S(1)} %stack.2.refs_0_), channel_id=1, source_target_pairs={{0,4},{1,5},{2,6},{3,7},{4,0},{5,1},{6,2},{7,3},{8,12},{9,13},{10,... | collective-permute-start | bytes 786440 | tf_op jit(solution)/shard_map/ppermute | solution.py:20
  94.9 9.5 %collective-permute-start.28 = (bf16[4,128,256]{2,1,0:T(8,128)(2,1)S(1)}, bf16[4,128,256]{2,1,0:T(8,128)(2,1)S(1)}, u32[]{:S(2)}, u32[]{:S(2)}) collective-permute-start(bf16[4,128,256]{2,1,0:T(8,128)(2,1)S(1)} %stack.2.refs_0_), channel_id=1, source_target_pairs={{0,2},{1,3},{2,0},{3,1},{4,6},{5,7},{6,4},{7,5},{8,10},{9,11},{10,... | collective-permute-start | bytes 786440 | tf_op jit(solution)/shard_map/ppermute | solution.py:20
  95.2 6.8 %collective-permute-start.31 = (bf16[128,256]{1,0:T(8,128)(2,1)S(1)}, bf16[128,256]{1,0:T(8,128)(2,1)S(1)}, u32[]{:S(2)}, u32[]{:S(2)}) collective-permute-start(bf16[128,256]{1,0:T(8,128)(2,1)S(1)} %collective-permute-done.26), channel_id=1, source_target_pairs={{0,24},{8,16},{16,8},{24,0},{1,25},{9,17},{17,9},{25,1},{2,26},{10... | collective-permute-start | bytes 196616 | tf_op jit(solution)/shard_map/ppermute | solution.py:20
  96.5 7.9 %collective-permute-start.30 = (bf16[128,256]{1,0:T(8,128)(2,1)S(1)}, bf16[128,256]{1,0:T(8,128)(2,1)S(1)}, u32[]{:S(2)}, u32[]{:S(2)}) collective-permute-start(bf16[128,256]{1,0:T(8,128)(2,1)S(1)} %collective-permute-done.26), channel_id=1, source_target_pairs={{0,16},{8,24},{16,0},{24,8},{1,17},{9,25},{17,1},{25,9},{2,18},{10... | collective-permute-start | bytes 196616 | tf_op jit(solution)/shard_map/ppermute | solution.py:20
  (12 other events, 56.5 us)

commit v8 on v6

--- a/solution.py
+++ b/solution.py
@@ -126,6 +126,49 @@
         in_specs=[WHOLE] * (3 + len(extra)) + [ANYWHERE] * len(after),
         out_specs=[WHOLE] * 2,
         scratch_shapes=[pltpu.VMEM((ntok, 2 * TILE), F32), pltpu.VMEM((ntok, SIDE), F32)],
+    )
+
+
+def gate_up_from_hbm(lhs, gate_part, up_part, n_tok, after):
+    ntok, depth = lhs.shape
+    start, width = gate_part[3:]
+    rows = ntok // n_tok
+    tiles = width // TILE
+
+    def body(lhs_ref, gate_hbm, up_hbm, *refs):
+        send_ref, keep_ref, gate_ref, up_ref, both, sems = refs[-6:]
+        places = ((keep_ref, 0), (send_ref, 0), (keep_ref, 1), (send_ref, 1))
+        z = lax.axis_index("tok")
+        copies = []
+        for tile in range(tiles):
+            for number, (source, target) in enumerate(((gate_hbm, gate_ref), (up_hbm, up_ref))):
+                copy = pltpu.make_async_copy(
+                    source.at[:, pl.ds(start + tile * TILE, TILE)], target.at[tile], sems.at[2 * tile + number]
+                )
+                copy.start()
+                copies.append(copy)
+        values = lhs_ref[...]
+        for tile in range(tiles):
+            copies[2 * tile].wait()
+            both[:, :TILE] = jnp.dot(values, gate_ref[tile], preferred_element_type=F32)
+            copies[2 * tile + 1].wait()
+            both[:, TILE:] = jnp.dot(values, up_ref[tile], preferred_element_type=F32)
+            for d, (out, slot) in enumerate(places):
+                at = pl.multiple_of((z ^ d) * rows, rows)
+                out[slot, :, 2 * tile * TILE:2 * (tile + 1) * TILE] = both[pl.ds(at, rows), :].astype(BF16)
+
+    shape = jax.ShapeDtypeStruct((2, rows, 2 * width), BF16)
+    in_hbm = [pltpu.with_memory_space_constraint(part[0], pltpu.HBM) for part in (gate_part, up_part)]
+    return run(
+        body, "gate_up_from_hbm", [shape, shape], [lhs, *in_hbm, *after], 0, 0,
+        in_specs=[WHOLE] + [ANYWHERE] * (2 + len(after)),
+        out_specs=[WHOLE] * 2,
+        scratch_shapes=[
+            pltpu.VMEM((tiles, depth, TILE), BF16),
+            pltpu.VMEM((tiles, depth, TILE), BF16),
+            pltpu.VMEM((ntok, 2 * TILE), F32),
+            pltpu.SemaphoreType.DMA((2 * tiles,)),
+        ],
     )
 
 
@@ -341,13 +384,11 @@
     widths = [ends[k + 1] - ends[k] for k in range(3)]
     send_0, keep_0 = gate_up(lhs, gate_0, up_0, squares, n_tok)
     got_0 = swap(send_0, "tok", n_tok, 1)
-    gate_1, up_1 = fetch([part(gate_weight, 1), part(up_weight, 1)], (send_0,), "fetch_gate_up")
-    send_1, keep_1 = gate_up(lhs, gate_1, up_1, None, n_tok)
+    send_1, keep_1 = gate_up_from_hbm(lhs, part(gate_weight, 1), part(up_weight, 1), n_tok, (send_0,))
     got_1 = swap(send_1, "tok", n_tok, 1)
     sum_0 = pair_total(keep_0, got_0, 2 * widths[0], (send_1,))
     over_0 = swap(sum_0, "tok", n_tok, 2)
-    gate_2, up_2 = fetch([part(gate_weight, 2), part(up_weight, 2)], (sum_0,), "fetch_gate_up")
-    send_2, keep_2 = gate_up(lhs, gate_2, up_2, None, n_tok)
+    send_2, keep_2 = gate_up_from_hbm(lhs, part(gate_weight, 2), part(up_weight, 2), n_tok, (sum_0,))
     got_2 = swap(send_2, "tok", n_tok, 1)
     sum_1 = pair_total(keep_1, got_1, 2 * widths[1], (send_2,))
     over_1 = swap(sum_1, "tok", n_tok, 2)

time: 106 us -> 106 us (level)
    pallas_call x25 -> x23, Pallas kernels: 33.6 us -> 33 us  [run(): pl.pallas_call(body, out_shape=out_shape, in_specs=[WHOLE] * len(operands...]
  transfers between devices with their start and end apart: 35 -> 35, of which waited for: 19 -> 19; matrix products, arithmetic and copies ran while one was open for 0% -> 0% of each run, Pallas kernels for 28% -> 27%
where the time goes in v8:
time: 106 us
  starting transfers between devices  39.9 us (38%)
  Pallas kernels  33 us (31%)
  waiting for transfers between devices  32 us (30%)
    ppermute x35, starting transfers between devices, swap(): return lax.ppermute(value, axis, [(i, i ^ mask) for i in range(size)])  39.9 us
    pallas_call x23, Pallas kernels, run(): pl.pallas_call(body, out_shape=out_shape, in_specs=[WHOLE] * len(operands...  33 us
    ppermute x35, waiting for transfers between devices, swap(): return lax.ppermute(value, axis, [(i, i ^ mask) for i in range(size)])  32 us
  transfers between devices with their start and end apart: 35, of which 19 were waited for; matrix products, arithmetic and copies ran while one was open for 0% of the time, Pallas kernels for 27%

profile of v8, /device:TPU:0, one launch (start us, length us, event | category | flops | bytes accessed | tf_op | source)
XLA Modules:
  0.0 105.8 jit_solution(8907635228448954039)
XLA Ops:
  0.6 3.0 %collective-permute-start.1 = (bf16[16,2048]{1,0:T(8,128)(2,1)}, bf16[16,2048]{1,0:T(8,128)(2,1)S(1)}, u32[]{:S(2)}, u32[]{:S(2)}) collective-permute-start(bf16[16,2048]{1,0:T(8,128)(2,1)} %refs_2_.1), channel_id=1, source_target_pairs={{0,4},{1,5},{2,6},{3,7},{4,0},{5,1},{6,2},{7,3},{8,12},{9,13},{10,... | collective-permute-start | bytes 196616 | tf_op jit(solution)/shard_map/ppermute | solution.py:20
  5.2 3.7 %fetch_first.1 = (bf16[2048,1024]{1,0:T(8,128)(2,1)S(1)}, bf16[2048,1024]{1,0:T(8,128)(2,1)S(1)}, bf16[16,2048]{1,0:T(8,128)(2,1)S(1)}, f32[1,2048]{1,0:T(1,128)S(1)}) custom-call(bf16[2048,3584]{1,0:T(8,128)(2,1)} %gate_hbm.3, bf16[2048,3584]{1,0:T(8,128)(2,1)} %up_hbm.3, bf16[16,2048]{1,0:T(8,128)(2,1)} %refs_2_.1, f32[1,2048]{1,0:T(1,128)} %bitcast.22), custom_call_target="tpu_custom_call" | custom-call | tf_op jit(solution)/shard_map/fetch_first/pallas_call | solution.py:24
  12.7 2.1 %collective-permute-start.7 = (bf16[2,32,2176]{2,1,0:T(8,128)(2,1)S(1)}, bf16[2,32,2176]{2,1,0:T(8,128)(2,1)S(1)}, u32[]{:S(2)}, u32[]{:S(2)}) collective-permute-start(bf16[2,32,2176]{2,1,0:T(8,128)(2,1)S(1)} %get-tuple-element.32.refs_0_), channel_id=1, source_target_pairs={{0,8},{8,0},{16,24},{24,16},{1,9},{9,1},{17,25},{25,17},{2,10},{10... | collective-permute-start | bytes 835592 | tf_op jit(solution)/shard_map/ppermute | solution.py:20
  14.8 5.6 %gate_up_from_hbm.2 = (bf16[2,32,2560]{2,1,0:T(8,128)(2,1)S(1)}, bf16[2,32,2560]{2,1,0:T(8,128)(2,1)S(1)}) custom-call(bf16[128,2048]{1,0:T(8,128)(2,1)S(1)} %get-tuple-element.27.lhs_ref, bf16[2048,3584]{1,0:T(8,128)(2,1)} %gate_hbm.3, bf16[2048,3584]{1,0:T(8,128)(2,1)} %up_hbm.3, bf16[2,32,2176]{2,1,0:T(8,128)(2,1)S(1)} %get-tuple-element.32.refs_0_), custom_call_target="tpu_custom_call" | custom-call | tf_op jit(solution)/shard_map/gate_up_from_hbm/pallas_call | solution.py:24
  22.1 5.6 %gate_up_from_hbm.3 = (bf16[2,32,2560]{2,1,0:T(8,128)(2,1)S(1)}, bf16[2,32,2560]{2,1,0:T(8,128)(2,1)S(1)}) custom-call(bf16[128,2048]{1,0:T(8,128)(2,1)S(1)} %get-tuple-element.27.lhs_ref, bf16[2048,3584]{1,0:T(8,128)(2,1)} %gate_hbm.3, bf16[2048,3584]{1,0:T(8,128)(2,1)} %up_hbm.3, bf16[32,2176]{1,0:T(8,128)(2,1)S(1)} %pair_total.3.refs_0_), custom_call_target="tpu_custom_call" | custom-call | tf_op jit(solution)/shard_map/gate_up_from_hbm/pallas_call | solution.py:24
  27.7 2.0 %collective-permute-start.8 = (bf16[2,32,2560]{2,1,0:T(8,128)(2,1)S(1)}, bf16[2,32,2560]{2,1,0:T(8,128)(2,1)S(1)}, u32[]{:S(2)}, u32[]{:S(2)}) collective-permute-start(bf16[2,32,2560]{2,1,0:T(8,128)(2,1)S(1)} %get-tuple-element.35.refs_0_), channel_id=1, source_target_pairs={{0,8},{8,0},{16,24},{24,16},{1,9},{9,1},{17,25},{25,17},{2,10},{10... | collective-permute-start | bytes 983048 | tf_op jit(solution)/shard_map/ppermute | solution.py:20
  30.2 2.7 %collective-permute-start.12 = (bf16[32,2560]{1,0:T(8,128)(2,1)S(1)}, bf16[32,2560]{1,0:T(8,128)(2,1)S(1)}, u32[]{:S(2)}, u32[]{:S(2)}) collective-permute-start(bf16[32,2560]{1,0:T(8,128)(2,1)S(1)} %pair_total.4.refs_1_), channel_id=1, source_target_pairs={{0,16},{8,24},{16,0},{24,8},{1,17},{9,25},{17,1},{25,9},{2,18},{10... | collective-permute-start | bytes 491528 | tf_op jit(solution)/shard_map/ppermute | solution.py:20
  33.2 2.5 %fetch_down.2.refs_0_.refs_4_ = bf16[1280,2048]{1,0:T(8,128)(2,1)S(1)} custom-call(bf16[3584,2048]{1,0:T(8,128)(2,1)} %refs_0_.5, bf16[32,2560]{1,0:T(8,128)(2,1)S(1)} %pair_total.4.refs_1_), custom_call_target="tpu_custom_call" | custom-call | tf_op jit(solution)/shard_map/fetch_down/pallas_call | solution.py:24
  35.7 7.8 %collective-permute-done.8.got_ref.refs_1_ = bf16[2,32,2560]{2,1,0:T(8,128)(2,1)S(1)} collective-permute-done((bf16[2,32,2560]{2,1,0:T(8,128)(2,1)S(1)}, bf16[2,32,2560]{2,1,0:T(8,128)(2,1)S(1)}, u32[]{:S(2)}, u32[]{:S(2)}) %collective-permute-start.8) | collective-permute-done | bytes 327712 | tf_op jit(solution)/shard_map/ppermute | solution.py:20
  43.7 3.8 %fetch_down.3.refs_6_.refs_4_ = bf16[2304,2048]{1,0:T(8,128)(2,1)S(1)} custom-call(bf16[3584,2048]{1,0:T(8,128)(2,1)} %refs_0_.5, bf16[32,2560]{1,0:T(8,128)(2,1)S(1)} %pair_total.5.refs_1_), custom_call_target="tpu_custom_call" | custom-call | tf_op jit(solution)/shard_map/fetch_down/pallas_call | solution.py:24
  47.5 2.2 %collective-permute-done.11.refs_2_ = bf16[32,2176]{1,0:T(8,128)(2,1)S(1)} collective-permute-done((bf16[32,2176]{1,0:T(8,128)(2,1)S(1)}, bf16[32,2176]{1,0:T(8,128)(2,1)S(1)}, u32[]{:S(2)}, u32[]{:S(2)}) %collective-permute-start.11) | collective-permute-done | bytes 139296 | tf_op jit(solution)/shard_map/ppermute | solution.py:20
  50.7 3.9 %collective-permute-start.16 = (bf16[32,2304]{1,0:T(8,128)(2,1)S(1)}, bf16[32,2304]{1,0:T(8,128)(2,1)S(1)}, u32[]{:S(2)}, u32[]{:S(2)}) collective-permute-start(bf16[32,2304]{1,0:T(8,128)(2,1)S(1)} %get-tuple-element.39.refs_0_), channel_id=1, source_target_pairs={{0,8},{8,0},{16,24},{24,16},{1,9},{9,1},{17,25},{25,17},{2,10},{10... | collective-permute-start | bytes 442376 | tf_op jit(solution)/shard_map/ppermute | solution.py:20
  55.5 4.0 %collective-permute-done.17.value_ref.refs_2_ = bf16[32,2304]{1,0:T(8,128)(2,1)S(1)} collective-permute-done((bf16[32,2304]{1,0:T(8,128)(2,1)S(1)}, bf16[32,2304]{1,0:T(8,128)(2,1)S(1)}, u32[]{:S(2)}, u32[]{:S(2)}) %collective-permute-start.17) | collective-permute-done | bytes 147488 | tf_op jit(solution)/shard_map/ppermute | solution.py:20
  59.6 3.3 %collective-permute-start.14 = (bf16[32,1280]{1,0:T(8,128)(2,1)S(1)}, bf16[32,1280]{1,0:T(8,128)(2,1)S(1)}, u32[]{:S(2)}, u32[]{:S(2)}) collective-permute-start(bf16[32,1280]{1,0:T(8,128)(2,1)S(1)} %get-tuple-element.38.refs_0_), channel_id=1, source_target_pairs={{0,16},{8,24},{16,0},{24,8},{1,17},{9,25},{17,1},{25,9},{2,18},{10... | collective-permute-start | bytes 245768 | tf_op jit(solution)/shard_map/ppermute | solution.py:20
  63.0 3.1 %collective-permute-done.14.refs_2_ = bf16[32,1280]{1,0:T(8,128)(2,1)S(1)} collective-permute-done((bf16[32,1280]{1,0:T(8,128)(2,1)S(1)}, bf16[32,1280]{1,0:T(8,128)(2,1)S(1)}, u32[]{:S(2)}, u32[]{:S(2)}) %collective-permute-start.14) | collective-permute-done | bytes 81952 | tf_op jit(solution)/shard_map/ppermute | solution.py:20
  66.1 2.6 %collective-permute-start.15 = (bf16[32,1280]{1,0:T(8,128)(2,1)S(1)}, bf16[32,1280]{1,0:T(8,128)(2,1)S(1)}, u32[]{:S(2)}, u32[]{:S(2)}) collective-permute-start(bf16[32,1280]{1,0:T(8,128)(2,1)S(1)} %collective-permute-done.14.refs_2_), channel_id=1, source_target_pairs={{0,8},{8,0},{16,24},{24,16},{1,9},{9,1},{17,25},{25,17},{2,10},{10... | collective-permute-start | bytes 245768 | tf_op jit(solution)/shard_map/ppermute | solution.py:20
  73.3 2.5 %collective-permute-start.20 = (bf16[128,256]{1,0:T(8,128)(2,1)S(1)}, bf16[128,256]{1,0:T(8,128)(2,1)S(1)}, u32[]{:S(2)}, u32[]{:S(2)}) collective-permute-start(bf16[128,256]{1,0:T(8,128)(2,1)S(1)} %get-tuple-element.41), channel_id=1, source_target_pairs={{0,6},{1,7},{2,4},{3,5},{4,2},{5,3},{6,0},{7,1},{8,14},{9,15},{10,... | collective-permute-start | bytes 196616 | tf_op jit(solution)/shard_map/ppermute | solution.py:20
  86.6 1.9 %collective-permute-done.25 = bf16[128,256]{1,0:T(8,128)(2,1)S(1)} collective-permute-done((bf16[128,256]{1,0:T(8,128)(2,1)S(1)}, bf16[128,256]{1,0:T(8,128)(2,1)S(1)}, u32[]{:S(2)}, u32[]{:S(2)}) %collective-permute-start.25) | collective-permute-done | bytes 65568 | tf_op jit(solution)/shard_map/ppermute | solution.py:20
  88.5 2.0 %collective-permute-done.24 = bf16[128,256]{1,0:T(8,128)(2,1)S(1)} collective-permute-done((bf16[128,256]{1,0:T(8,128)(2,1)S(1)}, bf16[128,256]{1,0:T(8,128)(2,1)S(1)}, u32[]{:S(2)}, u32[]{:S(2)}) %collective-permute-start.24) | collective-permute-done | bytes 65568 | tf_op jit(solution)/shard_map/ppermute | solution.py:20
  94.7 2.3 %collective-permute-start.29 = (bf16[128,256]{1,0:T(8,128)(2,1)S(1)}, bf16[128,256]{1,0:T(8,128)(2,1)S(1)}, u32[]{:S(2)}, u32[]{:S(2)}) collective-permute-start(bf16[128,256]{1,0:T(8,128)(2,1)S(1)} %collective-permute-done.26.refs_4_), channel_id=1, source_target_pairs={{0,8},{8,0},{16,24},{24,16},{1,9},{9,1},{17,25},{25,17},{2,10},{10... | collective-permute-start | bytes 196616 | tf_op jit(solution)/shard_map/ppermute | solution.py:20
  96.9 2.4 %gram.3 = (f32[256,8192]{1,0:T(8,128)}, f32[64,256]{1,0:T(8,128)}) custom-call(bf16[128,256]{1,0:T(8,128)(2,1)S(1)} %add_convert_fusion.own_ref, bf16[4,128,256]{2,1,0:T(8,128)(2,1)S(1)} %stack.2.refs_0_, bf16[4,128,256]{2,1,0:T(8,128)(2,1)S(1)} %collective-permute-done.32.refs_1_, bf16[1,128,256]{2,1,0:T(8,128)(2,1)S(1)} %bitcast.13, ...), custom_call_target="tpu_custom_call" | custom-call | flops 167772160 | bytes 2621440 | tf_op jit(solution)/shard_map/gram/pallas_call | solution.py:24
  99.4 2.2 %collective-permute-done.30 = bf16[128,256]{1,0:T(8,128)(2,1)S(1)} collective-permute-done((bf16[128,256]{1,0:T(8,128)(2,1)S(1)}, bf16[128,256]{1,0:T(8,128)(2,1)S(1)}, u32[]{:S(2)}, u32[]{:S(2)}) %collective-permute-start.30) | collective-permute-done | bytes 65568 | tf_op jit(solution)/shard_map/ppermute | solution.py:20
  101.8 1.9 %gram.4.refs_1_ = f32[256,8192]{1,0:T(8,128)} custom-call(bf16[128,256]{1,0:T(8,128)(2,1)S(1)} %add_convert_fusion.own_ref, bf16[11,128,256]{2,1,0:T(8,128)(2,1)S(1)} %stack.3.refs_0_, f32[256,8192]{1,0:T(8,128)} %get-tuple-element.44.refs_5_.refs_1_), custom_call_target="tpu_custom_call", output_to_operand_aliasing={{}: (2, {})} | custom-call | flops 184549376 | bytes 2883584 | tf_op jit(solution)/shard_map/gram/pallas_call | solution.py:24
  103.9 1.9 %gram.5 = f32[256,8192]{1,0:T(8,128)} custom-call(bf16[128,256]{1,0:T(8,128)(2,1)S(1)} %add_convert_fusion.own_ref, bf16[11,128,256]{2,1,0:T(8,128)(2,1)S(1)} %collective-permute-done.34.refs_0_, f32[256,8192]{1,0:T(8,128)} %gram.4.refs_1_), custom_call_target="tpu_custom_call", output_to_operand_aliasing={{}: (2, {})} | custom-call | flops 184549376 | bytes 2883584 | tf_op jit(solution)/shard_map/gram/pallas_call | solution.py:24
  (72 shorter events, 29.9 us)
Async XLA Ops:
  0.6 8.3 %collective-permute-start.1 = (bf16[16,2048]{1,0:T(8,128)(2,1)}, bf16[16,2048]{1,0:T(8,128)(2,1)S(1)}, u32[]{:S(2)}, u32[]{:S(2)}) collective-permute-start(bf16[16,2048]{1,0:T(8,128)(2,1)} %refs_2_.1), channel_id=1, source_target_pairs={{0,4},{1,5},{2,6},{3,7},{4,0},{5,1},{6,2},{7,3},{8,12},{9,13},{10,... | collective-permute-start | bytes 196616 | tf_op jit(solution)/shard_map/ppermute | solution.py:20
  3.7 5.9 %collective-permute-start.2 = (bf16[16,2048]{1,0:T(8,128)(2,1)}, bf16[16,2048]{1,0:T(8,128)(2,1)S(1)}, u32[]{:S(2)}, u32[]{:S(2)}) collective-permute-start(bf16[16,2048]{1,0:T(8,128)(2,1)} %refs_2_.1), channel_id=1, source_target_pairs={{0,6},{1,7},{2,4},{3,5},{4,2},{5,3},{6,0},{7,1},{8,14},{9,15},{10,... | collective-permute-start | bytes 196616 | tf_op jit(solution)/shard_map/ppermute | solution.py:20
  5.2 4.9 %collective-permute-start.3 = (bf16[16,2048]{1,0:T(8,128)(2,1)}, bf16[16,2048]{1,0:T(8,128)(2,1)S(1)}, u32[]{:S(2)}, u32[]{:S(2)}) collective-permute-start(bf16[16,2048]{1,0:T(8,128)(2,1)} %refs_2_.1), channel_id=1, source_target_pairs={{0,1},{1,0},{2,3},{3,2},{4,5},{5,4},{6,7},{7,6},{8,9},{9,8},{10,11... | collective-permute-start | bytes 196616 | tf_op jit(solution)/shard_map/ppermute | solution.py:20
  12.7 9.3 %collective-permute-start.7 = (bf16[2,32,2176]{2,1,0:T(8,128)(2,1)S(1)}, bf16[2,32,2176]{2,1,0:T(8,128)(2,1)S(1)}, u32[]{:S(2)}, u32[]{:S(2)}) collective-permute-start(bf16[2,32,2176]{2,1,0:T(8,128)(2,1)S(1)} %get-tuple-element.32.refs_0_), channel_id=1, source_target_pairs={{0,8},{8,0},{16,24},{24,16},{1,9},{9,1},{17,25},{25,17},{2,10},{10... | collective-permute-start | bytes 835592 | tf_op jit(solution)/shard_map/ppermute | solution.py:20
  20.4 9.8 %collective-permute-start.9 = (bf16[2,32,2560]{2,1,0:T(8,128)(2,1)S(1)}, bf16[2,32,2560]{2,1,0:T(8,128)(2,1)S(1)}, u32[]{:S(2)}, u32[]{:S(2)}) collective-permute-start(bf16[2,32,2560]{2,1,0:T(8,128)(2,1)S(1)} %get-tuple-element.33.refs_0_), channel_id=1, source_target_pairs={{0,8},{8,0},{16,24},{24,16},{1,9},{9,1},{17,25},{25,17},{2,10},{10... | collective-permute-start | bytes 983048 | tf_op jit(solution)/shard_map/ppermute | solution.py:20
  27.7 15.8 %collective-permute-start.8 = (bf16[2,32,2560]{2,1,0:T(8,128)(2,1)S(1)}, bf16[2,32,2560]{2,1,0:T(8,128)(2,1)S(1)}, u32[]{:S(2)}, u32[]{:S(2)}) collective-permute-start(bf16[2,32,2560]{2,1,0:T(8,128)(2,1)S(1)} %get-tuple-element.35.refs_0_), channel_id=1, source_target_pairs={{0,8},{8,0},{16,24},{24,16},{1,9},{9,1},{17,25},{25,17},{2,10},{10... | collective-permute-start | bytes 983048 | tf_op jit(solution)/shard_map/ppermute | solution.py:20
  30.2 19.5 %collective-permute-start.12 = (bf16[32,2560]{1,0:T(8,128)(2,1)S(1)}, bf16[32,2560]{1,0:T(8,128)(2,1)S(1)}, u32[]{:S(2)}, u32[]{:S(2)}) collective-permute-start(bf16[32,2560]{1,0:T(8,128)(2,1)S(1)} %pair_total.4.refs_1_), channel_id=1, source_target_pairs={{0,16},{8,24},{16,0},{24,8},{1,17},{9,25},{17,1},{25,9},{2,18},{10... | collective-permute-start | bytes 491528 | tf_op jit(solution)/shard_map/ppermute | solution.py:20
  32.9 16.8 %collective-permute-start.11 = (bf16[32,2176]{1,0:T(8,128)(2,1)S(1)}, bf16[32,2176]{1,0:T(8,128)(2,1)S(1)}, u32[]{:S(2)}, u32[]{:S(2)}) collective-permute-start(bf16[32,2176]{1,0:T(8,128)(2,1)S(1)} %pair_total.3.refs_0_), channel_id=1, source_target_pairs={{0,16},{8,24},{16,0},{24,8},{1,17},{9,25},{17,1},{25,9},{2,18},{10... | collective-permute-start | bytes 417800 | tf_op jit(solution)/shard_map/ppermute | solution.py:20
  43.6 11.3 %collective-permute-start.10 = (bf16[32,2560]{1,0:T(8,128)(2,1)S(1)}, bf16[32,2560]{1,0:T(8,128)(2,1)S(1)}, u32[]{:S(2)}, u32[]{:S(2)}) collective-permute-start(bf16[32,2560]{1,0:T(8,128)(2,1)S(1)} %pair_total.5.refs_1_), channel_id=1, source_target_pairs={{0,16},{8,24},{16,0},{24,8},{1,17},{9,25},{17,1},{25,9},{2,18},{10... | collective-permute-start | bytes 491528 | tf_op jit(solution)/shard_map/ppermute | solution.py:20
  49.9 9.6 %collective-permute-start.17 = (bf16[32,2304]{1,0:T(8,128)(2,1)S(1)}, bf16[32,2304]{1,0:T(8,128)(2,1)S(1)}, u32[]{:S(2)}, u32[]{:S(2)}) collective-permute-start(bf16[32,2304]{1,0:T(8,128)(2,1)S(1)} %get-tuple-element.39.refs_0_), channel_id=1, source_target_pairs={{0,16},{8,24},{16,0},{24,8},{1,17},{9,25},{17,1},{25,9},{2,18},{10... | collective-permute-start | bytes 442376 | tf_op jit(solution)/shard_map/ppermute | solution.py:20
  50.7 18.0 %collective-permute-start.16 = (bf16[32,2304]{1,0:T(8,128)(2,1)S(1)}, bf16[32,2304]{1,0:T(8,128)(2,1)S(1)}, u32[]{:S(2)}, u32[]{:S(2)}) collective-permute-start(bf16[32,2304]{1,0:T(8,128)(2,1)S(1)} %get-tuple-element.39.refs_0_), channel_id=1, source_target_pairs={{0,8},{8,0},{16,24},{24,16},{1,9},{9,1},{17,25},{25,17},{2,10},{10... | collective-permute-start | bytes 442376 | tf_op jit(solution)/shard_map/ppermute | solution.py:20
  59.5 9.1 %collective-permute-start.18 = (bf16[32,2304]{1,0:T(8,128)(2,1)S(1)}, bf16[32,2304]{1,0:T(8,128)(2,1)S(1)}, u32[]{:S(2)}, u32[]{:S(2)}) collective-permute-start(bf16[32,2304]{1,0:T(8,128)(2,1)S(1)} %copy.15), channel_id=1, source_target_pairs={{0,8},{8,0},{16,24},{24,16},{1,9},{9,1},{17,25},{25,17},{2,10},{10... | collective-permute-start | bytes 442376 | tf_op jit(solution)/shard_map/ppermute | solution.py:20
  59.6 6.5 %collective-permute-start.14 = (bf16[32,1280]{1,0:T(8,128)(2,1)S(1)}, bf16[32,1280]{1,0:T(8,128)(2,1)S(1)}, u32[]{:S(2)}, u32[]{:S(2)}) collective-permute-start(bf16[32,1280]{1,0:T(8,128)(2,1)S(1)} %get-tuple-element.38.refs_0_), channel_id=1, source_target_pairs={{0,16},{8,24},{16,0},{24,8},{1,17},{9,25},{17,1},{25,9},{2,18},{10... | collective-permute-start | bytes 245768 | tf_op jit(solution)/shard_map/ppermute | solution.py:20
  62.9 7.3 %collective-permute-start.13 = (bf16[32,1280]{1,0:T(8,128)(2,1)S(1)}, bf16[32,1280]{1,0:T(8,128)(2,1)S(1)}, u32[]{:S(2)}, u32[]{:S(2)}) collective-permute-start(bf16[32,1280]{1,0:T(8,128)(2,1)S(1)} %get-tuple-element.38.refs_0_), channel_id=1, source_target_pairs={{0,8},{8,0},{16,24},{24,16},{1,9},{9,1},{17,25},{25,17},{2,10},{10... | collective-permute-start | bytes 245768 | tf_op jit(solution)/shard_map/ppermute | solution.py:20
  66.1 5.0 %collective-permute-start.15 = (bf16[32,1280]{1,0:T(8,128)(2,1)S(1)}, bf16[32,1280]{1,0:T(8,128)(2,1)S(1)}, u32[]{:S(2)}, u32[]{:S(2)}) collective-permute-start(bf16[32,1280]{1,0:T(8,128)(2,1)S(1)} %collective-permute-done.14.refs_2_), channel_id=1, source_target_pairs={{0,8},{8,0},{16,24},{24,16},{1,9},{9,1},{17,25},{25,17},{2,10},{10... | collective-permute-start | bytes 245768 | tf_op jit(solution)/shard_map/ppermute | solution.py:20
  73.3 5.3 %collective-permute-start.20 = (bf16[128,256]{1,0:T(8,128)(2,1)S(1)}, bf16[128,256]{1,0:T(8,128)(2,1)S(1)}, u32[]{:S(2)}, u32[]{:S(2)}) collective-permute-start(bf16[128,256]{1,0:T(8,128)(2,1)S(1)} %get-tuple-element.41), channel_id=1, source_target_pairs={{0,6},{1,7},{2,4},{3,5},{4,2},{5,3},{6,0},{7,1},{8,14},{9,15},{10,... | collective-permute-start | bytes 196616 | tf_op jit(solution)/shard_map/ppermute | solution.py:20
  80.6 5.9 %collective-permute-start.26 = (bf16[128,256]{1,0:T(8,128)(2,1)S(1)}, bf16[128,256]{1,0:T(8,128)(2,1)S(1)}, u32[]{:S(2)}, u32[]{:S(2)}) collective-permute-start(bf16[128,256]{1,0:T(8,128)(2,1)S(1)} %add_convert_fusion.own_ref), channel_id=1, source_target_pairs={{0,6},{1,7},{2,4},{3,5},{4,2},{5,3},{6,0},{7,1},{8,14},{9,15},{10,... | collective-permute-start | bytes 196616 | tf_op jit(solution)/shard_map/ppermute | solution.py:20
  82.2 6.3 %collective-permute-start.25 = (bf16[128,256]{1,0:T(8,128)(2,1)S(1)}, bf16[128,256]{1,0:T(8,128)(2,1)S(1)}, u32[]{:S(2)}, u32[]{:S(2)}) collective-permute-start(bf16[128,256]{1,0:T(8,128)(2,1)S(1)} %add_convert_fusion.own_ref), channel_id=1, source_target_pairs={{0,24},{8,16},{16,8},{24,0},{1,25},{9,17},{17,9},{25,1},{2,26},{10... | collective-permute-start | bytes 196616 | tf_op jit(solution)/shard_map/ppermute | solution.py:20
  84.1 6.4 %collective-permute-start.24 = (bf16[128,256]{1,0:T(8,128)(2,1)S(1)}, bf16[128,256]{1,0:T(8,128)(2,1)S(1)}, u32[]{:S(2)}, u32[]{:S(2)}) collective-permute-start(bf16[128,256]{1,0:T(8,128)(2,1)S(1)} %add_convert_fusion.own_ref), channel_id=1, source_target_pairs={{0,16},{8,24},{16,0},{24,8},{1,17},{9,25},{17,1},{25,9},{2,18},{10... | collective-permute-start | bytes 196616 | tf_op jit(solution)/shard_map/ppermute | solution.py:20
  90.6 11.0 %collective-permute-start.28 = (bf16[4,128,256]{2,1,0:T(8,128)(2,1)S(1)}, bf16[4,128,256]{2,1,0:T(8,128)(2,1)S(1)}, u32[]{:S(2)}, u32[]{:S(2)}) collective-permute-start(bf16[4,128,256]{2,1,0:T(8,128)(2,1)S(1)} %stack.2.refs_0_), channel_id=1, source_target_pairs={{0,4},{1,5},{2,6},{3,7},{4,0},{5,1},{6,2},{7,3},{8,12},{9,13},{10,... | collective-permute-start | bytes 786440 | tf_op jit(solution)/shard_map/ppermute | solution.py:20
  92.4 9.2 %collective-permute-start.27 = (bf16[4,128,256]{2,1,0:T(8,128)(2,1)S(1)}, bf16[4,128,256]{2,1,0:T(8,128)(2,1)S(1)}, u32[]{:S(2)}, u32[]{:S(2)}) collective-permute-start(bf16[4,128,256]{2,1,0:T(8,128)(2,1)S(1)} %stack.2.refs_0_), channel_id=1, source_target_pairs={{0,2},{1,3},{2,0},{3,1},{4,6},{5,7},{6,4},{7,5},{8,10},{9,11},{10,... | collective-permute-start | bytes 786440 | tf_op jit(solution)/shard_map/ppermute | solution.py:20
  92.5 6.9 %collective-permute-start.31 = (bf16[128,256]{1,0:T(8,128)(2,1)S(1)}, bf16[128,256]{1,0:T(8,128)(2,1)S(1)}, u32[]{:S(2)}, u32[]{:S(2)}) collective-permute-start(bf16[128,256]{1,0:T(8,128)(2,1)S(1)} %collective-permute-done.26.refs_4_), channel_id=1, source_target_pairs={{0,24},{8,16},{16,8},{24,0},{1,25},{9,17},{17,9},{25,1},{2,26},{10... | collective-permute-start | bytes 196616 | tf_op jit(solution)/shard_map/ppermute | solution.py:20
  94.4 7.2 %collective-permute-start.30 = (bf16[128,256]{1,0:T(8,128)(2,1)S(1)}, bf16[128,256]{1,0:T(8,128)(2,1)S(1)}, u32[]{:S(2)}, u32[]{:S(2)}) collective-permute-start(bf16[128,256]{1,0:T(8,128)(2,1)S(1)} %collective-permute-done.26.refs_4_), channel_id=1, source_target_pairs={{0,16},{8,24},{16,0},{24,8},{1,17},{9,25},{17,1},{25,9},{2,18},{10... | collective-permute-start | bytes 196616 | tf_op jit(solution)/shard_map/ppermute | solution.py:20
  94.7 6.9 %collective-permute-start.29 = (bf16[128,256]{1,0:T(8,128)(2,1)S(1)}, bf16[128,256]{1,0:T(8,128)(2,1)S(1)}, u32[]{:S(2)}, u32[]{:S(2)}) collective-permute-start(bf16[128,256]{1,0:T(8,128)(2,1)S(1)} %collective-permute-done.26.refs_4_), channel_id=1, source_target_pairs={{0,8},{8,0},{16,24},{24,16},{1,9},{9,1},{17,25},{25,17},{2,10},{10... | collective-permute-start | bytes 196616 | tf_op jit(solution)/shard_map/ppermute | solution.py:20
  (12 other events, 58.6 us)

commit v9 on v6

--- a/solution.py
+++ b/solution.py
@@ -209,9 +209,9 @@
     )
 
 
-def down_kernel(masks, skip, panel, n_blocks, *refs):
+def down_kernel(masks, panel, n_blocks, add, *refs):
     blocks, weight, lhs, out = refs[:n_blocks], refs[n_blocks], refs[-1], refs[-2]
-    before = refs[n_blocks + 1] if len(refs) == n_blocks + 4 else None
+    before = refs[n_blocks + 1] if add else None
     z = lax.axis_index("tok")
     h = lax.axis_index("hid")
     rows = blocks[0].shape[0]
@@ -222,18 +222,19 @@
         column = pl.multiple_of((h ^ mask) * panel, panel)
         total = jnp.dot(values, weight[:, pl.ds(column, panel)], preferred_element_type=F32)
         if before is not None:
-            total = total + before[skip + slot]
+            total = total + before[slot]
         out[slot] = total.astype(out.dtype)
 
 
-def down(blocks, weight, masks, panel, kind, before=None, skip=0):
+def down(blocks, weight, masks, panel, kind, before=None, after=()):
     rows, depth = blocks[0].shape
     ntok = rows * len(blocks)
     return run(
-        functools.partial(down_kernel, masks, skip, panel, len(blocks)), "down",
+        functools.partial(down_kernel, masks, panel, len(blocks), before is not None), "down",
         jax.ShapeDtypeStruct((len(masks), ntok, panel), kind),
-        [*blocks, weight] + ([] if before is None else [before]),
+        [*blocks, weight] + ([] if before is None else [before]) + list(after),
         2 * ntok * depth * panel * len(masks), 2 * depth * panel * len(masks),
+        in_specs=[WHOLE] * (len(blocks) + 1 + (before is not None)) + [ANYWHERE] * len(after),
         scratch_shapes=[pltpu.VMEM((ntok, depth), BF16)],
     )
 
@@ -362,17 +363,16 @@
     b_own, _ = hidden_rows([(keep_2, got_2, over_2)], widths[2:], scale, ())
     b_two = swap(b_own, "tok", n_tok, 2)
     b_one = swap(b_own, "tok", n_tok, 1)
-    a_three = swap(copy_after(a_two, (b_own,)), "tok", n_tok, 1)
+    a_three = swap(copy_after(a_two, (b_two, b_one, a_one)), "tok", n_tok, 1)
     b_three = swap(b_two, "tok", n_tok, 1)
     hidden_a = [a_own, a_one, a_two, a_three]
     hidden_b = [b_own, b_one, b_two, b_three]
 
     here = [0] + chip_masks
     there = [mask + 1 for mask in here]
-    first = down(hidden_a, down_a, there + here, panel, F32)
-    other = down(hidden_b, down_b, there, panel, BF16, first, 0)
+    other = down(hidden_b, down_b, there, panel, BF16, down(hidden_a, down_a, there, panel, F32))
+    mine = down(hidden_b, down_b, here, panel, F32, down(hidden_a, down_a, here, panel, F32, after=(other,)))
     other = swap(other, "hid", n_hid, 1)
-    mine = down(hidden_b, down_b, here, panel, F32, first, len(there))
     summed, *sends = run(
         chip_sum_kernel, "chip_sum",
         [jax.ShapeDtypeStruct((ntok, panel), F32)] + [jax.ShapeDtypeStruct((ntok, panel), BF16)] * len(chip_masks),

time: 106 us -> 106 us (level)
  starting transfers between devices: 39.1 us -> 42.1 us
  waiting for transfers between devices: 32.3 us -> 29.6 us
    ppermute x35, starting transfers between devices: 39.1 us -> 42.1 us  [swap(): return lax.ppermute(value, axis, [(i, i ^ mask) for i in range(size)])]
    ppermute x35, waiting for transfers between devices: 32.3 us -> 29.6 us  [swap(): return lax.ppermute(value, axis, [(i, i ^ mask) for i in range(size)])]
    pallas_call x25 -> x26, Pallas kernels: 33.6 us -> 33.8 us  [run(): pl.pallas_call(body, out_shape=out_shape, in_specs=[WHOLE] * len(operands...]
where the time goes in v9:
time: 106 us
  starting transfers between devices  42.1 us (40%)
  Pallas kernels  33.8 us (32%)
  waiting for transfers between devices  29.6 us (28%)
    ppermute x35, starting transfers between devices, swap(): return lax.ppermute(value, axis, [(i, i ^ mask) for i in range(size)])  42.1 us
    pallas_call x26, Pallas kernels, run(): pl.pallas_call(body, out_shape=out_shape, in_specs=[WHOLE] * len(operands...  33.8 us
    ppermute x35, waiting for transfers between devices, swap(): return lax.ppermute(value, axis, [(i, i ^ mask) for i in range(size)])  29.6 us
  transfers between devices with their start and end apart: 35, of which 19 were waited for; matrix products, arithmetic and copies ran while one was open for 0% of the time, Pallas kernels for 28%

profile of v9, /device:TPU:0, one launch (start us, length us, event | category | flops | bytes accessed | tf_op | source)
XLA Modules:
  0.0 106.3 jit_solution(6067223954527072178)
XLA Ops:
  0.6 3.0 %collective-permute-start.1 = (bf16[16,2048]{1,0:T(8,128)(2,1)}, bf16[16,2048]{1,0:T(8,128)(2,1)S(1)}, u32[]{:S(2)}, u32[]{:S(2)}) collective-permute-start(bf16[16,2048]{1,0:T(8,128)(2,1)} %refs_2_.1), channel_id=1, source_target_pairs={{0,4},{1,5},{2,6},{3,7},{4,0},{5,1},{6,2},{7,3},{8,12},{9,13},{10,... | collective-permute-start | bytes 196616 | tf_op jit(solution)/shard_map/ppermute | solution.py:20
  5.2 3.7 %fetch_first.1 = (bf16[2048,1024]{1,0:T(8,128)(2,1)S(1)}, bf16[2048,1024]{1,0:T(8,128)(2,1)S(1)}, bf16[16,2048]{1,0:T(8,128)(2,1)S(1)}, f32[1,2048]{1,0:T(1,128)S(1)}) custom-call(bf16[2048,3584]{1,0:T(8,128)(2,1)} %refs_0_.7, bf16[2048,3584]{1,0:T(8,128)(2,1)} %refs_1_.5, bf16[16,2048]{1,0:T(8,128)(2,1)} %refs_2_.1, f32[1,2048]{1,0:T(1,128)} %bitcast.22), custom_call_target="tpu_custom_call" | custom-call | tf_op jit(solution)/shard_map/fetch_first/pallas_call | solution.py:24
  12.7 2.1 %collective-permute-start.7 = (bf16[2,32,2176]{2,1,0:T(8,128)(2,1)S(1)}, bf16[2,32,2176]{2,1,0:T(8,128)(2,1)S(1)}, u32[]{:S(2)}, u32[]{:S(2)}) collective-permute-start(bf16[2,32,2176]{2,1,0:T(8,128)(2,1)S(1)} %get-tuple-element.36.refs_2_), channel_id=1, source_target_pairs={{0,8},{8,0},{16,24},{24,16},{1,9},{9,1},{17,25},{25,17},{2,10},{10... | collective-permute-start | bytes 835592 | tf_op jit(solution)/shard_map/ppermute | solution.py:20
  14.8 4.3 %fetch_gate_up.2 = (bf16[2048,1280]{1,0:T(8,128)(2,1)S(1)}, bf16[2048,1280]{1,0:T(8,128)(2,1)S(1)}) custom-call(bf16[2048,3584]{1,0:T(8,128)(2,1)} %refs_0_.7, bf16[2048,3584]{1,0:T(8,128)(2,1)} %refs_1_.5, bf16[2,32,2176]{2,1,0:T(8,128)(2,1)S(1)} %get-tuple-element.36.refs_2_), custom_call_target="tpu_custom_call" | custom-call | tf_op jit(solution)/shard_map/fetch_gate_up/pallas_call | solution.py:24
  22.1 4.3 %fetch_gate_up.3 = (bf16[2048,1280]{1,0:T(8,128)(2,1)S(1)}, bf16[2048,1280]{1,0:T(8,128)(2,1)S(1)}) custom-call(bf16[2048,3584]{1,0:T(8,128)(2,1)} %refs_0_.7, bf16[2048,3584]{1,0:T(8,128)(2,1)} %refs_1_.5, bf16[32,2176]{1,0:T(8,128)(2,1)S(1)} %pair_total.3.refs_2_), custom_call_target="tpu_custom_call" | custom-call | tf_op jit(solution)/shard_map/fetch_gate_up/pallas_call | solution.py:24
  28.0 1.8 %collective-permute-start.8 = (bf16[2,32,2560]{2,1,0:T(8,128)(2,1)S(1)}, bf16[2,32,2560]{2,1,0:T(8,128)(2,1)S(1)}, u32[]{:S(2)}, u32[]{:S(2)}) collective-permute-start(bf16[2,32,2560]{2,1,0:T(8,128)(2,1)S(1)} %get-tuple-element.43.refs_0_), channel_id=1, source_target_pairs={{0,8},{8,0},{16,24},{24,16},{1,9},{9,1},{17,25},{25,17},{2,10},{10... | collective-permute-start | bytes 983048 | tf_op jit(solution)/shard_map/ppermute | solution.py:20
  30.5 2.7 %collective-permute-start.12 = (bf16[32,2560]{1,0:T(8,128)(2,1)S(1)}, bf16[32,2560]{1,0:T(8,128)(2,1)S(1)}, u32[]{:S(2)}, u32[]{:S(2)}) collective-permute-start(bf16[32,2560]{1,0:T(8,128)(2,1)S(1)} %pair_total.4.refs_1_), channel_id=1, source_target_pairs={{0,16},{8,24},{16,0},{24,8},{1,17},{9,25},{17,1},{25,9},{2,18},{10... | collective-permute-start | bytes 491528 | tf_op jit(solution)/shard_map/ppermute | solution.py:20
  33.5 2.5 %fetch_down.2.refs_0_.refs_4_ = bf16[1280,2048]{1,0:T(8,128)(2,1)S(1)} custom-call(bf16[3584,2048]{1,0:T(8,128)(2,1)} %refs_0_.9, bf16[32,2560]{1,0:T(8,128)(2,1)S(1)} %pair_total.4.refs_1_), custom_call_target="tpu_custom_call" | custom-call | tf_op jit(solution)/shard_map/fetch_down/pallas_call | solution.py:24
  36.0 7.8 %collective-permute-done.8.got_ref.refs_1_ = bf16[2,32,2560]{2,1,0:T(8,128)(2,1)S(1)} collective-permute-done((bf16[2,32,2560]{2,1,0:T(8,128)(2,1)S(1)}, bf16[2,32,2560]{2,1,0:T(8,128)(2,1)S(1)}, u32[]{:S(2)}, u32[]{:S(2)}) %collective-permute-start.8) | collective-permute-done | bytes 327712 | tf_op jit(solution)/shard_map/ppermute | solution.py:20
  44.3 3.8 %fetch_down.3.refs_6_.refs_4_ = bf16[2304,2048]{1,0:T(8,128)(2,1)S(1)} custom-call(bf16[3584,2048]{1,0:T(8,128)(2,1)} %refs_0_.9, bf16[32,2560]{1,0:T(8,128)(2,1)S(1)} %pair_total.5.refs_1_), custom_call_target="tpu_custom_call" | custom-call | tf_op jit(solution)/shard_map/fetch_down/pallas_call | solution.py:24
  48.1 1.9 %collective-permute-done.11.refs_2_ = bf16[32,2176]{1,0:T(8,128)(2,1)S(1)} collective-permute-done((bf16[32,2176]{1,0:T(8,128)(2,1)S(1)}, bf16[32,2176]{1,0:T(8,128)(2,1)S(1)}, u32[]{:S(2)}, u32[]{:S(2)}) %collective-permute-start.11) | collective-permute-done | bytes 139296 | tf_op jit(solution)/shard_map/ppermute | solution.py:20
  50.9 3.3 %collective-permute-start.16 = (bf16[32,2304]{1,0:T(8,128)(2,1)S(1)}, bf16[32,2304]{1,0:T(8,128)(2,1)S(1)}, u32[]{:S(2)}, u32[]{:S(2)}) collective-permute-start(bf16[32,2304]{1,0:T(8,128)(2,1)S(1)} %get-tuple-element.47.refs_0_), channel_id=1, source_target_pairs={{0,8},{8,0},{16,24},{24,16},{1,9},{9,1},{17,25},{25,17},{2,10},{10... | collective-permute-start | bytes 442376 | tf_op jit(solution)/shard_map/ppermute | solution.py:20
  55.7 5.7 %collective-permute-start.13 = (bf16[32,1280]{1,0:T(8,128)(2,1)S(1)}, bf16[32,1280]{1,0:T(8,128)(2,1)S(1)}, u32[]{:S(2)}, u32[]{:S(2)}) collective-permute-start(bf16[32,1280]{1,0:T(8,128)(2,1)S(1)} %get-tuple-element.46.refs_0_), channel_id=1, source_target_pairs={{0,8},{8,0},{16,24},{24,16},{1,9},{9,1},{17,25},{25,17},{2,10},{10... | collective-permute-start | bytes 245768 | tf_op jit(solution)/shard_map/ppermute | solution.py:20
  63.9 2.5 %collective-permute-start.18 = (bf16[32,2304]{1,0:T(8,128)(2,1)S(1)}, bf16[32,2304]{1,0:T(8,128)(2,1)S(1)}, u32[]{:S(2)}, u32[]{:S(2)}) collective-permute-start(bf16[32,2304]{1,0:T(8,128)(2,1)S(1)} %copy.15), channel_id=1, source_target_pairs={{0,8},{8,0},{16,24},{24,16},{1,9},{9,1},{17,25},{25,17},{2,10},{10... | collective-permute-start | bytes 442376 | tf_op jit(solution)/shard_map/ppermute | solution.py:20
  66.5 3.0 %collective-permute-done.18.refs_3_ = bf16[32,2304]{1,0:T(8,128)(2,1)S(1)} collective-permute-done((bf16[32,2304]{1,0:T(8,128)(2,1)S(1)}, bf16[32,2304]{1,0:T(8,128)(2,1)S(1)}, u32[]{:S(2)}, u32[]{:S(2)}) %collective-permute-start.18) | collective-permute-done | bytes 147488 | tf_op jit(solution)/shard_map/ppermute | solution.py:20
  73.1 3.1 %collective-permute-start.20 = (bf16[128,256]{1,0:T(8,128)(2,1)S(1)}, bf16[128,256]{1,0:T(8,128)(2,1)S(1)}, u32[]{:S(2)}, u32[]{:S(2)}) collective-permute-start(bf16[128,256]{1,0:T(8,128)(2,1)S(1)} %get-tuple-element.49), channel_id=1, source_target_pairs={{0,6},{1,7},{2,4},{3,5},{4,2},{5,3},{6,0},{7,1},{8,14},{9,15},{10,... | collective-permute-start | bytes 196616 | tf_op jit(solution)/shard_map/ppermute | solution.py:20
  76.8 2.1 %collective-permute-done.20 = bf16[128,256]{1,0:T(8,128)(2,1)S(1)} collective-permute-done((bf16[128,256]{1,0:T(8,128)(2,1)S(1)}, bf16[128,256]{1,0:T(8,128)(2,1)S(1)}, u32[]{:S(2)}, u32[]{:S(2)}) %collective-permute-start.20) | collective-permute-done | bytes 65568 | tf_op jit(solution)/shard_map/ppermute | solution.py:20
  83.9 1.8 %collective-permute-start.24 = (bf16[128,256]{1,0:T(8,128)(2,1)S(1)}, bf16[128,256]{1,0:T(8,128)(2,1)S(1)}, u32[]{:S(2)}, u32[]{:S(2)}) collective-permute-start(bf16[128,256]{1,0:T(8,128)(2,1)S(1)} %add_convert_fusion.own_ref), channel_id=1, source_target_pairs={{0,16},{8,24},{16,0},{24,8},{1,17},{9,25},{17,1},{25,9},{2,18},{10... | collective-permute-start | bytes 196616 | tf_op jit(solution)/shard_map/ppermute | solution.py:20
  88.8 2.0 %collective-permute-done.24 = bf16[128,256]{1,0:T(8,128)(2,1)S(1)} collective-permute-done((bf16[128,256]{1,0:T(8,128)(2,1)S(1)}, bf16[128,256]{1,0:T(8,128)(2,1)S(1)}, u32[]{:S(2)}, u32[]{:S(2)}) %collective-permute-start.24) | collective-permute-done | bytes 65568 | tf_op jit(solution)/shard_map/ppermute | solution.py:20
  94.8 2.7 %collective-permute-start.29 = (bf16[128,256]{1,0:T(8,128)(2,1)S(1)}, bf16[128,256]{1,0:T(8,128)(2,1)S(1)}, u32[]{:S(2)}, u32[]{:S(2)}) collective-permute-start(bf16[128,256]{1,0:T(8,128)(2,1)S(1)} %collective-permute-done.26.refs_4_), channel_id=1, source_target_pairs={{0,8},{8,0},{16,24},{24,16},{1,9},{9,1},{17,25},{25,17},{2,10},{10... | collective-permute-start | bytes 196616 | tf_op jit(solution)/shard_map/ppermute | solution.py:20
  97.5 2.4 %gram.3 = (f32[256,8192]{1,0:T(8,128)}, f32[64,256]{1,0:T(8,128)}) custom-call(bf16[128,256]{1,0:T(8,128)(2,1)S(1)} %add_convert_fusion.own_ref, bf16[4,128,256]{2,1,0:T(8,128)(2,1)S(1)} %stack.2.refs_0_, bf16[4,128,256]{2,1,0:T(8,128)(2,1)S(1)} %collective-permute-done.32.refs_1_, bf16[1,128,256]{2,1,0:T(8,128)(2,1)S(1)} %bitcast.13, ...), custom_call_target="tpu_custom_call" | custom-call | flops 167772160 | bytes 2621440 | tf_op jit(solution)/shard_map/gram/pallas_call | solution.py:24
  100.0 2.2 %collective-permute-done.30 = bf16[128,256]{1,0:T(8,128)(2,1)S(1)} collective-permute-done((bf16[128,256]{1,0:T(8,128)(2,1)S(1)}, bf16[128,256]{1,0:T(8,128)(2,1)S(1)}, u32[]{:S(2)}, u32[]{:S(2)}) %collective-permute-start.30) | collective-permute-done | bytes 65568 | tf_op jit(solution)/shard_map/ppermute | solution.py:20
  102.3 1.9 %gram.4.refs_1_ = f32[256,8192]{1,0:T(8,128)} custom-call(bf16[128,256]{1,0:T(8,128)(2,1)S(1)} %add_convert_fusion.own_ref, bf16[11,128,256]{2,1,0:T(8,128)(2,1)S(1)} %stack.3.refs_0_, f32[256,8192]{1,0:T(8,128)} %get-tuple-element.52.refs_5_.refs_1_), custom_call_target="tpu_custom_call", output_to_operand_aliasing={{}: (2, {})} | custom-call | flops 184549376 | bytes 2883584 | tf_op jit(solution)/shard_map/gram/pallas_call | solution.py:24
  104.5 1.9 %gram.5 = f32[256,8192]{1,0:T(8,128)} custom-call(bf16[128,256]{1,0:T(8,128)(2,1)S(1)} %add_convert_fusion.own_ref, bf16[11,128,256]{2,1,0:T(8,128)(2,1)S(1)} %collective-permute-done.34.refs_0_, f32[256,8192]{1,0:T(8,128)} %gram.4.refs_1_), custom_call_target="tpu_custom_call", output_to_operand_aliasing={{}: (2, {})} | custom-call | flops 184549376 | bytes 2883584 | tf_op jit(solution)/shard_map/gram/pallas_call | solution.py:24
  (75 shorter events, 32.9 us)
Async XLA Ops:
  0.6 8.3 %collective-permute-start.1 = (bf16[16,2048]{1,0:T(8,128)(2,1)}, bf16[16,2048]{1,0:T(8,128)(2,1)S(1)}, u32[]{:S(2)}, u32[]{:S(2)}) collective-permute-start(bf16[16,2048]{1,0:T(8,128)(2,1)} %refs_2_.1), channel_id=1, source_target_pairs={{0,4},{1,5},{2,6},{3,7},{4,0},{5,1},{6,2},{7,3},{8,12},{9,13},{10,... | collective-permute-start | bytes 196616 | tf_op jit(solution)/shard_map/ppermute | solution.py:20
  3.7 5.9 %collective-permute-start.2 = (bf16[16,2048]{1,0:T(8,128)(2,1)}, bf16[16,2048]{1,0:T(8,128)(2,1)S(1)}, u32[]{:S(2)}, u32[]{:S(2)}) collective-permute-start(bf16[16,2048]{1,0:T(8,128)(2,1)} %refs_2_.1), channel_id=1, source_target_pairs={{0,6},{1,7},{2,4},{3,5},{4,2},{5,3},{6,0},{7,1},{8,14},{9,15},{10,... | collective-permute-start | bytes 196616 | tf_op jit(solution)/shard_map/ppermute | solution.py:20
  5.2 4.9 %collective-permute-start.3 = (bf16[16,2048]{1,0:T(8,128)(2,1)}, bf16[16,2048]{1,0:T(8,128)(2,1)S(1)}, u32[]{:S(2)}, u32[]{:S(2)}) collective-permute-start(bf16[16,2048]{1,0:T(8,128)(2,1)} %refs_2_.1), channel_id=1, source_target_pairs={{0,1},{1,0},{2,3},{3,2},{4,5},{5,4},{6,7},{7,6},{8,9},{9,8},{10,11... | collective-permute-start | bytes 196616 | tf_op jit(solution)/shard_map/ppermute | solution.py:20
  12.7 9.3 %collective-permute-start.7 = (bf16[2,32,2176]{2,1,0:T(8,128)(2,1)S(1)}, bf16[2,32,2176]{2,1,0:T(8,128)(2,1)S(1)}, u32[]{:S(2)}, u32[]{:S(2)}) collective-permute-start(bf16[2,32,2176]{2,1,0:T(8,128)(2,1)S(1)} %get-tuple-element.36.refs_2_), channel_id=1, source_target_pairs={{0,8},{8,0},{16,24},{24,16},{1,9},{9,1},{17,25},{25,17},{2,10},{10... | collective-permute-start | bytes 835592 | tf_op jit(solution)/shard_map/ppermute | solution.py:20
  20.7 9.8 %collective-permute-start.9 = (bf16[2,32,2560]{2,1,0:T(8,128)(2,1)S(1)}, bf16[2,32,2560]{2,1,0:T(8,128)(2,1)S(1)}, u32[]{:S(2)}, u32[]{:S(2)}) collective-permute-start(bf16[2,32,2560]{2,1,0:T(8,128)(2,1)S(1)} %get-tuple-element.39.refs_0_), channel_id=1, source_target_pairs={{0,8},{8,0},{16,24},{24,16},{1,9},{9,1},{17,25},{25,17},{2,10},{10... | collective-permute-start | bytes 983048 | tf_op jit(solution)/shard_map/ppermute | solution.py:20
  28.0 15.8 %collective-permute-start.8 = (bf16[2,32,2560]{2,1,0:T(8,128)(2,1)S(1)}, bf16[2,32,2560]{2,1,0:T(8,128)(2,1)S(1)}, u32[]{:S(2)}, u32[]{:S(2)}) collective-permute-start(bf16[2,32,2560]{2,1,0:T(8,128)(2,1)S(1)} %get-tuple-element.43.refs_0_), channel_id=1, source_target_pairs={{0,8},{8,0},{16,24},{24,16},{1,9},{9,1},{17,25},{25,17},{2,10},{10... | collective-permute-start | bytes 983048 | tf_op jit(solution)/shard_map/ppermute | solution.py:20
  30.5 19.5 %collective-permute-start.12 = (bf16[32,2560]{1,0:T(8,128)(2,1)S(1)}, bf16[32,2560]{1,0:T(8,128)(2,1)S(1)}, u32[]{:S(2)}, u32[]{:S(2)}) collective-permute-start(bf16[32,2560]{1,0:T(8,128)(2,1)S(1)} %pair_total.4.refs_1_), channel_id=1, source_target_pairs={{0,16},{8,24},{16,0},{24,8},{1,17},{9,25},{17,1},{25,9},{2,18},{10... | collective-permute-start | bytes 491528 | tf_op jit(solution)/shard_map/ppermute | solution.py:20
  33.2 16.8 %collective-permute-start.11 = (bf16[32,2176]{1,0:T(8,128)(2,1)S(1)}, bf16[32,2176]{1,0:T(8,128)(2,1)S(1)}, u32[]{:S(2)}, u32[]{:S(2)}) collective-permute-start(bf16[32,2176]{1,0:T(8,128)(2,1)S(1)} %pair_total.3.refs_2_), channel_id=1, source_target_pairs={{0,16},{8,24},{16,0},{24,8},{1,17},{9,25},{17,1},{25,9},{2,18},{10... | collective-permute-start | bytes 417800 | tf_op jit(solution)/shard_map/ppermute | solution.py:20
  43.9 11.2 %collective-permute-start.10 = (bf16[32,2560]{1,0:T(8,128)(2,1)S(1)}, bf16[32,2560]{1,0:T(8,128)(2,1)S(1)}, u32[]{:S(2)}, u32[]{:S(2)}) collective-permute-start(bf16[32,2560]{1,0:T(8,128)(2,1)S(1)} %pair_total.5.refs_1_), channel_id=1, source_target_pairs={{0,16},{8,24},{16,0},{24,8},{1,17},{9,25},{17,1},{25,9},{2,18},{10... | collective-permute-start | bytes 491528 | tf_op jit(solution)/shard_map/ppermute | solution.py:20
  50.2 11.2 %collective-permute-start.17 = (bf16[32,2304]{1,0:T(8,128)(2,1)S(1)}, bf16[32,2304]{1,0:T(8,128)(2,1)S(1)}, u32[]{:S(2)}, u32[]{:S(2)}) collective-permute-start(bf16[32,2304]{1,0:T(8,128)(2,1)S(1)} %get-tuple-element.47.refs_0_), channel_id=1, source_target_pairs={{0,16},{8,24},{16,0},{24,8},{1,17},{9,25},{17,1},{25,9},{2,18},{10... | collective-permute-start | bytes 442376 | tf_op jit(solution)/shard_map/ppermute | solution.py:20
  50.9 10.5 %collective-permute-start.16 = (bf16[32,2304]{1,0:T(8,128)(2,1)S(1)}, bf16[32,2304]{1,0:T(8,128)(2,1)S(1)}, u32[]{:S(2)}, u32[]{:S(2)}) collective-permute-start(bf16[32,2304]{1,0:T(8,128)(2,1)S(1)} %get-tuple-element.47.refs_0_), channel_id=1, source_target_pairs={{0,8},{8,0},{16,24},{24,16},{1,9},{9,1},{17,25},{25,17},{2,10},{10... | collective-permute-start | bytes 442376 | tf_op jit(solution)/shard_map/ppermute | solution.py:20
  55.7 6.7 %collective-permute-start.14 = (bf16[32,1280]{1,0:T(8,128)(2,1)S(1)}, bf16[32,1280]{1,0:T(8,128)(2,1)S(1)}, u32[]{:S(2)}, u32[]{:S(2)}) collective-permute-start(bf16[32,1280]{1,0:T(8,128)(2,1)S(1)} %get-tuple-element.46.refs_0_), channel_id=1, source_target_pairs={{0,16},{8,24},{16,0},{24,8},{1,17},{9,25},{17,1},{25,9},{2,18},{10... | collective-permute-start | bytes 245768 | tf_op jit(solution)/shard_map/ppermute | solution.py:20
  55.7 8.1 %collective-permute-start.13 = (bf16[32,1280]{1,0:T(8,128)(2,1)S(1)}, bf16[32,1280]{1,0:T(8,128)(2,1)S(1)}, u32[]{:S(2)}, u32[]{:S(2)}) collective-permute-start(bf16[32,1280]{1,0:T(8,128)(2,1)S(1)} %get-tuple-element.46.refs_0_), channel_id=1, source_target_pairs={{0,8},{8,0},{16,24},{24,16},{1,9},{9,1},{17,25},{25,17},{2,10},{10... | collective-permute-start | bytes 245768 | tf_op jit(solution)/shard_map/ppermute | solution.py:20
  63.9 5.7 %collective-permute-start.18 = (bf16[32,2304]{1,0:T(8,128)(2,1)S(1)}, bf16[32,2304]{1,0:T(8,128)(2,1)S(1)}, u32[]{:S(2)}, u32[]{:S(2)}) collective-permute-start(bf16[32,2304]{1,0:T(8,128)(2,1)S(1)} %copy.15), channel_id=1, source_target_pairs={{0,8},{8,0},{16,24},{24,16},{1,9},{9,1},{17,25},{25,17},{2,10},{10... | collective-permute-start | bytes 442376 | tf_op jit(solution)/shard_map/ppermute | solution.py:20
  73.1 5.8 %collective-permute-start.20 = (bf16[128,256]{1,0:T(8,128)(2,1)S(1)}, bf16[128,256]{1,0:T(8,128)(2,1)S(1)}, u32[]{:S(2)}, u32[]{:S(2)}) collective-permute-start(bf16[128,256]{1,0:T(8,128)(2,1)S(1)} %get-tuple-element.49), channel_id=1, source_target_pairs={{0,6},{1,7},{2,4},{3,5},{4,2},{5,3},{6,0},{7,1},{8,14},{9,15},{10,... | collective-permute-start | bytes 196616 | tf_op jit(solution)/shard_map/ppermute | solution.py:20
  81.0 6.1 %collective-permute-start.26 = (bf16[128,256]{1,0:T(8,128)(2,1)S(1)}, bf16[128,256]{1,0:T(8,128)(2,1)S(1)}, u32[]{:S(2)}, u32[]{:S(2)}) collective-permute-start(bf16[128,256]{1,0:T(8,128)(2,1)S(1)} %add_convert_fusion.own_ref), channel_id=1, source_target_pairs={{0,6},{1,7},{2,4},{3,5},{4,2},{5,3},{6,0},{7,1},{8,14},{9,15},{10,... | collective-permute-start | bytes 196616 | tf_op jit(solution)/shard_map/ppermute | solution.py:20
  82.6 6.2 %collective-permute-start.25 = (bf16[128,256]{1,0:T(8,128)(2,1)S(1)}, bf16[128,256]{1,0:T(8,128)(2,1)S(1)}, u32[]{:S(2)}, u32[]{:S(2)}) collective-permute-start(bf16[128,256]{1,0:T(8,128)(2,1)S(1)} %add_convert_fusion.own_ref), channel_id=1, source_target_pairs={{0,24},{8,16},{16,8},{24,0},{1,25},{9,17},{17,9},{25,1},{2,26},{10... | collective-permute-start | bytes 196616 | tf_op jit(solution)/shard_map/ppermute | solution.py:20
  83.9 7.0 %collective-permute-start.24 = (bf16[128,256]{1,0:T(8,128)(2,1)S(1)}, bf16[128,256]{1,0:T(8,128)(2,1)S(1)}, u32[]{:S(2)}, u32[]{:S(2)}) collective-permute-start(bf16[128,256]{1,0:T(8,128)(2,1)S(1)} %add_convert_fusion.own_ref), channel_id=1, source_target_pairs={{0,16},{8,24},{16,0},{24,8},{1,17},{9,25},{17,1},{25,9},{2,18},{10... | collective-permute-start | bytes 196616 | tf_op jit(solution)/shard_map/ppermute | solution.py:20
  85.7 5.2 %collective-permute-start.23 = (bf16[128,256]{1,0:T(8,128)(2,1)S(1)}, bf16[128,256]{1,0:T(8,128)(2,1)S(1)}, u32[]{:S(2)}, u32[]{:S(2)}) collective-permute-start(bf16[128,256]{1,0:T(8,128)(2,1)S(1)} %add_convert_fusion.own_ref), channel_id=1, source_target_pairs={{0,8},{8,0},{16,24},{24,16},{1,9},{9,1},{17,25},{25,17},{2,10},{10... | collective-permute-start | bytes 196616 | tf_op jit(solution)/shard_map/ppermute | solution.py:20
  91.0 11.2 %collective-permute-start.28 = (bf16[4,128,256]{2,1,0:T(8,128)(2,1)S(1)}, bf16[4,128,256]{2,1,0:T(8,128)(2,1)S(1)}, u32[]{:S(2)}, u32[]{:S(2)}) collective-permute-start(bf16[4,128,256]{2,1,0:T(8,128)(2,1)S(1)} %stack.2.refs_0_), channel_id=1, source_target_pairs={{0,4},{1,5},{2,6},{3,7},{4,0},{5,1},{6,2},{7,3},{8,12},{9,13},{10,... | collective-permute-start | bytes 786440 | tf_op jit(solution)/shard_map/ppermute | solution.py:20
  92.8 9.4 %collective-permute-start.27 = (bf16[4,128,256]{2,1,0:T(8,128)(2,1)S(1)}, bf16[4,128,256]{2,1,0:T(8,128)(2,1)S(1)}, u32[]{:S(2)}, u32[]{:S(2)}) collective-permute-start(bf16[4,128,256]{2,1,0:T(8,128)(2,1)S(1)} %stack.2.refs_0_), channel_id=1, source_target_pairs={{0,2},{1,3},{2,0},{3,1},{4,6},{5,7},{6,4},{7,5},{8,10},{9,11},{10,... | collective-permute-start | bytes 786440 | tf_op jit(solution)/shard_map/ppermute | solution.py:20
  93.1 6.9 %collective-permute-start.31 = (bf16[128,256]{1,0:T(8,128)(2,1)S(1)}, bf16[128,256]{1,0:T(8,128)(2,1)S(1)}, u32[]{:S(2)}, u32[]{:S(2)}) collective-permute-start(bf16[128,256]{1,0:T(8,128)(2,1)S(1)} %collective-permute-done.26.refs_4_), channel_id=1, source_target_pairs={{0,24},{8,16},{16,8},{24,0},{1,25},{9,17},{17,9},{25,1},{2,26},{10... | collective-permute-start | bytes 196616 | tf_op jit(solution)/shard_map/ppermute | solution.py:20
  94.4 7.7 %collective-permute-start.30 = (bf16[128,256]{1,0:T(8,128)(2,1)S(1)}, bf16[128,256]{1,0:T(8,128)(2,1)S(1)}, u32[]{:S(2)}, u32[]{:S(2)}) collective-permute-start(bf16[128,256]{1,0:T(8,128)(2,1)S(1)} %collective-permute-done.26.refs_4_), channel_id=1, source_target_pairs={{0,16},{8,24},{16,0},{24,8},{1,17},{9,25},{17,1},{25,9},{2,18},{10... | collective-permute-start | bytes 196616 | tf_op jit(solution)/shard_map/ppermute | solution.py:20
  94.8 7.3 %collective-permute-start.29 = (bf16[128,256]{1,0:T(8,128)(2,1)S(1)}, bf16[128,256]{1,0:T(8,128)(2,1)S(1)}, u32[]{:S(2)}, u32[]{:S(2)}) collective-permute-start(bf16[128,256]{1,0:T(8,128)(2,1)S(1)} %collective-permute-done.26.refs_4_), channel_id=1, source_target_pairs={{0,8},{8,0},{16,24},{24,16},{1,9},{9,1},{17,25},{25,17},{2,10},{10... | collective-permute-start | bytes 196616 | tf_op jit(solution)/shard_map/ppermute | solution.py:20
  (12 other events, 56.8 us)

commit v10 on v9

--- a/solution.py
+++ b/solution.py
@@ -307,7 +307,7 @@
     ntok, panel = rows * n_hid, block // n_hid
     depth, shard_ff = gate_weight.shape
     tiles = shard_ff // TILE
-    ends = [TILE * (tiles * k // 3) for k in range(4)]
+    ends = [0, TILE * (3 * tiles // 7), TILE * (11 * tiles // 14), shard_ff]
     chip_masks = list(range(2, n_hid, 2))
 
     def part(weight, k):
@@ -352,18 +352,18 @@
     got_2 = swap(send_2, "tok", n_tok, 1)
     sum_1 = pair_total(keep_1, got_1, 2 * widths[1], (send_2,))
     over_1 = swap(sum_1, "tok", n_tok, 2)
-    down_b, = fetch([(down_weight, ends[2], widths[2], 0, block)], (sum_1,), "fetch_down")
-    sum_2 = pair_total(keep_2, got_2, 2 * widths[2], (down_b,))
+    sum_2 = pair_total(keep_2, got_2, 2 * widths[2], (sum_1,))
     over_2 = swap(sum_2, "tok", n_tok, 2)
-    down_a, = fetch([(down_weight, 0, ends[2], 0, block)], (sum_2,), "fetch_down")
-
-    a_own, scale = hidden_rows([(keep_0, got_0, over_0), (keep_1, got_1, over_1)], widths[:2], None, (down_a,))
+
+    a_own, scale = hidden_rows([(keep_0, got_0, over_0)], widths[:1], None, (sum_1,))
     a_two = swap(a_own, "tok", n_tok, 2)
     a_one = swap(a_own, "tok", n_tok, 1)
-    b_own, _ = hidden_rows([(keep_2, got_2, over_2)], widths[2:], scale, ())
+    a_three = swap(a_two, "tok", n_tok, 1)
+    down_b, = fetch([(down_weight, ends[1], shard_ff - ends[1], 0, block)], (sum_2,), "fetch_down")
+    down_a, = fetch([(down_weight, 0, ends[1], 0, block)], (down_b,), "fetch_down")
+    b_own, _ = hidden_rows([(keep_1, got_1, over_1), (keep_2, got_2, over_2)], widths[1:], scale, (a_one, a_two, down_b))
     b_two = swap(b_own, "tok", n_tok, 2)
     b_one = swap(b_own, "tok", n_tok, 1)
-    a_three = swap(copy_after(a_two, (b_two, b_one, a_one)), "tok", n_tok, 1)
     b_three = swap(b_two, "tok", n_tok, 1)
     hidden_a = [a_own, a_one, a_two, a_three]
     hidden_b = [b_own, b_one, b_two, b_three]
@@ -387,7 +387,7 @@
     across = swap(resid_cols, "hid", n_hid, 6)
     line = stack_after([resid_cols, *column], (across,))
     beside = [swap(line, "hid", n_hid, mask) for mask in (2, 4)]
-    across_line = [swap(across, "tok", n_tok, d) for d in range(1, n_tok)]
+    across_line = [swap(across, "tok", n_tok, d) for d in (1, 2)] + [swap(column[2], "hid", n_hid, 6)]
     line_far = swap(line, "hid", n_hid, 1)
     across_far = swap(across, "hid", n_hid, 1)
     line_slots = [[(d, mask) for d in range(n_tok)] for mask in range(n_hid)]

time: 106 us -> 106 us (level)
  starting transfers between devices: 42.1 us -> 36.9 us
  waiting for transfers between devices: 29.6 us -> 34.5 us
    ppermute x35, starting transfers between devices: 42.1 us -> 36.9 us  [swap(): return lax.ppermute(value, axis, [(i, i ^ mask) for i in range(size)])]
    ppermute x35, waiting for transfers between devices: 29.6 us -> 34.5 us  [swap(): return lax.ppermute(value, axis, [(i, i ^ mask) for i in range(size)])]
    pallas_call x26 -> x25, Pallas kernels: 33.8 us -> 33.6 us  [run(): pl.pallas_call(body, out_shape=out_shape, in_specs=[WHOLE] * len(operands...]
  transfers between devices with their start and end apart: 35 -> 35, of which waited for: 19 -> 20; matrix products, arithmetic and copies ran while one was open for 0% -> 0% of each run, Pallas kernels for 28% -> 26%
where the time goes in v10:
time: 106 us
  starting transfers between devices  36.9 us (35%)
  waiting for transfers between devices  34.5 us (33%)
  Pallas kernels  33.6 us (32%)
    ppermute x35, starting transfers between devices, swap(): return lax.ppermute(value, axis, [(i, i ^ mask) for i in range(size)])  36.9 us
    ppermute x35, waiting for transfers between devices, swap(): return lax.ppermute(value, axis, [(i, i ^ mask) for i in range(size)])  34.5 us
    pallas_call x25, Pallas kernels, run(): pl.pallas_call(body, out_shape=out_shape, in_specs=[WHOLE] * len(operands...  33.6 us
  transfers between devices with their start and end apart: 35, of which 20 were waited for; matrix products, arithmetic and copies ran while one was open for 0% of the time, Pallas kernels for 26%

profile of v10, /device:TPU:0, one launch (start us, length us, event | category | flops | bytes accessed | tf_op | source)
XLA Modules:
  0.0 105.9 jit_solution(13041484273947091340)
XLA Ops:
  0.6 3.0 %collective-permute-start.1 = (bf16[16,2048]{1,0:T(8,128)(2,1)}, bf16[16,2048]{1,0:T(8,128)(2,1)S(1)}, u32[]{:S(2)}, u32[]{:S(2)}) collective-permute-start(bf16[16,2048]{1,0:T(8,128)(2,1)} %refs_2_.1), channel_id=1, source_target_pairs={{0,4},{1,5},{2,6},{3,7},{4,0},{5,1},{6,2},{7,3},{8,12},{9,13},{10,... | collective-permute-start | bytes 196616 | tf_op jit(solution)/shard_map/ppermute | solution.py:20
  5.2 4.9 %fetch_first.1 = (bf16[2048,1536]{1,0:T(8,128)(2,1)S(1)}, bf16[2048,1536]{1,0:T(8,128)(2,1)S(1)}, bf16[16,2048]{1,0:T(8,128)(2,1)S(1)}, f32[1,2048]{1,0:T(1,128)S(1)}) custom-call(bf16[2048,3584]{1,0:T(8,128)(2,1)} %refs_0_.7, bf16[2048,3584]{1,0:T(8,128)(2,1)} %refs_1_.5, bf16[16,2048]{1,0:T(8,128)(2,1)} %refs_2_.1, f32[1,2048]{1,0:T(1,128)} %bitcast.22), custom_call_target="tpu_custom_call" | custom-call | tf_op jit(solution)/shard_map/fetch_first/pallas_call | solution.py:24
  12.5 2.0 %gate_up.3 = (bf16[2,32,3200]{2,1,0:T(8,128)(2,1)S(1)}, bf16[2,32,3200]{2,1,0:T(8,128)(2,1)S(1)}) custom-call(bf16[128,2048]{1,0:T(8,128)(2,1)S(1)} %get-tuple-element.31.lhs_ref, bf16[2048,1536]{1,0:T(8,128)(2,1)S(1)} %get-tuple-element.32.gate_ref, bf16[2048,1536]{1,0:T(8,128)(2,1)S(1)} %get-tuple-element.33.up_ref, f32[128,1]{1,0:T(8,128)S(1)} %get-tuple-element.34.refs_0_), custom_call_target="tpu_custom_call" | custom-call | tf_op jit(solution)/shard_map/gate_up/pallas_call | solution.py:24
  14.4 2.1 %collective-permute-start.8 = (bf16[2,32,3200]{2,1,0:T(8,128)(2,1)S(1)}, bf16[2,32,3200]{2,1,0:T(8,128)(2,1)S(1)}, u32[]{:S(2)}, u32[]{:S(2)}) collective-permute-start(bf16[2,32,3200]{2,1,0:T(8,128)(2,1)S(1)} %get-tuple-element.35.refs_2_), channel_id=1, source_target_pairs={{0,8},{8,0},{16,24},{24,16},{1,9},{9,1},{17,25},{25,17},{2,10},{10... | collective-permute-start | bytes 1228808 | tf_op jit(solution)/shard_map/ppermute | solution.py:20
  16.5 4.1 %fetch_gate_up.2 = (bf16[2048,1280]{1,0:T(8,128)(2,1)S(1)}, bf16[2048,1280]{1,0:T(8,128)(2,1)S(1)}) custom-call(bf16[2048,3584]{1,0:T(8,128)(2,1)} %refs_0_.7, bf16[2048,3584]{1,0:T(8,128)(2,1)} %refs_1_.5, bf16[2,32,3200]{2,1,0:T(8,128)(2,1)S(1)} %get-tuple-element.35.refs_2_), custom_call_target="tpu_custom_call" | custom-call | tf_op jit(solution)/shard_map/fetch_gate_up/pallas_call | solution.py:24
  22.4 4.3 %collective-permute-done.8.got_ref.refs_1_ = bf16[2,32,3200]{2,1,0:T(8,128)(2,1)S(1)} collective-permute-done((bf16[2,32,3200]{2,1,0:T(8,128)(2,1)S(1)}, bf16[2,32,3200]{2,1,0:T(8,128)(2,1)S(1)}, u32[]{:S(2)}, u32[]{:S(2)}) %collective-permute-start.8) | collective-permute-done | bytes 409632 | tf_op jit(solution)/shard_map/ppermute | solution.py:20
  26.9 3.1 %collective-permute-start.12 = (bf16[32,3200]{1,0:T(8,128)(2,1)S(1)}, bf16[32,3200]{1,0:T(8,128)(2,1)S(1)}, u32[]{:S(2)}, u32[]{:S(2)}) collective-permute-start(bf16[32,3200]{1,0:T(8,128)(2,1)S(1)} %pair_total.3.refs_2_), channel_id=1, source_target_pairs={{0,16},{8,24},{16,0},{24,8},{1,17},{9,25},{17,1},{25,9},{2,18},{10... | collective-permute-start | bytes 614408 | tf_op jit(solution)/shard_map/ppermute | solution.py:20
  30.0 2.9 %fetch_gate_up.3 = (bf16[2048,768]{1,0:T(8,128)(2,1)S(1)}, bf16[2048,768]{1,0:T(8,128)(2,1)S(1)}) custom-call(bf16[2048,3584]{1,0:T(8,128)(2,1)} %refs_0_.7, bf16[2048,3584]{1,0:T(8,128)(2,1)} %refs_1_.5, bf16[32,3200]{1,0:T(8,128)(2,1)S(1)} %pair_total.3.refs_2_), custom_call_target="tpu_custom_call" | custom-call | tf_op jit(solution)/shard_map/fetch_gate_up/pallas_call | solution.py:24
  35.7 2.4 %collective-permute-done.7.got_ref.refs_1_ = bf16[2,32,2560]{2,1,0:T(8,128)(2,1)S(1)} collective-permute-done((bf16[2,32,2560]{2,1,0:T(8,128)(2,1)S(1)}, bf16[2,32,2560]{2,1,0:T(8,128)(2,1)S(1)}, u32[]{:S(2)}, u32[]{:S(2)}) %collective-permute-start.7) | collective-permute-done | bytes 327712 | tf_op jit(solution)/shard_map/ppermute | solution.py:20
  39.5 5.6 %collective-permute-done.10.got_ref.refs_4_ = bf16[2,32,1536]{2,1,0:T(8,128)(2,1)S(1)} collective-permute-done((bf16[2,32,1536]{2,1,0:T(8,128)(2,1)S(1)}, bf16[2,32,1536]{2,1,0:T(8,128)(2,1)S(1)}, u32[]{:S(2)}, u32[]{:S(2)}) %collective-permute-start.10) | collective-permute-done | bytes 196640 | tf_op jit(solution)/shard_map/ppermute | solution.py:20
  46.0 2.4 %collective-permute-start.14 = (bf16[32,1536]{1,0:T(8,128)(2,1)S(1)}, bf16[32,1536]{1,0:T(8,128)(2,1)S(1)}, u32[]{:S(2)}, u32[]{:S(2)}) collective-permute-start(bf16[32,1536]{1,0:T(8,128)(2,1)S(1)} %get-tuple-element.46.refs_0_), channel_id=1, source_target_pairs={{0,16},{8,24},{16,0},{24,8},{1,17},{9,25},{17,1},{25,9},{2,18},{10... | collective-permute-start | bytes 294920 | tf_op jit(solution)/shard_map/ppermute | solution.py:20
  48.7 3.5 %fetch_down.2.refs_9_.refs_1_.refs_4_ = bf16[2048,2048]{1,0:T(8,128)(2,1)S(1)} custom-call(bf16[3584,2048]{1,0:T(8,128)(2,1)} %refs_0_.9, bf16[32,1536]{1,0:T(8,128)(2,1)S(1)} %pair_total.5.refs_1_), custom_call_target="tpu_custom_call" | custom-call | tf_op jit(solution)/shard_map/fetch_down/pallas_call | solution.py:24
  52.1 2.8 %collective-permute-done.11.refs_5_ = bf16[32,1536]{1,0:T(8,128)(2,1)S(1)} collective-permute-done((bf16[32,1536]{1,0:T(8,128)(2,1)S(1)}, bf16[32,1536]{1,0:T(8,128)(2,1)S(1)}, u32[]{:S(2)}, u32[]{:S(2)}) %collective-permute-start.11) | collective-permute-done | bytes 98336 | tf_op jit(solution)/shard_map/ppermute | solution.py:20
  54.9 1.9 %collective-permute-done.14.refs_8_.refs_2_ = bf16[32,1536]{1,0:T(8,128)(2,1)S(1)} collective-permute-done((bf16[32,1536]{1,0:T(8,128)(2,1)S(1)}, bf16[32,1536]{1,0:T(8,128)(2,1)S(1)}, u32[]{:S(2)}, u32[]{:S(2)}) %collective-permute-start.14) | collective-permute-done | bytes 98336 | tf_op jit(solution)/shard_map/ppermute | solution.py:20
  58.6 2.4 %collective-permute-start.18 = (bf16[32,1536]{1,0:T(8,128)(2,1)S(1)}, bf16[32,1536]{1,0:T(8,128)(2,1)S(1)}, u32[]{:S(2)}, u32[]{:S(2)}) collective-permute-start(bf16[32,1536]{1,0:T(8,128)(2,1)S(1)} %collective-permute-done.14.refs_8_.refs_2_), channel_id=1, source_target_pairs={{0,8},{8,0},{16,24},{24,16},{1,9},{9,1},{17,25},{25,17},{2,10},{10... | collective-permute-start | bytes 294920 | tf_op jit(solution)/shard_map/ppermute | solution.py:20
  61.1 4.5 %collective-permute-done.16.refs_2_ = bf16[32,2048]{1,0:T(8,128)(2,1)S(1)} collective-permute-done((bf16[32,2048]{1,0:T(8,128)(2,1)S(1)}, bf16[32,2048]{1,0:T(8,128)(2,1)S(1)}, u32[]{:S(2)}, u32[]{:S(2)}) %collective-permute-start.16) | collective-permute-done | bytes 131104 | tf_op jit(solution)/shard_map/ppermute | solution.py:20
  65.6 2.9 %fetch_down.3.refs_4_ = bf16[1536,2048]{1,0:T(8,128)(2,1)S(1)} custom-call(bf16[3584,2048]{1,0:T(8,128)(2,1)} %refs_0_.9, bf16[2048,2048]{1,0:T(8,128)(2,1)S(1)} %fetch_down.2.refs_9_.refs_1_.refs_4_), custom_call_target="tpu_custom_call" | custom-call | tf_op jit(solution)/shard_map/fetch_down/pallas_call | solution.py:24
  73.3 2.5 %collective-permute-start.20 = (bf16[128,256]{1,0:T(8,128)(2,1)S(1)}, bf16[128,256]{1,0:T(8,128)(2,1)S(1)}, u32[]{:S(2)}, u32[]{:S(2)}) collective-permute-start(bf16[128,256]{1,0:T(8,128)(2,1)S(1)} %get-tuple-element.49), channel_id=1, source_target_pairs={{0,6},{1,7},{2,4},{3,5},{4,2},{5,3},{6,0},{7,1},{8,14},{9,15},{10,... | collective-permute-start | bytes 196616 | tf_op jit(solution)/shard_map/ppermute | solution.py:20
  76.8 1.9 %collective-permute-done.20 = bf16[128,256]{1,0:T(8,128)(2,1)S(1)} collective-permute-done((bf16[128,256]{1,0:T(8,128)(2,1)S(1)}, bf16[128,256]{1,0:T(8,128)(2,1)S(1)}, u32[]{:S(2)}, u32[]{:S(2)}) %collective-permute-start.20) | collective-permute-done | bytes 65568 | tf_op jit(solution)/shard_map/ppermute | solution.py:20
  82.2 2.2 %collective-permute-start.25 = (bf16[128,256]{1,0:T(8,128)(2,1)S(1)}, bf16[128,256]{1,0:T(8,128)(2,1)S(1)}, u32[]{:S(2)}, u32[]{:S(2)}) collective-permute-start(bf16[128,256]{1,0:T(8,128)(2,1)S(1)} %add_convert_fusion.own_ref), channel_id=1, source_target_pairs={{0,24},{8,16},{16,8},{24,0},{1,25},{9,17},{17,9},{25,1},{2,26},{10... | collective-permute-start | bytes 196616 | tf_op jit(solution)/shard_map/ppermute | solution.py:20
  84.4 2.1 %collective-permute-start.23 = (bf16[128,256]{1,0:T(8,128)(2,1)S(1)}, bf16[128,256]{1,0:T(8,128)(2,1)S(1)}, u32[]{:S(2)}, u32[]{:S(2)}) collective-permute-start(bf16[128,256]{1,0:T(8,128)(2,1)S(1)} %add_convert_fusion.own_ref), channel_id=1, source_target_pairs={{0,8},{8,0},{16,24},{24,16},{1,9},{9,1},{17,25},{25,17},{2,10},{10... | collective-permute-start | bytes 196616 | tf_op jit(solution)/shard_map/ppermute | solution.py:20
  86.5 2.3 %collective-permute-done.25 = bf16[128,256]{1,0:T(8,128)(2,1)S(1)} collective-permute-done((bf16[128,256]{1,0:T(8,128)(2,1)S(1)}, bf16[128,256]{1,0:T(8,128)(2,1)S(1)}, u32[]{:S(2)}, u32[]{:S(2)}) %collective-permute-start.25) | collective-permute-done | bytes 65568 | tf_op jit(solution)/shard_map/ppermute | solution.py:20
  96.7 2.4 %gram.3 = (f32[256,8192]{1,0:T(8,128)}, f32[64,256]{1,0:T(8,128)}) custom-call(bf16[128,256]{1,0:T(8,128)(2,1)S(1)} %add_convert_fusion.own_ref, bf16[4,128,256]{2,1,0:T(8,128)(2,1)S(1)} %stack.2.refs_0_, bf16[4,128,256]{2,1,0:T(8,128)(2,1)S(1)} %collective-permute-done.32.refs_1_, bf16[1,128,256]{2,1,0:T(8,128)(2,1)S(1)} %bitcast.13, ...), custom_call_target="tpu_custom_call" | custom-call | flops 167772160 | bytes 2621440 | tf_op jit(solution)/shard_map/gram/pallas_call | solution.py:24
  99.4 2.3 %collective-permute-done.31 = bf16[128,256]{1,0:T(8,128)(2,1)S(1)} collective-permute-done((bf16[128,256]{1,0:T(8,128)(2,1)S(1)}, bf16[128,256]{1,0:T(8,128)(2,1)S(1)}, u32[]{:S(2)}, u32[]{:S(2)}) %collective-permute-start.31) | collective-permute-done | bytes 65568 | tf_op jit(solution)/shard_map/ppermute | solution.py:20
  (74 shorter events, 34.3 us)
Async XLA Ops:
  0.6 9.5 %collective-permute-start.1 = (bf16[16,2048]{1,0:T(8,128)(2,1)}, bf16[16,2048]{1,0:T(8,128)(2,1)S(1)}, u32[]{:S(2)}, u32[]{:S(2)}) collective-permute-start(bf16[16,2048]{1,0:T(8,128)(2,1)} %refs_2_.1), channel_id=1, source_target_pairs={{0,4},{1,5},{2,6},{3,7},{4,0},{5,1},{6,2},{7,3},{8,12},{9,13},{10,... | collective-permute-start | bytes 196616 | tf_op jit(solution)/shard_map/ppermute | solution.py:20
  3.7 7.0 %collective-permute-start.2 = (bf16[16,2048]{1,0:T(8,128)(2,1)}, bf16[16,2048]{1,0:T(8,128)(2,1)S(1)}, u32[]{:S(2)}, u32[]{:S(2)}) collective-permute-start(bf16[16,2048]{1,0:T(8,128)(2,1)} %refs_2_.1), channel_id=1, source_target_pairs={{0,6},{1,7},{2,4},{3,5},{4,2},{5,3},{6,0},{7,1},{8,14},{9,15},{10,... | collective-permute-start | bytes 196616 | tf_op jit(solution)/shard_map/ppermute | solution.py:20
  5.1 5.7 %collective-permute-start = (bf16[16,2048]{1,0:T(8,128)(2,1)}, bf16[16,2048]{1,0:T(8,128)(2,1)S(1)}, u32[]{:S(2)}, u32[]{:S(2)}) collective-permute-start(bf16[16,2048]{1,0:T(8,128)(2,1)} %refs_2_.1), channel_id=1, source_target_pairs={{0,2},{1,3},{2,0},{3,1},{4,6},{5,7},{6,4},{7,5},{8,10},{9,11},{10,... | collective-permute-start | bytes 196616 | tf_op jit(solution)/shard_map/ppermute | solution.py:20
  5.2 6.1 %collective-permute-start.3 = (bf16[16,2048]{1,0:T(8,128)(2,1)}, bf16[16,2048]{1,0:T(8,128)(2,1)S(1)}, u32[]{:S(2)}, u32[]{:S(2)}) collective-permute-start(bf16[16,2048]{1,0:T(8,128)(2,1)} %refs_2_.1), channel_id=1, source_target_pairs={{0,1},{1,0},{2,3},{3,2},{4,5},{5,4},{6,7},{7,6},{8,9},{9,8},{10,11... | collective-permute-start | bytes 196616 | tf_op jit(solution)/shard_map/ppermute | solution.py:20
  14.4 12.3 %collective-permute-start.8 = (bf16[2,32,3200]{2,1,0:T(8,128)(2,1)S(1)}, bf16[2,32,3200]{2,1,0:T(8,128)(2,1)S(1)}, u32[]{:S(2)}, u32[]{:S(2)}) collective-permute-start(bf16[2,32,3200]{2,1,0:T(8,128)(2,1)S(1)} %get-tuple-element.35.refs_2_), channel_id=1, source_target_pairs={{0,8},{8,0},{16,24},{24,16},{1,9},{9,1},{17,25},{25,17},{2,10},{10... | collective-permute-start | bytes 1228808 | tf_op jit(solution)/shard_map/ppermute | solution.py:20
  22.3 15.8 %collective-permute-start.7 = (bf16[2,32,2560]{2,1,0:T(8,128)(2,1)S(1)}, bf16[2,32,2560]{2,1,0:T(8,128)(2,1)S(1)}, u32[]{:S(2)}, u32[]{:S(2)}) collective-permute-start(bf16[2,32,2560]{2,1,0:T(8,128)(2,1)S(1)} %get-tuple-element.39.refs_0_), channel_id=1, source_target_pairs={{0,8},{8,0},{16,24},{24,16},{1,9},{9,1},{17,25},{25,17},{2,10},{10... | collective-permute-start | bytes 983048 | tf_op jit(solution)/shard_map/ppermute | solution.py:20
  26.9 18.9 %collective-permute-start.12 = (bf16[32,3200]{1,0:T(8,128)(2,1)S(1)}, bf16[32,3200]{1,0:T(8,128)(2,1)S(1)}, u32[]{:S(2)}, u32[]{:S(2)}) collective-permute-start(bf16[32,3200]{1,0:T(8,128)(2,1)S(1)} %pair_total.3.refs_2_), channel_id=1, source_target_pairs={{0,16},{8,24},{16,0},{24,8},{1,17},{9,25},{17,1},{25,9},{2,18},{10... | collective-permute-start | bytes 614408 | tf_op jit(solution)/shard_map/ppermute | solution.py:20
  34.1 11.1 %collective-permute-start.10 = (bf16[2,32,1536]{2,1,0:T(8,128)(2,1)S(1)}, bf16[2,32,1536]{2,1,0:T(8,128)(2,1)S(1)}, u32[]{:S(2)}, u32[]{:S(2)}) collective-permute-start(bf16[2,32,1536]{2,1,0:T(8,128)(2,1)S(1)} %get-tuple-element.43.refs_0_), channel_id=1, source_target_pairs={{0,8},{8,0},{16,24},{24,16},{1,9},{9,1},{17,25},{25,17},{2,10},{10... | collective-permute-start | bytes 589832 | tf_op jit(solution)/shard_map/ppermute | solution.py:20
  38.2 13.9 %collective-permute-start.9 = (bf16[32,2560]{1,0:T(8,128)(2,1)S(1)}, bf16[32,2560]{1,0:T(8,128)(2,1)S(1)}, u32[]{:S(2)}, u32[]{:S(2)}) collective-permute-start(bf16[32,2560]{1,0:T(8,128)(2,1)S(1)} %pair_total.4.refs_0_.refs_3_), channel_id=1, source_target_pairs={{0,16},{8,24},{16,0},{24,8},{1,17},{9,25},{17,1},{25,9},{2,18},{10... | collective-permute-start | bytes 491528 | tf_op jit(solution)/shard_map/ppermute | solution.py:20
  45.2 9.8 %collective-permute-start.11 = (bf16[32,1536]{1,0:T(8,128)(2,1)S(1)}, bf16[32,1536]{1,0:T(8,128)(2,1)S(1)}, u32[]{:S(2)}, u32[]{:S(2)}) collective-permute-start(bf16[32,1536]{1,0:T(8,128)(2,1)S(1)} %pair_total.5.refs_1_), channel_id=1, source_target_pairs={{0,16},{8,24},{16,0},{24,8},{1,17},{9,25},{17,1},{25,9},{2,18},{10... | collective-permute-start | bytes 294920 | tf_op jit(solution)/shard_map/ppermute | solution.py:20
  46.0 10.8 %collective-permute-start.14 = (bf16[32,1536]{1,0:T(8,128)(2,1)S(1)}, bf16[32,1536]{1,0:T(8,128)(2,1)S(1)}, u32[]{:S(2)}, u32[]{:S(2)}) collective-permute-start(bf16[32,1536]{1,0:T(8,128)(2,1)S(1)} %get-tuple-element.46.refs_0_), channel_id=1, source_target_pairs={{0,16},{8,24},{16,0},{24,8},{1,17},{9,25},{17,1},{25,9},{2,18},{10... | collective-permute-start | bytes 294920 | tf_op jit(solution)/shard_map/ppermute | solution.py:20
  48.4 8.4 %collective-permute-start.13 = (bf16[32,1536]{1,0:T(8,128)(2,1)S(1)}, bf16[32,1536]{1,0:T(8,128)(2,1)S(1)}, u32[]{:S(2)}, u32[]{:S(2)}) collective-permute-start(bf16[32,1536]{1,0:T(8,128)(2,1)S(1)} %get-tuple-element.46.refs_0_), channel_id=1, source_target_pairs={{0,8},{8,0},{16,24},{24,16},{1,9},{9,1},{17,25},{25,17},{2,10},{10... | collective-permute-start | bytes 294920 | tf_op jit(solution)/shard_map/ppermute | solution.py:20
  57.5 8.1 %collective-permute-start.16 = (bf16[32,2048]{1,0:T(8,128)(2,1)S(1)}, bf16[32,2048]{1,0:T(8,128)(2,1)S(1)}, u32[]{:S(2)}, u32[]{:S(2)}) collective-permute-start(bf16[32,2048]{1,0:T(8,128)(2,1)S(1)} %get-tuple-element.47.refs_0_), channel_id=1, source_target_pairs={{0,16},{8,24},{16,0},{24,8},{1,17},{9,25},{17,1},{25,9},{2,18},{10... | collective-permute-start | bytes 393224 | tf_op jit(solution)/shard_map/ppermute | solution.py:20
  58.6 9.8 %collective-permute-start.18 = (bf16[32,1536]{1,0:T(8,128)(2,1)S(1)}, bf16[32,1536]{1,0:T(8,128)(2,1)S(1)}, u32[]{:S(2)}, u32[]{:S(2)}) collective-permute-start(bf16[32,1536]{1,0:T(8,128)(2,1)S(1)} %collective-permute-done.14.refs_8_.refs_2_), channel_id=1, source_target_pairs={{0,8},{8,0},{16,24},{24,16},{1,9},{9,1},{17,25},{25,17},{2,10},{10... | collective-permute-start | bytes 294920 | tf_op jit(solution)/shard_map/ppermute | solution.py:20
  61.0 8.1 %collective-permute-start.15 = (bf16[32,2048]{1,0:T(8,128)(2,1)S(1)}, bf16[32,2048]{1,0:T(8,128)(2,1)S(1)}, u32[]{:S(2)}, u32[]{:S(2)}) collective-permute-start(bf16[32,2048]{1,0:T(8,128)(2,1)S(1)} %get-tuple-element.47.refs_0_), channel_id=1, source_target_pairs={{0,8},{8,0},{16,24},{24,16},{1,9},{9,1},{17,25},{25,17},{2,10},{10... | collective-permute-start | bytes 393224 | tf_op jit(solution)/shard_map/ppermute | solution.py:20
  80.6 6.0 %collective-permute-start.26 = (bf16[128,256]{1,0:T(8,128)(2,1)S(1)}, bf16[128,256]{1,0:T(8,128)(2,1)S(1)}, u32[]{:S(2)}, u32[]{:S(2)}) collective-permute-start(bf16[128,256]{1,0:T(8,128)(2,1)S(1)} %add_convert_fusion.own_ref), channel_id=1, source_target_pairs={{0,6},{1,7},{2,4},{3,5},{4,2},{5,3},{6,0},{7,1},{8,14},{9,15},{10,... | collective-permute-start | bytes 196616 | tf_op jit(solution)/shard_map/ppermute | solution.py:20
  82.2 6.7 %collective-permute-start.25 = (bf16[128,256]{1,0:T(8,128)(2,1)S(1)}, bf16[128,256]{1,0:T(8,128)(2,1)S(1)}, u32[]{:S(2)}, u32[]{:S(2)}) collective-permute-start(bf16[128,256]{1,0:T(8,128)(2,1)S(1)} %add_convert_fusion.own_ref), channel_id=1, source_target_pairs={{0,24},{8,16},{16,8},{24,0},{1,25},{9,17},{17,9},{25,1},{2,26},{10... | collective-permute-start | bytes 196616 | tf_op jit(solution)/shard_map/ppermute | solution.py:20
  84.4 5.9 %collective-permute-start.24 = (bf16[128,256]{1,0:T(8,128)(2,1)S(1)}, bf16[128,256]{1,0:T(8,128)(2,1)S(1)}, u32[]{:S(2)}, u32[]{:S(2)}) collective-permute-start(bf16[128,256]{1,0:T(8,128)(2,1)S(1)} %add_convert_fusion.own_ref), channel_id=1, source_target_pairs={{0,16},{8,24},{16,0},{24,8},{1,17},{9,25},{17,1},{25,9},{2,18},{10... | collective-permute-start | bytes 196616 | tf_op jit(solution)/shard_map/ppermute | solution.py:20
  84.4 5.9 %collective-permute-start.23 = (bf16[128,256]{1,0:T(8,128)(2,1)S(1)}, bf16[128,256]{1,0:T(8,128)(2,1)S(1)}, u32[]{:S(2)}, u32[]{:S(2)}) collective-permute-start(bf16[128,256]{1,0:T(8,128)(2,1)S(1)} %add_convert_fusion.own_ref), channel_id=1, source_target_pairs={{0,8},{8,0},{16,24},{24,16},{1,9},{9,1},{17,25},{25,17},{2,10},{10... | collective-permute-start | bytes 196616 | tf_op jit(solution)/shard_map/ppermute | solution.py:20
  90.4 11.3 %collective-permute-start.28 = (bf16[4,128,256]{2,1,0:T(8,128)(2,1)S(1)}, bf16[4,128,256]{2,1,0:T(8,128)(2,1)S(1)}, u32[]{:S(2)}, u32[]{:S(2)}) collective-permute-start(bf16[4,128,256]{2,1,0:T(8,128)(2,1)S(1)} %stack.2.refs_0_), channel_id=1, source_target_pairs={{0,4},{1,5},{2,6},{3,7},{4,0},{5,1},{6,2},{7,3},{8,12},{9,13},{10,... | collective-permute-start | bytes 786440 | tf_op jit(solution)/shard_map/ppermute | solution.py:20
  91.7 10.0 %collective-permute-start.27 = (bf16[4,128,256]{2,1,0:T(8,128)(2,1)S(1)}, bf16[4,128,256]{2,1,0:T(8,128)(2,1)S(1)}, u32[]{:S(2)}, u32[]{:S(2)}) collective-permute-start(bf16[4,128,256]{2,1,0:T(8,128)(2,1)S(1)} %stack.2.refs_0_), channel_id=1, source_target_pairs={{0,2},{1,3},{2,0},{3,1},{4,6},{5,7},{6,4},{7,5},{8,10},{9,11},{10,... | collective-permute-start | bytes 786440 | tf_op jit(solution)/shard_map/ppermute | solution.py:20
  92.5 6.8 %collective-permute-start.30 = (bf16[128,256]{1,0:T(8,128)(2,1)S(1)}, bf16[128,256]{1,0:T(8,128)(2,1)S(1)}, u32[]{:S(2)}, u32[]{:S(2)}) collective-permute-start(bf16[128,256]{1,0:T(8,128)(2,1)S(1)} %collective-permute-done.26.refs_4_), channel_id=1, source_target_pairs={{0,16},{8,24},{16,0},{24,8},{1,17},{9,25},{17,1},{25,9},{2,18},{10... | collective-permute-start | bytes 196616 | tf_op jit(solution)/shard_map/ppermute | solution.py:20
  93.8 5.6 %collective-permute-start.29 = (bf16[128,256]{1,0:T(8,128)(2,1)S(1)}, bf16[128,256]{1,0:T(8,128)(2,1)S(1)}, u32[]{:S(2)}, u32[]{:S(2)}) collective-permute-start(bf16[128,256]{1,0:T(8,128)(2,1)S(1)} %collective-permute-done.26.refs_4_), channel_id=1, source_target_pairs={{0,8},{8,0},{16,24},{24,16},{1,9},{9,1},{17,25},{25,17},{2,10},{10... | collective-permute-start | bytes 196616 | tf_op jit(solution)/shard_map/ppermute | solution.py:20
  95.2 6.4 %collective-permute-start.31 = (bf16[128,256]{1,0:T(8,128)(2,1)S(1)}, bf16[128,256]{1,0:T(8,128)(2,1)S(1)}, u32[]{:S(2)}, u32[]{:S(2)}) collective-permute-start(bf16[128,256]{1,0:T(8,128)(2,1)S(1)} %collective-permute-done.25), channel_id=1, source_target_pairs={{0,6},{1,7},{2,4},{3,5},{4,2},{5,3},{6,0},{7,1},{8,14},{9,15},{10,... | collective-permute-start | bytes 196616 | tf_op jit(solution)/shard_map/ppermute | solution.py:20
  (12 other events, 58.7 us)

commit v11 on v10

--- a/solution.py
+++ b/solution.py
@@ -387,7 +387,10 @@
     across = swap(resid_cols, "hid", n_hid, 6)
     line = stack_after([resid_cols, *column], (across,))
     beside = [swap(line, "hid", n_hid, mask) for mask in (2, 4)]
-    across_line = [swap(across, "tok", n_tok, d) for d in (1, 2)] + [swap(column[2], "hid", n_hid, 6)]
+    across_line = [
+        swap(across, "tok", n_tok, 1),
+        swap(stack_after(column[1:], (across,)), "hid", n_hid, 6),
+    ]
     line_far = swap(line, "hid", n_hid, 1)
     across_far = swap(across, "hid", n_hid, 1)
     line_slots = [[(d, mask) for d in range(n_tok)] for mask in range(n_hid)]

time: 106 us -> 107 us (level)
  waiting for transfers between devices: 34.5 us -> 38 us
  starting transfers between devices: 36.9 us -> 34.7 us
    ppermute x35 -> x34, waiting for transfers between devices: 34.5 us -> 38 us  [swap(): return lax.ppermute(value, axis, [(i, i ^ mask) for i in range(size)])]
    ppermute x35 -> x34, starting transfers between devices: 36.9 us -> 34.7 us  [swap(): return lax.ppermute(value, axis, [(i, i ^ mask) for i in range(size)])]
    pallas_call x25 -> x26, Pallas kernels: 33.6 us -> 33.6 us  [run(): pl.pallas_call(body, out_shape=out_shape, in_specs=[WHOLE] * len(operands...]
  transfers between devices with their start and end apart: 35 -> 34, of which waited for: 20 -> 19; matrix products, arithmetic and copies ran while one was open for 0% -> 0% of each run, Pallas kernels for 26% -> 26%
where the time goes in v11:
time: 107 us
  waiting for transfers between devices  38 us (36%)
  starting transfers between devices  34.7 us (32%)
  Pallas kernels  33.6 us (31%)
    ppermute x34, waiting for transfers between devices, swap(): return lax.ppermute(value, axis, [(i, i ^ mask) for i in range(size)])  38 us
    ppermute x34, starting transfers between devices, swap(): return lax.ppermute(value, axis, [(i, i ^ mask) for i in range(size)])  34.7 us
    pallas_call x26, Pallas kernels, run(): pl.pallas_call(body, out_shape=out_shape, in_specs=[WHOLE] * len(operands...  33.6 us
  transfers between devices with their start and end apart: 34, of which 19 were waited for; matrix products, arithmetic and copies ran while one was open for 0% of the time, Pallas kernels for 26%

profile of v11, /device:TPU:0, one launch (start us, length us, event | category | flops | bytes accessed | tf_op | source)
XLA Modules:
  0.0 107.3 jit_solution(5480431994079637234)
XLA Ops:
  0.6 3.0 %collective-permute-start.1 = (bf16[16,2048]{1,0:T(8,128)(2,1)}, bf16[16,2048]{1,0:T(8,128)(2,1)S(1)}, u32[]{:S(2)}, u32[]{:S(2)}) collective-permute-start(bf16[16,2048]{1,0:T(8,128)(2,1)} %refs_2_.1), channel_id=1, source_target_pairs={{0,4},{1,5},{2,6},{3,7},{4,0},{5,1},{6,2},{7,3},{8,12},{9,13},{10,... | collective-permute-start | bytes 196616 | tf_op jit(solution)/shard_map/ppermute | solution.py:20
  5.2 4.9 %fetch_first.1 = (bf16[2048,1536]{1,0:T(8,128)(2,1)S(1)}, bf16[2048,1536]{1,0:T(8,128)(2,1)S(1)}, bf16[16,2048]{1,0:T(8,128)(2,1)S(1)}, f32[1,2048]{1,0:T(1,128)S(1)}) custom-call(bf16[2048,3584]{1,0:T(8,128)(2,1)} %refs_0_.7, bf16[2048,3584]{1,0:T(8,128)(2,1)} %refs_1_.5, bf16[16,2048]{1,0:T(8,128)(2,1)} %refs_2_.1, f32[1,2048]{1,0:T(1,128)} %bitcast.20), custom_call_target="tpu_custom_call" | custom-call | tf_op jit(solution)/shard_map/fetch_first/pallas_call | solution.py:24
  12.5 2.0 %gate_up.3 = (bf16[2,32,3200]{2,1,0:T(8,128)(2,1)S(1)}, bf16[2,32,3200]{2,1,0:T(8,128)(2,1)S(1)}) custom-call(bf16[128,2048]{1,0:T(8,128)(2,1)S(1)} %get-tuple-element.31.lhs_ref, bf16[2048,1536]{1,0:T(8,128)(2,1)S(1)} %get-tuple-element.32.gate_ref, bf16[2048,1536]{1,0:T(8,128)(2,1)S(1)} %get-tuple-element.33.up_ref, f32[128,1]{1,0:T(8,128)S(1)} %get-tuple-element.34.refs_0_), custom_call_target="tpu_custom_call" | custom-call | tf_op jit(solution)/shard_map/gate_up/pallas_call | solution.py:24
  14.4 2.1 %collective-permute-start.8 = (bf16[2,32,3200]{2,1,0:T(8,128)(2,1)S(1)}, bf16[2,32,3200]{2,1,0:T(8,128)(2,1)S(1)}, u32[]{:S(2)}, u32[]{:S(2)}) collective-permute-start(bf16[2,32,3200]{2,1,0:T(8,128)(2,1)S(1)} %get-tuple-element.35.refs_2_), channel_id=1, source_target_pairs={{0,8},{8,0},{16,24},{24,16},{1,9},{9,1},{17,25},{25,17},{2,10},{10... | collective-permute-start | bytes 1228808 | tf_op jit(solution)/shard_map/ppermute | solution.py:20
  16.5 4.1 %fetch_gate_up.2 = (bf16[2048,1280]{1,0:T(8,128)(2,1)S(1)}, bf16[2048,1280]{1,0:T(8,128)(2,1)S(1)}) custom-call(bf16[2048,3584]{1,0:T(8,128)(2,1)} %refs_0_.7, bf16[2048,3584]{1,0:T(8,128)(2,1)} %refs_1_.5, bf16[2,32,3200]{2,1,0:T(8,128)(2,1)S(1)} %get-tuple-element.35.refs_2_), custom_call_target="tpu_custom_call" | custom-call | tf_op jit(solution)/shard_map/fetch_gate_up/pallas_call | solution.py:24
  22.4 4.3 %collective-permute-done.8.got_ref.refs_1_ = bf16[2,32,3200]{2,1,0:T(8,128)(2,1)S(1)} collective-permute-done((bf16[2,32,3200]{2,1,0:T(8,128)(2,1)S(1)}, bf16[2,32,3200]{2,1,0:T(8,128)(2,1)S(1)}, u32[]{:S(2)}, u32[]{:S(2)}) %collective-permute-start.8) | collective-permute-done | bytes 409632 | tf_op jit(solution)/shard_map/ppermute | solution.py:20
  26.9 3.1 %collective-permute-start.12 = (bf16[32,3200]{1,0:T(8,128)(2,1)S(1)}, bf16[32,3200]{1,0:T(8,128)(2,1)S(1)}, u32[]{:S(2)}, u32[]{:S(2)}) collective-permute-start(bf16[32,3200]{1,0:T(8,128)(2,1)S(1)} %pair_total.3.refs_2_), channel_id=1, source_target_pairs={{0,16},{8,24},{16,0},{24,8},{1,17},{9,25},{17,1},{25,9},{2,18},{10... | collective-permute-start | bytes 614408 | tf_op jit(solution)/shard_map/ppermute | solution.py:20
  30.0 2.9 %fetch_gate_up.3 = (bf16[2048,768]{1,0:T(8,128)(2,1)S(1)}, bf16[2048,768]{1,0:T(8,128)(2,1)S(1)}) custom-call(bf16[2048,3584]{1,0:T(8,128)(2,1)} %refs_0_.7, bf16[2048,3584]{1,0:T(8,128)(2,1)} %refs_1_.5, bf16[32,3200]{1,0:T(8,128)(2,1)S(1)} %pair_total.3.refs_2_), custom_call_target="tpu_custom_call" | custom-call | tf_op jit(solution)/shard_map/fetch_gate_up/pallas_call | solution.py:24
  35.7 2.4 %collective-permute-done.7.got_ref.refs_1_ = bf16[2,32,2560]{2,1,0:T(8,128)(2,1)S(1)} collective-permute-done((bf16[2,32,2560]{2,1,0:T(8,128)(2,1)S(1)}, bf16[2,32,2560]{2,1,0:T(8,128)(2,1)S(1)}, u32[]{:S(2)}, u32[]{:S(2)}) %collective-permute-start.7) | collective-permute-done | bytes 327712 | tf_op jit(solution)/shard_map/ppermute | solution.py:20
  39.5 5.6 %collective-permute-done.10.got_ref.refs_4_ = bf16[2,32,1536]{2,1,0:T(8,128)(2,1)S(1)} collective-permute-done((bf16[2,32,1536]{2,1,0:T(8,128)(2,1)S(1)}, bf16[2,32,1536]{2,1,0:T(8,128)(2,1)S(1)}, u32[]{:S(2)}, u32[]{:S(2)}) %collective-permute-start.10) | collective-permute-done | bytes 196640 | tf_op jit(solution)/shard_map/ppermute | solution.py:20
  46.0 2.4 %collective-permute-start.14 = (bf16[32,1536]{1,0:T(8,128)(2,1)S(1)}, bf16[32,1536]{1,0:T(8,128)(2,1)S(1)}, u32[]{:S(2)}, u32[]{:S(2)}) collective-permute-start(bf16[32,1536]{1,0:T(8,128)(2,1)S(1)} %get-tuple-element.46.refs_0_), channel_id=1, source_target_pairs={{0,16},{8,24},{16,0},{24,8},{1,17},{9,25},{17,1},{25,9},{2,18},{10... | collective-permute-start | bytes 294920 | tf_op jit(solution)/shard_map/ppermute | solution.py:20
  48.7 3.5 %fetch_down.2.refs_9_.refs_1_.refs_4_ = bf16[2048,2048]{1,0:T(8,128)(2,1)S(1)} custom-call(bf16[3584,2048]{1,0:T(8,128)(2,1)} %refs_0_.9, bf16[32,1536]{1,0:T(8,128)(2,1)S(1)} %pair_total.5.refs_1_), custom_call_target="tpu_custom_call" | custom-call | tf_op jit(solution)/shard_map/fetch_down/pallas_call | solution.py:24
  52.1 2.8 %collective-permute-done.11.refs_5_ = bf16[32,1536]{1,0:T(8,128)(2,1)S(1)} collective-permute-done((bf16[32,1536]{1,0:T(8,128)(2,1)S(1)}, bf16[32,1536]{1,0:T(8,128)(2,1)S(1)}, u32[]{:S(2)}, u32[]{:S(2)}) %collective-permute-start.11) | collective-permute-done | bytes 98336 | tf_op jit(solution)/shard_map/ppermute | solution.py:20
  54.9 1.9 %collective-permute-done.14.refs_8_.refs_2_ = bf16[32,1536]{1,0:T(8,128)(2,1)S(1)} collective-permute-done((bf16[32,1536]{1,0:T(8,128)(2,1)S(1)}, bf16[32,1536]{1,0:T(8,128)(2,1)S(1)}, u32[]{:S(2)}, u32[]{:S(2)}) %collective-permute-start.14) | collective-permute-done | bytes 98336 | tf_op jit(solution)/shard_map/ppermute | solution.py:20
  58.6 2.4 %collective-permute-start.18 = (bf16[32,1536]{1,0:T(8,128)(2,1)S(1)}, bf16[32,1536]{1,0:T(8,128)(2,1)S(1)}, u32[]{:S(2)}, u32[]{:S(2)}) collective-permute-start(bf16[32,1536]{1,0:T(8,128)(2,1)S(1)} %collective-permute-done.14.refs_8_.refs_2_), channel_id=1, source_target_pairs={{0,8},{8,0},{16,24},{24,16},{1,9},{9,1},{17,25},{25,17},{2,10},{10... | collective-permute-start | bytes 294920 | tf_op jit(solution)/shard_map/ppermute | solution.py:20
  61.1 4.5 %collective-permute-done.16.refs_2_ = bf16[32,2048]{1,0:T(8,128)(2,1)S(1)} collective-permute-done((bf16[32,2048]{1,0:T(8,128)(2,1)S(1)}, bf16[32,2048]{1,0:T(8,128)(2,1)S(1)}, u32[]{:S(2)}, u32[]{:S(2)}) %collective-permute-start.16) | collective-permute-done | bytes 131104 | tf_op jit(solution)/shard_map/ppermute | solution.py:20
  65.6 2.9 %fetch_down.3.refs_4_ = bf16[1536,2048]{1,0:T(8,128)(2,1)S(1)} custom-call(bf16[3584,2048]{1,0:T(8,128)(2,1)} %refs_0_.9, bf16[2048,2048]{1,0:T(8,128)(2,1)S(1)} %fetch_down.2.refs_9_.refs_1_.refs_4_), custom_call_target="tpu_custom_call" | custom-call | tf_op jit(solution)/shard_map/fetch_down/pallas_call | solution.py:24
  73.3 2.5 %collective-permute-start.20 = (bf16[128,256]{1,0:T(8,128)(2,1)S(1)}, bf16[128,256]{1,0:T(8,128)(2,1)S(1)}, u32[]{:S(2)}, u32[]{:S(2)}) collective-permute-start(bf16[128,256]{1,0:T(8,128)(2,1)S(1)} %get-tuple-element.49), channel_id=1, source_target_pairs={{0,6},{1,7},{2,4},{3,5},{4,2},{5,3},{6,0},{7,1},{8,14},{9,15},{10,... | collective-permute-start | bytes 196616 | tf_op jit(solution)/shard_map/ppermute | solution.py:20
  76.8 1.9 %collective-permute-done.20 = bf16[128,256]{1,0:T(8,128)(2,1)S(1)} collective-permute-done((bf16[128,256]{1,0:T(8,128)(2,1)S(1)}, bf16[128,256]{1,0:T(8,128)(2,1)S(1)}, u32[]{:S(2)}, u32[]{:S(2)}) %collective-permute-start.20) | collective-permute-done | bytes 65568 | tf_op jit(solution)/shard_map/ppermute | solution.py:20
  82.2 2.2 %collective-permute-start.25 = (bf16[128,256]{1,0:T(8,128)(2,1)S(1)}, bf16[128,256]{1,0:T(8,128)(2,1)S(1)}, u32[]{:S(2)}, u32[]{:S(2)}) collective-permute-start(bf16[128,256]{1,0:T(8,128)(2,1)S(1)} %add_convert_fusion.own_ref), channel_id=1, source_target_pairs={{0,24},{8,16},{16,8},{24,0},{1,25},{9,17},{17,9},{25,1},{2,26},{10... | collective-permute-start | bytes 196616 | tf_op jit(solution)/shard_map/ppermute | solution.py:20
  84.4 2.1 %collective-permute-start.23 = (bf16[128,256]{1,0:T(8,128)(2,1)S(1)}, bf16[128,256]{1,0:T(8,128)(2,1)S(1)}, u32[]{:S(2)}, u32[]{:S(2)}) collective-permute-start(bf16[128,256]{1,0:T(8,128)(2,1)S(1)} %add_convert_fusion.own_ref), channel_id=1, source_target_pairs={{0,8},{8,0},{16,24},{24,16},{1,9},{9,1},{17,25},{25,17},{2,10},{10... | collective-permute-start | bytes 196616 | tf_op jit(solution)/shard_map/ppermute | solution.py:20
  86.5 2.3 %collective-permute-done.25 = bf16[128,256]{1,0:T(8,128)(2,1)S(1)} collective-permute-done((bf16[128,256]{1,0:T(8,128)(2,1)S(1)}, bf16[128,256]{1,0:T(8,128)(2,1)S(1)}, u32[]{:S(2)}, u32[]{:S(2)}) %collective-permute-start.25) | collective-permute-done | bytes 65568 | tf_op jit(solution)/shard_map/ppermute | solution.py:20
  94.6 2.5 %gram.3 = (f32[256,8192]{1,0:T(8,128)}, f32[64,256]{1,0:T(8,128)}) custom-call(bf16[128,256]{1,0:T(8,128)(2,1)S(1)} %add_convert_fusion.own_ref, bf16[4,128,256]{2,1,0:T(8,128)(2,1)S(1)} %stack.3.refs_0_, bf16[4,128,256]{2,1,0:T(8,128)(2,1)S(1)} %collective-permute-done.31.refs_1_, bf16[1,128,256]{2,1,0:T(8,128)(2,1)S(1)} %bitcast.11, ...), custom_call_target="tpu_custom_call" | custom-call | flops 167772160 | bytes 2621440 | tf_op jit(solution)/shard_map/gram/pallas_call | solution.py:24
  98.3 4.8 %collective-permute-done.30.refs_3_ = bf16[2,128,256]{2,1,0:T(8,128)(2,1)S(1)} collective-permute-done((bf16[2,128,256]{2,1,0:T(8,128)(2,1)S(1)}, bf16[2,128,256]{2,1,0:T(8,128)(2,1)S(1)}, u32[]{:S(2)}, u32[]{:S(2)}) %collective-permute-start.30) | collective-permute-done | bytes 131104 | tf_op jit(solution)/shard_map/ppermute | solution.py:20
  (73 shorter events, 33.1 us)
Async XLA Ops:
  0.6 9.5 %collective-permute-start.1 = (bf16[16,2048]{1,0:T(8,128)(2,1)}, bf16[16,2048]{1,0:T(8,128)(2,1)S(1)}, u32[]{:S(2)}, u32[]{:S(2)}) collective-permute-start(bf16[16,2048]{1,0:T(8,128)(2,1)} %refs_2_.1), channel_id=1, source_target_pairs={{0,4},{1,5},{2,6},{3,7},{4,0},{5,1},{6,2},{7,3},{8,12},{9,13},{10,... | collective-permute-start | bytes 196616 | tf_op jit(solution)/shard_map/ppermute | solution.py:20
  3.7 7.0 %collective-permute-start.2 = (bf16[16,2048]{1,0:T(8,128)(2,1)}, bf16[16,2048]{1,0:T(8,128)(2,1)S(1)}, u32[]{:S(2)}, u32[]{:S(2)}) collective-permute-start(bf16[16,2048]{1,0:T(8,128)(2,1)} %refs_2_.1), channel_id=1, source_target_pairs={{0,6},{1,7},{2,4},{3,5},{4,2},{5,3},{6,0},{7,1},{8,14},{9,15},{10,... | collective-permute-start | bytes 196616 | tf_op jit(solution)/shard_map/ppermute | solution.py:20
  5.1 5.7 %collective-permute-start = (bf16[16,2048]{1,0:T(8,128)(2,1)}, bf16[16,2048]{1,0:T(8,128)(2,1)S(1)}, u32[]{:S(2)}, u32[]{:S(2)}) collective-permute-start(bf16[16,2048]{1,0:T(8,128)(2,1)} %refs_2_.1), channel_id=1, source_target_pairs={{0,2},{1,3},{2,0},{3,1},{4,6},{5,7},{6,4},{7,5},{8,10},{9,11},{10,... | collective-permute-start | bytes 196616 | tf_op jit(solution)/shard_map/ppermute | solution.py:20
  5.2 6.1 %collective-permute-start.3 = (bf16[16,2048]{1,0:T(8,128)(2,1)}, bf16[16,2048]{1,0:T(8,128)(2,1)S(1)}, u32[]{:S(2)}, u32[]{:S(2)}) collective-permute-start(bf16[16,2048]{1,0:T(8,128)(2,1)} %refs_2_.1), channel_id=1, source_target_pairs={{0,1},{1,0},{2,3},{3,2},{4,5},{5,4},{6,7},{7,6},{8,9},{9,8},{10,11... | collective-permute-start | bytes 196616 | tf_op jit(solution)/shard_map/ppermute | solution.py:20
  14.4 12.3 %collective-permute-start.8 = (bf16[2,32,3200]{2,1,0:T(8,128)(2,1)S(1)}, bf16[2,32,3200]{2,1,0:T(8,128)(2,1)S(1)}, u32[]{:S(2)}, u32[]{:S(2)}) collective-permute-start(bf16[2,32,3200]{2,1,0:T(8,128)(2,1)S(1)} %get-tuple-element.35.refs_2_), channel_id=1, source_target_pairs={{0,8},{8,0},{16,24},{24,16},{1,9},{9,1},{17,25},{25,17},{2,10},{10... | collective-permute-start | bytes 1228808 | tf_op jit(solution)/shard_map/ppermute | solution.py:20
  22.3 15.8 %collective-permute-start.7 = (bf16[2,32,2560]{2,1,0:T(8,128)(2,1)S(1)}, bf16[2,32,2560]{2,1,0:T(8,128)(2,1)S(1)}, u32[]{:S(2)}, u32[]{:S(2)}) collective-permute-start(bf16[2,32,2560]{2,1,0:T(8,128)(2,1)S(1)} %get-tuple-element.39.refs_0_), channel_id=1, source_target_pairs={{0,8},{8,0},{16,24},{24,16},{1,9},{9,1},{17,25},{25,17},{2,10},{10... | collective-permute-start | bytes 983048 | tf_op jit(solution)/shard_map/ppermute | solution.py:20
  26.9 18.9 %collective-permute-start.12 = (bf16[32,3200]{1,0:T(8,128)(2,1)S(1)}, bf16[32,3200]{1,0:T(8,128)(2,1)S(1)}, u32[]{:S(2)}, u32[]{:S(2)}) collective-permute-start(bf16[32,3200]{1,0:T(8,128)(2,1)S(1)} %pair_total.3.refs_2_), channel_id=1, source_target_pairs={{0,16},{8,24},{16,0},{24,8},{1,17},{9,25},{17,1},{25,9},{2,18},{10... | collective-permute-start | bytes 614408 | tf_op jit(solution)/shard_map/ppermute | solution.py:20
  34.1 11.1 %collective-permute-start.10 = (bf16[2,32,1536]{2,1,0:T(8,128)(2,1)S(1)}, bf16[2,32,1536]{2,1,0:T(8,128)(2,1)S(1)}, u32[]{:S(2)}, u32[]{:S(2)}) collective-permute-start(bf16[2,32,1536]{2,1,0:T(8,128)(2,1)S(1)} %get-tuple-element.43.refs_0_), channel_id=1, source_target_pairs={{0,8},{8,0},{16,24},{24,16},{1,9},{9,1},{17,25},{25,17},{2,10},{10... | collective-permute-start | bytes 589832 | tf_op jit(solution)/shard_map/ppermute | solution.py:20
  38.2 13.9 %collective-permute-start.9 = (bf16[32,2560]{1,0:T(8,128)(2,1)S(1)}, bf16[32,2560]{1,0:T(8,128)(2,1)S(1)}, u32[]{:S(2)}, u32[]{:S(2)}) collective-permute-start(bf16[32,2560]{1,0:T(8,128)(2,1)S(1)} %pair_total.4.refs_0_.refs_3_), channel_id=1, source_target_pairs={{0,16},{8,24},{16,0},{24,8},{1,17},{9,25},{17,1},{25,9},{2,18},{10... | collective-permute-start | bytes 491528 | tf_op jit(solution)/shard_map/ppermute | solution.py:20
  45.2 9.8 %collective-permute-start.11 = (bf16[32,1536]{1,0:T(8,128)(2,1)S(1)}, bf16[32,1536]{1,0:T(8,128)(2,1)S(1)}, u32[]{:S(2)}, u32[]{:S(2)}) collective-permute-start(bf16[32,1536]{1,0:T(8,128)(2,1)S(1)} %pair_total.5.refs_1_), channel_id=1, source_target_pairs={{0,16},{8,24},{16,0},{24,8},{1,17},{9,25},{17,1},{25,9},{2,18},{10... | collective-permute-start | bytes 294920 | tf_op jit(solution)/shard_map/ppermute | solution.py:20
  46.0 10.8 %collective-permute-start.14 = (bf16[32,1536]{1,0:T(8,128)(2,1)S(1)}, bf16[32,1536]{1,0:T(8,128)(2,1)S(1)}, u32[]{:S(2)}, u32[]{:S(2)}) collective-permute-start(bf16[32,1536]{1,0:T(8,128)(2,1)S(1)} %get-tuple-element.46.refs_0_), channel_id=1, source_target_pairs={{0,16},{8,24},{16,0},{24,8},{1,17},{9,25},{17,1},{25,9},{2,18},{10... | collective-permute-start | bytes 294920 | tf_op jit(solution)/shard_map/ppermute | solution.py:20
  48.4 8.4 %collective-permute-start.13 = (bf16[32,1536]{1,0:T(8,128)(2,1)S(1)}, bf16[32,1536]{1,0:T(8,128)(2,1)S(1)}, u32[]{:S(2)}, u32[]{:S(2)}) collective-permute-start(bf16[32,1536]{1,0:T(8,128)(2,1)S(1)} %get-tuple-element.46.refs_0_), channel_id=1, source_target_pairs={{0,8},{8,0},{16,24},{24,16},{1,9},{9,1},{17,25},{25,17},{2,10},{10... | collective-permute-start | bytes 294920 | tf_op jit(solution)/shard_map/ppermute | solution.py:20
  57.5 8.1 %collective-permute-start.16 = (bf16[32,2048]{1,0:T(8,128)(2,1)S(1)}, bf16[32,2048]{1,0:T(8,128)(2,1)S(1)}, u32[]{:S(2)}, u32[]{:S(2)}) collective-permute-start(bf16[32,2048]{1,0:T(8,128)(2,1)S(1)} %get-tuple-element.47.refs_0_), channel_id=1, source_target_pairs={{0,16},{8,24},{16,0},{24,8},{1,17},{9,25},{17,1},{25,9},{2,18},{10... | collective-permute-start | bytes 393224 | tf_op jit(solution)/shard_map/ppermute | solution.py:20
  58.6 9.8 %collective-permute-start.18 = (bf16[32,1536]{1,0:T(8,128)(2,1)S(1)}, bf16[32,1536]{1,0:T(8,128)(2,1)S(1)}, u32[]{:S(2)}, u32[]{:S(2)}) collective-permute-start(bf16[32,1536]{1,0:T(8,128)(2,1)S(1)} %collective-permute-done.14.refs_8_.refs_2_), channel_id=1, source_target_pairs={{0,8},{8,0},{16,24},{24,16},{1,9},{9,1},{17,25},{25,17},{2,10},{10... | collective-permute-start | bytes 294920 | tf_op jit(solution)/shard_map/ppermute | solution.py:20
  61.0 8.1 %collective-permute-start.15 = (bf16[32,2048]{1,0:T(8,128)(2,1)S(1)}, bf16[32,2048]{1,0:T(8,128)(2,1)S(1)}, u32[]{:S(2)}, u32[]{:S(2)}) collective-permute-start(bf16[32,2048]{1,0:T(8,128)(2,1)S(1)} %get-tuple-element.47.refs_0_), channel_id=1, source_target_pairs={{0,8},{8,0},{16,24},{24,16},{1,9},{9,1},{17,25},{25,17},{2,10},{10... | collective-permute-start | bytes 393224 | tf_op jit(solution)/shard_map/ppermute | solution.py:20
  65.6 5.2 %collective-permute-start.17 = (bf16[32,2048]{1,0:T(8,128)(2,1)S(1)}, bf16[32,2048]{1,0:T(8,128)(2,1)S(1)}, u32[]{:S(2)}, u32[]{:S(2)}) collective-permute-start(bf16[32,2048]{1,0:T(8,128)(2,1)S(1)} %collective-permute-done.16.refs_2_), channel_id=1, source_target_pairs={{0,8},{8,0},{16,24},{24,16},{1,9},{9,1},{17,25},{25,17},{2,10},{10... | collective-permute-start | bytes 393224 | tf_op jit(solution)/shard_map/ppermute | solution.py:20
  73.3 5.5 %collective-permute-start.20 = (bf16[128,256]{1,0:T(8,128)(2,1)S(1)}, bf16[128,256]{1,0:T(8,128)(2,1)S(1)}, u32[]{:S(2)}, u32[]{:S(2)}) collective-permute-start(bf16[128,256]{1,0:T(8,128)(2,1)S(1)} %get-tuple-element.49), channel_id=1, source_target_pairs={{0,6},{1,7},{2,4},{3,5},{4,2},{5,3},{6,0},{7,1},{8,14},{9,15},{10,... | collective-permute-start | bytes 196616 | tf_op jit(solution)/shard_map/ppermute | solution.py:20
  80.6 6.0 %collective-permute-start.26 = (bf16[128,256]{1,0:T(8,128)(2,1)S(1)}, bf16[128,256]{1,0:T(8,128)(2,1)S(1)}, u32[]{:S(2)}, u32[]{:S(2)}) collective-permute-start(bf16[128,256]{1,0:T(8,128)(2,1)S(1)} %add_convert_fusion.own_ref), channel_id=1, source_target_pairs={{0,6},{1,7},{2,4},{3,5},{4,2},{5,3},{6,0},{7,1},{8,14},{9,15},{10,... | collective-permute-start | bytes 196616 | tf_op jit(solution)/shard_map/ppermute | solution.py:20
  82.2 6.7 %collective-permute-start.25 = (bf16[128,256]{1,0:T(8,128)(2,1)S(1)}, bf16[128,256]{1,0:T(8,128)(2,1)S(1)}, u32[]{:S(2)}, u32[]{:S(2)}) collective-permute-start(bf16[128,256]{1,0:T(8,128)(2,1)S(1)} %add_convert_fusion.own_ref), channel_id=1, source_target_pairs={{0,24},{8,16},{16,8},{24,0},{1,25},{9,17},{17,9},{25,1},{2,26},{10... | collective-permute-start | bytes 196616 | tf_op jit(solution)/shard_map/ppermute | solution.py:20
  84.4 5.9 %collective-permute-start.24 = (bf16[128,256]{1,0:T(8,128)(2,1)S(1)}, bf16[128,256]{1,0:T(8,128)(2,1)S(1)}, u32[]{:S(2)}, u32[]{:S(2)}) collective-permute-start(bf16[128,256]{1,0:T(8,128)(2,1)S(1)} %add_convert_fusion.own_ref), channel_id=1, source_target_pairs={{0,16},{8,24},{16,0},{24,8},{1,17},{9,25},{17,1},{25,9},{2,18},{10... | collective-permute-start | bytes 196616 | tf_op jit(solution)/shard_map/ppermute | solution.py:20
  84.4 5.9 %collective-permute-start.23 = (bf16[128,256]{1,0:T(8,128)(2,1)S(1)}, bf16[128,256]{1,0:T(8,128)(2,1)S(1)}, u32[]{:S(2)}, u32[]{:S(2)}) collective-permute-start(bf16[128,256]{1,0:T(8,128)(2,1)S(1)} %add_convert_fusion.own_ref), channel_id=1, source_target_pairs={{0,8},{8,0},{16,24},{24,16},{1,9},{9,1},{17,25},{25,17},{2,10},{10... | collective-permute-start | bytes 196616 | tf_op jit(solution)/shard_map/ppermute | solution.py:20
  90.4 12.7 %collective-permute-start.28 = (bf16[4,128,256]{2,1,0:T(8,128)(2,1)S(1)}, bf16[4,128,256]{2,1,0:T(8,128)(2,1)S(1)}, u32[]{:S(2)}, u32[]{:S(2)}) collective-permute-start(bf16[4,128,256]{2,1,0:T(8,128)(2,1)S(1)} %stack.3.refs_0_), channel_id=1, source_target_pairs={{0,4},{1,5},{2,6},{3,7},{4,0},{5,1},{6,2},{7,3},{8,12},{9,13},{10,... | collective-permute-start | bytes 786440 | tf_op jit(solution)/shard_map/ppermute | solution.py:20
  91.7 11.4 %collective-permute-start.27 = (bf16[4,128,256]{2,1,0:T(8,128)(2,1)S(1)}, bf16[4,128,256]{2,1,0:T(8,128)(2,1)S(1)}, u32[]{:S(2)}, u32[]{:S(2)}) collective-permute-start(bf16[4,128,256]{2,1,0:T(8,128)(2,1)S(1)} %stack.3.refs_0_), channel_id=1, source_target_pairs={{0,2},{1,3},{2,0},{3,1},{4,6},{5,7},{6,4},{7,5},{8,10},{9,11},{10,... | collective-permute-start | bytes 786440 | tf_op jit(solution)/shard_map/ppermute | solution.py:20
  92.5 10.6 %collective-permute-start.30 = (bf16[2,128,256]{2,1,0:T(8,128)(2,1)S(1)}, bf16[2,128,256]{2,1,0:T(8,128)(2,1)S(1)}, u32[]{:S(2)}, u32[]{:S(2)}) collective-permute-start(bf16[2,128,256]{2,1,0:T(8,128)(2,1)S(1)} %stack.4), channel_id=1, source_target_pairs={{0,6},{1,7},{2,4},{3,5},{4,2},{5,3},{6,0},{7,1},{8,14},{9,15},{10,... | collective-permute-start | bytes 393224 | tf_op jit(solution)/shard_map/ppermute | solution.py:20
  (11 other events, 49.6 us)

commit v12 on v10

--- a/solution.py
+++ b/solution.py
@@ -153,21 +153,30 @@
     )
 
 
-def stack_after(blocks, after):
+def stack_after(blocks, after, extra=0):
     stacks = [block if block.ndim == 3 else block[None] for block in blocks]
     total = sum(stack.shape[0] for stack in stacks)
+    rows = stacks[0].shape[1]
 
     def body(*refs):
+        out = refs[len(stacks) + len(after)]
         at = 0
         for ref in refs[:len(stacks)]:
-            refs[-1][at:at + ref.shape[0]] = ref[...]
+            out[at:at + ref.shape[0]] = ref[:, :rows, :]
             at += ref.shape[0]
-
-    shape = jax.ShapeDtypeStruct((total, *stacks[0].shape[1:]), blocks[0].dtype)
-    return run(
-        body, "stack", shape, [*stacks, *after], 0, 4 * sum(stack.size for stack in stacks),
+        if extra:
+            refs[-1][:rows, :] = out[at - 1]
+            refs[-1][rows:, :] = out[at - 1, :extra, :]
+
+    width, kind = blocks[0].shape[-1], blocks[0].dtype
+    shapes = [jax.ShapeDtypeStruct((total, rows, width), kind)]
+    shapes += [jax.ShapeDtypeStruct((rows + extra, width), kind)] if extra else []
+    outs = run(
+        body, "stack", shapes, [*stacks, *after], 0, 4 * sum(stack.size for stack in stacks),
         in_specs=[WHOLE] * len(stacks) + [ANYWHERE] * len(after),
-    )
+        out_specs=[WHOLE] * len(shapes),
+    )
+    return outs if extra else outs[0]
 
 
 def hidden_rows(chunks, widths, scale, after):
@@ -385,9 +394,9 @@
 
     column = [swap(resid_cols, "tok", n_tok, d) for d in range(1, n_tok)]
     across = swap(resid_cols, "hid", n_hid, 6)
-    line = stack_after([resid_cols, *column], (across,))
+    line, farthest = stack_after([resid_cols, *column], (across,), 16)
     beside = [swap(line, "hid", n_hid, mask) for mask in (2, 4)]
-    across_line = [swap(across, "tok", n_tok, d) for d in (1, 2)] + [swap(column[2], "hid", n_hid, 6)]
+    across_line = [swap(across, "tok", n_tok, d) for d in (1, 2)] + [swap(farthest, "hid", n_hid, 6)]
     line_far = swap(line, "hid", n_hid, 1)
     across_far = swap(across, "hid", n_hid, 1)
     line_slots = [[(d, mask) for d in range(n_tok)] for mask in range(n_hid)]

time: 106 us -> 106 us (level)
  no operation moved by 1% of the time
where the time goes in v12:
time: 106 us
  starting transfers between devices  36.7 us (35%)
  waiting for transfers between devices  34.5 us (33%)
  Pallas kernels  33.6 us (32%)
    ppermute x35, starting transfers between devices, swap(): return lax.ppermute(value, axis, [(i, i ^ mask) for i in range(size)])  36.7 us
    ppermute x35, waiting for transfers between devices, swap(): return lax.ppermute(value, axis, [(i, i ^ mask) for i in range(size)])  34.5 us
    pallas_call x25, Pallas kernels, run(): pl.pallas_call(body, out_shape=out_shape, in_specs=[WHOLE] * len(operands...  33.6 us
  transfers between devices with their start and end apart: 35, of which 20 were waited for; matrix products, arithmetic and copies ran while one was open for 0% of the time, Pallas kernels for 26%

profile of v12, /device:TPU:0, one launch (start us, length us, event | category | flops | bytes accessed | tf_op | source)
XLA Modules:
  0.0 105.7 jit_solution(13404586517938587741)
XLA Ops:
  0.6 3.0 %collective-permute-start = (bf16[16,2048]{1,0:T(8,128)(2,1)}, bf16[16,2048]{1,0:T(8,128)(2,1)S(1)}, u32[]{:S(2)}, u32[]{:S(2)}) collective-permute-start(bf16[16,2048]{1,0:T(8,128)(2,1)} %refs_2_.1), channel_id=1, source_target_pairs={{0,2},{1,3},{2,0},{3,1},{4,6},{5,7},{6,4},{7,5},{8,10},{9,11},{10,... | collective-permute-start | bytes 196616 | tf_op jit(solution)/shard_map/ppermute | solution.py:20
  5.2 4.9 %fetch_first.1 = (bf16[2048,1536]{1,0:T(8,128)(2,1)S(1)}, bf16[2048,1536]{1,0:T(8,128)(2,1)S(1)}, bf16[16,2048]{1,0:T(8,128)(2,1)S(1)}, f32[1,2048]{1,0:T(1,128)S(1)}) custom-call(bf16[2048,3584]{1,0:T(8,128)(2,1)} %refs_0_.7, bf16[2048,3584]{1,0:T(8,128)(2,1)} %refs_1_.5, bf16[16,2048]{1,0:T(8,128)(2,1)} %refs_2_.1, f32[1,2048]{1,0:T(1,128)} %bitcast.22), custom_call_target="tpu_custom_call" | custom-call | tf_op jit(solution)/shard_map/fetch_first/pallas_call | solution.py:24
  12.4 2.0 %gate_up.3 = (bf16[2,32,3200]{2,1,0:T(8,128)(2,1)S(1)}, bf16[2,32,3200]{2,1,0:T(8,128)(2,1)S(1)}) custom-call(bf16[128,2048]{1,0:T(8,128)(2,1)S(1)} %get-tuple-element.33.lhs_ref, bf16[2048,1536]{1,0:T(8,128)(2,1)S(1)} %get-tuple-element.34.gate_ref, bf16[2048,1536]{1,0:T(8,128)(2,1)S(1)} %get-tuple-element.35.up_ref, f32[128,1]{1,0:T(8,128)S(1)} %get-tuple-element.36.refs_0_), custom_call_target="tpu_custom_call" | custom-call | tf_op jit(solution)/shard_map/gate_up/pallas_call | solution.py:24
  14.3 2.1 %collective-permute-start.8 = (bf16[2,32,3200]{2,1,0:T(8,128)(2,1)S(1)}, bf16[2,32,3200]{2,1,0:T(8,128)(2,1)S(1)}, u32[]{:S(2)}, u32[]{:S(2)}) collective-permute-start(bf16[2,32,3200]{2,1,0:T(8,128)(2,1)S(1)} %get-tuple-element.37.refs_2_), channel_id=1, source_target_pairs={{0,8},{8,0},{16,24},{24,16},{1,9},{9,1},{17,25},{25,17},{2,10},{10... | collective-permute-start | bytes 1228808 | tf_op jit(solution)/shard_map/ppermute | solution.py:20
  16.5 4.1 %fetch_gate_up.2 = (bf16[2048,1280]{1,0:T(8,128)(2,1)S(1)}, bf16[2048,1280]{1,0:T(8,128)(2,1)S(1)}) custom-call(bf16[2048,3584]{1,0:T(8,128)(2,1)} %refs_0_.7, bf16[2048,3584]{1,0:T(8,128)(2,1)} %refs_1_.5, bf16[2,32,3200]{2,1,0:T(8,128)(2,1)S(1)} %get-tuple-element.37.refs_2_), custom_call_target="tpu_custom_call" | custom-call | tf_op jit(solution)/shard_map/fetch_gate_up/pallas_call | solution.py:24
  22.3 4.4 %collective-permute-done.8.got_ref.refs_1_ = bf16[2,32,3200]{2,1,0:T(8,128)(2,1)S(1)} collective-permute-done((bf16[2,32,3200]{2,1,0:T(8,128)(2,1)S(1)}, bf16[2,32,3200]{2,1,0:T(8,128)(2,1)S(1)}, u32[]{:S(2)}, u32[]{:S(2)}) %collective-permute-start.8) | collective-permute-done | bytes 409632 | tf_op jit(solution)/shard_map/ppermute | solution.py:20
  26.9 3.1 %collective-permute-start.12 = (bf16[32,3200]{1,0:T(8,128)(2,1)S(1)}, bf16[32,3200]{1,0:T(8,128)(2,1)S(1)}, u32[]{:S(2)}, u32[]{:S(2)}) collective-permute-start(bf16[32,3200]{1,0:T(8,128)(2,1)S(1)} %pair_total.3.refs_2_), channel_id=1, source_target_pairs={{0,16},{8,24},{16,0},{24,8},{1,17},{9,25},{17,1},{25,9},{2,18},{10... | collective-permute-start | bytes 614408 | tf_op jit(solution)/shard_map/ppermute | solution.py:20
  30.0 2.9 %fetch_gate_up.3 = (bf16[2048,768]{1,0:T(8,128)(2,1)S(1)}, bf16[2048,768]{1,0:T(8,128)(2,1)S(1)}) custom-call(bf16[2048,3584]{1,0:T(8,128)(2,1)} %refs_0_.7, bf16[2048,3584]{1,0:T(8,128)(2,1)} %refs_1_.5, bf16[32,3200]{1,0:T(8,128)(2,1)S(1)} %pair_total.3.refs_2_), custom_call_target="tpu_custom_call" | custom-call | tf_op jit(solution)/shard_map/fetch_gate_up/pallas_call | solution.py:24
  35.7 2.5 %collective-permute-done.7.got_ref.refs_1_ = bf16[2,32,2560]{2,1,0:T(8,128)(2,1)S(1)} collective-permute-done((bf16[2,32,2560]{2,1,0:T(8,128)(2,1)S(1)}, bf16[2,32,2560]{2,1,0:T(8,128)(2,1)S(1)}, u32[]{:S(2)}, u32[]{:S(2)}) %collective-permute-start.7) | collective-permute-done | bytes 327712 | tf_op jit(solution)/shard_map/ppermute | solution.py:20
  39.5 5.7 %collective-permute-done.10.got_ref.refs_4_ = bf16[2,32,1536]{2,1,0:T(8,128)(2,1)S(1)} collective-permute-done((bf16[2,32,1536]{2,1,0:T(8,128)(2,1)S(1)}, bf16[2,32,1536]{2,1,0:T(8,128)(2,1)S(1)}, u32[]{:S(2)}, u32[]{:S(2)}) %collective-permute-start.10) | collective-permute-done | bytes 196640 | tf_op jit(solution)/shard_map/ppermute | solution.py:20
  46.0 2.5 %collective-permute-start.14 = (bf16[32,1536]{1,0:T(8,128)(2,1)S(1)}, bf16[32,1536]{1,0:T(8,128)(2,1)S(1)}, u32[]{:S(2)}, u32[]{:S(2)}) collective-permute-start(bf16[32,1536]{1,0:T(8,128)(2,1)S(1)} %get-tuple-element.48.refs_0_), channel_id=1, source_target_pairs={{0,16},{8,24},{16,0},{24,8},{1,17},{9,25},{17,1},{25,9},{2,18},{10... | collective-permute-start | bytes 294920 | tf_op jit(solution)/shard_map/ppermute | solution.py:20
  48.6 3.5 %fetch_down.2.refs_9_.refs_1_.refs_4_ = bf16[2048,2048]{1,0:T(8,128)(2,1)S(1)} custom-call(bf16[3584,2048]{1,0:T(8,128)(2,1)} %refs_0_.9, bf16[32,1536]{1,0:T(8,128)(2,1)S(1)} %pair_total.5.refs_1_), custom_call_target="tpu_custom_call" | custom-call | tf_op jit(solution)/shard_map/fetch_down/pallas_call | solution.py:24
  52.1 2.7 %collective-permute-done.11.refs_5_ = bf16[32,1536]{1,0:T(8,128)(2,1)S(1)} collective-permute-done((bf16[32,1536]{1,0:T(8,128)(2,1)S(1)}, bf16[32,1536]{1,0:T(8,128)(2,1)S(1)}, u32[]{:S(2)}, u32[]{:S(2)}) %collective-permute-start.11) | collective-permute-done | bytes 98336 | tf_op jit(solution)/shard_map/ppermute | solution.py:20
  54.8 2.0 %collective-permute-done.14.refs_8_.refs_2_ = bf16[32,1536]{1,0:T(8,128)(2,1)S(1)} collective-permute-done((bf16[32,1536]{1,0:T(8,128)(2,1)S(1)}, bf16[32,1536]{1,0:T(8,128)(2,1)S(1)}, u32[]{:S(2)}, u32[]{:S(2)}) %collective-permute-start.14) | collective-permute-done | bytes 98336 | tf_op jit(solution)/shard_map/ppermute | solution.py:20
  58.5 2.4 %collective-permute-start.18 = (bf16[32,1536]{1,0:T(8,128)(2,1)S(1)}, bf16[32,1536]{1,0:T(8,128)(2,1)S(1)}, u32[]{:S(2)}, u32[]{:S(2)}) collective-permute-start(bf16[32,1536]{1,0:T(8,128)(2,1)S(1)} %collective-permute-done.14.refs_8_.refs_2_), channel_id=1, source_target_pairs={{0,8},{8,0},{16,24},{24,16},{1,9},{9,1},{17,25},{25,17},{2,10},{10... | collective-permute-start | bytes 294920 | tf_op jit(solution)/shard_map/ppermute | solution.py:20
  61.0 4.5 %collective-permute-done.16.refs_2_ = bf16[32,2048]{1,0:T(8,128)(2,1)S(1)} collective-permute-done((bf16[32,2048]{1,0:T(8,128)(2,1)S(1)}, bf16[32,2048]{1,0:T(8,128)(2,1)S(1)}, u32[]{:S(2)}, u32[]{:S(2)}) %collective-permute-start.16) | collective-permute-done | bytes 131104 | tf_op jit(solution)/shard_map/ppermute | solution.py:20
  65.5 2.9 %fetch_down.3.refs_4_ = bf16[1536,2048]{1,0:T(8,128)(2,1)S(1)} custom-call(bf16[3584,2048]{1,0:T(8,128)(2,1)} %refs_0_.9, bf16[2048,2048]{1,0:T(8,128)(2,1)S(1)} %fetch_down.2.refs_9_.refs_1_.refs_4_), custom_call_target="tpu_custom_call" | custom-call | tf_op jit(solution)/shard_map/fetch_down/pallas_call | solution.py:24
  73.2 2.5 %collective-permute-start.20 = (bf16[128,256]{1,0:T(8,128)(2,1)S(1)}, bf16[128,256]{1,0:T(8,128)(2,1)S(1)}, u32[]{:S(2)}, u32[]{:S(2)}) collective-permute-start(bf16[128,256]{1,0:T(8,128)(2,1)S(1)} %get-tuple-element.51), channel_id=1, source_target_pairs={{0,6},{1,7},{2,4},{3,5},{4,2},{5,3},{6,0},{7,1},{8,14},{9,15},{10,... | collective-permute-start | bytes 196616 | tf_op jit(solution)/shard_map/ppermute | solution.py:20
  76.8 1.9 %collective-permute-done.20 = bf16[128,256]{1,0:T(8,128)(2,1)S(1)} collective-permute-done((bf16[128,256]{1,0:T(8,128)(2,1)S(1)}, bf16[128,256]{1,0:T(8,128)(2,1)S(1)}, u32[]{:S(2)}, u32[]{:S(2)}) %collective-permute-start.20) | collective-permute-done | bytes 65568 | tf_op jit(solution)/shard_map/ppermute | solution.py:20
  81.0 2.4 %collective-permute-start.24 = (bf16[128,256]{1,0:T(8,128)(2,1)S(1)}, bf16[128,256]{1,0:T(8,128)(2,1)S(1)}, u32[]{:S(2)}, u32[]{:S(2)}) collective-permute-start(bf16[128,256]{1,0:T(8,128)(2,1)S(1)} %add_convert_fusion.own_ref), channel_id=1, source_target_pairs={{0,16},{8,24},{16,0},{24,8},{1,17},{9,25},{17,1},{25,9},{2,18},{10... | collective-permute-start | bytes 196616 | tf_op jit(solution)/shard_map/ppermute | solution.py:20
  86.5 3.0 %collective-permute-done.25 = bf16[128,256]{1,0:T(8,128)(2,1)S(1)} collective-permute-done((bf16[128,256]{1,0:T(8,128)(2,1)S(1)}, bf16[128,256]{1,0:T(8,128)(2,1)S(1)}, u32[]{:S(2)}, u32[]{:S(2)}) %collective-permute-start.25) | collective-permute-done | bytes 65568 | tf_op jit(solution)/shard_map/ppermute | solution.py:20
  93.8 2.8 %collective-permute-start.30 = (bf16[128,256]{1,0:T(8,128)(2,1)S(1)}, bf16[128,256]{1,0:T(8,128)(2,1)S(1)}, u32[]{:S(2)}, u32[]{:S(2)}) collective-permute-start(bf16[128,256]{1,0:T(8,128)(2,1)S(1)} %collective-permute-done.26.refs_4_), channel_id=1, source_target_pairs={{0,16},{8,24},{16,0},{24,8},{1,17},{9,25},{17,1},{25,9},{2,18},{10... | collective-permute-start | bytes 196616 | tf_op jit(solution)/shard_map/ppermute | solution.py:20
  96.6 2.4 %gram.3 = (f32[256,8192]{1,0:T(8,128)}, f32[64,256]{1,0:T(8,128)}) custom-call(bf16[128,256]{1,0:T(8,128)(2,1)S(1)} %add_convert_fusion.own_ref, bf16[4,128,256]{2,1,0:T(8,128)(2,1)S(1)} %get-tuple-element.54.refs_0_, bf16[4,128,256]{2,1,0:T(8,128)(2,1)S(1)} %collective-permute-done.32.refs_1_, bf16[1,128,256]{2,1,0:T(8,128)(2,1)S(1)} %bitcast.13, ...), custom_call_target="tpu_custom_call" | custom-call | flops 167772160 | bytes 2621440 | tf_op jit(solution)/shard_map/gram/pallas_call | solution.py:24
  101.7 1.9 %gram.4.refs_1_ = f32[256,8192]{1,0:T(8,128)} custom-call(bf16[128,256]{1,0:T(8,128)(2,1)S(1)} %add_convert_fusion.own_ref, bf16[11,128,256]{2,1,0:T(8,128)(2,1)S(1)} %stack.3.refs_0_, f32[256,8192]{1,0:T(8,128)} %get-tuple-element.56.refs_5_.refs_1_), custom_call_target="tpu_custom_call", output_to_operand_aliasing={{}: (2, {})} | custom-call | flops 184549376 | bytes 2883584 | tf_op jit(solution)/shard_map/gram/pallas_call | solution.py:24
  (74 shorter events, 32.8 us)
Async XLA Ops:
  0.6 9.4 %collective-permute-start = (bf16[16,2048]{1,0:T(8,128)(2,1)}, bf16[16,2048]{1,0:T(8,128)(2,1)S(1)}, u32[]{:S(2)}, u32[]{:S(2)}) collective-permute-start(bf16[16,2048]{1,0:T(8,128)(2,1)} %refs_2_.1), channel_id=1, source_target_pairs={{0,2},{1,3},{2,0},{3,1},{4,6},{5,7},{6,4},{7,5},{8,10},{9,11},{10,... | collective-permute-start | bytes 196616 | tf_op jit(solution)/shard_map/ppermute | solution.py:20
  3.6 7.0 %collective-permute-start.1 = (bf16[16,2048]{1,0:T(8,128)(2,1)}, bf16[16,2048]{1,0:T(8,128)(2,1)S(1)}, u32[]{:S(2)}, u32[]{:S(2)}) collective-permute-start(bf16[16,2048]{1,0:T(8,128)(2,1)} %refs_2_.1), channel_id=1, source_target_pairs={{0,4},{1,5},{2,6},{3,7},{4,0},{5,1},{6,2},{7,3},{8,12},{9,13},{10,... | collective-permute-start | bytes 196616 | tf_op jit(solution)/shard_map/ppermute | solution.py:20
  5.2 5.6 %collective-permute-start.2 = (bf16[16,2048]{1,0:T(8,128)(2,1)}, bf16[16,2048]{1,0:T(8,128)(2,1)S(1)}, u32[]{:S(2)}, u32[]{:S(2)}) collective-permute-start(bf16[16,2048]{1,0:T(8,128)(2,1)} %refs_2_.1), channel_id=1, source_target_pairs={{0,6},{1,7},{2,4},{3,5},{4,2},{5,3},{6,0},{7,1},{8,14},{9,15},{10,... | collective-permute-start | bytes 196616 | tf_op jit(solution)/shard_map/ppermute | solution.py:20
  5.2 6.0 %collective-permute-start.3 = (bf16[16,2048]{1,0:T(8,128)(2,1)}, bf16[16,2048]{1,0:T(8,128)(2,1)S(1)}, u32[]{:S(2)}, u32[]{:S(2)}) collective-permute-start(bf16[16,2048]{1,0:T(8,128)(2,1)} %refs_2_.1), channel_id=1, source_target_pairs={{0,1},{1,0},{2,3},{3,2},{4,5},{5,4},{6,7},{7,6},{8,9},{9,8},{10,11... | collective-permute-start | bytes 196616 | tf_op jit(solution)/shard_map/ppermute | solution.py:20
  14.3 12.4 %collective-permute-start.8 = (bf16[2,32,3200]{2,1,0:T(8,128)(2,1)S(1)}, bf16[2,32,3200]{2,1,0:T(8,128)(2,1)S(1)}, u32[]{:S(2)}, u32[]{:S(2)}) collective-permute-start(bf16[2,32,3200]{2,1,0:T(8,128)(2,1)S(1)} %get-tuple-element.37.refs_2_), channel_id=1, source_target_pairs={{0,8},{8,0},{16,24},{24,16},{1,9},{9,1},{17,25},{25,17},{2,10},{10... | collective-permute-start | bytes 1228808 | tf_op jit(solution)/shard_map/ppermute | solution.py:20
  22.3 15.9 %collective-permute-start.7 = (bf16[2,32,2560]{2,1,0:T(8,128)(2,1)S(1)}, bf16[2,32,2560]{2,1,0:T(8,128)(2,1)S(1)}, u32[]{:S(2)}, u32[]{:S(2)}) collective-permute-start(bf16[2,32,2560]{2,1,0:T(8,128)(2,1)S(1)} %get-tuple-element.41.refs_0_), channel_id=1, source_target_pairs={{0,8},{8,0},{16,24},{24,16},{1,9},{9,1},{17,25},{25,17},{2,10},{10... | collective-permute-start | bytes 983048 | tf_op jit(solution)/shard_map/ppermute | solution.py:20
  26.9 18.8 %collective-permute-start.12 = (bf16[32,3200]{1,0:T(8,128)(2,1)S(1)}, bf16[32,3200]{1,0:T(8,128)(2,1)S(1)}, u32[]{:S(2)}, u32[]{:S(2)}) collective-permute-start(bf16[32,3200]{1,0:T(8,128)(2,1)S(1)} %pair_total.3.refs_2_), channel_id=1, source_target_pairs={{0,16},{8,24},{16,0},{24,8},{1,17},{9,25},{17,1},{25,9},{2,18},{10... | collective-permute-start | bytes 614408 | tf_op jit(solution)/shard_map/ppermute | solution.py:20
  34.0 11.1 %collective-permute-start.10 = (bf16[2,32,1536]{2,1,0:T(8,128)(2,1)S(1)}, bf16[2,32,1536]{2,1,0:T(8,128)(2,1)S(1)}, u32[]{:S(2)}, u32[]{:S(2)}) collective-permute-start(bf16[2,32,1536]{2,1,0:T(8,128)(2,1)S(1)} %get-tuple-element.45.refs_0_), channel_id=1, source_target_pairs={{0,8},{8,0},{16,24},{24,16},{1,9},{9,1},{17,25},{25,17},{2,10},{10... | collective-permute-start | bytes 589832 | tf_op jit(solution)/shard_map/ppermute | solution.py:20
  38.2 13.9 %collective-permute-start.9 = (bf16[32,2560]{1,0:T(8,128)(2,1)S(1)}, bf16[32,2560]{1,0:T(8,128)(2,1)S(1)}, u32[]{:S(2)}, u32[]{:S(2)}) collective-permute-start(bf16[32,2560]{1,0:T(8,128)(2,1)S(1)} %pair_total.4.refs_0_.refs_3_), channel_id=1, source_target_pairs={{0,16},{8,24},{16,0},{24,8},{1,17},{9,25},{17,1},{25,9},{2,18},{10... | collective-permute-start | bytes 491528 | tf_op jit(solution)/shard_map/ppermute | solution.py:20
  45.2 9.6 %collective-permute-start.11 = (bf16[32,1536]{1,0:T(8,128)(2,1)S(1)}, bf16[32,1536]{1,0:T(8,128)(2,1)S(1)}, u32[]{:S(2)}, u32[]{:S(2)}) collective-permute-start(bf16[32,1536]{1,0:T(8,128)(2,1)S(1)} %pair_total.5.refs_1_), channel_id=1, source_target_pairs={{0,16},{8,24},{16,0},{24,8},{1,17},{9,25},{17,1},{25,9},{2,18},{10... | collective-permute-start | bytes 294920 | tf_op jit(solution)/shard_map/ppermute | solution.py:20
  46.0 10.7 %collective-permute-start.14 = (bf16[32,1536]{1,0:T(8,128)(2,1)S(1)}, bf16[32,1536]{1,0:T(8,128)(2,1)S(1)}, u32[]{:S(2)}, u32[]{:S(2)}) collective-permute-start(bf16[32,1536]{1,0:T(8,128)(2,1)S(1)} %get-tuple-element.48.refs_0_), channel_id=1, source_target_pairs={{0,16},{8,24},{16,0},{24,8},{1,17},{9,25},{17,1},{25,9},{2,18},{10... | collective-permute-start | bytes 294920 | tf_op jit(solution)/shard_map/ppermute | solution.py:20
  48.4 8.3 %collective-permute-start.13 = (bf16[32,1536]{1,0:T(8,128)(2,1)S(1)}, bf16[32,1536]{1,0:T(8,128)(2,1)S(1)}, u32[]{:S(2)}, u32[]{:S(2)}) collective-permute-start(bf16[32,1536]{1,0:T(8,128)(2,1)S(1)} %get-tuple-element.48.refs_0_), channel_id=1, source_target_pairs={{0,8},{8,0},{16,24},{24,16},{1,9},{9,1},{17,25},{25,17},{2,10},{10... | collective-permute-start | bytes 294920 | tf_op jit(solution)/shard_map/ppermute | solution.py:20
  57.4 8.1 %collective-permute-start.16 = (bf16[32,2048]{1,0:T(8,128)(2,1)S(1)}, bf16[32,2048]{1,0:T(8,128)(2,1)S(1)}, u32[]{:S(2)}, u32[]{:S(2)}) collective-permute-start(bf16[32,2048]{1,0:T(8,128)(2,1)S(1)} %get-tuple-element.49.refs_0_), channel_id=1, source_target_pairs={{0,16},{8,24},{16,0},{24,8},{1,17},{9,25},{17,1},{25,9},{2,18},{10... | collective-permute-start | bytes 393224 | tf_op jit(solution)/shard_map/ppermute | solution.py:20
  58.5 9.9 %collective-permute-start.18 = (bf16[32,1536]{1,0:T(8,128)(2,1)S(1)}, bf16[32,1536]{1,0:T(8,128)(2,1)S(1)}, u32[]{:S(2)}, u32[]{:S(2)}) collective-permute-start(bf16[32,1536]{1,0:T(8,128)(2,1)S(1)} %collective-permute-done.14.refs_8_.refs_2_), channel_id=1, source_target_pairs={{0,8},{8,0},{16,24},{24,16},{1,9},{9,1},{17,25},{25,17},{2,10},{10... | collective-permute-start | bytes 294920 | tf_op jit(solution)/shard_map/ppermute | solution.py:20
  60.9 8.1 %collective-permute-start.15 = (bf16[32,2048]{1,0:T(8,128)(2,1)S(1)}, bf16[32,2048]{1,0:T(8,128)(2,1)S(1)}, u32[]{:S(2)}, u32[]{:S(2)}) collective-permute-start(bf16[32,2048]{1,0:T(8,128)(2,1)S(1)} %get-tuple-element.49.refs_0_), channel_id=1, source_target_pairs={{0,8},{8,0},{16,24},{24,16},{1,9},{9,1},{17,25},{25,17},{2,10},{10... | collective-permute-start | bytes 393224 | tf_op jit(solution)/shard_map/ppermute | solution.py:20
  73.2 5.5 %collective-permute-start.20 = (bf16[128,256]{1,0:T(8,128)(2,1)S(1)}, bf16[128,256]{1,0:T(8,128)(2,1)S(1)}, u32[]{:S(2)}, u32[]{:S(2)}) collective-permute-start(bf16[128,256]{1,0:T(8,128)(2,1)S(1)} %get-tuple-element.51), channel_id=1, source_target_pairs={{0,6},{1,7},{2,4},{3,5},{4,2},{5,3},{6,0},{7,1},{8,14},{9,15},{10,... | collective-permute-start | bytes 196616 | tf_op jit(solution)/shard_map/ppermute | solution.py:20
  80.5 6.0 %collective-permute-start.23 = (bf16[128,256]{1,0:T(8,128)(2,1)S(1)}, bf16[128,256]{1,0:T(8,128)(2,1)S(1)}, u32[]{:S(2)}, u32[]{:S(2)}) collective-permute-start(bf16[128,256]{1,0:T(8,128)(2,1)S(1)} %add_convert_fusion.own_ref), channel_id=1, source_target_pairs={{0,8},{8,0},{16,24},{24,16},{1,9},{9,1},{17,25},{25,17},{2,10},{10... | collective-permute-start | bytes 196616 | tf_op jit(solution)/shard_map/ppermute | solution.py:20
  81.0 5.5 %collective-permute-start.24 = (bf16[128,256]{1,0:T(8,128)(2,1)S(1)}, bf16[128,256]{1,0:T(8,128)(2,1)S(1)}, u32[]{:S(2)}, u32[]{:S(2)}) collective-permute-start(bf16[128,256]{1,0:T(8,128)(2,1)S(1)} %add_convert_fusion.own_ref), channel_id=1, source_target_pairs={{0,16},{8,24},{16,0},{24,8},{1,17},{9,25},{17,1},{25,9},{2,18},{10... | collective-permute-start | bytes 196616 | tf_op jit(solution)/shard_map/ppermute | solution.py:20
  83.4 6.1 %collective-permute-start.25 = (bf16[128,256]{1,0:T(8,128)(2,1)S(1)}, bf16[128,256]{1,0:T(8,128)(2,1)S(1)}, u32[]{:S(2)}, u32[]{:S(2)}) collective-permute-start(bf16[128,256]{1,0:T(8,128)(2,1)S(1)} %add_convert_fusion.own_ref), channel_id=1, source_target_pairs={{0,24},{8,16},{16,8},{24,0},{1,25},{9,17},{17,9},{25,1},{2,26},{10... | collective-permute-start | bytes 196616 | tf_op jit(solution)/shard_map/ppermute | solution.py:20
  90.2 11.3 %collective-permute-start.27 = (bf16[4,128,256]{2,1,0:T(8,128)(2,1)S(1)}, bf16[4,128,256]{2,1,0:T(8,128)(2,1)S(1)}, u32[]{:S(2)}, u32[]{:S(2)}) collective-permute-start(bf16[4,128,256]{2,1,0:T(8,128)(2,1)S(1)} %get-tuple-element.54.refs_0_), channel_id=1, source_target_pairs={{0,2},{1,3},{2,0},{3,1},{4,6},{5,7},{6,4},{7,5},{8,10},{9,11},{10,... | collective-permute-start | bytes 786440 | tf_op jit(solution)/shard_map/ppermute | solution.py:20
  91.4 10.1 %collective-permute-start.28 = (bf16[4,128,256]{2,1,0:T(8,128)(2,1)S(1)}, bf16[4,128,256]{2,1,0:T(8,128)(2,1)S(1)}, u32[]{:S(2)}, u32[]{:S(2)}) collective-permute-start(bf16[4,128,256]{2,1,0:T(8,128)(2,1)S(1)} %get-tuple-element.54.refs_0_), channel_id=1, source_target_pairs={{0,4},{1,5},{2,6},{3,7},{4,0},{5,1},{6,2},{7,3},{8,12},{9,13},{10,... | collective-permute-start | bytes 786440 | tf_op jit(solution)/shard_map/ppermute | solution.py:20
  92.4 9.1 %collective-permute-start.31 = (bf16[144,256]{1,0:T(8,128)(2,1)S(1)}, bf16[144,256]{1,0:T(8,128)(2,1)S(1)}, u32[]{:S(2)}, u32[]{:S(2)}) collective-permute-start(bf16[144,256]{1,0:T(8,128)(2,1)S(1)} %get-tuple-element.55), channel_id=1, source_target_pairs={{0,6},{1,7},{2,4},{3,5},{4,2},{5,3},{6,0},{7,1},{8,14},{9,15},{10,... | collective-permute-start | bytes 221192 | tf_op jit(solution)/shard_map/ppermute | solution.py:20
  93.8 5.4 %collective-permute-start.29 = (bf16[128,256]{1,0:T(8,128)(2,1)S(1)}, bf16[128,256]{1,0:T(8,128)(2,1)S(1)}, u32[]{:S(2)}, u32[]{:S(2)}) collective-permute-start(bf16[128,256]{1,0:T(8,128)(2,1)S(1)} %collective-permute-done.26.refs_4_), channel_id=1, source_target_pairs={{0,8},{8,0},{16,24},{24,16},{1,9},{9,1},{17,25},{25,17},{2,10},{10... | collective-permute-start | bytes 196616 | tf_op jit(solution)/shard_map/ppermute | solution.py:20
  93.8 6.6 %collective-permute-start.30 = (bf16[128,256]{1,0:T(8,128)(2,1)S(1)}, bf16[128,256]{1,0:T(8,128)(2,1)S(1)}, u32[]{:S(2)}, u32[]{:S(2)}) collective-permute-start(bf16[128,256]{1,0:T(8,128)(2,1)S(1)} %collective-permute-done.26.refs_4_), channel_id=1, source_target_pairs={{0,16},{8,24},{16,0},{24,8},{1,17},{9,25},{17,1},{25,9},{2,18},{10... | collective-permute-start | bytes 196616 | tf_op jit(solution)/shard_map/ppermute | solution.py:20
  (12 other events, 57.1 us)

commit v13 on v12

--- a/solution.py
+++ b/solution.py
@@ -361,16 +361,16 @@
     got_2 = swap(send_2, "tok", n_tok, 1)
     sum_1 = pair_total(keep_1, got_1, 2 * widths[1], (send_2,))
     over_1 = swap(sum_1, "tok", n_tok, 2)
-    sum_2 = pair_total(keep_2, got_2, 2 * widths[2], (sum_1,))
+    down_b, = fetch([(down_weight, ends[1], shard_ff - ends[1], 0, block)], (sum_1,), "fetch_down")
+    sum_2 = pair_total(keep_2, got_2, 2 * widths[2], (down_b,))
     over_2 = swap(sum_2, "tok", n_tok, 2)
 
     a_own, scale = hidden_rows([(keep_0, got_0, over_0)], widths[:1], None, (sum_1,))
     a_two = swap(a_own, "tok", n_tok, 2)
     a_one = swap(a_own, "tok", n_tok, 1)
     a_three = swap(a_two, "tok", n_tok, 1)
-    down_b, = fetch([(down_weight, ends[1], shard_ff - ends[1], 0, block)], (sum_2,), "fetch_down")
-    down_a, = fetch([(down_weight, 0, ends[1], 0, block)], (down_b,), "fetch_down")
-    b_own, _ = hidden_rows([(keep_1, got_1, over_1), (keep_2, got_2, over_2)], widths[1:], scale, (a_one, a_two, down_b))
+    down_a, = fetch([(down_weight, 0, ends[1], 0, block)], (sum_2,), "fetch_down")
+    b_own, _ = hidden_rows([(keep_1, got_1, over_1), (keep_2, got_2, over_2)], widths[1:], scale, (a_one, a_three, down_a))
     b_two = swap(b_own, "tok", n_tok, 2)
     b_one = swap(b_own, "tok", n_tok, 1)
     b_three = swap(b_two, "tok", n_tok, 1)

time: 106 us -> 107 us (level)
  starting transfers between devices: 36.7 us -> 41.6 us
  waiting for transfers between devices: 34.5 us -> 30.7 us
    ppermute x35, starting transfers between devices: 36.7 us -> 41.6 us  [swap(): return lax.ppermute(value, axis, [(i, i ^ mask) for i in range(size)])]
    ppermute x35, waiting for transfers between devices: 34.5 us -> 30.7 us  [swap(): return lax.ppermute(value, axis, [(i, i ^ mask) for i in range(size)])]
  transfers between devices with their start and end apart: 35 -> 35, of which waited for: 20 -> 22; matrix products, arithmetic and copies ran while one was open for 0% -> 0% of each run, Pallas kernels for 26% -> 26%
where the time goes in v13:
time: 107 us
  starting transfers between devices  41.6 us (39%)
  Pallas kernels  33.6 us (31%)
  waiting for transfers between devices  30.7 us (29%)
    ppermute x35, starting transfers between devices, swap(): return lax.ppermute(value, axis, [(i, i ^ mask) for i in range(size)])  41.6 us
    pallas_call x25, Pallas kernels, run(): pl.pallas_call(body, out_shape=out_shape, in_specs=[WHOLE] * len(operands...  33.6 us
    ppermute x35, waiting for transfers between devices, swap(): return lax.ppermute(value, axis, [(i, i ^ mask) for i in range(size)])  30.7 us
  transfers between devices with their start and end apart: 35, of which 22 were waited for; matrix products, arithmetic and copies ran while one was open for 0% of the time, Pallas kernels for 26%

profile of v13, /device:TPU:0, one launch (start us, length us, event | category | flops | bytes accessed | tf_op | source)
XLA Modules:
  0.0 106.8 jit_solution(5719032247005502339)
XLA Ops:
  0.6 3.0 %collective-permute-start = (bf16[16,2048]{1,0:T(8,128)(2,1)}, bf16[16,2048]{1,0:T(8,128)(2,1)S(1)}, u32[]{:S(2)}, u32[]{:S(2)}) collective-permute-start(bf16[16,2048]{1,0:T(8,128)(2,1)} %refs_2_.1), channel_id=1, source_target_pairs={{0,2},{1,3},{2,0},{3,1},{4,6},{5,7},{6,4},{7,5},{8,10},{9,11},{10,... | collective-permute-start | bytes 196616 | tf_op jit(solution)/shard_map/ppermute | solution.py:20
  5.2 4.9 %fetch_first.1 = (bf16[2048,1536]{1,0:T(8,128)(2,1)S(1)}, bf16[2048,1536]{1,0:T(8,128)(2,1)S(1)}, bf16[16,2048]{1,0:T(8,128)(2,1)S(1)}, f32[1,2048]{1,0:T(1,128)S(1)}) custom-call(bf16[2048,3584]{1,0:T(8,128)(2,1)} %refs_0_.7, bf16[2048,3584]{1,0:T(8,128)(2,1)} %refs_1_.5, bf16[16,2048]{1,0:T(8,128)(2,1)} %refs_2_.1, f32[1,2048]{1,0:T(1,128)} %bitcast.22), custom_call_target="tpu_custom_call" | custom-call | tf_op jit(solution)/shard_map/fetch_first/pallas_call | solution.py:24
  12.4 2.0 %gate_up.3 = (bf16[2,32,3200]{2,1,0:T(8,128)(2,1)S(1)}, bf16[2,32,3200]{2,1,0:T(8,128)(2,1)S(1)}) custom-call(bf16[128,2048]{1,0:T(8,128)(2,1)S(1)} %get-tuple-element.33.lhs_ref, bf16[2048,1536]{1,0:T(8,128)(2,1)S(1)} %get-tuple-element.34.gate_ref, bf16[2048,1536]{1,0:T(8,128)(2,1)S(1)} %get-tuple-element.35.up_ref, f32[128,1]{1,0:T(8,128)S(1)} %get-tuple-element.36.refs_0_), custom_call_target="tpu_custom_call" | custom-call | tf_op jit(solution)/shard_map/gate_up/pallas_call | solution.py:24
  14.3 2.1 %collective-permute-start.8 = (bf16[2,32,3200]{2,1,0:T(8,128)(2,1)S(1)}, bf16[2,32,3200]{2,1,0:T(8,128)(2,1)S(1)}, u32[]{:S(2)}, u32[]{:S(2)}) collective-permute-start(bf16[2,32,3200]{2,1,0:T(8,128)(2,1)S(1)} %get-tuple-element.37.refs_2_), channel_id=1, source_target_pairs={{0,8},{8,0},{16,24},{24,16},{1,9},{9,1},{17,25},{25,17},{2,10},{10... | collective-permute-start | bytes 1228808 | tf_op jit(solution)/shard_map/ppermute | solution.py:20
  16.5 4.1 %fetch_gate_up.2 = (bf16[2048,1280]{1,0:T(8,128)(2,1)S(1)}, bf16[2048,1280]{1,0:T(8,128)(2,1)S(1)}) custom-call(bf16[2048,3584]{1,0:T(8,128)(2,1)} %refs_0_.7, bf16[2048,3584]{1,0:T(8,128)(2,1)} %refs_1_.5, bf16[2,32,3200]{2,1,0:T(8,128)(2,1)S(1)} %get-tuple-element.37.refs_2_), custom_call_target="tpu_custom_call" | custom-call | tf_op jit(solution)/shard_map/fetch_gate_up/pallas_call | solution.py:24
  22.3 4.4 %collective-permute-done.8.got_ref.refs_1_ = bf16[2,32,3200]{2,1,0:T(8,128)(2,1)S(1)} collective-permute-done((bf16[2,32,3200]{2,1,0:T(8,128)(2,1)S(1)}, bf16[2,32,3200]{2,1,0:T(8,128)(2,1)S(1)}, u32[]{:S(2)}, u32[]{:S(2)}) %collective-permute-start.8) | collective-permute-done | bytes 409632 | tf_op jit(solution)/shard_map/ppermute | solution.py:20
  26.9 3.1 %collective-permute-start.12 = (bf16[32,3200]{1,0:T(8,128)(2,1)S(1)}, bf16[32,3200]{1,0:T(8,128)(2,1)S(1)}, u32[]{:S(2)}, u32[]{:S(2)}) collective-permute-start(bf16[32,3200]{1,0:T(8,128)(2,1)S(1)} %pair_total.3.refs_2_), channel_id=1, source_target_pairs={{0,16},{8,24},{16,0},{24,8},{1,17},{9,25},{17,1},{25,9},{2,18},{10... | collective-permute-start | bytes 614408 | tf_op jit(solution)/shard_map/ppermute | solution.py:20
  30.0 2.9 %fetch_gate_up.3 = (bf16[2048,768]{1,0:T(8,128)(2,1)S(1)}, bf16[2048,768]{1,0:T(8,128)(2,1)S(1)}) custom-call(bf16[2048,3584]{1,0:T(8,128)(2,1)} %refs_0_.7, bf16[2048,3584]{1,0:T(8,128)(2,1)} %refs_1_.5, bf16[32,3200]{1,0:T(8,128)(2,1)S(1)} %pair_total.3.refs_2_), custom_call_target="tpu_custom_call" | custom-call | tf_op jit(solution)/shard_map/fetch_gate_up/pallas_call | solution.py:24
  35.7 2.5 %collective-permute-done.7.got_ref.refs_1_ = bf16[2,32,2560]{2,1,0:T(8,128)(2,1)S(1)} collective-permute-done((bf16[2,32,2560]{2,1,0:T(8,128)(2,1)S(1)}, bf16[2,32,2560]{2,1,0:T(8,128)(2,1)S(1)}, u32[]{:S(2)}, u32[]{:S(2)}) %collective-permute-start.7) | collective-permute-done | bytes 327712 | tf_op jit(solution)/shard_map/ppermute | solution.py:20
  38.4 2.9 %collective-permute-start.14 = (bf16[32,1536]{1,0:T(8,128)(2,1)S(1)}, bf16[32,1536]{1,0:T(8,128)(2,1)S(1)}, u32[]{:S(2)}, u32[]{:S(2)}) collective-permute-start(bf16[32,1536]{1,0:T(8,128)(2,1)S(1)} %get-tuple-element.48.refs_0_), channel_id=1, source_target_pairs={{0,16},{8,24},{16,0},{24,8},{1,17},{9,25},{17,1},{25,9},{2,18},{10... | collective-permute-start | bytes 294920 | tf_op jit(solution)/shard_map/ppermute | solution.py:20
  41.4 3.5 %fetch_down.2.refs_0_.refs_4_ = bf16[2048,2048]{1,0:T(8,128)(2,1)S(1)} custom-call(bf16[3584,2048]{1,0:T(8,128)(2,1)} %refs_0_.9, bf16[32,2560]{1,0:T(8,128)(2,1)S(1)} %pair_total.4.refs_1_.refs_3_), custom_call_target="tpu_custom_call" | custom-call | tf_op jit(solution)/shard_map/fetch_down/pallas_call | solution.py:24
  45.0 2.9 %collective-permute-start.11 = (bf16[32,1536]{1,0:T(8,128)(2,1)S(1)}, bf16[32,1536]{1,0:T(8,128)(2,1)S(1)}, u32[]{:S(2)}, u32[]{:S(2)}) collective-permute-start(bf16[32,1536]{1,0:T(8,128)(2,1)S(1)} %pair_total.5.refs_1_), channel_id=1, source_target_pairs={{0,16},{8,24},{16,0},{24,8},{1,17},{9,25},{17,1},{25,9},{2,18},{10... | collective-permute-start | bytes 294920 | tf_op jit(solution)/shard_map/ppermute | solution.py:20
  47.9 1.9 %collective-permute-start.13 = (bf16[32,1536]{1,0:T(8,128)(2,1)S(1)}, bf16[32,1536]{1,0:T(8,128)(2,1)S(1)}, u32[]{:S(2)}, u32[]{:S(2)}) collective-permute-start(bf16[32,1536]{1,0:T(8,128)(2,1)S(1)} %get-tuple-element.48.refs_0_), channel_id=1, source_target_pairs={{0,8},{8,0},{16,24},{24,16},{1,9},{9,1},{17,25},{25,17},{2,10},{10... | collective-permute-start | bytes 294920 | tf_op jit(solution)/shard_map/ppermute | solution.py:20
  52.4 2.9 %fetch_down.3.refs_9_.refs_4_ = bf16[1536,2048]{1,0:T(8,128)(2,1)S(1)} custom-call(bf16[3584,2048]{1,0:T(8,128)(2,1)} %refs_0_.9, bf16[32,1536]{1,0:T(8,128)(2,1)S(1)} %pair_total.5.refs_1_), custom_call_target="tpu_custom_call" | custom-call | tf_op jit(solution)/shard_map/fetch_down/pallas_call | solution.py:24
  60.4 2.5 %collective-permute-start.16 = (bf16[32,2048]{1,0:T(8,128)(2,1)S(1)}, bf16[32,2048]{1,0:T(8,128)(2,1)S(1)}, u32[]{:S(2)}, u32[]{:S(2)}) collective-permute-start(bf16[32,2048]{1,0:T(8,128)(2,1)S(1)} %get-tuple-element.49.refs_0_), channel_id=1, source_target_pairs={{0,8},{8,0},{16,24},{24,16},{1,9},{9,1},{17,25},{25,17},{2,10},{10... | collective-permute-start | bytes 393224 | tf_op jit(solution)/shard_map/ppermute | solution.py:20
  62.9 3.9 %collective-permute-done.17.refs_2_ = bf16[32,2048]{1,0:T(8,128)(2,1)S(1)} collective-permute-done((bf16[32,2048]{1,0:T(8,128)(2,1)S(1)}, bf16[32,2048]{1,0:T(8,128)(2,1)S(1)}, u32[]{:S(2)}, u32[]{:S(2)}) %collective-permute-start.17) | collective-permute-done | bytes 131104 | tf_op jit(solution)/shard_map/ppermute | solution.py:20
  67.5 4.3 %collective-permute-done.18.refs_3_ = bf16[32,2048]{1,0:T(8,128)(2,1)S(1)} collective-permute-done((bf16[32,2048]{1,0:T(8,128)(2,1)S(1)}, bf16[32,2048]{1,0:T(8,128)(2,1)S(1)}, u32[]{:S(2)}, u32[]{:S(2)}) %collective-permute-start.18) | collective-permute-done | bytes 131104 | tf_op jit(solution)/shard_map/ppermute | solution.py:20
  74.3 2.5 %collective-permute-start.20 = (bf16[128,256]{1,0:T(8,128)(2,1)S(1)}, bf16[128,256]{1,0:T(8,128)(2,1)S(1)}, u32[]{:S(2)}, u32[]{:S(2)}) collective-permute-start(bf16[128,256]{1,0:T(8,128)(2,1)S(1)} %get-tuple-element.51), channel_id=1, source_target_pairs={{0,6},{1,7},{2,4},{3,5},{4,2},{5,3},{6,0},{7,1},{8,14},{9,15},{10,... | collective-permute-start | bytes 196616 | tf_op jit(solution)/shard_map/ppermute | solution.py:20
  77.8 1.9 %collective-permute-done.20 = bf16[128,256]{1,0:T(8,128)(2,1)S(1)} collective-permute-done((bf16[128,256]{1,0:T(8,128)(2,1)S(1)}, bf16[128,256]{1,0:T(8,128)(2,1)S(1)}, u32[]{:S(2)}, u32[]{:S(2)}) %collective-permute-start.20) | collective-permute-done | bytes 65568 | tf_op jit(solution)/shard_map/ppermute | solution.py:20
  81.7 2.8 %collective-permute-start.24 = (bf16[128,256]{1,0:T(8,128)(2,1)S(1)}, bf16[128,256]{1,0:T(8,128)(2,1)S(1)}, u32[]{:S(2)}, u32[]{:S(2)}) collective-permute-start(bf16[128,256]{1,0:T(8,128)(2,1)S(1)} %add_convert_fusion.own_ref), channel_id=1, source_target_pairs={{0,16},{8,24},{16,0},{24,8},{1,17},{9,25},{17,1},{25,9},{2,18},{10... | collective-permute-start | bytes 196616 | tf_op jit(solution)/shard_map/ppermute | solution.py:20
  94.9 2.8 %collective-permute-start.30 = (bf16[128,256]{1,0:T(8,128)(2,1)S(1)}, bf16[128,256]{1,0:T(8,128)(2,1)S(1)}, u32[]{:S(2)}, u32[]{:S(2)}) collective-permute-start(bf16[128,256]{1,0:T(8,128)(2,1)S(1)} %collective-permute-done.26.refs_4_), channel_id=1, source_target_pairs={{0,16},{8,24},{16,0},{24,8},{1,17},{9,25},{17,1},{25,9},{2,18},{10... | collective-permute-start | bytes 196616 | tf_op jit(solution)/shard_map/ppermute | solution.py:20
  97.8 2.5 %gram.3 = (f32[256,8192]{1,0:T(8,128)}, f32[64,256]{1,0:T(8,128)}) custom-call(bf16[128,256]{1,0:T(8,128)(2,1)S(1)} %add_convert_fusion.own_ref, bf16[4,128,256]{2,1,0:T(8,128)(2,1)S(1)} %get-tuple-element.54.refs_0_, bf16[4,128,256]{2,1,0:T(8,128)(2,1)S(1)} %collective-permute-done.32.refs_1_, bf16[1,128,256]{2,1,0:T(8,128)(2,1)S(1)} %bitcast.13, ...), custom_call_target="tpu_custom_call" | custom-call | flops 167772160 | bytes 2621440 | tf_op jit(solution)/shard_map/gram/pallas_call | solution.py:24
  102.7 1.9 %gram.4.refs_1_ = f32[256,8192]{1,0:T(8,128)} custom-call(bf16[128,256]{1,0:T(8,128)(2,1)S(1)} %add_convert_fusion.own_ref, bf16[11,128,256]{2,1,0:T(8,128)(2,1)S(1)} %stack.3.refs_0_, f32[256,8192]{1,0:T(8,128)} %get-tuple-element.56.refs_5_.refs_1_), custom_call_target="tpu_custom_call", output_to_operand_aliasing={{}: (2, {})} | custom-call | flops 184549376 | bytes 2883584 | tf_op jit(solution)/shard_map/gram/pallas_call | solution.py:24
  104.9 1.9 %gram.5 = f32[256,8192]{1,0:T(8,128)} custom-call(bf16[128,256]{1,0:T(8,128)(2,1)S(1)} %add_convert_fusion.own_ref, bf16[11,128,256]{2,1,0:T(8,128)(2,1)S(1)} %collective-permute-done.34.refs_0_, f32[256,8192]{1,0:T(8,128)} %gram.4.refs_1_), custom_call_target="tpu_custom_call", output_to_operand_aliasing={{}: (2, {})} | custom-call | flops 184549376 | bytes 2883584 | tf_op jit(solution)/shard_map/gram/pallas_call | solution.py:24
  (74 shorter events, 35.9 us)
Async XLA Ops:
  0.6 9.4 %collective-permute-start = (bf16[16,2048]{1,0:T(8,128)(2,1)}, bf16[16,2048]{1,0:T(8,128)(2,1)S(1)}, u32[]{:S(2)}, u32[]{:S(2)}) collective-permute-start(bf16[16,2048]{1,0:T(8,128)(2,1)} %refs_2_.1), channel_id=1, source_target_pairs={{0,2},{1,3},{2,0},{3,1},{4,6},{5,7},{6,4},{7,5},{8,10},{9,11},{10,... | collective-permute-start | bytes 196616 | tf_op jit(solution)/shard_map/ppermute | solution.py:20
  3.6 7.0 %collective-permute-start.1 = (bf16[16,2048]{1,0:T(8,128)(2,1)}, bf16[16,2048]{1,0:T(8,128)(2,1)S(1)}, u32[]{:S(2)}, u32[]{:S(2)}) collective-permute-start(bf16[16,2048]{1,0:T(8,128)(2,1)} %refs_2_.1), channel_id=1, source_target_pairs={{0,4},{1,5},{2,6},{3,7},{4,0},{5,1},{6,2},{7,3},{8,12},{9,13},{10,... | collective-permute-start | bytes 196616 | tf_op jit(solution)/shard_map/ppermute | solution.py:20
  5.2 5.6 %collective-permute-start.2 = (bf16[16,2048]{1,0:T(8,128)(2,1)}, bf16[16,2048]{1,0:T(8,128)(2,1)S(1)}, u32[]{:S(2)}, u32[]{:S(2)}) collective-permute-start(bf16[16,2048]{1,0:T(8,128)(2,1)} %refs_2_.1), channel_id=1, source_target_pairs={{0,6},{1,7},{2,4},{3,5},{4,2},{5,3},{6,0},{7,1},{8,14},{9,15},{10,... | collective-permute-start | bytes 196616 | tf_op jit(solution)/shard_map/ppermute | solution.py:20
  5.2 6.0 %collective-permute-start.3 = (bf16[16,2048]{1,0:T(8,128)(2,1)}, bf16[16,2048]{1,0:T(8,128)(2,1)S(1)}, u32[]{:S(2)}, u32[]{:S(2)}) collective-permute-start(bf16[16,2048]{1,0:T(8,128)(2,1)} %refs_2_.1), channel_id=1, source_target_pairs={{0,1},{1,0},{2,3},{3,2},{4,5},{5,4},{6,7},{7,6},{8,9},{9,8},{10,11... | collective-permute-start | bytes 196616 | tf_op jit(solution)/shard_map/ppermute | solution.py:20
  14.3 12.4 %collective-permute-start.8 = (bf16[2,32,3200]{2,1,0:T(8,128)(2,1)S(1)}, bf16[2,32,3200]{2,1,0:T(8,128)(2,1)S(1)}, u32[]{:S(2)}, u32[]{:S(2)}) collective-permute-start(bf16[2,32,3200]{2,1,0:T(8,128)(2,1)S(1)} %get-tuple-element.37.refs_2_), channel_id=1, source_target_pairs={{0,8},{8,0},{16,24},{24,16},{1,9},{9,1},{17,25},{25,17},{2,10},{10... | collective-permute-start | bytes 1228808 | tf_op jit(solution)/shard_map/ppermute | solution.py:20
  22.3 15.9 %collective-permute-start.7 = (bf16[2,32,2560]{2,1,0:T(8,128)(2,1)S(1)}, bf16[2,32,2560]{2,1,0:T(8,128)(2,1)S(1)}, u32[]{:S(2)}, u32[]{:S(2)}) collective-permute-start(bf16[2,32,2560]{2,1,0:T(8,128)(2,1)S(1)} %get-tuple-element.41.refs_0_), channel_id=1, source_target_pairs={{0,8},{8,0},{16,24},{24,16},{1,9},{9,1},{17,25},{25,17},{2,10},{10... | collective-permute-start | bytes 983048 | tf_op jit(solution)/shard_map/ppermute | solution.py:20
  26.9 11.3 %collective-permute-start.12 = (bf16[32,3200]{1,0:T(8,128)(2,1)S(1)}, bf16[32,3200]{1,0:T(8,128)(2,1)S(1)}, u32[]{:S(2)}, u32[]{:S(2)}) collective-permute-start(bf16[32,3200]{1,0:T(8,128)(2,1)S(1)} %pair_total.3.refs_2_), channel_id=1, source_target_pairs={{0,16},{8,24},{16,0},{24,8},{1,17},{9,25},{17,1},{25,9},{2,18},{10... | collective-permute-start | bytes 614408 | tf_op jit(solution)/shard_map/ppermute | solution.py:20
  34.0 10.9 %collective-permute-start.10 = (bf16[2,32,1536]{2,1,0:T(8,128)(2,1)S(1)}, bf16[2,32,1536]{2,1,0:T(8,128)(2,1)S(1)}, u32[]{:S(2)}, u32[]{:S(2)}) collective-permute-start(bf16[2,32,1536]{2,1,0:T(8,128)(2,1)S(1)} %get-tuple-element.45.refs_0_), channel_id=1, source_target_pairs={{0,8},{8,0},{16,24},{24,16},{1,9},{9,1},{17,25},{25,17},{2,10},{10... | collective-permute-start | bytes 589832 | tf_op jit(solution)/shard_map/ppermute | solution.py:20
  38.4 12.8 %collective-permute-start.14 = (bf16[32,1536]{1,0:T(8,128)(2,1)S(1)}, bf16[32,1536]{1,0:T(8,128)(2,1)S(1)}, u32[]{:S(2)}, u32[]{:S(2)}) collective-permute-start(bf16[32,1536]{1,0:T(8,128)(2,1)S(1)} %get-tuple-element.48.refs_0_), channel_id=1, source_target_pairs={{0,16},{8,24},{16,0},{24,8},{1,17},{9,25},{17,1},{25,9},{2,18},{10... | collective-permute-start | bytes 294920 | tf_op jit(solution)/shard_map/ppermute | solution.py:20
  41.4 14.5 %collective-permute-start.9 = (bf16[32,2560]{1,0:T(8,128)(2,1)S(1)}, bf16[32,2560]{1,0:T(8,128)(2,1)S(1)}, u32[]{:S(2)}, u32[]{:S(2)}) collective-permute-start(bf16[32,2560]{1,0:T(8,128)(2,1)S(1)} %pair_total.4.refs_1_.refs_3_), channel_id=1, source_target_pairs={{0,16},{8,24},{16,0},{24,8},{1,17},{9,25},{17,1},{25,9},{2,18},{10... | collective-permute-start | bytes 491528 | tf_op jit(solution)/shard_map/ppermute | solution.py:20
  45.0 12.4 %collective-permute-start.11 = (bf16[32,1536]{1,0:T(8,128)(2,1)S(1)}, bf16[32,1536]{1,0:T(8,128)(2,1)S(1)}, u32[]{:S(2)}, u32[]{:S(2)}) collective-permute-start(bf16[32,1536]{1,0:T(8,128)(2,1)S(1)} %pair_total.5.refs_1_), channel_id=1, source_target_pairs={{0,16},{8,24},{16,0},{24,8},{1,17},{9,25},{17,1},{25,9},{2,18},{10... | collective-permute-start | bytes 294920 | tf_op jit(solution)/shard_map/ppermute | solution.py:20
  47.9 9.5 %collective-permute-start.13 = (bf16[32,1536]{1,0:T(8,128)(2,1)S(1)}, bf16[32,1536]{1,0:T(8,128)(2,1)S(1)}, u32[]{:S(2)}, u32[]{:S(2)}) collective-permute-start(bf16[32,1536]{1,0:T(8,128)(2,1)S(1)} %get-tuple-element.48.refs_0_), channel_id=1, source_target_pairs={{0,8},{8,0},{16,24},{24,16},{1,9},{9,1},{17,25},{25,17},{2,10},{10... | collective-permute-start | bytes 294920 | tf_op jit(solution)/shard_map/ppermute | solution.py:20
  51.2 7.2 %collective-permute-start.15 = (bf16[32,1536]{1,0:T(8,128)(2,1)S(1)}, bf16[32,1536]{1,0:T(8,128)(2,1)S(1)}, u32[]{:S(2)}, u32[]{:S(2)}) collective-permute-start(bf16[32,1536]{1,0:T(8,128)(2,1)S(1)} %collective-permute-done.14.refs_2_), channel_id=1, source_target_pairs={{0,8},{8,0},{16,24},{24,16},{1,9},{9,1},{17,25},{25,17},{2,10},{10... | collective-permute-start | bytes 294920 | tf_op jit(solution)/shard_map/ppermute | solution.py:20
  59.1 7.8 %collective-permute-start.17 = (bf16[32,2048]{1,0:T(8,128)(2,1)S(1)}, bf16[32,2048]{1,0:T(8,128)(2,1)S(1)}, u32[]{:S(2)}, u32[]{:S(2)}) collective-permute-start(bf16[32,2048]{1,0:T(8,128)(2,1)S(1)} %get-tuple-element.49.refs_0_), channel_id=1, source_target_pairs={{0,16},{8,24},{16,0},{24,8},{1,17},{9,25},{17,1},{25,9},{2,18},{10... | collective-permute-start | bytes 393224 | tf_op jit(solution)/shard_map/ppermute | solution.py:20
  60.4 7.0 %collective-permute-start.16 = (bf16[32,2048]{1,0:T(8,128)(2,1)S(1)}, bf16[32,2048]{1,0:T(8,128)(2,1)S(1)}, u32[]{:S(2)}, u32[]{:S(2)}) collective-permute-start(bf16[32,2048]{1,0:T(8,128)(2,1)S(1)} %get-tuple-element.49.refs_0_), channel_id=1, source_target_pairs={{0,8},{8,0},{16,24},{24,16},{1,9},{9,1},{17,25},{25,17},{2,10},{10... | collective-permute-start | bytes 393224 | tf_op jit(solution)/shard_map/ppermute | solution.py:20
  74.3 5.5 %collective-permute-start.20 = (bf16[128,256]{1,0:T(8,128)(2,1)S(1)}, bf16[128,256]{1,0:T(8,128)(2,1)S(1)}, u32[]{:S(2)}, u32[]{:S(2)}) collective-permute-start(bf16[128,256]{1,0:T(8,128)(2,1)S(1)} %get-tuple-element.51), channel_id=1, source_target_pairs={{0,6},{1,7},{2,4},{3,5},{4,2},{5,3},{6,0},{7,1},{8,14},{9,15},{10,... | collective-permute-start | bytes 196616 | tf_op jit(solution)/shard_map/ppermute | solution.py:20
  81.7 6.0 %collective-permute-start.23 = (bf16[128,256]{1,0:T(8,128)(2,1)S(1)}, bf16[128,256]{1,0:T(8,128)(2,1)S(1)}, u32[]{:S(2)}, u32[]{:S(2)}) collective-permute-start(bf16[128,256]{1,0:T(8,128)(2,1)S(1)} %add_convert_fusion.own_ref), channel_id=1, source_target_pairs={{0,8},{8,0},{16,24},{24,16},{1,9},{9,1},{17,25},{25,17},{2,10},{10... | collective-permute-start | bytes 196616 | tf_op jit(solution)/shard_map/ppermute | solution.py:20
  81.7 7.5 %collective-permute-start.24 = (bf16[128,256]{1,0:T(8,128)(2,1)S(1)}, bf16[128,256]{1,0:T(8,128)(2,1)S(1)}, u32[]{:S(2)}, u32[]{:S(2)}) collective-permute-start(bf16[128,256]{1,0:T(8,128)(2,1)S(1)} %add_convert_fusion.own_ref), channel_id=1, source_target_pairs={{0,16},{8,24},{16,0},{24,8},{1,17},{9,25},{17,1},{25,9},{2,18},{10... | collective-permute-start | bytes 196616 | tf_op jit(solution)/shard_map/ppermute | solution.py:20
  84.6 6.1 %collective-permute-start.25 = (bf16[128,256]{1,0:T(8,128)(2,1)S(1)}, bf16[128,256]{1,0:T(8,128)(2,1)S(1)}, u32[]{:S(2)}, u32[]{:S(2)}) collective-permute-start(bf16[128,256]{1,0:T(8,128)(2,1)S(1)} %add_convert_fusion.own_ref), channel_id=1, source_target_pairs={{0,24},{8,16},{16,8},{24,0},{1,25},{9,17},{17,9},{25,1},{2,26},{10... | collective-permute-start | bytes 196616 | tf_op jit(solution)/shard_map/ppermute | solution.py:20
  91.4 11.2 %collective-permute-start.27 = (bf16[4,128,256]{2,1,0:T(8,128)(2,1)S(1)}, bf16[4,128,256]{2,1,0:T(8,128)(2,1)S(1)}, u32[]{:S(2)}, u32[]{:S(2)}) collective-permute-start(bf16[4,128,256]{2,1,0:T(8,128)(2,1)S(1)} %get-tuple-element.54.refs_0_), channel_id=1, source_target_pairs={{0,2},{1,3},{2,0},{3,1},{4,6},{5,7},{6,4},{7,5},{8,10},{9,11},{10,... | collective-permute-start | bytes 786440 | tf_op jit(solution)/shard_map/ppermute | solution.py:20
  92.5 10.1 %collective-permute-start.28 = (bf16[4,128,256]{2,1,0:T(8,128)(2,1)S(1)}, bf16[4,128,256]{2,1,0:T(8,128)(2,1)S(1)}, u32[]{:S(2)}, u32[]{:S(2)}) collective-permute-start(bf16[4,128,256]{2,1,0:T(8,128)(2,1)S(1)} %get-tuple-element.54.refs_0_), channel_id=1, source_target_pairs={{0,4},{1,5},{2,6},{3,7},{4,0},{5,1},{6,2},{7,3},{8,12},{9,13},{10,... | collective-permute-start | bytes 786440 | tf_op jit(solution)/shard_map/ppermute | solution.py:20
  93.5 9.0 %collective-permute-start.31 = (bf16[144,256]{1,0:T(8,128)(2,1)S(1)}, bf16[144,256]{1,0:T(8,128)(2,1)S(1)}, u32[]{:S(2)}, u32[]{:S(2)}) collective-permute-start(bf16[144,256]{1,0:T(8,128)(2,1)S(1)} %get-tuple-element.55), channel_id=1, source_target_pairs={{0,6},{1,7},{2,4},{3,5},{4,2},{5,3},{6,0},{7,1},{8,14},{9,15},{10,... | collective-permute-start | bytes 221192 | tf_op jit(solution)/shard_map/ppermute | solution.py:20
  94.9 5.4 %collective-permute-start.29 = (bf16[128,256]{1,0:T(8,128)(2,1)S(1)}, bf16[128,256]{1,0:T(8,128)(2,1)S(1)}, u32[]{:S(2)}, u32[]{:S(2)}) collective-permute-start(bf16[128,256]{1,0:T(8,128)(2,1)S(1)} %collective-permute-done.26.refs_4_), channel_id=1, source_target_pairs={{0,8},{8,0},{16,24},{24,16},{1,9},{9,1},{17,25},{25,17},{2,10},{10... | collective-permute-start | bytes 196616 | tf_op jit(solution)/shard_map/ppermute | solution.py:20
  94.9 6.6 %collective-permute-start.30 = (bf16[128,256]{1,0:T(8,128)(2,1)S(1)}, bf16[128,256]{1,0:T(8,128)(2,1)S(1)}, u32[]{:S(2)}, u32[]{:S(2)}) collective-permute-start(bf16[128,256]{1,0:T(8,128)(2,1)S(1)} %collective-permute-done.26.refs_4_), channel_id=1, source_target_pairs={{0,16},{8,24},{16,0},{24,8},{1,17},{9,25},{17,1},{25,9},{2,18},{10... | collective-permute-start | bytes 196616 | tf_op jit(solution)/shard_map/ppermute | solution.py:20
  (12 other events, 56.9 us)

commit v14 on v13

--- a/solution.py
+++ b/solution.py
@@ -316,7 +316,7 @@
     ntok, panel = rows * n_hid, block // n_hid
     depth, shard_ff = gate_weight.shape
     tiles = shard_ff // TILE
-    ends = [0, TILE * (3 * tiles // 7), TILE * (11 * tiles // 14), shard_ff]
+    ends = [0, TILE * (4 * tiles // 7), shard_ff]
     chip_masks = list(range(2, n_hid, 2))
 
     def part(weight, k):
@@ -348,7 +348,7 @@
         scratch_shapes=[pltpu.VMEM((ntok, block), BF16)],
     )
 
-    widths = [ends[k + 1] - ends[k] for k in range(3)]
+    widths = [ends[k + 1] - ends[k] for k in range(2)]
     send_0, keep_0 = gate_up(lhs, gate_0, up_0, squares, n_tok)
     got_0 = swap(send_0, "tok", n_tok, 1)
     gate_1, up_1 = fetch([part(gate_weight, 1), part(up_weight, 1)], (send_0,), "fetch_gate_up")
@@ -356,21 +356,17 @@
     got_1 = swap(send_1, "tok", n_tok, 1)
     sum_0 = pair_total(keep_0, got_0, 2 * widths[0], (send_1,))
     over_0 = swap(sum_0, "tok", n_tok, 2)
-    gate_2, up_2 = fetch([part(gate_weight, 2), part(up_weight, 2)], (sum_0,), "fetch_gate_up")
-    send_2, keep_2 = gate_up(lhs, gate_2, up_2, None, n_tok)
-    got_2 = swap(send_2, "tok", n_tok, 1)
-    sum_1 = pair_total(keep_1, got_1, 2 * widths[1], (send_2,))
+    down_a, down_b = fetch(
+        [(down_weight, 0, ends[1], 0, block), (down_weight, ends[1], widths[1], 0, block)], (sum_0,), "fetch_down"
+    )
+    sum_1 = pair_total(keep_1, got_1, 2 * widths[1], (down_a,))
     over_1 = swap(sum_1, "tok", n_tok, 2)
-    down_b, = fetch([(down_weight, ends[1], shard_ff - ends[1], 0, block)], (sum_1,), "fetch_down")
-    sum_2 = pair_total(keep_2, got_2, 2 * widths[2], (down_b,))
-    over_2 = swap(sum_2, "tok", n_tok, 2)
 
     a_own, scale = hidden_rows([(keep_0, got_0, over_0)], widths[:1], None, (sum_1,))
     a_two = swap(a_own, "tok", n_tok, 2)
     a_one = swap(a_own, "tok", n_tok, 1)
     a_three = swap(a_two, "tok", n_tok, 1)
-    down_a, = fetch([(down_weight, 0, ends[1], 0, block)], (sum_2,), "fetch_down")
-    b_own, _ = hidden_rows([(keep_1, got_1, over_1), (keep_2, got_2, over_2)], widths[1:], scale, (a_one, a_three, down_a))
+    b_own, _ = hidden_rows([(keep_1, got_1, over_1)], widths[1:], scale, (a_one, a_two))
     b_two = swap(b_own, "tok", n_tok, 2)
     b_one = swap(b_own, "tok", n_tok, 1)
     b_three = swap(b_two, "tok", n_tok, 1)

time: 107 us -> 111 us (1.037)
  waiting for transfers between devices: 30.7 us -> 45.2 us
  starting transfers between devices: 41.6 us -> 33 us
  Pallas kernels: 33.6 us -> 31.5 us
    ppermute x35 -> x33, waiting for transfers between devices: 30.7 us -> 45.2 us  [swap(): return lax.ppermute(value, axis, [(i, i ^ mask) for i in range(size)])]
    ppermute x35 -> x33, starting transfers between devices: 41.6 us -> 33 us  [swap(): return lax.ppermute(value, axis, [(i, i ^ mask) for i in range(size)])]
    pallas_call x25 -> x21, Pallas kernels: 33.6 us -> 31.5 us  [run(): pl.pallas_call(body, out_shape=out_shape, in_specs=[WHOLE] * len(operands...]
  transfers between devices with their start and end apart: 35 -> 33, of which waited for: 22 -> 23; matrix products, arithmetic and copies ran while one was open for 0% -> 0% of each run, Pallas kernels for 26% -> 23%
where the time goes in v14:
time: 111 us
  waiting for transfers between devices  45.2 us (41%)
  starting transfers between devices  33 us (30%)
  Pallas kernels  31.5 us (28%)
    ppermute x33, waiting for transfers between devices, swap(): return lax.ppermute(value, axis, [(i, i ^ mask) for i in range(size)])  45.2 us
    ppermute x33, starting transfers between devices, swap(): return lax.ppermute(value, axis, [(i, i ^ mask) for i in range(size)])  33 us
    pallas_call x21, Pallas kernels, run(): pl.pallas_call(body, out_shape=out_shape, in_specs=[WHOLE] * len(operands...  31.5 us
  transfers between devices with their start and end apart: 33, of which 23 were waited for; matrix products, arithmetic and copies ran while one was open for 0% of the time, Pallas kernels for 23%

profile of v14, /device:TPU:0, one launch (start us, length us, event | category | flops | bytes accessed | tf_op | source)
XLA Modules:
  0.0 110.6 jit_solution(18023617436031572090)
XLA Ops:
  0.6 3.0 %collective-permute-start = (bf16[16,2048]{1,0:T(8,128)(2,1)}, bf16[16,2048]{1,0:T(8,128)(2,1)S(1)}, u32[]{:S(2)}, u32[]{:S(2)}) collective-permute-start(bf16[16,2048]{1,0:T(8,128)(2,1)} %refs_2_.1), channel_id=1, source_target_pairs={{0,2},{1,3},{2,0},{3,1},{4,6},{5,7},{6,4},{7,5},{8,10},{9,11},{10,... | collective-permute-start | bytes 196616 | tf_op jit(solution)/shard_map/ppermute | solution.py:20
  5.2 6.2 %fetch_first.1 = (bf16[2048,2048]{1,0:T(8,128)(2,1)S(1)}, bf16[2048,2048]{1,0:T(8,128)(2,1)S(1)}, bf16[16,2048]{1,0:T(8,128)(2,1)S(1)}, f32[1,2048]{1,0:T(1,128)S(1)}) custom-call(bf16[2048,3584]{1,0:T(8,128)(2,1)} %refs_0_.4, bf16[2048,3584]{1,0:T(8,128)(2,1)} %refs_1_.4, bf16[16,2048]{1,0:T(8,128)(2,1)} %refs_2_.1, f32[1,2048]{1,0:T(1,128)} %bitcast.22), custom_call_target="tpu_custom_call" | custom-call | tf_op jit(solution)/shard_map/fetch_first/pallas_call | solution.py:24
  13.7 2.7 %gate_up.2 = (bf16[2,32,4224]{2,1,0:T(8,128)(2,1)S(1)}, bf16[2,32,4224]{2,1,0:T(8,128)(2,1)S(1)}) custom-call(bf16[128,2048]{1,0:T(8,128)(2,1)S(1)} %get-tuple-element.31.lhs_ref, bf16[2048,2048]{1,0:T(8,128)(2,1)S(1)} %get-tuple-element.32.gate_ref, bf16[2048,2048]{1,0:T(8,128)(2,1)S(1)} %get-tuple-element.33.up_ref, f32[128,1]{1,0:T(8,128)S(1)} %get-tuple-element.34.refs_0_), custom_call_target="tpu_custom_call" | custom-call | tf_op jit(solution)/shard_map/gate_up/pallas_call | solution.py:24
  16.4 2.1 %collective-permute-start.8 = (bf16[2,32,4224]{2,1,0:T(8,128)(2,1)S(1)}, bf16[2,32,4224]{2,1,0:T(8,128)(2,1)S(1)}, u32[]{:S(2)}, u32[]{:S(2)}) collective-permute-start(bf16[2,32,4224]{2,1,0:T(8,128)(2,1)S(1)} %get-tuple-element.35.refs_2_), channel_id=1, source_target_pairs={{0,8},{8,0},{16,24},{24,16},{1,9},{9,1},{17,25},{25,17},{2,10},{10... | collective-permute-start | bytes 1622024 | tf_op jit(solution)/shard_map/ppermute | solution.py:20
  18.5 4.8 %fetch_gate_up.1 = (bf16[2048,1536]{1,0:T(8,128)(2,1)S(1)}, bf16[2048,1536]{1,0:T(8,128)(2,1)S(1)}) custom-call(bf16[2048,3584]{1,0:T(8,128)(2,1)} %refs_0_.4, bf16[2048,3584]{1,0:T(8,128)(2,1)} %refs_1_.4, bf16[2,32,4224]{2,1,0:T(8,128)(2,1)S(1)} %get-tuple-element.35.refs_2_), custom_call_target="tpu_custom_call" | custom-call | tf_op jit(solution)/shard_map/fetch_gate_up/pallas_call | solution.py:24
  23.3 1.9 %gate_up.3 = (bf16[2,32,3072]{2,1,0:T(8,128)(2,1)S(1)}, bf16[2,32,3072]{2,1,0:T(8,128)(2,1)S(1)}) custom-call(bf16[128,2048]{1,0:T(8,128)(2,1)S(1)} %get-tuple-element.31.lhs_ref, bf16[2048,1536]{1,0:T(8,128)(2,1)S(1)} %get-tuple-element.36.gate_ref, bf16[2048,1536]{1,0:T(8,128)(2,1)S(1)} %get-tuple-element.37.up_ref), custom_call_target="tpu_custom_call" | custom-call | tf_op jit(solution)/shard_map/gate_up/pallas_call | solution.py:24
  25.3 6.3 %collective-permute-done.8.got_ref.refs_1_ = bf16[2,32,4224]{2,1,0:T(8,128)(2,1)S(1)} collective-permute-done((bf16[2,32,4224]{2,1,0:T(8,128)(2,1)S(1)}, bf16[2,32,4224]{2,1,0:T(8,128)(2,1)S(1)}, u32[]{:S(2)}, u32[]{:S(2)}) %collective-permute-start.8) | collective-permute-done | bytes 540704 | tf_op jit(solution)/shard_map/ppermute | solution.py:20
  31.8 3.0 %collective-permute-start.10 = (bf16[32,4224]{1,0:T(8,128)(2,1)S(1)}, bf16[32,4224]{1,0:T(8,128)(2,1)S(1)}, u32[]{:S(2)}, u32[]{:S(2)}) collective-permute-start(bf16[32,4224]{1,0:T(8,128)(2,1)S(1)} %pair_total.2.refs_2_), channel_id=1, source_target_pairs={{0,16},{8,24},{16,0},{24,8},{1,17},{9,25},{17,1},{25,9},{2,18},{10... | collective-permute-start | bytes 811016 | tf_op jit(solution)/shard_map/ppermute | solution.py:20
  34.9 5.3 %fetch_down.1 = (bf16[2048,2048]{1,0:T(8,128)(2,1)S(1)}, bf16[1536,2048]{1,0:T(8,128)(2,1)S(1)}) custom-call(bf16[3584,2048]{1,0:T(8,128)(2,1)} %refs_1_.5, bf16[3584,2048]{1,0:T(8,128)(2,1)} %refs_1_.5, bf16[32,4224]{1,0:T(8,128)(2,1)S(1)} %pair_total.2.refs_2_), custom_call_target="tpu_custom_call" | custom-call | tf_op jit(solution)/shard_map/fetch_down/pallas_call | solution.py:24
  40.2 5.3 %collective-permute-done.7.got_ref.refs_1_ = bf16[2,32,3072]{2,1,0:T(8,128)(2,1)S(1)} collective-permute-done((bf16[2,32,3072]{2,1,0:T(8,128)(2,1)S(1)}, bf16[2,32,3072]{2,1,0:T(8,128)(2,1)S(1)}, u32[]{:S(2)}, u32[]{:S(2)}) %collective-permute-start.7) | collective-permute-done | bytes 393248 | tf_op jit(solution)/shard_map/ppermute | solution.py:20
  46.9 2.5 %collective-permute-start.11 = (bf16[32,2048]{1,0:T(8,128)(2,1)S(1)}, bf16[32,2048]{1,0:T(8,128)(2,1)S(1)}, u32[]{:S(2)}, u32[]{:S(2)}) collective-permute-start(bf16[32,2048]{1,0:T(8,128)(2,1)S(1)} %get-tuple-element.43.refs_0_), channel_id=1, source_target_pairs={{0,8},{8,0},{16,24},{24,16},{1,9},{9,1},{17,25},{25,17},{2,10},{10... | collective-permute-start | bytes 393224 | tf_op jit(solution)/shard_map/ppermute | solution.py:20
  50.9 9.4 %collective-permute-done.9.refs_2_ = bf16[32,3072]{1,0:T(8,128)(2,1)S(1)} collective-permute-done((bf16[32,3072]{1,0:T(8,128)(2,1)S(1)}, bf16[32,3072]{1,0:T(8,128)(2,1)S(1)}, u32[]{:S(2)}, u32[]{:S(2)}) %collective-permute-start.9) | collective-permute-done | bytes 196640 | tf_op jit(solution)/shard_map/ppermute | solution.py:20
  60.3 2.7 %collective-permute-done.12.refs_5_.refs_2_ = bf16[32,2048]{1,0:T(8,128)(2,1)S(1)} collective-permute-done((bf16[32,2048]{1,0:T(8,128)(2,1)S(1)}, bf16[32,2048]{1,0:T(8,128)(2,1)S(1)}, u32[]{:S(2)}, u32[]{:S(2)}) %collective-permute-start.12) | collective-permute-done | bytes 131104 | tf_op jit(solution)/shard_map/ppermute | solution.py:20
  63.6 2.2 %collective-permute-start.16 = (bf16[32,2048]{1,0:T(8,128)(2,1)S(1)}, bf16[32,2048]{1,0:T(8,128)(2,1)S(1)}, u32[]{:S(2)}, u32[]{:S(2)}) collective-permute-start(bf16[32,2048]{1,0:T(8,128)(2,1)S(1)} %collective-permute-done.12.refs_5_.refs_2_), channel_id=1, source_target_pairs={{0,8},{8,0},{16,24},{24,16},{1,9},{9,1},{17,25},{25,17},{2,10},{10... | collective-permute-start | bytes 393224 | tf_op jit(solution)/shard_map/ppermute | solution.py:20
  65.8 4.6 %collective-permute-done.14.refs_2_ = bf16[32,1536]{1,0:T(8,128)(2,1)S(1)} collective-permute-done((bf16[32,1536]{1,0:T(8,128)(2,1)S(1)}, bf16[32,1536]{1,0:T(8,128)(2,1)S(1)}, u32[]{:S(2)}, u32[]{:S(2)}) %collective-permute-start.14) | collective-permute-done | bytes 98336 | tf_op jit(solution)/shard_map/ppermute | solution.py:20
  83.7 2.4 %collective-permute-done.18 = bf16[128,256]{1,0:T(8,128)(2,1)S(1)} collective-permute-done((bf16[128,256]{1,0:T(8,128)(2,1)S(1)}, bf16[128,256]{1,0:T(8,128)(2,1)S(1)}, u32[]{:S(2)}, u32[]{:S(2)}) %collective-permute-start.18) | collective-permute-done | bytes 65568 | tf_op jit(solution)/shard_map/ppermute | solution.py:20
  86.2 2.5 %collective-permute-start.22 = (bf16[128,256]{1,0:T(8,128)(2,1)S(1)}, bf16[128,256]{1,0:T(8,128)(2,1)S(1)}, u32[]{:S(2)}, u32[]{:S(2)}) collective-permute-start(bf16[128,256]{1,0:T(8,128)(2,1)S(1)} %add_convert_fusion.own_ref), channel_id=1, source_target_pairs={{0,16},{8,24},{16,0},{24,8},{1,17},{9,25},{17,1},{25,9},{2,18},{10... | collective-permute-start | bytes 196616 | tf_op jit(solution)/shard_map/ppermute | solution.py:20
  88.8 1.9 %collective-permute-start.23 = (bf16[128,256]{1,0:T(8,128)(2,1)S(1)}, bf16[128,256]{1,0:T(8,128)(2,1)S(1)}, u32[]{:S(2)}, u32[]{:S(2)}) collective-permute-start(bf16[128,256]{1,0:T(8,128)(2,1)S(1)} %add_convert_fusion.own_ref), channel_id=1, source_target_pairs={{0,24},{8,16},{16,8},{24,0},{1,25},{9,17},{17,9},{25,1},{2,26},{10... | collective-permute-start | bytes 196616 | tf_op jit(solution)/shard_map/ppermute | solution.py:20
  91.1 1.9 %collective-permute-done.22 = bf16[128,256]{1,0:T(8,128)(2,1)S(1)} collective-permute-done((bf16[128,256]{1,0:T(8,128)(2,1)S(1)}, bf16[128,256]{1,0:T(8,128)(2,1)S(1)}, u32[]{:S(2)}, u32[]{:S(2)}) %collective-permute-start.22) | collective-permute-done | bytes 65568 | tf_op jit(solution)/shard_map/ppermute | solution.py:20
  97.0 2.5 %collective-permute-start.29 = (bf16[144,256]{1,0:T(8,128)(2,1)S(1)}, bf16[144,256]{1,0:T(8,128)(2,1)S(1)}, u32[]{:S(2)}, u32[]{:S(2)}) collective-permute-start(bf16[144,256]{1,0:T(8,128)(2,1)S(1)} %get-tuple-element.51), channel_id=1, source_target_pairs={{0,6},{1,7},{2,4},{3,5},{4,2},{5,3},{6,0},{7,1},{8,14},{9,15},{10,... | collective-permute-start | bytes 221192 | tf_op jit(solution)/shard_map/ppermute | solution.py:20
  99.4 2.5 %collective-permute-start.28 = (bf16[128,256]{1,0:T(8,128)(2,1)S(1)}, bf16[128,256]{1,0:T(8,128)(2,1)S(1)}, u32[]{:S(2)}, u32[]{:S(2)}) collective-permute-start(bf16[128,256]{1,0:T(8,128)(2,1)S(1)} %collective-permute-done.24.refs_4_), channel_id=1, source_target_pairs={{0,16},{8,24},{16,0},{24,8},{1,17},{9,25},{17,1},{25,9},{2,18},{10... | collective-permute-start | bytes 196616 | tf_op jit(solution)/shard_map/ppermute | solution.py:20
  102.0 2.4 %gram.3 = (f32[256,8192]{1,0:T(8,128)}, f32[64,256]{1,0:T(8,128)}) custom-call(bf16[128,256]{1,0:T(8,128)(2,1)S(1)} %add_convert_fusion.own_ref, bf16[4,128,256]{2,1,0:T(8,128)(2,1)S(1)} %get-tuple-element.50.refs_0_, bf16[4,128,256]{2,1,0:T(8,128)(2,1)S(1)} %collective-permute-done.30.refs_1_, bf16[1,128,256]{2,1,0:T(8,128)(2,1)S(1)} %bitcast.13, ...), custom_call_target="tpu_custom_call" | custom-call | flops 167772160 | bytes 2621440 | tf_op jit(solution)/shard_map/gram/pallas_call | solution.py:24
  106.6 1.9 %gram.4.refs_1_ = f32[256,8192]{1,0:T(8,128)} custom-call(bf16[128,256]{1,0:T(8,128)(2,1)S(1)} %add_convert_fusion.own_ref, bf16[11,128,256]{2,1,0:T(8,128)(2,1)S(1)} %stack.3.refs_0_, f32[256,8192]{1,0:T(8,128)} %get-tuple-element.52.refs_5_.refs_1_), custom_call_target="tpu_custom_call", output_to_operand_aliasing={{}: (2, {})} | custom-call | flops 184549376 | bytes 2883584 | tf_op jit(solution)/shard_map/gram/pallas_call | solution.py:24
  108.7 1.9 %gram.5 = f32[256,8192]{1,0:T(8,128)} custom-call(bf16[128,256]{1,0:T(8,128)(2,1)S(1)} %add_convert_fusion.own_ref, bf16[11,128,256]{2,1,0:T(8,128)(2,1)S(1)} %collective-permute-done.32.refs_0_, f32[256,8192]{1,0:T(8,128)} %gram.4.refs_1_), custom_call_target="tpu_custom_call", output_to_operand_aliasing={{}: (2, {})} | custom-call | flops 184549376 | bytes 2883584 | tf_op jit(solution)/shard_map/gram/pallas_call | solution.py:24
  (66 shorter events, 27.7 us)
Async XLA Ops:
  0.6 10.8 %collective-permute-start = (bf16[16,2048]{1,0:T(8,128)(2,1)}, bf16[16,2048]{1,0:T(8,128)(2,1)S(1)}, u32[]{:S(2)}, u32[]{:S(2)}) collective-permute-start(bf16[16,2048]{1,0:T(8,128)(2,1)} %refs_2_.1), channel_id=1, source_target_pairs={{0,2},{1,3},{2,0},{3,1},{4,6},{5,7},{6,4},{7,5},{8,10},{9,11},{10,... | collective-permute-start | bytes 196616 | tf_op jit(solution)/shard_map/ppermute | solution.py:20
  3.6 8.4 %collective-permute-start.1 = (bf16[16,2048]{1,0:T(8,128)(2,1)}, bf16[16,2048]{1,0:T(8,128)(2,1)S(1)}, u32[]{:S(2)}, u32[]{:S(2)}) collective-permute-start(bf16[16,2048]{1,0:T(8,128)(2,1)} %refs_2_.1), channel_id=1, source_target_pairs={{0,4},{1,5},{2,6},{3,7},{4,0},{5,1},{6,2},{7,3},{8,12},{9,13},{10,... | collective-permute-start | bytes 196616 | tf_op jit(solution)/shard_map/ppermute | solution.py:20
  5.2 6.9 %collective-permute-start.2 = (bf16[16,2048]{1,0:T(8,128)(2,1)}, bf16[16,2048]{1,0:T(8,128)(2,1)S(1)}, u32[]{:S(2)}, u32[]{:S(2)}) collective-permute-start(bf16[16,2048]{1,0:T(8,128)(2,1)} %refs_2_.1), channel_id=1, source_target_pairs={{0,6},{1,7},{2,4},{3,5},{4,2},{5,3},{6,0},{7,1},{8,14},{9,15},{10,... | collective-permute-start | bytes 196616 | tf_op jit(solution)/shard_map/ppermute | solution.py:20
  5.2 7.3 %collective-permute-start.3 = (bf16[16,2048]{1,0:T(8,128)(2,1)}, bf16[16,2048]{1,0:T(8,128)(2,1)S(1)}, u32[]{:S(2)}, u32[]{:S(2)}) collective-permute-start(bf16[16,2048]{1,0:T(8,128)(2,1)} %refs_2_.1), channel_id=1, source_target_pairs={{0,1},{1,0},{2,3},{3,2},{4,5},{5,4},{6,7},{7,6},{8,9},{9,8},{10,11... | collective-permute-start | bytes 196616 | tf_op jit(solution)/shard_map/ppermute | solution.py:20
  16.4 15.2 %collective-permute-start.8 = (bf16[2,32,4224]{2,1,0:T(8,128)(2,1)S(1)}, bf16[2,32,4224]{2,1,0:T(8,128)(2,1)S(1)}, u32[]{:S(2)}, u32[]{:S(2)}) collective-permute-start(bf16[2,32,4224]{2,1,0:T(8,128)(2,1)S(1)} %get-tuple-element.35.refs_2_), channel_id=1, source_target_pairs={{0,8},{8,0},{16,24},{24,16},{1,9},{9,1},{17,25},{25,17},{2,10},{10... | collective-permute-start | bytes 1622024 | tf_op jit(solution)/shard_map/ppermute | solution.py:20
  25.2 20.3 %collective-permute-start.7 = (bf16[2,32,3072]{2,1,0:T(8,128)(2,1)S(1)}, bf16[2,32,3072]{2,1,0:T(8,128)(2,1)S(1)}, u32[]{:S(2)}, u32[]{:S(2)}) collective-permute-start(bf16[2,32,3072]{2,1,0:T(8,128)(2,1)S(1)} %get-tuple-element.39.refs_0_), channel_id=1, source_target_pairs={{0,8},{8,0},{16,24},{24,16},{1,9},{9,1},{17,25},{25,17},{2,10},{10... | collective-permute-start | bytes 1179656 | tf_op jit(solution)/shard_map/ppermute | solution.py:20
  31.8 14.8 %collective-permute-start.10 = (bf16[32,4224]{1,0:T(8,128)(2,1)S(1)}, bf16[32,4224]{1,0:T(8,128)(2,1)S(1)}, u32[]{:S(2)}, u32[]{:S(2)}) collective-permute-start(bf16[32,4224]{1,0:T(8,128)(2,1)S(1)} %pair_total.2.refs_2_), channel_id=1, source_target_pairs={{0,16},{8,24},{16,0},{24,8},{1,17},{9,25},{17,1},{25,9},{2,18},{10... | collective-permute-start | bytes 811016 | tf_op jit(solution)/shard_map/ppermute | solution.py:20
  45.6 14.7 %collective-permute-start.9 = (bf16[32,3072]{1,0:T(8,128)(2,1)S(1)}, bf16[32,3072]{1,0:T(8,128)(2,1)S(1)}, u32[]{:S(2)}, u32[]{:S(2)}) collective-permute-start(bf16[32,3072]{1,0:T(8,128)(2,1)S(1)} %pair_total.3.refs_3_), channel_id=1, source_target_pairs={{0,16},{8,24},{16,0},{24,8},{1,17},{9,25},{17,1},{25,9},{2,18},{10... | collective-permute-start | bytes 589832 | tf_op jit(solution)/shard_map/ppermute | solution.py:20
  46.9 13.4 %collective-permute-start.11 = (bf16[32,2048]{1,0:T(8,128)(2,1)S(1)}, bf16[32,2048]{1,0:T(8,128)(2,1)S(1)}, u32[]{:S(2)}, u32[]{:S(2)}) collective-permute-start(bf16[32,2048]{1,0:T(8,128)(2,1)S(1)} %get-tuple-element.43.refs_0_), channel_id=1, source_target_pairs={{0,8},{8,0},{16,24},{24,16},{1,9},{9,1},{17,25},{25,17},{2,10},{10... | collective-permute-start | bytes 393224 | tf_op jit(solution)/shard_map/ppermute | solution.py:20
  49.4 13.5 %collective-permute-start.12 = (bf16[32,2048]{1,0:T(8,128)(2,1)S(1)}, bf16[32,2048]{1,0:T(8,128)(2,1)S(1)}, u32[]{:S(2)}, u32[]{:S(2)}) collective-permute-start(bf16[32,2048]{1,0:T(8,128)(2,1)S(1)} %get-tuple-element.43.refs_0_), channel_id=1, source_target_pairs={{0,16},{8,24},{16,0},{24,8},{1,17},{9,25},{17,1},{25,9},{2,18},{10... | collective-permute-start | bytes 393224 | tf_op jit(solution)/shard_map/ppermute | solution.py:20
  63.5 6.9 %collective-permute-start.14 = (bf16[32,1536]{1,0:T(8,128)(2,1)S(1)}, bf16[32,1536]{1,0:T(8,128)(2,1)S(1)}, u32[]{:S(2)}, u32[]{:S(2)}) collective-permute-start(bf16[32,1536]{1,0:T(8,128)(2,1)S(1)} %get-tuple-element.44.refs_0_), channel_id=1, source_target_pairs={{0,16},{8,24},{16,0},{24,8},{1,17},{9,25},{17,1},{25,9},{2,18},{10... | collective-permute-start | bytes 294920 | tf_op jit(solution)/shard_map/ppermute | solution.py:20
  63.6 8.6 %collective-permute-start.16 = (bf16[32,2048]{1,0:T(8,128)(2,1)S(1)}, bf16[32,2048]{1,0:T(8,128)(2,1)S(1)}, u32[]{:S(2)}, u32[]{:S(2)}) collective-permute-start(bf16[32,2048]{1,0:T(8,128)(2,1)S(1)} %collective-permute-done.12.refs_5_.refs_2_), channel_id=1, source_target_pairs={{0,8},{8,0},{16,24},{24,16},{1,9},{9,1},{17,25},{25,17},{2,10},{10... | collective-permute-start | bytes 393224 | tf_op jit(solution)/shard_map/ppermute | solution.py:20
  65.8 8.0 %collective-permute-start.13 = (bf16[32,1536]{1,0:T(8,128)(2,1)S(1)}, bf16[32,1536]{1,0:T(8,128)(2,1)S(1)}, u32[]{:S(2)}, u32[]{:S(2)}) collective-permute-start(bf16[32,1536]{1,0:T(8,128)(2,1)S(1)} %get-tuple-element.44.refs_0_), channel_id=1, source_target_pairs={{0,8},{8,0},{16,24},{24,16},{1,9},{9,1},{17,25},{25,17},{2,10},{10... | collective-permute-start | bytes 294920 | tf_op jit(solution)/shard_map/ppermute | solution.py:20
  70.4 5.1 %collective-permute-start.15 = (bf16[32,1536]{1,0:T(8,128)(2,1)S(1)}, bf16[32,1536]{1,0:T(8,128)(2,1)S(1)}, u32[]{:S(2)}, u32[]{:S(2)}) collective-permute-start(bf16[32,1536]{1,0:T(8,128)(2,1)S(1)} %collective-permute-done.14.refs_2_), channel_id=1, source_target_pairs={{0,8},{8,0},{16,24},{24,16},{1,9},{9,1},{17,25},{25,17},{2,10},{10... | collective-permute-start | bytes 294920 | tf_op jit(solution)/shard_map/ppermute | solution.py:20
  80.9 5.2 %collective-permute-start.18 = (bf16[128,256]{1,0:T(8,128)(2,1)S(1)}, bf16[128,256]{1,0:T(8,128)(2,1)S(1)}, u32[]{:S(2)}, u32[]{:S(2)}) collective-permute-start(bf16[128,256]{1,0:T(8,128)(2,1)S(1)} %get-tuple-element.47), channel_id=1, source_target_pairs={{0,6},{1,7},{2,4},{3,5},{4,2},{5,3},{6,0},{7,1},{8,14},{9,15},{10,... | collective-permute-start | bytes 196616 | tf_op jit(solution)/shard_map/ppermute | solution.py:20
  86.2 4.9 %collective-permute-start.21 = (bf16[128,256]{1,0:T(8,128)(2,1)S(1)}, bf16[128,256]{1,0:T(8,128)(2,1)S(1)}, u32[]{:S(2)}, u32[]{:S(2)}) collective-permute-start(bf16[128,256]{1,0:T(8,128)(2,1)S(1)} %add_convert_fusion.own_ref), channel_id=1, source_target_pairs={{0,8},{8,0},{16,24},{24,16},{1,9},{9,1},{17,25},{25,17},{2,10},{10... | collective-permute-start | bytes 196616 | tf_op jit(solution)/shard_map/ppermute | solution.py:20
  86.2 6.8 %collective-permute-start.22 = (bf16[128,256]{1,0:T(8,128)(2,1)S(1)}, bf16[128,256]{1,0:T(8,128)(2,1)S(1)}, u32[]{:S(2)}, u32[]{:S(2)}) collective-permute-start(bf16[128,256]{1,0:T(8,128)(2,1)S(1)} %add_convert_fusion.own_ref), channel_id=1, source_target_pairs={{0,16},{8,24},{16,0},{24,8},{1,17},{9,25},{17,1},{25,9},{2,18},{10... | collective-permute-start | bytes 196616 | tf_op jit(solution)/shard_map/ppermute | solution.py:20
  88.8 6.1 %collective-permute-start.23 = (bf16[128,256]{1,0:T(8,128)(2,1)S(1)}, bf16[128,256]{1,0:T(8,128)(2,1)S(1)}, u32[]{:S(2)}, u32[]{:S(2)}) collective-permute-start(bf16[128,256]{1,0:T(8,128)(2,1)S(1)} %add_convert_fusion.own_ref), channel_id=1, source_target_pairs={{0,24},{8,16},{16,8},{24,0},{1,25},{9,17},{17,9},{25,1},{2,26},{10... | collective-permute-start | bytes 196616 | tf_op jit(solution)/shard_map/ppermute | solution.py:20
  90.6 5.2 %collective-permute-start.24 = (bf16[128,256]{1,0:T(8,128)(2,1)S(1)}, bf16[128,256]{1,0:T(8,128)(2,1)S(1)}, u32[]{:S(2)}, u32[]{:S(2)}) collective-permute-start(bf16[128,256]{1,0:T(8,128)(2,1)S(1)} %add_convert_fusion.own_ref), channel_id=1, source_target_pairs={{0,6},{1,7},{2,4},{3,5},{4,2},{5,3},{6,0},{7,1},{8,14},{9,15},{10,... | collective-permute-start | bytes 196616 | tf_op jit(solution)/shard_map/ppermute | solution.py:20
  95.9 10.4 %collective-permute-start.25 = (bf16[4,128,256]{2,1,0:T(8,128)(2,1)S(1)}, bf16[4,128,256]{2,1,0:T(8,128)(2,1)S(1)}, u32[]{:S(2)}, u32[]{:S(2)}) collective-permute-start(bf16[4,128,256]{2,1,0:T(8,128)(2,1)S(1)} %get-tuple-element.50.refs_0_), channel_id=1, source_target_pairs={{0,2},{1,3},{2,0},{3,1},{4,6},{5,7},{6,4},{7,5},{8,10},{9,11},{10,... | collective-permute-start | bytes 786440 | tf_op jit(solution)/shard_map/ppermute | solution.py:20
  96.5 10.0 %collective-permute-start.26 = (bf16[4,128,256]{2,1,0:T(8,128)(2,1)S(1)}, bf16[4,128,256]{2,1,0:T(8,128)(2,1)S(1)}, u32[]{:S(2)}, u32[]{:S(2)}) collective-permute-start(bf16[4,128,256]{2,1,0:T(8,128)(2,1)S(1)} %get-tuple-element.50.refs_0_), channel_id=1, source_target_pairs={{0,4},{1,5},{2,6},{3,7},{4,0},{5,1},{6,2},{7,3},{8,12},{9,13},{10,... | collective-permute-start | bytes 786440 | tf_op jit(solution)/shard_map/ppermute | solution.py:20
  97.0 9.3 %collective-permute-start.29 = (bf16[144,256]{1,0:T(8,128)(2,1)S(1)}, bf16[144,256]{1,0:T(8,128)(2,1)S(1)}, u32[]{:S(2)}, u32[]{:S(2)}) collective-permute-start(bf16[144,256]{1,0:T(8,128)(2,1)S(1)} %get-tuple-element.51), channel_id=1, source_target_pairs={{0,6},{1,7},{2,4},{3,5},{4,2},{5,3},{6,0},{7,1},{8,14},{9,15},{10,... | collective-permute-start | bytes 221192 | tf_op jit(solution)/shard_map/ppermute | solution.py:20
  99.4 5.4 %collective-permute-start.27 = (bf16[128,256]{1,0:T(8,128)(2,1)S(1)}, bf16[128,256]{1,0:T(8,128)(2,1)S(1)}, u32[]{:S(2)}, u32[]{:S(2)}) collective-permute-start(bf16[128,256]{1,0:T(8,128)(2,1)S(1)} %collective-permute-done.24.refs_4_), channel_id=1, source_target_pairs={{0,8},{8,0},{16,24},{24,16},{1,9},{9,1},{17,25},{25,17},{2,10},{10... | collective-permute-start | bytes 196616 | tf_op jit(solution)/shard_map/ppermute | solution.py:20
  99.4 6.6 %collective-permute-start.28 = (bf16[128,256]{1,0:T(8,128)(2,1)S(1)}, bf16[128,256]{1,0:T(8,128)(2,1)S(1)}, u32[]{:S(2)}, u32[]{:S(2)}) collective-permute-start(bf16[128,256]{1,0:T(8,128)(2,1)S(1)} %collective-permute-done.24.refs_4_), channel_id=1, source_target_pairs={{0,16},{8,24},{16,0},{24,8},{1,17},{9,25},{17,1},{25,9},{2,18},{10... | collective-permute-start | bytes 196616 | tf_op jit(solution)/shard_map/ppermute | solution.py:20
  (10 other events, 48.6 us)

commit v15 on v13

--- a/solution.py
+++ b/solution.py
@@ -316,7 +316,7 @@
     ntok, panel = rows * n_hid, block // n_hid
     depth, shard_ff = gate_weight.shape
     tiles = shard_ff // TILE
-    ends = [0, TILE * (3 * tiles // 7), TILE * (11 * tiles // 14), shard_ff]
+    ends = [TILE * (tiles * k // 3) for k in range(4)]
     chip_masks = list(range(2, n_hid, 2))
 
     def part(weight, k):
@@ -361,18 +361,18 @@
     got_2 = swap(send_2, "tok", n_tok, 1)
     sum_1 = pair_total(keep_1, got_1, 2 * widths[1], (send_2,))
     over_1 = swap(sum_1, "tok", n_tok, 2)
-    down_b, = fetch([(down_weight, ends[1], shard_ff - ends[1], 0, block)], (sum_1,), "fetch_down")
+    down_b, = fetch([(down_weight, ends[2], widths[2], 0, block)], (sum_1,), "fetch_down")
     sum_2 = pair_total(keep_2, got_2, 2 * widths[2], (down_b,))
     over_2 = swap(sum_2, "tok", n_tok, 2)
-
-    a_own, scale = hidden_rows([(keep_0, got_0, over_0)], widths[:1], None, (sum_1,))
+    down_a, = fetch([(down_weight, 0, ends[2], 0, block)], (sum_2,), "fetch_down")
+
+    a_own, scale = hidden_rows([(keep_0, got_0, over_0), (keep_1, got_1, over_1)], widths[:2], None, (down_a,))
     a_two = swap(a_own, "tok", n_tok, 2)
     a_one = swap(a_own, "tok", n_tok, 1)
-    a_three = swap(a_two, "tok", n_tok, 1)
-    down_a, = fetch([(down_weight, 0, ends[1], 0, block)], (sum_2,), "fetch_down")
-    b_own, _ = hidden_rows([(keep_1, got_1, over_1), (keep_2, got_2, over_2)], widths[1:], scale, (a_one, a_three, down_a))
+    b_own, _ = hidden_rows([(keep_2, got_2, over_2)], widths[2:], scale, ())
     b_two = swap(b_own, "tok", n_tok, 2)
     b_one = swap(b_own, "tok", n_tok, 1)
+    a_three = swap(copy_after(a_two, (b_two, b_one, a_one)), "tok", n_tok, 1)
     b_three = swap(b_two, "tok", n_tok, 1)
     hidden_a = [a_own, a_one, a_two, a_three]
     hidden_b = [b_own, b_one, b_two, b_three]

time: 107 us -> 104 us (0.972)
  starting transfers between devices: 41.6 us -> 38.3 us
    ppermute x35, starting transfers between devices: 41.6 us -> 38.3 us  [swap(): return lax.ppermute(value, axis, [(i, i ^ mask) for i in range(size)])]
    pallas_call x25 -> x26, Pallas kernels: 33.6 us -> 33.8 us  [run(): pl.pallas_call(body, out_shape=out_shape, in_specs=[WHOLE] * len(operands...]
  transfers between devices with their start and end apart: 35 -> 35, of which waited for: 22 -> 21; matrix products, arithmetic and copies ran while one was open for 0% -> 0% of each run, Pallas kernels for 26% -> 28%
where the time goes in v15:
time: 104 us
  starting transfers between devices  38.3 us (37%)
  Pallas kernels  33.8 us (32%)
  waiting for transfers between devices  31.2 us (30%)
    ppermute x35, starting transfers between devices, swap(): return lax.ppermute(value, axis, [(i, i ^ mask) for i in range(size)])  38.3 us
    pallas_call x26, Pallas kernels, run(): pl.pallas_call(body, out_shape=out_shape, in_specs=[WHOLE] * len(operands...  33.8 us
    ppermute x35, waiting for transfers between devices, swap(): return lax.ppermute(value, axis, [(i, i ^ mask) for i in range(size)])  31.2 us
  transfers between devices with their start and end apart: 35, of which 21 were waited for; matrix products, arithmetic and copies ran while one was open for 0% of the time, Pallas kernels for 28%

profile of v15, /device:TPU:0, one launch (start us, length us, event | category | flops | bytes accessed | tf_op | source)
XLA Modules:
  0.0 104.2 jit_solution(11252896788211217200)
XLA Ops:
  0.6 3.0 %collective-permute-start = (bf16[16,2048]{1,0:T(8,128)(2,1)}, bf16[16,2048]{1,0:T(8,128)(2,1)S(1)}, u32[]{:S(2)}, u32[]{:S(2)}) collective-permute-start(bf16[16,2048]{1,0:T(8,128)(2,1)} %refs_2_.1), channel_id=1, source_target_pairs={{0,2},{1,3},{2,0},{3,1},{4,6},{5,7},{6,4},{7,5},{8,10},{9,11},{10,... | collective-permute-start | bytes 196616 | tf_op jit(solution)/shard_map/ppermute | solution.py:20
  5.2 3.7 %fetch_first.1 = (bf16[2048,1024]{1,0:T(8,128)(2,1)S(1)}, bf16[2048,1024]{1,0:T(8,128)(2,1)S(1)}, bf16[16,2048]{1,0:T(8,128)(2,1)S(1)}, f32[1,2048]{1,0:T(1,128)S(1)}) custom-call(bf16[2048,3584]{1,0:T(8,128)(2,1)} %refs_0_.7, bf16[2048,3584]{1,0:T(8,128)(2,1)} %refs_1_.5, bf16[16,2048]{1,0:T(8,128)(2,1)} %refs_2_.1, f32[1,2048]{1,0:T(1,128)} %bitcast.22), custom_call_target="tpu_custom_call" | custom-call | tf_op jit(solution)/shard_map/fetch_first/pallas_call | solution.py:24
  13.5 1.6 %collective-permute-start.7 = (bf16[2,32,2176]{2,1,0:T(8,128)(2,1)S(1)}, bf16[2,32,2176]{2,1,0:T(8,128)(2,1)S(1)}, u32[]{:S(2)}, u32[]{:S(2)}) collective-permute-start(bf16[2,32,2176]{2,1,0:T(8,128)(2,1)S(1)} %get-tuple-element.38.refs_2_), channel_id=1, source_target_pairs={{0,8},{8,0},{16,24},{24,16},{1,9},{9,1},{17,25},{25,17},{2,10},{10... | collective-permute-start | bytes 835592 | tf_op jit(solution)/shard_map/ppermute | solution.py:20
  15.1 4.3 %fetch_gate_up.2 = (bf16[2048,1280]{1,0:T(8,128)(2,1)S(1)}, bf16[2048,1280]{1,0:T(8,128)(2,1)S(1)}) custom-call(bf16[2048,3584]{1,0:T(8,128)(2,1)} %refs_0_.7, bf16[2048,3584]{1,0:T(8,128)(2,1)} %refs_1_.5, bf16[2,32,2176]{2,1,0:T(8,128)(2,1)S(1)} %get-tuple-element.38.refs_2_), custom_call_target="tpu_custom_call" | custom-call | tf_op jit(solution)/shard_map/fetch_gate_up/pallas_call | solution.py:24
  22.4 4.3 %fetch_gate_up.3 = (bf16[2048,1280]{1,0:T(8,128)(2,1)S(1)}, bf16[2048,1280]{1,0:T(8,128)(2,1)S(1)}) custom-call(bf16[2048,3584]{1,0:T(8,128)(2,1)} %refs_0_.7, bf16[2048,3584]{1,0:T(8,128)(2,1)} %refs_1_.5, bf16[32,2176]{1,0:T(8,128)(2,1)S(1)} %pair_total.3.refs_2_), custom_call_target="tpu_custom_call" | custom-call | tf_op jit(solution)/shard_map/fetch_gate_up/pallas_call | solution.py:24
  28.3 1.6 %collective-permute-start.8 = (bf16[2,32,2560]{2,1,0:T(8,128)(2,1)S(1)}, bf16[2,32,2560]{2,1,0:T(8,128)(2,1)S(1)}, u32[]{:S(2)}, u32[]{:S(2)}) collective-permute-start(bf16[2,32,2560]{2,1,0:T(8,128)(2,1)S(1)} %get-tuple-element.45.refs_0_), channel_id=1, source_target_pairs={{0,8},{8,0},{16,24},{24,16},{1,9},{9,1},{17,25},{25,17},{2,10},{10... | collective-permute-start | bytes 983048 | tf_op jit(solution)/shard_map/ppermute | solution.py:20
  30.8 2.7 %collective-permute-start.12 = (bf16[32,2560]{1,0:T(8,128)(2,1)S(1)}, bf16[32,2560]{1,0:T(8,128)(2,1)S(1)}, u32[]{:S(2)}, u32[]{:S(2)}) collective-permute-start(bf16[32,2560]{1,0:T(8,128)(2,1)S(1)} %pair_total.4.refs_1_), channel_id=1, source_target_pairs={{0,16},{8,24},{16,0},{24,8},{1,17},{9,25},{17,1},{25,9},{2,18},{10... | collective-permute-start | bytes 491528 | tf_op jit(solution)/shard_map/ppermute | solution.py:20
  33.8 2.5 %fetch_down.2.refs_0_.refs_4_ = bf16[1280,2048]{1,0:T(8,128)(2,1)S(1)} custom-call(bf16[3584,2048]{1,0:T(8,128)(2,1)} %refs_0_.9, bf16[32,2560]{1,0:T(8,128)(2,1)S(1)} %pair_total.4.refs_1_), custom_call_target="tpu_custom_call" | custom-call | tf_op jit(solution)/shard_map/fetch_down/pallas_call | solution.py:24
  36.4 7.4 %collective-permute-done.8.got_ref.refs_1_ = bf16[2,32,2560]{2,1,0:T(8,128)(2,1)S(1)} collective-permute-done((bf16[2,32,2560]{2,1,0:T(8,128)(2,1)S(1)}, bf16[2,32,2560]{2,1,0:T(8,128)(2,1)S(1)}, u32[]{:S(2)}, u32[]{:S(2)}) %collective-permute-start.8) | collective-permute-done | bytes 327712 | tf_op jit(solution)/shard_map/ppermute | solution.py:20
  44.3 3.8 %fetch_down.3.refs_6_.refs_4_ = bf16[2304,2048]{1,0:T(8,128)(2,1)S(1)} custom-call(bf16[3584,2048]{1,0:T(8,128)(2,1)} %refs_0_.9, bf16[32,2560]{1,0:T(8,128)(2,1)S(1)} %pair_total.5.refs_1_), custom_call_target="tpu_custom_call" | custom-call | tf_op jit(solution)/shard_map/fetch_down/pallas_call | solution.py:24
  48.1 2.4 %collective-permute-done.11.refs_2_ = bf16[32,2176]{1,0:T(8,128)(2,1)S(1)} collective-permute-done((bf16[32,2176]{1,0:T(8,128)(2,1)S(1)}, bf16[32,2176]{1,0:T(8,128)(2,1)S(1)}, u32[]{:S(2)}, u32[]{:S(2)}) %collective-permute-start.11) | collective-permute-done | bytes 139296 | tf_op jit(solution)/shard_map/ppermute | solution.py:20
  51.0 3.4 %collective-permute-start.17 = (bf16[32,2304]{1,0:T(8,128)(2,1)S(1)}, bf16[32,2304]{1,0:T(8,128)(2,1)S(1)}, u32[]{:S(2)}, u32[]{:S(2)}) collective-permute-start(bf16[32,2304]{1,0:T(8,128)(2,1)S(1)} %get-tuple-element.49.refs_0_), channel_id=1, source_target_pairs={{0,16},{8,24},{16,0},{24,8},{1,17},{9,25},{17,1},{25,9},{2,18},{10... | collective-permute-start | bytes 442376 | tf_op jit(solution)/shard_map/ppermute | solution.py:20
  56.5 3.5 %collective-permute-start.14 = (bf16[32,1280]{1,0:T(8,128)(2,1)S(1)}, bf16[32,1280]{1,0:T(8,128)(2,1)S(1)}, u32[]{:S(2)}, u32[]{:S(2)}) collective-permute-start(bf16[32,1280]{1,0:T(8,128)(2,1)S(1)} %get-tuple-element.48.refs_0_), channel_id=1, source_target_pairs={{0,16},{8,24},{16,0},{24,8},{1,17},{9,25},{17,1},{25,9},{2,18},{10... | collective-permute-start | bytes 245768 | tf_op jit(solution)/shard_map/ppermute | solution.py:20
  61.2 1.9 %collective-permute-done.13.refs_1_ = bf16[32,1280]{1,0:T(8,128)(2,1)S(1)} collective-permute-done((bf16[32,1280]{1,0:T(8,128)(2,1)S(1)}, bf16[32,1280]{1,0:T(8,128)(2,1)S(1)}, u32[]{:S(2)}, u32[]{:S(2)}) %collective-permute-start.13) | collective-permute-done | bytes 81952 | tf_op jit(solution)/shard_map/ppermute | solution.py:20
  63.8 1.9 %collective-permute-start.15 = (bf16[32,1280]{1,0:T(8,128)(2,1)S(1)}, bf16[32,1280]{1,0:T(8,128)(2,1)S(1)}, u32[]{:S(2)}, u32[]{:S(2)}) collective-permute-start(bf16[32,1280]{1,0:T(8,128)(2,1)S(1)} %collective-permute-done.14.refs_0_.refs_2_), channel_id=1, source_target_pairs={{0,8},{8,0},{16,24},{24,16},{1,9},{9,1},{17,25},{25,17},{2,10},{10... | collective-permute-start | bytes 245768 | tf_op jit(solution)/shard_map/ppermute | solution.py:20
  65.7 3.1 %collective-permute-done.18.refs_3_ = bf16[32,2304]{1,0:T(8,128)(2,1)S(1)} collective-permute-done((bf16[32,2304]{1,0:T(8,128)(2,1)S(1)}, bf16[32,2304]{1,0:T(8,128)(2,1)S(1)}, u32[]{:S(2)}, u32[]{:S(2)}) %collective-permute-start.18) | collective-permute-done | bytes 147488 | tf_op jit(solution)/shard_map/ppermute | solution.py:20
  71.9 2.3 %collective-permute-start.20 = (bf16[128,256]{1,0:T(8,128)(2,1)S(1)}, bf16[128,256]{1,0:T(8,128)(2,1)S(1)}, u32[]{:S(2)}, u32[]{:S(2)}) collective-permute-start(bf16[128,256]{1,0:T(8,128)(2,1)S(1)} %get-tuple-element.51), channel_id=1, source_target_pairs={{0,6},{1,7},{2,4},{3,5},{4,2},{5,3},{6,0},{7,1},{8,14},{9,15},{10,... | collective-permute-start | bytes 196616 | tf_op jit(solution)/shard_map/ppermute | solution.py:20
  75.5 1.9 %collective-permute-done.20 = bf16[128,256]{1,0:T(8,128)(2,1)S(1)} collective-permute-done((bf16[128,256]{1,0:T(8,128)(2,1)S(1)}, bf16[128,256]{1,0:T(8,128)(2,1)S(1)}, u32[]{:S(2)}, u32[]{:S(2)}) %collective-permute-start.20) | collective-permute-done | bytes 65568 | tf_op jit(solution)/shard_map/ppermute | solution.py:20
  79.5 2.5 %collective-permute-start.24 = (bf16[128,256]{1,0:T(8,128)(2,1)S(1)}, bf16[128,256]{1,0:T(8,128)(2,1)S(1)}, u32[]{:S(2)}, u32[]{:S(2)}) collective-permute-start(bf16[128,256]{1,0:T(8,128)(2,1)S(1)} %add_convert_fusion.own_ref), channel_id=1, source_target_pairs={{0,16},{8,24},{16,0},{24,8},{1,17},{9,25},{17,1},{25,9},{2,18},{10... | collective-permute-start | bytes 196616 | tf_op jit(solution)/shard_map/ppermute | solution.py:20
  85.0 1.8 %collective-permute-done.24 = bf16[128,256]{1,0:T(8,128)(2,1)S(1)} collective-permute-done((bf16[128,256]{1,0:T(8,128)(2,1)S(1)}, bf16[128,256]{1,0:T(8,128)(2,1)S(1)}, u32[]{:S(2)}, u32[]{:S(2)}) %collective-permute-start.24) | collective-permute-done | bytes 65568 | tf_op jit(solution)/shard_map/ppermute | solution.py:20
  92.5 2.7 %collective-permute-start.30 = (bf16[128,256]{1,0:T(8,128)(2,1)S(1)}, bf16[128,256]{1,0:T(8,128)(2,1)S(1)}, u32[]{:S(2)}, u32[]{:S(2)}) collective-permute-start(bf16[128,256]{1,0:T(8,128)(2,1)S(1)} %collective-permute-done.26.refs_4_), channel_id=1, source_target_pairs={{0,16},{8,24},{16,0},{24,8},{1,17},{9,25},{17,1},{25,9},{2,18},{10... | collective-permute-start | bytes 196616 | tf_op jit(solution)/shard_map/ppermute | solution.py:20
  95.2 2.5 %gram.3 = (f32[256,8192]{1,0:T(8,128)}, f32[64,256]{1,0:T(8,128)}) custom-call(bf16[128,256]{1,0:T(8,128)(2,1)S(1)} %add_convert_fusion.own_ref, bf16[4,128,256]{2,1,0:T(8,128)(2,1)S(1)} %get-tuple-element.54.refs_0_, bf16[4,128,256]{2,1,0:T(8,128)(2,1)S(1)} %collective-permute-done.32.refs_1_, bf16[1,128,256]{2,1,0:T(8,128)(2,1)S(1)} %bitcast.13, ...), custom_call_target="tpu_custom_call" | custom-call | flops 167772160 | bytes 2621440 | tf_op jit(solution)/shard_map/gram/pallas_call | solution.py:24
  100.2 1.9 %gram.4.refs_1_ = f32[256,8192]{1,0:T(8,128)} custom-call(bf16[128,256]{1,0:T(8,128)(2,1)S(1)} %add_convert_fusion.own_ref, bf16[11,128,256]{2,1,0:T(8,128)(2,1)S(1)} %stack.3.refs_0_, f32[256,8192]{1,0:T(8,128)} %get-tuple-element.56.refs_5_.refs_1_), custom_call_target="tpu_custom_call", output_to_operand_aliasing={{}: (2, {})} | custom-call | flops 184549376 | bytes 2883584 | tf_op jit(solution)/shard_map/gram/pallas_call | solution.py:24
  102.3 1.9 %gram.5 = f32[256,8192]{1,0:T(8,128)} custom-call(bf16[128,256]{1,0:T(8,128)(2,1)S(1)} %add_convert_fusion.own_ref, bf16[11,128,256]{2,1,0:T(8,128)(2,1)S(1)} %collective-permute-done.34.refs_0_, f32[256,8192]{1,0:T(8,128)} %gram.4.refs_1_), custom_call_target="tpu_custom_call", output_to_operand_aliasing={{}: (2, {})} | custom-call | flops 184549376 | bytes 2883584 | tf_op jit(solution)/shard_map/gram/pallas_call | solution.py:24
  (75 shorter events, 34.8 us)
Async XLA Ops:
  0.6 8.3 %collective-permute-start = (bf16[16,2048]{1,0:T(8,128)(2,1)}, bf16[16,2048]{1,0:T(8,128)(2,1)S(1)}, u32[]{:S(2)}, u32[]{:S(2)}) collective-permute-start(bf16[16,2048]{1,0:T(8,128)(2,1)} %refs_2_.1), channel_id=1, source_target_pairs={{0,2},{1,3},{2,0},{3,1},{4,6},{5,7},{6,4},{7,5},{8,10},{9,11},{10,... | collective-permute-start | bytes 196616 | tf_op jit(solution)/shard_map/ppermute | solution.py:20
  3.6 5.9 %collective-permute-start.1 = (bf16[16,2048]{1,0:T(8,128)(2,1)}, bf16[16,2048]{1,0:T(8,128)(2,1)S(1)}, u32[]{:S(2)}, u32[]{:S(2)}) collective-permute-start(bf16[16,2048]{1,0:T(8,128)(2,1)} %refs_2_.1), channel_id=1, source_target_pairs={{0,4},{1,5},{2,6},{3,7},{4,0},{5,1},{6,2},{7,3},{8,12},{9,13},{10,... | collective-permute-start | bytes 196616 | tf_op jit(solution)/shard_map/ppermute | solution.py:20
  5.2 5.4 %collective-permute-start.2 = (bf16[16,2048]{1,0:T(8,128)(2,1)}, bf16[16,2048]{1,0:T(8,128)(2,1)S(1)}, u32[]{:S(2)}, u32[]{:S(2)}) collective-permute-start(bf16[16,2048]{1,0:T(8,128)(2,1)} %refs_2_.1), channel_id=1, source_target_pairs={{0,6},{1,7},{2,4},{3,5},{4,2},{5,3},{6,0},{7,1},{8,14},{9,15},{10,... | collective-permute-start | bytes 196616 | tf_op jit(solution)/shard_map/ppermute | solution.py:20
  5.2 5.4 %collective-permute-start.3 = (bf16[16,2048]{1,0:T(8,128)(2,1)}, bf16[16,2048]{1,0:T(8,128)(2,1)S(1)}, u32[]{:S(2)}, u32[]{:S(2)}) collective-permute-start(bf16[16,2048]{1,0:T(8,128)(2,1)} %refs_2_.1), channel_id=1, source_target_pairs={{0,1},{1,0},{2,3},{3,2},{4,5},{5,4},{6,7},{7,6},{8,9},{9,8},{10,11... | collective-permute-start | bytes 196616 | tf_op jit(solution)/shard_map/ppermute | solution.py:20
  13.5 8.8 %collective-permute-start.7 = (bf16[2,32,2176]{2,1,0:T(8,128)(2,1)S(1)}, bf16[2,32,2176]{2,1,0:T(8,128)(2,1)S(1)}, u32[]{:S(2)}, u32[]{:S(2)}) collective-permute-start(bf16[2,32,2176]{2,1,0:T(8,128)(2,1)S(1)} %get-tuple-element.38.refs_2_), channel_id=1, source_target_pairs={{0,8},{8,0},{16,24},{24,16},{1,9},{9,1},{17,25},{25,17},{2,10},{10... | collective-permute-start | bytes 835592 | tf_op jit(solution)/shard_map/ppermute | solution.py:20
  21.0 9.8 %collective-permute-start.9 = (bf16[2,32,2560]{2,1,0:T(8,128)(2,1)S(1)}, bf16[2,32,2560]{2,1,0:T(8,128)(2,1)S(1)}, u32[]{:S(2)}, u32[]{:S(2)}) collective-permute-start(bf16[2,32,2560]{2,1,0:T(8,128)(2,1)S(1)} %get-tuple-element.41.refs_0_), channel_id=1, source_target_pairs={{0,8},{8,0},{16,24},{24,16},{1,9},{9,1},{17,25},{25,17},{2,10},{10... | collective-permute-start | bytes 983048 | tf_op jit(solution)/shard_map/ppermute | solution.py:20
  28.3 15.4 %collective-permute-start.8 = (bf16[2,32,2560]{2,1,0:T(8,128)(2,1)S(1)}, bf16[2,32,2560]{2,1,0:T(8,128)(2,1)S(1)}, u32[]{:S(2)}, u32[]{:S(2)}) collective-permute-start(bf16[2,32,2560]{2,1,0:T(8,128)(2,1)S(1)} %get-tuple-element.45.refs_0_), channel_id=1, source_target_pairs={{0,8},{8,0},{16,24},{24,16},{1,9},{9,1},{17,25},{25,17},{2,10},{10... | collective-permute-start | bytes 983048 | tf_op jit(solution)/shard_map/ppermute | solution.py:20
  30.8 19.6 %collective-permute-start.12 = (bf16[32,2560]{1,0:T(8,128)(2,1)S(1)}, bf16[32,2560]{1,0:T(8,128)(2,1)S(1)}, u32[]{:S(2)}, u32[]{:S(2)}) collective-permute-start(bf16[32,2560]{1,0:T(8,128)(2,1)S(1)} %pair_total.4.refs_1_), channel_id=1, source_target_pairs={{0,16},{8,24},{16,0},{24,8},{1,17},{9,25},{17,1},{25,9},{2,18},{10... | collective-permute-start | bytes 491528 | tf_op jit(solution)/shard_map/ppermute | solution.py:20
  33.6 16.9 %collective-permute-start.11 = (bf16[32,2176]{1,0:T(8,128)(2,1)S(1)}, bf16[32,2176]{1,0:T(8,128)(2,1)S(1)}, u32[]{:S(2)}, u32[]{:S(2)}) collective-permute-start(bf16[32,2176]{1,0:T(8,128)(2,1)S(1)} %pair_total.3.refs_2_), channel_id=1, source_target_pairs={{0,16},{8,24},{16,0},{24,8},{1,17},{9,25},{17,1},{25,9},{2,18},{10... | collective-permute-start | bytes 417800 | tf_op jit(solution)/shard_map/ppermute | solution.py:20
  43.8 11.8 %collective-permute-start.10 = (bf16[32,2560]{1,0:T(8,128)(2,1)S(1)}, bf16[32,2560]{1,0:T(8,128)(2,1)S(1)}, u32[]{:S(2)}, u32[]{:S(2)}) collective-permute-start(bf16[32,2560]{1,0:T(8,128)(2,1)S(1)} %pair_total.5.refs_1_), channel_id=1, source_target_pairs={{0,16},{8,24},{16,0},{24,8},{1,17},{9,25},{17,1},{25,9},{2,18},{10... | collective-permute-start | bytes 491528 | tf_op jit(solution)/shard_map/ppermute | solution.py:20
  50.7 10.5 %collective-permute-start.16 = (bf16[32,2304]{1,0:T(8,128)(2,1)S(1)}, bf16[32,2304]{1,0:T(8,128)(2,1)S(1)}, u32[]{:S(2)}, u32[]{:S(2)}) collective-permute-start(bf16[32,2304]{1,0:T(8,128)(2,1)S(1)} %get-tuple-element.49.refs_0_), channel_id=1, source_target_pairs={{0,8},{8,0},{16,24},{24,16},{1,9},{9,1},{17,25},{25,17},{2,10},{10... | collective-permute-start | bytes 442376 | tf_op jit(solution)/shard_map/ppermute | solution.py:20
  51.0 10.1 %collective-permute-start.17 = (bf16[32,2304]{1,0:T(8,128)(2,1)S(1)}, bf16[32,2304]{1,0:T(8,128)(2,1)S(1)}, u32[]{:S(2)}, u32[]{:S(2)}) collective-permute-start(bf16[32,2304]{1,0:T(8,128)(2,1)S(1)} %get-tuple-element.49.refs_0_), channel_id=1, source_target_pairs={{0,16},{8,24},{16,0},{24,8},{1,17},{9,25},{17,1},{25,9},{2,18},{10... | collective-permute-start | bytes 442376 | tf_op jit(solution)/shard_map/ppermute | solution.py:20
  56.2 6.8 %collective-permute-start.13 = (bf16[32,1280]{1,0:T(8,128)(2,1)S(1)}, bf16[32,1280]{1,0:T(8,128)(2,1)S(1)}, u32[]{:S(2)}, u32[]{:S(2)}) collective-permute-start(bf16[32,1280]{1,0:T(8,128)(2,1)S(1)} %get-tuple-element.48.refs_0_), channel_id=1, source_target_pairs={{0,8},{8,0},{16,24},{24,16},{1,9},{9,1},{17,25},{25,17},{2,10},{10... | collective-permute-start | bytes 245768 | tf_op jit(solution)/shard_map/ppermute | solution.py:20
  56.5 7.1 %collective-permute-start.14 = (bf16[32,1280]{1,0:T(8,128)(2,1)S(1)}, bf16[32,1280]{1,0:T(8,128)(2,1)S(1)}, u32[]{:S(2)}, u32[]{:S(2)}) collective-permute-start(bf16[32,1280]{1,0:T(8,128)(2,1)S(1)} %get-tuple-element.48.refs_0_), channel_id=1, source_target_pairs={{0,16},{8,24},{16,0},{24,8},{1,17},{9,25},{17,1},{25,9},{2,18},{10... | collective-permute-start | bytes 245768 | tf_op jit(solution)/shard_map/ppermute | solution.py:20
  63.8 5.9 %collective-permute-start.15 = (bf16[32,1280]{1,0:T(8,128)(2,1)S(1)}, bf16[32,1280]{1,0:T(8,128)(2,1)S(1)}, u32[]{:S(2)}, u32[]{:S(2)}) collective-permute-start(bf16[32,1280]{1,0:T(8,128)(2,1)S(1)} %collective-permute-done.14.refs_0_.refs_2_), channel_id=1, source_target_pairs={{0,8},{8,0},{16,24},{24,16},{1,9},{9,1},{17,25},{25,17},{2,10},{10... | collective-permute-start | bytes 245768 | tf_op jit(solution)/shard_map/ppermute | solution.py:20
  71.9 5.5 %collective-permute-start.20 = (bf16[128,256]{1,0:T(8,128)(2,1)S(1)}, bf16[128,256]{1,0:T(8,128)(2,1)S(1)}, u32[]{:S(2)}, u32[]{:S(2)}) collective-permute-start(bf16[128,256]{1,0:T(8,128)(2,1)S(1)} %get-tuple-element.51), channel_id=1, source_target_pairs={{0,6},{1,7},{2,4},{3,5},{4,2},{5,3},{6,0},{7,1},{8,14},{9,15},{10,... | collective-permute-start | bytes 196616 | tf_op jit(solution)/shard_map/ppermute | solution.py:20
  79.0 6.0 %collective-permute-start.23 = (bf16[128,256]{1,0:T(8,128)(2,1)S(1)}, bf16[128,256]{1,0:T(8,128)(2,1)S(1)}, u32[]{:S(2)}, u32[]{:S(2)}) collective-permute-start(bf16[128,256]{1,0:T(8,128)(2,1)S(1)} %add_convert_fusion.own_ref), channel_id=1, source_target_pairs={{0,8},{8,0},{16,24},{24,16},{1,9},{9,1},{17,25},{25,17},{2,10},{10... | collective-permute-start | bytes 196616 | tf_op jit(solution)/shard_map/ppermute | solution.py:20
  79.5 7.3 %collective-permute-start.24 = (bf16[128,256]{1,0:T(8,128)(2,1)S(1)}, bf16[128,256]{1,0:T(8,128)(2,1)S(1)}, u32[]{:S(2)}, u32[]{:S(2)}) collective-permute-start(bf16[128,256]{1,0:T(8,128)(2,1)S(1)} %add_convert_fusion.own_ref), channel_id=1, source_target_pairs={{0,16},{8,24},{16,0},{24,8},{1,17},{9,25},{17,1},{25,9},{2,18},{10... | collective-permute-start | bytes 196616 | tf_op jit(solution)/shard_map/ppermute | solution.py:20
  82.0 6.2 %collective-permute-start.25 = (bf16[128,256]{1,0:T(8,128)(2,1)S(1)}, bf16[128,256]{1,0:T(8,128)(2,1)S(1)}, u32[]{:S(2)}, u32[]{:S(2)}) collective-permute-start(bf16[128,256]{1,0:T(8,128)(2,1)S(1)} %add_convert_fusion.own_ref), channel_id=1, source_target_pairs={{0,24},{8,16},{16,8},{24,0},{1,25},{9,17},{17,9},{25,1},{2,26},{10... | collective-permute-start | bytes 196616 | tf_op jit(solution)/shard_map/ppermute | solution.py:20
  88.7 11.3 %collective-permute-start.27 = (bf16[4,128,256]{2,1,0:T(8,128)(2,1)S(1)}, bf16[4,128,256]{2,1,0:T(8,128)(2,1)S(1)}, u32[]{:S(2)}, u32[]{:S(2)}) collective-permute-start(bf16[4,128,256]{2,1,0:T(8,128)(2,1)S(1)} %get-tuple-element.54.refs_0_), channel_id=1, source_target_pairs={{0,2},{1,3},{2,0},{3,1},{4,6},{5,7},{6,4},{7,5},{8,10},{9,11},{10,... | collective-permute-start | bytes 786440 | tf_op jit(solution)/shard_map/ppermute | solution.py:20
  90.0 10.1 %collective-permute-start.28 = (bf16[4,128,256]{2,1,0:T(8,128)(2,1)S(1)}, bf16[4,128,256]{2,1,0:T(8,128)(2,1)S(1)}, u32[]{:S(2)}, u32[]{:S(2)}) collective-permute-start(bf16[4,128,256]{2,1,0:T(8,128)(2,1)S(1)} %get-tuple-element.54.refs_0_), channel_id=1, source_target_pairs={{0,4},{1,5},{2,6},{3,7},{4,0},{5,1},{6,2},{7,3},{8,12},{9,13},{10,... | collective-permute-start | bytes 786440 | tf_op jit(solution)/shard_map/ppermute | solution.py:20
  90.9 9.1 %collective-permute-start.31 = (bf16[144,256]{1,0:T(8,128)(2,1)S(1)}, bf16[144,256]{1,0:T(8,128)(2,1)S(1)}, u32[]{:S(2)}, u32[]{:S(2)}) collective-permute-start(bf16[144,256]{1,0:T(8,128)(2,1)S(1)} %get-tuple-element.55), channel_id=1, source_target_pairs={{0,6},{1,7},{2,4},{3,5},{4,2},{5,3},{6,0},{7,1},{8,14},{9,15},{10,... | collective-permute-start | bytes 221192 | tf_op jit(solution)/shard_map/ppermute | solution.py:20
  92.3 5.4 %collective-permute-start.29 = (bf16[128,256]{1,0:T(8,128)(2,1)S(1)}, bf16[128,256]{1,0:T(8,128)(2,1)S(1)}, u32[]{:S(2)}, u32[]{:S(2)}) collective-permute-start(bf16[128,256]{1,0:T(8,128)(2,1)S(1)} %collective-permute-done.26.refs_4_), channel_id=1, source_target_pairs={{0,8},{8,0},{16,24},{24,16},{1,9},{9,1},{17,25},{25,17},{2,10},{10... | collective-permute-start | bytes 196616 | tf_op jit(solution)/shard_map/ppermute | solution.py:20
  92.5 6.6 %collective-permute-start.30 = (bf16[128,256]{1,0:T(8,128)(2,1)S(1)}, bf16[128,256]{1,0:T(8,128)(2,1)S(1)}, u32[]{:S(2)}, u32[]{:S(2)}) collective-permute-start(bf16[128,256]{1,0:T(8,128)(2,1)S(1)} %collective-permute-done.26.refs_4_), channel_id=1, source_target_pairs={{0,16},{8,24},{16,0},{24,8},{1,17},{9,25},{17,1},{25,9},{2,18},{10... | collective-permute-start | bytes 196616 | tf_op jit(solution)/shard_map/ppermute | solution.py:20
  (12 other events, 57.3 us)

commit v16 on v15

--- a/solution.py
+++ b/solution.py
@@ -224,7 +224,7 @@
     z = lax.axis_index("tok")
     h = lax.axis_index("hid")
     rows = blocks[0].shape[0]
-    for d, block in enumerate(blocks):
+    for d, block in zip((0, 2, 1, 3), blocks):
         lhs[pl.ds(pl.multiple_of((z ^ d) * rows, rows), rows), :] = block[...]
     values = lhs[...]
     for slot, mask in enumerate(masks):
@@ -374,8 +374,8 @@
     b_one = swap(b_own, "tok", n_tok, 1)
     a_three = swap(copy_after(a_two, (b_two, b_one, a_one)), "tok", n_tok, 1)
     b_three = swap(b_two, "tok", n_tok, 1)
-    hidden_a = [a_own, a_one, a_two, a_three]
-    hidden_b = [b_own, b_one, b_two, b_three]
+    hidden_a = [a_own, a_two, a_one, a_three]
+    hidden_b = [b_own, b_two, b_one, b_three]
 
     here = [0] + chip_masks
     there = [mask + 1 for mask in here]

time: 104 us -> 106 us (1.019)
  waiting for transfers between devices: 31.2 us -> 33.7 us
    ppermute x35, waiting for transfers between devices: 31.2 us -> 33.7 us  [swap(): return lax.ppermute(value, axis, [(i, i ^ mask) for i in range(size)])]
where the time goes in v16:
time: 106 us
  starting transfers between devices  37.8 us (36%)
  Pallas kernels  33.8 us (32%)
  waiting for transfers between devices  33.7 us (32%)
    ppermute x35, starting transfers between devices, swap(): return lax.ppermute(value, axis, [(i, i ^ mask) for i in range(size)])  37.8 us
    pallas_call x26, Pallas kernels, run(): pl.pallas_call(body, out_shape=out_shape, in_specs=[WHOLE] * len(operands...  33.8 us
    ppermute x35, waiting for transfers between devices, swap(): return lax.ppermute(value, axis, [(i, i ^ mask) for i in range(size)])  33.7 us
  transfers between devices with their start and end apart: 35, of which 21 were waited for; matrix products, arithmetic and copies ran while one was open for 0% of the time, Pallas kernels for 28%

profile of v16, /device:TPU:0, one launch (start us, length us, event | category | flops | bytes accessed | tf_op | source)
XLA Modules:
  0.0 106.2 jit_solution(7939493037820921984)
XLA Ops:
  0.6 3.0 %collective-permute-start = (bf16[16,2048]{1,0:T(8,128)(2,1)}, bf16[16,2048]{1,0:T(8,128)(2,1)S(1)}, u32[]{:S(2)}, u32[]{:S(2)}) collective-permute-start(bf16[16,2048]{1,0:T(8,128)(2,1)} %refs_2_.1), channel_id=1, source_target_pairs={{0,2},{1,3},{2,0},{3,1},{4,6},{5,7},{6,4},{7,5},{8,10},{9,11},{10,... | collective-permute-start | bytes 196616 | tf_op jit(solution)/shard_map/ppermute | solution.py:20
  5.2 3.7 %fetch_first.1 = (bf16[2048,1024]{1,0:T(8,128)(2,1)S(1)}, bf16[2048,1024]{1,0:T(8,128)(2,1)S(1)}, bf16[16,2048]{1,0:T(8,128)(2,1)S(1)}, f32[1,2048]{1,0:T(1,128)S(1)}) custom-call(bf16[2048,3584]{1,0:T(8,128)(2,1)} %refs_0_.7, bf16[2048,3584]{1,0:T(8,128)(2,1)} %refs_1_.5, bf16[16,2048]{1,0:T(8,128)(2,1)} %refs_2_.1, f32[1,2048]{1,0:T(1,128)} %bitcast.22), custom_call_target="tpu_custom_call" | custom-call | tf_op jit(solution)/shard_map/fetch_first/pallas_call | solution.py:24
  15.1 4.3 %fetch_gate_up.2 = (bf16[2048,1280]{1,0:T(8,128)(2,1)S(1)}, bf16[2048,1280]{1,0:T(8,128)(2,1)S(1)}) custom-call(bf16[2048,3584]{1,0:T(8,128)(2,1)} %refs_0_.7, bf16[2048,3584]{1,0:T(8,128)(2,1)} %refs_1_.5, bf16[2,32,2176]{2,1,0:T(8,128)(2,1)S(1)} %get-tuple-element.38.refs_2_), custom_call_target="tpu_custom_call" | custom-call | tf_op jit(solution)/shard_map/fetch_gate_up/pallas_call | solution.py:24
  22.4 4.3 %fetch_gate_up.3 = (bf16[2048,1280]{1,0:T(8,128)(2,1)S(1)}, bf16[2048,1280]{1,0:T(8,128)(2,1)S(1)}) custom-call(bf16[2048,3584]{1,0:T(8,128)(2,1)} %refs_0_.7, bf16[2048,3584]{1,0:T(8,128)(2,1)} %refs_1_.5, bf16[32,2176]{1,0:T(8,128)(2,1)S(1)} %pair_total.3.refs_2_), custom_call_target="tpu_custom_call" | custom-call | tf_op jit(solution)/shard_map/fetch_gate_up/pallas_call | solution.py:24
  30.8 2.7 %collective-permute-start.12 = (bf16[32,2560]{1,0:T(8,128)(2,1)S(1)}, bf16[32,2560]{1,0:T(8,128)(2,1)S(1)}, u32[]{:S(2)}, u32[]{:S(2)}) collective-permute-start(bf16[32,2560]{1,0:T(8,128)(2,1)S(1)} %pair_total.4.refs_1_), channel_id=1, source_target_pairs={{0,16},{8,24},{16,0},{24,8},{1,17},{9,25},{17,1},{25,9},{2,18},{10... | collective-permute-start | bytes 491528 | tf_op jit(solution)/shard_map/ppermute | solution.py:20
  33.8 2.5 %fetch_down.2.refs_0_.refs_4_ = bf16[1280,2048]{1,0:T(8,128)(2,1)S(1)} custom-call(bf16[3584,2048]{1,0:T(8,128)(2,1)} %refs_0_.9, bf16[32,2560]{1,0:T(8,128)(2,1)S(1)} %pair_total.4.refs_1_), custom_call_target="tpu_custom_call" | custom-call | tf_op jit(solution)/shard_map/fetch_down/pallas_call | solution.py:24
  36.4 7.4 %collective-permute-done.8.got_ref.refs_1_ = bf16[2,32,2560]{2,1,0:T(8,128)(2,1)S(1)} collective-permute-done((bf16[2,32,2560]{2,1,0:T(8,128)(2,1)S(1)}, bf16[2,32,2560]{2,1,0:T(8,128)(2,1)S(1)}, u32[]{:S(2)}, u32[]{:S(2)}) %collective-permute-start.8) | collective-permute-done | bytes 327712 | tf_op jit(solution)/shard_map/ppermute | solution.py:20
  44.3 3.8 %fetch_down.3.refs_6_.refs_4_ = bf16[2304,2048]{1,0:T(8,128)(2,1)S(1)} custom-call(bf16[3584,2048]{1,0:T(8,128)(2,1)} %refs_0_.9, bf16[32,2560]{1,0:T(8,128)(2,1)S(1)} %pair_total.5.refs_1_), custom_call_target="tpu_custom_call" | custom-call | tf_op jit(solution)/shard_map/fetch_down/pallas_call | solution.py:24
  48.1 2.4 %collective-permute-done.11.refs_2_ = bf16[32,2176]{1,0:T(8,128)(2,1)S(1)} collective-permute-done((bf16[32,2176]{1,0:T(8,128)(2,1)S(1)}, bf16[32,2176]{1,0:T(8,128)(2,1)S(1)}, u32[]{:S(2)}, u32[]{:S(2)}) %collective-permute-start.11) | collective-permute-done | bytes 139296 | tf_op jit(solution)/shard_map/ppermute | solution.py:20
  50.9 3.5 %collective-permute-start.17 = (bf16[32,2304]{1,0:T(8,128)(2,1)S(1)}, bf16[32,2304]{1,0:T(8,128)(2,1)S(1)}, u32[]{:S(2)}, u32[]{:S(2)}) collective-permute-start(bf16[32,2304]{1,0:T(8,128)(2,1)S(1)} %get-tuple-element.49.refs_0_), channel_id=1, source_target_pairs={{0,8},{8,0},{16,24},{24,16},{1,9},{9,1},{17,25},{25,17},{2,10},{10... | collective-permute-start | bytes 442376 | tf_op jit(solution)/shard_map/ppermute | solution.py:20
  54.4 2.8 %collective-permute-done.10.refs_2_ = bf16[32,2560]{1,0:T(8,128)(2,1)S(1)} collective-permute-done((bf16[32,2560]{1,0:T(8,128)(2,1)S(1)}, bf16[32,2560]{1,0:T(8,128)(2,1)S(1)}, u32[]{:S(2)}, u32[]{:S(2)}) %collective-permute-start.10) | collective-permute-done | bytes 163872 | tf_op jit(solution)/shard_map/ppermute | solution.py:20
  57.8 3.7 %collective-permute-start.14 = (bf16[32,1280]{1,0:T(8,128)(2,1)S(1)}, bf16[32,1280]{1,0:T(8,128)(2,1)S(1)}, u32[]{:S(2)}, u32[]{:S(2)}) collective-permute-start(bf16[32,1280]{1,0:T(8,128)(2,1)S(1)} %get-tuple-element.48.refs_0_), channel_id=1, source_target_pairs={{0,8},{8,0},{16,24},{24,16},{1,9},{9,1},{17,25},{25,17},{2,10},{10... | collective-permute-start | bytes 245768 | tf_op jit(solution)/shard_map/ppermute | solution.py:20
  61.5 2.6 %collective-permute-done.13.refs_0_.refs_1_ = bf16[32,1280]{1,0:T(8,128)(2,1)S(1)} collective-permute-done((bf16[32,1280]{1,0:T(8,128)(2,1)S(1)}, bf16[32,1280]{1,0:T(8,128)(2,1)S(1)}, u32[]{:S(2)}, u32[]{:S(2)}) %collective-permute-start.13) | collective-permute-done | bytes 81952 | tf_op jit(solution)/shard_map/ppermute | solution.py:20
  64.5 2.4 %collective-permute-start.18 = (bf16[32,2304]{1,0:T(8,128)(2,1)S(1)}, bf16[32,2304]{1,0:T(8,128)(2,1)S(1)}, u32[]{:S(2)}, u32[]{:S(2)}) collective-permute-start(bf16[32,2304]{1,0:T(8,128)(2,1)S(1)} %copy.15), channel_id=1, source_target_pairs={{0,8},{8,0},{16,24},{24,16},{1,9},{9,1},{17,25},{25,17},{2,10},{10... | collective-permute-start | bytes 442376 | tf_op jit(solution)/shard_map/ppermute | solution.py:20
  67.0 3.0 %collective-permute-done.18.refs_3_ = bf16[32,2304]{1,0:T(8,128)(2,1)S(1)} collective-permute-done((bf16[32,2304]{1,0:T(8,128)(2,1)S(1)}, bf16[32,2304]{1,0:T(8,128)(2,1)S(1)}, u32[]{:S(2)}, u32[]{:S(2)}) %collective-permute-start.18) | collective-permute-done | bytes 147488 | tf_op jit(solution)/shard_map/ppermute | solution.py:20
  73.6 2.6 %collective-permute-start.20 = (bf16[128,256]{1,0:T(8,128)(2,1)S(1)}, bf16[128,256]{1,0:T(8,128)(2,1)S(1)}, u32[]{:S(2)}, u32[]{:S(2)}) collective-permute-start(bf16[128,256]{1,0:T(8,128)(2,1)S(1)} %get-tuple-element.51), channel_id=1, source_target_pairs={{0,6},{1,7},{2,4},{3,5},{4,2},{5,3},{6,0},{7,1},{8,14},{9,15},{10,... | collective-permute-start | bytes 196616 | tf_op jit(solution)/shard_map/ppermute | solution.py:20
  77.1 1.9 %collective-permute-done.20 = bf16[128,256]{1,0:T(8,128)(2,1)S(1)} collective-permute-done((bf16[128,256]{1,0:T(8,128)(2,1)S(1)}, bf16[128,256]{1,0:T(8,128)(2,1)S(1)}, u32[]{:S(2)}, u32[]{:S(2)}) %collective-permute-start.20) | collective-permute-done | bytes 65568 | tf_op jit(solution)/shard_map/ppermute | solution.py:20
  80.9 1.7 %collective-permute-start.23 = (bf16[128,256]{1,0:T(8,128)(2,1)S(1)}, bf16[128,256]{1,0:T(8,128)(2,1)S(1)}, u32[]{:S(2)}, u32[]{:S(2)}) collective-permute-start(bf16[128,256]{1,0:T(8,128)(2,1)S(1)} %add_convert_fusion.own_ref), channel_id=1, source_target_pairs={{0,8},{8,0},{16,24},{24,16},{1,9},{9,1},{17,25},{25,17},{2,10},{10... | collective-permute-start | bytes 196616 | tf_op jit(solution)/shard_map/ppermute | solution.py:20
  82.9 2.5 %collective-permute-start.25 = (bf16[128,256]{1,0:T(8,128)(2,1)S(1)}, bf16[128,256]{1,0:T(8,128)(2,1)S(1)}, u32[]{:S(2)}, u32[]{:S(2)}) collective-permute-start(bf16[128,256]{1,0:T(8,128)(2,1)S(1)} %add_convert_fusion.own_ref), channel_id=1, source_target_pairs={{0,24},{8,16},{16,8},{24,0},{1,25},{9,17},{17,9},{25,1},{2,26},{10... | collective-permute-start | bytes 196616 | tf_op jit(solution)/shard_map/ppermute | solution.py:20
  87.0 2.7 %collective-permute-done.24 = bf16[128,256]{1,0:T(8,128)(2,1)S(1)} collective-permute-done((bf16[128,256]{1,0:T(8,128)(2,1)S(1)}, bf16[128,256]{1,0:T(8,128)(2,1)S(1)}, u32[]{:S(2)}, u32[]{:S(2)}) %collective-permute-start.24) | collective-permute-done | bytes 65568 | tf_op jit(solution)/shard_map/ppermute | solution.py:20
  96.1 2.4 %gram.3 = (f32[256,8192]{1,0:T(8,128)}, f32[64,256]{1,0:T(8,128)}) custom-call(bf16[128,256]{1,0:T(8,128)(2,1)S(1)} %add_convert_fusion.own_ref, bf16[4,128,256]{2,1,0:T(8,128)(2,1)S(1)} %get-tuple-element.54.refs_0_, bf16[4,128,256]{2,1,0:T(8,128)(2,1)S(1)} %collective-permute-done.32.refs_1_, bf16[1,128,256]{2,1,0:T(8,128)(2,1)S(1)} %bitcast.13, ...), custom_call_target="tpu_custom_call" | custom-call | flops 167772160 | bytes 2621440 | tf_op jit(solution)/shard_map/gram/pallas_call | solution.py:24
  99.1 2.0 %collective-permute-done.30 = bf16[128,256]{1,0:T(8,128)(2,1)S(1)} collective-permute-done((bf16[128,256]{1,0:T(8,128)(2,1)S(1)}, bf16[128,256]{1,0:T(8,128)(2,1)S(1)}, u32[]{:S(2)}, u32[]{:S(2)}) %collective-permute-start.30) | collective-permute-done | bytes 65568 | tf_op jit(solution)/shard_map/ppermute | solution.py:20
  102.1 1.9 %gram.4.refs_1_ = f32[256,8192]{1,0:T(8,128)} custom-call(bf16[128,256]{1,0:T(8,128)(2,1)S(1)} %add_convert_fusion.own_ref, bf16[11,128,256]{2,1,0:T(8,128)(2,1)S(1)} %stack.3.refs_0_, f32[256,8192]{1,0:T(8,128)} %get-tuple-element.56.refs_5_.refs_1_), custom_call_target="tpu_custom_call", output_to_operand_aliasing={{}: (2, {})} | custom-call | flops 184549376 | bytes 2883584 | tf_op jit(solution)/shard_map/gram/pallas_call | solution.py:24
  104.3 1.9 %gram.5 = f32[256,8192]{1,0:T(8,128)} custom-call(bf16[128,256]{1,0:T(8,128)(2,1)S(1)} %add_convert_fusion.own_ref, bf16[11,128,256]{2,1,0:T(8,128)(2,1)S(1)} %collective-permute-done.34.refs_0_, f32[256,8192]{1,0:T(8,128)} %gram.4.refs_1_), custom_call_target="tpu_custom_call", output_to_operand_aliasing={{}: (2, {})} | custom-call | flops 184549376 | bytes 2883584 | tf_op jit(solution)/shard_map/gram/pallas_call | solution.py:24
  (75 shorter events, 33.6 us)
Async XLA Ops:
  0.6 8.3 %collective-permute-start = (bf16[16,2048]{1,0:T(8,128)(2,1)}, bf16[16,2048]{1,0:T(8,128)(2,1)S(1)}, u32[]{:S(2)}, u32[]{:S(2)}) collective-permute-start(bf16[16,2048]{1,0:T(8,128)(2,1)} %refs_2_.1), channel_id=1, source_target_pairs={{0,2},{1,3},{2,0},{3,1},{4,6},{5,7},{6,4},{7,5},{8,10},{9,11},{10,... | collective-permute-start | bytes 196616 | tf_op jit(solution)/shard_map/ppermute | solution.py:20
  3.6 5.9 %collective-permute-start.1 = (bf16[16,2048]{1,0:T(8,128)(2,1)}, bf16[16,2048]{1,0:T(8,128)(2,1)S(1)}, u32[]{:S(2)}, u32[]{:S(2)}) collective-permute-start(bf16[16,2048]{1,0:T(8,128)(2,1)} %refs_2_.1), channel_id=1, source_target_pairs={{0,4},{1,5},{2,6},{3,7},{4,0},{5,1},{6,2},{7,3},{8,12},{9,13},{10,... | collective-permute-start | bytes 196616 | tf_op jit(solution)/shard_map/ppermute | solution.py:20
  5.2 5.4 %collective-permute-start.2 = (bf16[16,2048]{1,0:T(8,128)(2,1)}, bf16[16,2048]{1,0:T(8,128)(2,1)S(1)}, u32[]{:S(2)}, u32[]{:S(2)}) collective-permute-start(bf16[16,2048]{1,0:T(8,128)(2,1)} %refs_2_.1), channel_id=1, source_target_pairs={{0,6},{1,7},{2,4},{3,5},{4,2},{5,3},{6,0},{7,1},{8,14},{9,15},{10,... | collective-permute-start | bytes 196616 | tf_op jit(solution)/shard_map/ppermute | solution.py:20
  5.2 5.4 %collective-permute-start.3 = (bf16[16,2048]{1,0:T(8,128)(2,1)}, bf16[16,2048]{1,0:T(8,128)(2,1)S(1)}, u32[]{:S(2)}, u32[]{:S(2)}) collective-permute-start(bf16[16,2048]{1,0:T(8,128)(2,1)} %refs_2_.1), channel_id=1, source_target_pairs={{0,1},{1,0},{2,3},{3,2},{4,5},{5,4},{6,7},{7,6},{8,9},{9,8},{10,11... | collective-permute-start | bytes 196616 | tf_op jit(solution)/shard_map/ppermute | solution.py:20
  13.5 8.8 %collective-permute-start.7 = (bf16[2,32,2176]{2,1,0:T(8,128)(2,1)S(1)}, bf16[2,32,2176]{2,1,0:T(8,128)(2,1)S(1)}, u32[]{:S(2)}, u32[]{:S(2)}) collective-permute-start(bf16[2,32,2176]{2,1,0:T(8,128)(2,1)S(1)} %get-tuple-element.38.refs_2_), channel_id=1, source_target_pairs={{0,8},{8,0},{16,24},{24,16},{1,9},{9,1},{17,25},{25,17},{2,10},{10... | collective-permute-start | bytes 835592 | tf_op jit(solution)/shard_map/ppermute | solution.py:20
  21.0 9.8 %collective-permute-start.9 = (bf16[2,32,2560]{2,1,0:T(8,128)(2,1)S(1)}, bf16[2,32,2560]{2,1,0:T(8,128)(2,1)S(1)}, u32[]{:S(2)}, u32[]{:S(2)}) collective-permute-start(bf16[2,32,2560]{2,1,0:T(8,128)(2,1)S(1)} %get-tuple-element.41.refs_0_), channel_id=1, source_target_pairs={{0,8},{8,0},{16,24},{24,16},{1,9},{9,1},{17,25},{25,17},{2,10},{10... | collective-permute-start | bytes 983048 | tf_op jit(solution)/shard_map/ppermute | solution.py:20
  28.3 15.4 %collective-permute-start.8 = (bf16[2,32,2560]{2,1,0:T(8,128)(2,1)S(1)}, bf16[2,32,2560]{2,1,0:T(8,128)(2,1)S(1)}, u32[]{:S(2)}, u32[]{:S(2)}) collective-permute-start(bf16[2,32,2560]{2,1,0:T(8,128)(2,1)S(1)} %get-tuple-element.45.refs_0_), channel_id=1, source_target_pairs={{0,8},{8,0},{16,24},{24,16},{1,9},{9,1},{17,25},{25,17},{2,10},{10... | collective-permute-start | bytes 983048 | tf_op jit(solution)/shard_map/ppermute | solution.py:20
  30.8 19.6 %collective-permute-start.12 = (bf16[32,2560]{1,0:T(8,128)(2,1)S(1)}, bf16[32,2560]{1,0:T(8,128)(2,1)S(1)}, u32[]{:S(2)}, u32[]{:S(2)}) collective-permute-start(bf16[32,2560]{1,0:T(8,128)(2,1)S(1)} %pair_total.4.refs_1_), channel_id=1, source_target_pairs={{0,16},{8,24},{16,0},{24,8},{1,17},{9,25},{17,1},{25,9},{2,18},{10... | collective-permute-start | bytes 491528 | tf_op jit(solution)/shard_map/ppermute | solution.py:20
  33.6 16.8 %collective-permute-start.11 = (bf16[32,2176]{1,0:T(8,128)(2,1)S(1)}, bf16[32,2176]{1,0:T(8,128)(2,1)S(1)}, u32[]{:S(2)}, u32[]{:S(2)}) collective-permute-start(bf16[32,2176]{1,0:T(8,128)(2,1)S(1)} %pair_total.3.refs_2_), channel_id=1, source_target_pairs={{0,16},{8,24},{16,0},{24,8},{1,17},{9,25},{17,1},{25,9},{2,18},{10... | collective-permute-start | bytes 417800 | tf_op jit(solution)/shard_map/ppermute | solution.py:20
  43.8 13.4 %collective-permute-start.10 = (bf16[32,2560]{1,0:T(8,128)(2,1)S(1)}, bf16[32,2560]{1,0:T(8,128)(2,1)S(1)}, u32[]{:S(2)}, u32[]{:S(2)}) collective-permute-start(bf16[32,2560]{1,0:T(8,128)(2,1)S(1)} %pair_total.5.refs_1_), channel_id=1, source_target_pairs={{0,16},{8,24},{16,0},{24,8},{1,17},{9,25},{17,1},{25,9},{2,18},{10... | collective-permute-start | bytes 491528 | tf_op jit(solution)/shard_map/ppermute | solution.py:20
  50.6 10.9 %collective-permute-start.16 = (bf16[32,2304]{1,0:T(8,128)(2,1)S(1)}, bf16[32,2304]{1,0:T(8,128)(2,1)S(1)}, u32[]{:S(2)}, u32[]{:S(2)}) collective-permute-start(bf16[32,2304]{1,0:T(8,128)(2,1)S(1)} %get-tuple-element.49.refs_0_), channel_id=1, source_target_pairs={{0,16},{8,24},{16,0},{24,8},{1,17},{9,25},{17,1},{25,9},{2,18},{10... | collective-permute-start | bytes 442376 | tf_op jit(solution)/shard_map/ppermute | solution.py:20
  50.9 10.6 %collective-permute-start.17 = (bf16[32,2304]{1,0:T(8,128)(2,1)S(1)}, bf16[32,2304]{1,0:T(8,128)(2,1)S(1)}, u32[]{:S(2)}, u32[]{:S(2)}) collective-permute-start(bf16[32,2304]{1,0:T(8,128)(2,1)S(1)} %get-tuple-element.49.refs_0_), channel_id=1, source_target_pairs={{0,8},{8,0},{16,24},{24,16},{1,9},{9,1},{17,25},{25,17},{2,10},{10... | collective-permute-start | bytes 442376 | tf_op jit(solution)/shard_map/ppermute | solution.py:20
  57.8 6.3 %collective-permute-start.13 = (bf16[32,1280]{1,0:T(8,128)(2,1)S(1)}, bf16[32,1280]{1,0:T(8,128)(2,1)S(1)}, u32[]{:S(2)}, u32[]{:S(2)}) collective-permute-start(bf16[32,1280]{1,0:T(8,128)(2,1)S(1)} %get-tuple-element.48.refs_0_), channel_id=1, source_target_pairs={{0,16},{8,24},{16,0},{24,8},{1,17},{9,25},{17,1},{25,9},{2,18},{10... | collective-permute-start | bytes 245768 | tf_op jit(solution)/shard_map/ppermute | solution.py:20
  57.8 6.7 %collective-permute-start.14 = (bf16[32,1280]{1,0:T(8,128)(2,1)S(1)}, bf16[32,1280]{1,0:T(8,128)(2,1)S(1)}, u32[]{:S(2)}, u32[]{:S(2)}) collective-permute-start(bf16[32,1280]{1,0:T(8,128)(2,1)S(1)} %get-tuple-element.48.refs_0_), channel_id=1, source_target_pairs={{0,8},{8,0},{16,24},{24,16},{1,9},{9,1},{17,25},{25,17},{2,10},{10... | collective-permute-start | bytes 245768 | tf_op jit(solution)/shard_map/ppermute | solution.py:20
  64.5 5.5 %collective-permute-start.18 = (bf16[32,2304]{1,0:T(8,128)(2,1)S(1)}, bf16[32,2304]{1,0:T(8,128)(2,1)S(1)}, u32[]{:S(2)}, u32[]{:S(2)}) collective-permute-start(bf16[32,2304]{1,0:T(8,128)(2,1)S(1)} %copy.15), channel_id=1, source_target_pairs={{0,8},{8,0},{16,24},{24,16},{1,9},{9,1},{17,25},{25,17},{2,10},{10... | collective-permute-start | bytes 442376 | tf_op jit(solution)/shard_map/ppermute | solution.py:20
  73.6 5.4 %collective-permute-start.20 = (bf16[128,256]{1,0:T(8,128)(2,1)S(1)}, bf16[128,256]{1,0:T(8,128)(2,1)S(1)}, u32[]{:S(2)}, u32[]{:S(2)}) collective-permute-start(bf16[128,256]{1,0:T(8,128)(2,1)S(1)} %get-tuple-element.51), channel_id=1, source_target_pairs={{0,6},{1,7},{2,4},{3,5},{4,2},{5,3},{6,0},{7,1},{8,14},{9,15},{10,... | collective-permute-start | bytes 196616 | tf_op jit(solution)/shard_map/ppermute | solution.py:20
  80.9 6.1 %collective-permute-start.23 = (bf16[128,256]{1,0:T(8,128)(2,1)S(1)}, bf16[128,256]{1,0:T(8,128)(2,1)S(1)}, u32[]{:S(2)}, u32[]{:S(2)}) collective-permute-start(bf16[128,256]{1,0:T(8,128)(2,1)S(1)} %add_convert_fusion.own_ref), channel_id=1, source_target_pairs={{0,8},{8,0},{16,24},{24,16},{1,9},{9,1},{17,25},{25,17},{2,10},{10... | collective-permute-start | bytes 196616 | tf_op jit(solution)/shard_map/ppermute | solution.py:20
  82.5 7.2 %collective-permute-start.24 = (bf16[128,256]{1,0:T(8,128)(2,1)S(1)}, bf16[128,256]{1,0:T(8,128)(2,1)S(1)}, u32[]{:S(2)}, u32[]{:S(2)}) collective-permute-start(bf16[128,256]{1,0:T(8,128)(2,1)S(1)} %add_convert_fusion.own_ref), channel_id=1, source_target_pairs={{0,16},{8,24},{16,0},{24,8},{1,17},{9,25},{17,1},{25,9},{2,18},{10... | collective-permute-start | bytes 196616 | tf_op jit(solution)/shard_map/ppermute | solution.py:20
  82.9 6.9 %collective-permute-start.25 = (bf16[128,256]{1,0:T(8,128)(2,1)S(1)}, bf16[128,256]{1,0:T(8,128)(2,1)S(1)}, u32[]{:S(2)}, u32[]{:S(2)}) collective-permute-start(bf16[128,256]{1,0:T(8,128)(2,1)S(1)} %add_convert_fusion.own_ref), channel_id=1, source_target_pairs={{0,24},{8,16},{16,8},{24,0},{1,25},{9,17},{17,9},{25,1},{2,26},{10... | collective-permute-start | bytes 196616 | tf_op jit(solution)/shard_map/ppermute | solution.py:20
  85.3 5.2 %collective-permute-start.26 = (bf16[128,256]{1,0:T(8,128)(2,1)S(1)}, bf16[128,256]{1,0:T(8,128)(2,1)S(1)}, u32[]{:S(2)}, u32[]{:S(2)}) collective-permute-start(bf16[128,256]{1,0:T(8,128)(2,1)S(1)} %add_convert_fusion.own_ref), channel_id=1, source_target_pairs={{0,6},{1,7},{2,4},{3,5},{4,2},{5,3},{6,0},{7,1},{8,14},{9,15},{10,... | collective-permute-start | bytes 196616 | tf_op jit(solution)/shard_map/ppermute | solution.py:20
  90.6 11.4 %collective-permute-start.27 = (bf16[4,128,256]{2,1,0:T(8,128)(2,1)S(1)}, bf16[4,128,256]{2,1,0:T(8,128)(2,1)S(1)}, u32[]{:S(2)}, u32[]{:S(2)}) collective-permute-start(bf16[4,128,256]{2,1,0:T(8,128)(2,1)S(1)} %get-tuple-element.54.refs_0_), channel_id=1, source_target_pairs={{0,2},{1,3},{2,0},{3,1},{4,6},{5,7},{6,4},{7,5},{8,10},{9,11},{10,... | collective-permute-start | bytes 786440 | tf_op jit(solution)/shard_map/ppermute | solution.py:20
  91.9 10.0 %collective-permute-start.28 = (bf16[4,128,256]{2,1,0:T(8,128)(2,1)S(1)}, bf16[4,128,256]{2,1,0:T(8,128)(2,1)S(1)}, u32[]{:S(2)}, u32[]{:S(2)}) collective-permute-start(bf16[4,128,256]{2,1,0:T(8,128)(2,1)S(1)} %get-tuple-element.54.refs_0_), channel_id=1, source_target_pairs={{0,4},{1,5},{2,6},{3,7},{4,0},{5,1},{6,2},{7,3},{8,12},{9,13},{10,... | collective-permute-start | bytes 786440 | tf_op jit(solution)/shard_map/ppermute | solution.py:20
  92.9 9.1 %collective-permute-start.31 = (bf16[144,256]{1,0:T(8,128)(2,1)S(1)}, bf16[144,256]{1,0:T(8,128)(2,1)S(1)}, u32[]{:S(2)}, u32[]{:S(2)}) collective-permute-start(bf16[144,256]{1,0:T(8,128)(2,1)S(1)} %get-tuple-element.55), channel_id=1, source_target_pairs={{0,6},{1,7},{2,4},{3,5},{4,2},{5,3},{6,0},{7,1},{8,14},{9,15},{10,... | collective-permute-start | bytes 221192 | tf_op jit(solution)/shard_map/ppermute | solution.py:20
  94.9 6.3 %collective-permute-start.30 = (bf16[128,256]{1,0:T(8,128)(2,1)S(1)}, bf16[128,256]{1,0:T(8,128)(2,1)S(1)}, u32[]{:S(2)}, u32[]{:S(2)}) collective-permute-start(bf16[128,256]{1,0:T(8,128)(2,1)S(1)} %collective-permute-done.26.refs_4_), channel_id=1, source_target_pairs={{0,16},{8,24},{16,0},{24,8},{1,17},{9,25},{17,1},{25,9},{2,18},{10... | collective-permute-start | bytes 196616 | tf_op jit(solution)/shard_map/ppermute | solution.py:20
  (12 other events, 55.7 us)
